TPU v7x, 32 devices: a whole 2x2x4 slice. The times are simulated.
32 devices in a mesh: grp: 4 (over x, core), blk: 8 (over z, y).
Axes of the slice: x: 2, y: 2, z: 4, core: 2. Of those that a mesh axis runs over, the one named last changes fastest.
Arguments:
- tokens: bfloat16 [8192, 768], P(('grp', 'blk')), may hold values from -6 to 6
- seg_ids: int32 [8192], P(('grp', 'blk')), may hold values from 0 to 1, as said below
- turn_ids: int32 [8192], P(('grp', 'blk')), may hold values from 0 to 8192, as said below
- prev_ids: int32 [8192], P(('grp', 'blk')), may hold values 0 or 1
- answer_table: bfloat16 [2, 768], replicated, may hold values from -3 to 3
- query_weight: bfloat16 [768, 768], replicated, may hold values from -0.21875 to 0.21875
- query_bias: bfloat16 [768], replicated, may hold values from -3 to 3
- key_weight: bfloat16 [768, 768], replicated, may hold values from -0.21875 to 0.21875
- value_weight: bfloat16 [768, 768], replicated, may hold values from -0.21875 to 0.21875
- value_bias: bfloat16 [768], replicated, may hold values from -3 to 3
- out_weight: bfloat16 [768, 768], replicated, may hold values from -3.5 to 3.5
- out_bias: bfloat16 [768], replicated, may hold values from -3 to 3
- norm_gain: bfloat16 [768], replicated, may hold values from 0.5 to 1.5
- norm_shift: bfloat16 [768], replicated, may hold values from -3 to 3
- up_weight: bfloat16 [768, 3072], replicated, may hold values from -0.21875 to 0.21875
- up_bias: bfloat16 [3072], replicated, may hold values from -3 to 3
- down_weight: bfloat16 [3072, 768], replicated, may hold values from -0.109375 to 0.109375
- down_bias: bfloat16 [768], replicated, may hold values from -3 to 3
- final_gain: bfloat16 [768], replicated, may hold values from 0.5 to 1.5
- final_shift: bfloat16 [768], replicated, may hold values from -3 to 3
- cotangent: bfloat16 [8192, 768], P(('grp', 'blk')), may hold values from -6 to 6
Outputs:
- mixed: bfloat16 [8192, 768], P(('grp', 'blk'))
- grad_tokens: float32 [8192, 768], P(('grp', 'blk'))
- grad_answer: float32 [2, 768], P(None, 'blk')
- grad_query_weight: float32 [768, 768], P('blk')
- grad_query_bias: float32 [768], P('blk')
- grad_key_weight: float32 [768, 768], P('blk')
- grad_value_weight: float32 [768, 768], P('blk')
- grad_value_bias: float32 [768], P('blk')
- grad_out_weight: float32 [768, 768], P('blk')
- grad_out_bias: float32 [768], P('blk')
- grad_norm_gain: float32 [768], P('blk')
- grad_norm_shift: float32 [768], P('blk')
- grad_up_weight: float32 [768, 3072], P('blk')
- grad_up_bias: float32 [3072], P('blk')
- grad_down_weight: float32 [3072, 768], P('blk')
- grad_down_bias: float32 [768], P('blk')
- grad_final_gain: float32 [768], P('blk')
- grad_final_shift: float32 [768], P('blk')
Inputs may be any that keep to these rules, and one draw needn't show every extreme that they name: `seg_ids`: in each aligned block of 256 tokens the table tokens (0) come first, at least 32 and at most 64 of them, followed by at least one question token; some block has exactly 64. `turn_ids`: 0 exactly on table tokens; the tokens of one question are contiguous, lie within one aligned block of 256 tokens and share one number, which no other question of the group carries.
All inputs are finite; a program needn't handle non-finite values. No bound on the sum of `prev_ids` on one device may be relied on, other than what follows from the above.
Results may differ from a plain program's by a relative error of at most 0.02.
Values may be sent and summed in bfloat16 or wider, within the bound.
No kernel may reach another device: no remote copies, remote signals or barrier semaphores. Data moves between devices by JAX's collectives and lax.ppermute only.
A program may use at most 384 MiB of HBM per device.

v0:
```python
import math

import jax
import jax.numpy as jnp
from jax import lax
from jax.sharding import PartitionSpec as P

HEADS = 12
HEAD_DIM = 64


far_below = -1e30


def row_norm(values, gain_vec, shift_vec):
    average = jnp.mean(values, axis=-1, keepdims=True)
    centred = values - average
    spread = jnp.mean(centred * centred, axis=-1, keepdims=True)
    return centred * lax.rsqrt(spread + 1e-06) * gain_vec + shift_vec


def exact_gelu(values):
    return jax.nn.gelu(values, approximate=False)


def outer_sum(left, right):
    return lax.dot_general(
        left, right, (((0,), (0,)), ((), ())), preferred_element_type=jnp.float32
    )


def back_dot(left, right):
    return lax.dot_general(
        left, right, (((1,), (1,)), ((), ())), preferred_element_type=jnp.float32
    )


def split_blocks(array, block_size):
    return array.reshape((array.shape[0] // block_size, block_size) + array.shape[1:])


def make_blocks(key_rows, value_rows, key_flag, key_turn):
    block_size = math.gcd(key_rows.shape[0], 2048)
    return tuple(
        (split_blocks(array, block_size) for array in (key_rows, value_rows, key_flag, key_turn))
    )


def block_scores(query_heads, block_args, query_turn, score_scale):
    key_block = block_args[0].reshape(block_args[0].shape[0], HEADS, HEAD_DIM)
    scores = (
        jnp.einsum("qhd,khd->hqk", query_heads, key_block, preferred_element_type=jnp.float32)
        * score_scale
    )
    allowed = (block_args[2] > 0)[None, :] | (query_turn[:, None] == block_args[3][None, :])
    return (scores, allowed)


def attend_forward(query_heads, stacked, query_turn, score_scale):
    row_count = query_heads.shape[0]

    def online_pass(state, block_args):
        running_max, running_sum, context = state
        scores, allowed = block_scores(query_heads, block_args, query_turn, score_scale)
        masked = jnp.where(allowed[None], scores, far_below)
        new_max = jnp.maximum(running_max, jnp.max(masked, axis=-1))
        weights = jnp.where(allowed[None], jnp.exp(masked - new_max[..., None]), 0.0)
        factor = jnp.exp(running_max - new_max)
        new_sum = running_sum * factor + jnp.sum(weights, axis=-1)
        value_block = block_args[1].reshape(block_args[1].shape[0], HEADS, HEAD_DIM)
        added = jnp.einsum(
            "hqk,khd->qhd",
            weights.astype(jnp.bfloat16),
            value_block,
            preferred_element_type=jnp.float32,
        )
        context = context * jnp.transpose(factor)[..., None] + added
        return ((new_max, new_sum, context), None)

    start_state = (
        jnp.full((HEADS, row_count), far_below, jnp.float32),
        jnp.zeros((HEADS, row_count), jnp.float32),
        jnp.zeros((row_count, HEADS, HEAD_DIM), jnp.float32),
    )
    top_score, total_weight, context = lax.scan(online_pass, start_state, stacked)[0]
    log_total = top_score + jnp.log(total_weight)
    context = context / jnp.transpose(total_weight)[..., None]
    return (context, log_total)


def attend_grads(
    block_args, query_heads, grad_context, log_total, row_dot, query_turn, score_scale
):
    scores, allowed = block_scores(query_heads, block_args, query_turn, score_scale)
    masked = jnp.where(allowed[None], scores, far_below)
    prob_full = jnp.where(allowed[None], jnp.exp(masked - log_total[..., None]), 0.0)
    value_block = block_args[1].reshape(block_args[1].shape[0], HEADS, HEAD_DIM)
    grad_probs = jnp.einsum(
        "qhd,khd->hqk", grad_context, value_block, preferred_element_type=jnp.float32
    )
    grad_scores = (prob_full * (grad_probs - row_dot[..., None])).astype(jnp.bfloat16)
    return (prob_full.astype(jnp.bfloat16), grad_scores)


def local(
    tokens,
    seg_ids,
    turn_ids,
    prev_ids,
    answer_table,
    query_weight,
    query_bias,
    key_weight,
    value_weight,
    value_bias,
    out_weight,
    out_bias,
    norm_gain,
    norm_shift,
    up_weight,
    up_bias,
    down_weight,
    down_bias,
    final_gain,
    final_shift,
    cotangent,
):
    row_count = tokens.shape[0]
    model_width = tokens.shape[1]
    score_scale = HEAD_DIM ** (-0.5)
    highest = lax.Precision.HIGHEST
    one_hot = (prev_ids[:, None] == jnp.arange(2)[None, :]).astype(jnp.float32)
    resid_in = tokens.astype(jnp.float32) + jnp.dot(
        one_hot, answer_table.astype(jnp.float32), precision=highest
    )
    layer_input = resid_in.astype(jnp.bfloat16)
    queries = (
        jnp.dot(layer_input, query_weight, preferred_element_type=jnp.float32)
        + query_bias.astype(jnp.float32)
    ).astype(jnp.bfloat16)
    key_rows = jnp.dot(layer_input, key_weight, preferred_element_type=jnp.float32).astype(
        jnp.bfloat16
    )
    value_rows = (
        jnp.dot(layer_input, value_weight, preferred_element_type=jnp.float32)
        + value_bias.astype(jnp.float32)
    ).astype(jnp.bfloat16)
    query_heads = queries.reshape(row_count, HEADS, HEAD_DIM)
    in_table = seg_ids == 0
    table_flag = in_table.astype(jnp.bfloat16)
    all_keys, all_values, all_flags = (
        lax.all_gather(key_rows, "blk", axis=0, tiled=True),
        lax.all_gather(value_rows, "blk", axis=0, tiled=True),
        lax.all_gather(table_flag, "blk", axis=0, tiled=True),
    )
    own_first = lax.axis_index("blk") * row_count
    all_turns = lax.dynamic_update_slice_in_dim(
        jnp.full((all_keys.shape[0],), -1, jnp.int32), turn_ids, own_first, 0
    )
    stacked = make_blocks(all_keys, all_values, all_flags, all_turns)
    context, log_total = attend_forward(query_heads, stacked, turn_ids, score_scale)
    context_low = context.reshape(row_count, model_width).astype(jnp.bfloat16)
    attn_out = jnp.dot(
        context_low, out_weight, preferred_element_type=jnp.float32
    ) + out_bias.astype(jnp.float32)
    middle, norm_back = jax.vjp(
        row_norm, resid_in + attn_out, norm_gain.astype(jnp.float32), norm_shift.astype(jnp.float32)
    )
    middle_low = middle.astype(jnp.bfloat16)
    pre_act = jnp.dot(middle_low, up_weight, preferred_element_type=jnp.float32) + up_bias.astype(
        jnp.float32
    )
    activated, gelu_back = jax.vjp(exact_gelu, pre_act)
    act_low = activated.astype(jnp.bfloat16)
    ffn_out = jnp.dot(act_low, down_weight, preferred_element_type=jnp.float32) + down_bias.astype(
        jnp.float32
    )
    final, final_back = jax.vjp(
        row_norm, middle + ffn_out, final_gain.astype(jnp.float32), final_shift.astype(jnp.float32)
    )
    mixed = final.astype(jnp.bfloat16)
    grad_final_sum, grad_final_gain, grad_final_shift = final_back(cotangent.astype(jnp.float32))
    grad_ffn = grad_final_sum.astype(jnp.bfloat16)
    grad_down_weight = outer_sum(act_low, grad_ffn)
    grad_down_bias = jnp.sum(grad_ffn.astype(jnp.float32), axis=0)
    grad_pre = gelu_back(back_dot(grad_ffn, down_weight))[0].astype(jnp.bfloat16)
    grad_up_weight = outer_sum(middle_low, grad_pre)
    grad_up_bias = jnp.sum(grad_pre.astype(jnp.float32), axis=0)
    grad_middle = grad_final_sum + back_dot(grad_pre, up_weight)
    grad_mid_sum, grad_norm_gain, grad_norm_shift = norm_back(grad_middle)
    grad_attn = grad_mid_sum.astype(jnp.bfloat16)
    grad_out_weight = outer_sum(context_low, grad_attn)
    grad_out_bias = jnp.sum(grad_attn.astype(jnp.float32), axis=0)
    grad_context = (
        back_dot(grad_attn, out_weight).astype(jnp.bfloat16).reshape(row_count, HEADS, HEAD_DIM)
    )
    row_dot = jnp.einsum("qhd,qhd->hq", grad_context.astype(jnp.float32), context)

    def grad_pass(grad_query, block_args):
        prob_low, grad_scores = attend_grads(
            block_args, query_heads, grad_context, log_total, row_dot, turn_ids, score_scale
        )
        key_block = block_args[0].reshape(block_args[0].shape[0], HEADS, HEAD_DIM)
        grad_query = grad_query + jnp.einsum(
            "hqk,khd->qhd", grad_scores, key_block, preferred_element_type=jnp.float32
        )
        grad_keys_block = (
            jnp.einsum("hqk,qhd->khd", grad_scores, query_heads, preferred_element_type=jnp.float32)
            * score_scale
        )
        grad_values_block = jnp.einsum(
            "hqk,qhd->khd", prob_low, grad_context, preferred_element_type=jnp.float32
        )
        block_rows = key_block.shape[0]
        joined = jnp.concatenate(
            [grad_keys_block.reshape(block_rows, -1), grad_values_block.reshape(block_rows, -1)],
            axis=1,
        )
        return (grad_query, joined)

    query_sum, stacked_grads = lax.scan(
        grad_pass, jnp.zeros((row_count, HEADS, HEAD_DIM), jnp.float32), stacked
    )
    joined_all = stacked_grads.reshape(all_keys.shape[0], 2 * model_width)
    grad_queries = (query_sum * score_scale).reshape(row_count, model_width).astype(jnp.bfloat16)
    key_value_grad = lax.psum_scatter(joined_all, "blk", scatter_dimension=0, tiled=True)
    grad_keys = key_value_grad[:, :model_width].astype(jnp.bfloat16)
    grad_values = key_value_grad[:, model_width:].astype(jnp.bfloat16)
    grad_query_weight = outer_sum(layer_input, grad_queries)
    grad_query_bias = jnp.sum(grad_queries.astype(jnp.float32), axis=0)
    grad_key_weight = outer_sum(layer_input, grad_keys)
    grad_value_weight = outer_sum(layer_input, grad_values)
    grad_value_bias = jnp.sum(grad_values.astype(jnp.float32), axis=0)
    grad_input = (
        grad_mid_sum
        + back_dot(grad_queries, query_weight)
        + back_dot(grad_keys, key_weight)
        + back_dot(grad_values, value_weight)
    )
    grad_answer = lax.dot_general(
        one_hot,
        grad_input,
        (((0,), (0,)), ((), ())),
        precision=highest,
        preferred_element_type=jnp.float32,
    )
    local_grads = (
        grad_answer,
        grad_query_weight,
        grad_query_bias,
        grad_key_weight,
        grad_value_weight,
        grad_value_bias,
        grad_out_weight,
        grad_out_bias,
        grad_norm_gain,
        grad_norm_shift,
        grad_up_weight,
        grad_up_bias,
        grad_down_weight,
        grad_down_bias,
        grad_final_gain,
        grad_final_shift,
    )
    shares = (
        lax.psum_scatter(local_grads[0], "blk", scatter_dimension=1, tiled=True),
        lax.psum_scatter(local_grads[1], "blk", scatter_dimension=0, tiled=True),
        lax.psum_scatter(local_grads[2], "blk", scatter_dimension=0, tiled=True),
        lax.psum_scatter(local_grads[3], "blk", scatter_dimension=0, tiled=True),
        lax.psum_scatter(local_grads[4], "blk", scatter_dimension=0, tiled=True),
        lax.psum_scatter(local_grads[5], "blk", scatter_dimension=0, tiled=True),
        lax.psum_scatter(local_grads[6], "blk", scatter_dimension=0, tiled=True),
        lax.psum_scatter(local_grads[7], "blk", scatter_dimension=0, tiled=True),
        lax.psum_scatter(local_grads[8], "blk", scatter_dimension=0, tiled=True),
        lax.psum_scatter(local_grads[9], "blk", scatter_dimension=0, tiled=True),
        lax.psum_scatter(local_grads[10], "blk", scatter_dimension=0, tiled=True),
        lax.psum_scatter(local_grads[11], "blk", scatter_dimension=0, tiled=True),
        lax.psum_scatter(local_grads[12], "blk", scatter_dimension=0, tiled=True),
        lax.psum_scatter(local_grads[13], "blk", scatter_dimension=0, tiled=True),
        lax.psum_scatter(local_grads[14], "blk", scatter_dimension=0, tiled=True),
        lax.psum_scatter(local_grads[15], "blk", scatter_dimension=0, tiled=True),
    )
    totals = (
        lax.psum(shares[0].astype(jnp.bfloat16), "grp").astype(jnp.float32),
        lax.psum(shares[1].astype(jnp.bfloat16), "grp").astype(jnp.float32),
        lax.psum(shares[2].astype(jnp.bfloat16), "grp").astype(jnp.float32),
        lax.psum(shares[3].astype(jnp.bfloat16), "grp").astype(jnp.float32),
        lax.psum(shares[4].astype(jnp.bfloat16), "grp").astype(jnp.float32),
        lax.psum(shares[5].astype(jnp.bfloat16), "grp").astype(jnp.float32),
        lax.psum(shares[6].astype(jnp.bfloat16), "grp").astype(jnp.float32),
        lax.psum(shares[7].astype(jnp.bfloat16), "grp").astype(jnp.float32),
        lax.psum(shares[8].astype(jnp.bfloat16), "grp").astype(jnp.float32),
        lax.psum(shares[9].astype(jnp.bfloat16), "grp").astype(jnp.float32),
        lax.psum(shares[10].astype(jnp.bfloat16), "grp").astype(jnp.float32),
        lax.psum(shares[11].astype(jnp.bfloat16), "grp").astype(jnp.float32),
        lax.psum(shares[12].astype(jnp.bfloat16), "grp").astype(jnp.float32),
        lax.psum(shares[13].astype(jnp.bfloat16), "grp").astype(jnp.float32),
        lax.psum(shares[14].astype(jnp.bfloat16), "grp").astype(jnp.float32),
        lax.psum(shares[15].astype(jnp.bfloat16), "grp").astype(jnp.float32),
    )
    return (
        mixed,
        grad_input,
        totals[0],
        totals[1],
        totals[2],
        totals[3],
        totals[4],
        totals[5],
        totals[6],
        totals[7],
        totals[8],
        totals[9],
        totals[10],
        totals[11],
        totals[12],
        totals[13],
        totals[14],
        totals[15],
    )


def solution(mesh):
    placed = (
        P(("grp", "blk"), None),
        P(("grp", "blk")),
        P(("grp", "blk")),
        P(("grp", "blk")),
        P(),
        P(),
        P(),
        P(),
        P(),
        P(),
        P(),
        P(),
        P(),
        P(),
        P(),
        P(),
        P(),
        P(),
        P(),
        P(),
        P(("grp", "blk"), None),
    )
    return jax.shard_map(
        local,
        mesh=mesh,
        in_specs=placed,
        out_specs=(
            P(("grp", "blk"), None),
            P(("grp", "blk"), None),
            P(None, "blk"),
            P("blk", None),
            P("blk"),
            P("blk", None),
            P("blk", None),
            P("blk"),
            P("blk", None),
            P("blk"),
            P("blk"),
            P("blk"),
            P("blk", None),
            P("blk"),
            P("blk", None),
            P("blk"),
            P("blk"),
            P("blk"),
        ),
        check_vma=False,
    )
```

profile of v0, /device:TPU:0, one launch (start us, length us, event | category | flops | bytes accessed | tf_op | source)
XLA Modules:
  0.0 1189.7 jit_solution(5813435795066377123)
XLA Ops:
  7.3 2.3 fusion.59
  9.7 2.5 convolution_convert_fusion.1
  13.7 22.3 %all-gather = bf16[8,1,256]{2,1,0:T(2,128)(2,1)S(1)} all-gather(bf16[1,1,256]{2,1,0:T(2,128)(2,1)S(1)} %reshape.238), channel_id=1, replica_groups=mesh['grp'=4,'blk'=8] {'blk'}, dimensions={0}, use_global_device_ids=true | all-gather | bytes 4608 | tf_op jit(solution)/shard_map/all_gather | solution.py:154
  36.1 1.8 fusion.24
  38.8 36.7 %all-gather.4.cloned.1.call-done = bf16[2048,768]{1,0:T(8,128)(2,1)} async-done(((bf16[256,768]{1,0:T(8,128)(2,1)}), bf16[2048,768]{1,0:T(8,128)(2,1)}) %all-gather.4.cloned.1.call-update) | async-done | bytes 3145744 | tf_op jit(solution)/shard_map/all_gather | solution.py:152
  75.5 4.7 copy.52
  80.2 12.5 %fusion.3 = (f32[12,256]{1,0:T(8,128)S(1)}, f32[12,256,2048]{2,1,0:T(8,128)}) fusion(pred[256,2048]{1,0:T(8,128)(4,1)S(1)} %compare_or_fusion, bf16[256,12,64]{0,2,1:T(8,128)(2,1)S(1)} %bitcast.82, bf16[2048,12,64]{0,2,1:T(8,128)(2,1)} %bitcast.78), kind=kOutput, calls=%fused_computation.7 | convolution fusion | flops 824177664 | bytes 29241344 | tf_op jit(solution)/shard_map/while/body/eval_jaxpr/qhd,khd->hqk/dot_general | solution.py:52
  92.7 12.0 %fusion = f32[12,256]{1,0:T(8,128)S(1)} fusion(f32[12,256,2048]{2,1,0:T(8,128)} %get-tuple-element.133, f32[12,256]{1,0:T(8,128)S(1)} %broadcast_maximum_fusion, pred[256,2048]{1,0:T(8,128)(4,1)S(1)} %compare_or_fusion), kind=kLoop, calls=%fused_computation.4 | loop fusion | flops 31454208 | bytes 25714688 | tf_op jit(solution)/shard_map/while/body/eval_jaxpr/reduce_sum | solution.py:69
  104.7 32.7 %all-gather.6.cloned.1.call-done = bf16[2048,768]{1,0:T(8,128)(2,1)} async-done(((bf16[256,768]{1,0:T(8,128)(2,1)}), bf16[2048,768]{1,0:T(8,128)(2,1)}) %all-gather.6.cloned.1.call-update) | async-done | bytes 3145744 | tf_op jit(solution)/shard_map/all_gather | solution.py:153
  137.4 4.7 copy.53
  142.1 13.7 %fusion.60 = (bf16[256,12,64]{0,2,1:T(8,128)(2,1)S(1)}, f32[256,12,64]{0,2,1:T(8,128)}) fusion(f32[256,12]{0,1:T(8,128)S(1)} %bitcast_add_fusion, bf16[2048,12,64]{0,2,1:T(8,128)(2,1)} %bitcast.86, f32[12,256,2048]{2,1,0:T(8,128)} %get-tuple-element.133, f32[12,256]{1,0:T(8,128)S(1)} %broadcast_maximum_fusion, pred[256,2048]{1,0:T(8,128)(4,1)S(1)} %compare_or_fusion, ...), kind=kOutput, calls=%fused_computation.124 | convolution fusion | flops 837353472 | bytes 30052352 | tf_op jit(solution)/shard_map/while/body/eval_jaxpr/hqk,khd->qhd/dot_general | solution.py:71
  156.7 10.4 multiply_convert_fusion.1
  170.6 2.2 convert_reduce_fusion
  172.9 1.7 multiply_reduce_fusion
  180.4 13.5 %fusion.4 = f32[12,64,2048]{2,1,0:T(8,128)} fusion(bf16[256,12,64]{0,2,1:T(8,128)(2,1)S(1)} %bitcast.89, f32[12,256,2048]{2,1,0:T(8,128)} %get-tuple-element.133, f32[12,256]{1,0:T(8,128)S(1)} %get-tuple-element.128, pred[256,2048]{1,0:T(8,128)(4,1)S(1)} %compare_or_fusion), kind=kOutput, calls=%fused_computation.9 | convolution fusion | flops 836763648 | bytes 32387072 | tf_op jit(solution)/shard_map/while/body/eval_jaxpr/hqk,qhd->khd/dot_general | solution.py:211
  194.0 18.5 %multiply_convert_fusion = bf16[12,256,2048]{2,1,0:T(8,128)(2,1)} fusion(f32[12,256,2048]{2,1,0:T(8,128)} %get-tuple-element.133, f32[12,256]{1,0:T(8,128)S(1)} %fusion.34, f32[12,256]{1,0:T(8,128)S(1)} %get-tuple-element.128, pred[256,2048]{1,0:T(8,128)(4,1)S(1)} %compare_or_fusion, bf16[256,12,64]{0,2,1:T(8,128)(2,1)S(1)} %bitcast.90, ...), kind=kOutput, calls=%fused_computation | convolution fusion | flops 849346560 | bytes 41836544 | tf_op jit(solution)/shard_map/while/body/eval_jaxpr/qhd,khd->hqk/dot_general | solution.py:98
  212.5 9.5 convolution_multiply_fusion
  222.0 11.4 pad_maximum_fusion
  233.6 9.5 convert_reduce_fusion.5
  243.2 1.9 fusion.63
  245.2 1.8 fusion.64
  247.1 6.6 fusion.53
  254.7 6.5 fusion.65
  261.3 178.6 %reduce-scatter.11.cloned.1.call-done = f32[256,1536]{0,1:T(8,128)} async-done(((f32[2048,1536]{0,1:T(8,128)}), f32[256,1536]{0,1:T(8,128)}) %reduce-scatter.11.cloned.1.call-update) | async-done | bytes 1572880 | tf_op jit(solution)/shard_map/reduce_scatter | solution.py:226
  441.3 1.9 fusion.36
  443.4 1.9 fusion.39
  445.4 1.9 convolution_add_fusion.3
  450.1 61.5 %reduce-scatter.13.cloned.1.call-done = f32[96,768]{1,0:T(8,128)} async-done(((f32[768,768]{1,0:T(8,128)}), f32[96,768]{1,0:T(8,128)}) %reduce-scatter.13.cloned.1.call-update) | async-done | bytes 294928 | tf_op jit(solution)/shard_map/reduce_scatter | solution.py:267
  511.6 1.6 convert_element_type.249
  513.3 69.7 %reduce-scatter.19.cloned.1.call-done = f32[96,768]{1,0:T(8,128)} async-done(((f32[768,768]{1,0:T(8,128)}), f32[96,768]{1,0:T(8,128)}) %reduce-scatter.19.cloned.1.call-update) | async-done | bytes 294928 | tf_op jit(solution)/shard_map/reduce_scatter | solution.py:272
  583.0 1.6 convert_element_type.261
  584.6 164.4 %reduce-scatter.21.cloned.1.call-done = f32[96,3072]{1,0:T(8,128)} async-done(((f32[768,3072]{1,0:T(8,128)}), f32[96,3072]{1,0:T(8,128)}) %reduce-scatter.21.cloned.1.call-update) | async-done | bytes 1179664 | tf_op jit(solution)/shard_map/reduce_scatter | solution.py:276
  749.0 2.2 convert_element_type.270
  751.1 164.1 %reduce-scatter.23.cloned.1.call-done = f32[384,768]{1,0:T(8,128)} async-done(((f32[3072,768]{1,0:T(8,128)}), f32[384,768]{1,0:T(8,128)}) %reduce-scatter.23.cloned.1.call-update) | async-done | bytes 1179664 | tf_op jit(solution)/shard_map/reduce_scatter | solution.py:278
  915.2 2.1 convert_element_type.275
  917.3 70.1 %reduce-scatter.15.cloned.1.call-done = f32[96,768]{1,0:T(8,128)} async-done(((f32[768,768]{1,0:T(8,128)}), f32[96,768]{1,0:T(8,128)}) %reduce-scatter.15.cloned.1.call-update) | async-done | bytes 294928 | tf_op jit(solution)/shard_map/reduce_scatter | solution.py:269
  987.4 1.6 convert_element_type.254
  989.0 70.2 %reduce-scatter.17.cloned.1.call-done = f32[96,768]{1,0:T(8,128)} async-done(((f32[768,768]{1,0:T(8,128)}), f32[96,768]{1,0:T(8,128)}) %reduce-scatter.17.cloned.1.call-update) | async-done | bytes 294928 | tf_op jit(solution)/shard_map/reduce_scatter | solution.py:270
  1059.2 1.6 convert_element_type.256
  1063.0 35.4 %all-reduce.9 = (bf16[768]{0:T(1024)(128)(2,1)S(1)}, bf16[768]{0:T(1024)(128)(2,1)S(1)}, bf16[768]{0:T(1024)(128)(2,1)S(1)}, bf16[768]{0:T(1024)(128)(2,1)S(1)},...) all-reduce(f32[768]{0:T(1024)S(1)} %reduce_sum.210, ...), channel_id=5, replica_groups=mesh['grp'=4,'blk'=8] {'blk'}, use_global_device_ids=true, to_apply=%region_16.17.clone | all-reduce | flops 9216 | bytes 55296
  1099.1 23.7 %reduce-scatter.25.cloned.1.call-done = f32[96,2]{1,0:T(8,128)} async-done(((f32[768,2]{1,0:T(8,128)}), f32[96,2]{1,0:T(8,128)}) %reduce-scatter.25.cloned.1.call-update) | async-done | bytes 784
  1123.7 5.7 all-reduce.10
  1134.7 38.1 %all-reduce.14.cloned.1.call-done = (bf16[96,768]{1,0:T(8,128)(2,1)}, bf16[96,768]{1,0:T(8,128)(2,1)}, bf16[96,768]{1,0:T(8,128)(2,1)}, bf16[96,768]{1,0:T(8,128...) async-done(((bf16[96,768]{1,0:T(8,128)(2,1)}, bf16[96,768]{1,0:T(8,128)(2,1)}, bf16[96,768]{1,0:T(8,128)(2,1)}, bf16[96,768]{1,0:T(8,128)(2,1)}, ...) | async-done | bytes 1769488 | tf_op jit(solution)/shard_map/psum | solution.py:285
  1172.8 1.7 convert_element_type.250
  1174.5 1.6 convert_element_type.255
  1176.2 1.6 convert_element_type.257
  1177.8 1.6 convert_element_type.262
  1179.4 2.2 convert_element_type.271
  (165 shorter events, 27.0 us)
Async XLA Ops:
  7.2 148.7 %copy-start = (bf16[768,768]{1,0:T(8,128)(2,1)S(1)}, bf16[768,768]{1,0:T(8,128)(2,1)}, u32[]{:S(2)}) copy-start(bf16[768,768]{1,0:T(8,128)(2,1)} %param.31) | copy-start | bytes 3538948
  7.2 5.1 copy-start.22
  7.2 5.1 copy-start.16
  7.2 6.4 copy-start.23
  7.2 6.4 copy-start.19
  7.3 6.4 copy-start.24
  7.3 6.4 copy-start.30
  7.3 28.8 %copy-start.25 = (bf16[768]{0:T(1024)(128)(2,1)S(1)}, bf16[768]{0:T(1024)(128)(2,1)}, u32[]{:S(2)}) copy-start(bf16[768]{0:T(1024)(128)(2,1)} %param.27) | copy-start | bytes 4612
  7.3 68.2 %all-gather.4.cloned.1.call-start = ((), (), s32[]{:S(2)}) async-start(), calls=%async_computation.8 | async-start | bytes 3538944 | tf_op jit(solution)/shard_map/all_gather | solution.py:152
  12.2 25.9 %copy-start.26 = (bf16[768]{0:T(1024)(128)(2,1)S(1)}, bf16[768]{0:T(1024)(128)(2,1)}, u32[]{:S(2)}) copy-start(bf16[768]{0:T(1024)(128)(2,1)} %param.34) | copy-start | bytes 4612
  12.2 25.9 %copy-start.27 = (bf16[768]{0:T(1024)(128)(2,1)S(1)}, bf16[768]{0:T(1024)(128)(2,1)}, u32[]{:S(2)}) copy-start(bf16[768]{0:T(1024)(128)(2,1)} %param.33) | copy-start | bytes 4612
  12.2 25.9 %copy-start.28 = (bf16[768]{0:T(1024)(128)(2,1)S(1)}, bf16[768]{0:T(1024)(128)(2,1)}, u32[]{:S(2)}) copy-start(bf16[768]{0:T(1024)(128)(2,1)} %param.39) | copy-start | bytes 4612
  12.2 25.9 %copy-start.29 = (bf16[768]{0:T(1024)(128)(2,1)S(1)}, bf16[768]{0:T(1024)(128)(2,1)}, u32[]{:S(2)}) copy-start(bf16[768]{0:T(1024)(128)(2,1)} %param.40) | copy-start | bytes 4612
  12.2 26.0 %copy-start.20 = (s32[256]{0:T(256)S(1)}, s32[256]{0:T(256)}, u32[]{:S(2)}) copy-start(s32[256]{0:T(256)} %param.23) | copy-start | bytes 3076
  12.2 125.2 %all-gather.6.cloned.1.call-start = ((), (), s32[]{:S(2)}) async-start(), calls=%async_computation.9 | async-start | bytes 3538944 | tf_op jit(solution)/shard_map/all_gather | solution.py:153
  13.5 426.3 %reduce-scatter.11.cloned.1.call-start = ((), (), s32[]{:S(2)}) async-start(), calls=%async_computation.10 | async-start | bytes 14155776 | tf_op jit(solution)/shard_map/reduce_scatter | solution.py:226
  142.1 13.7 %copy-start.7 = (f32[256,768]{1,0:T(8,128)S(1)}, f32[256,768]{1,0:T(8,128)}, u32[]{:S(2)}) copy-start(f32[256,768]{1,0:T(8,128)} %get-tuple-element.131) | copy-start | bytes 2359300
  155.8 11.3 copy-start.13
  155.9 11.3 slice-start
  156.7 10.4 slice-start.1
  167.1 1.6 copy-start.9
  167.2 1.8 copy-start.12
  169.3 3.5 slice-start.2
  170.6 2.2 copy-start.10
  170.6 2.2 slice-start.3
  172.9 1.8 copy-start.15
  175.0 0.9 copy-start.2
  176.0 0.7 copy-start.5
  233.3 278.3 %reduce-scatter.13.cloned.1.call-start = ((), (), s32[]{:S(2)}) async-start(), calls=%async_computation.11 | async-start | bytes 2654208 | tf_op jit(solution)/shard_map/reduce_scatter | solution.py:267
  243.2 2.0 copy-start.6
  243.2 2.0 copy-start.14
  245.1 337.8 %reduce-scatter.19.cloned.1.call-start = ((), (), s32[]{:S(2)}) async-start(), calls=%async_computation.14 | async-start | bytes 2654208 | tf_op jit(solution)/shard_map/reduce_scatter | solution.py:272
  247.1 501.9 %reduce-scatter.21.cloned.1.call-start = ((), (), s32[]{:S(2)}) async-start(), calls=%async_computation.15 | async-start | bytes 10616832 | tf_op jit(solution)/shard_map/reduce_scatter | solution.py:276
  253.7 1.0 copy-start.11
  253.7 661.5 %reduce-scatter.23.cloned.1.call-start = ((), (), s32[]{:S(2)}) async-start(), calls=%async_computation.16 | async-start | bytes 10616832 | tf_op jit(solution)/shard_map/reduce_scatter | solution.py:278
  261.2 726.2 %reduce-scatter.15.cloned.1.call-start = ((), (), s32[]{:S(2)}) async-start(), calls=%async_computation.12 | async-start | bytes 2654208 | tf_op jit(solution)/shard_map/reduce_scatter | solution.py:269
  443.3 2.0 copy-start.3
  443.3 615.9 %reduce-scatter.17.cloned.1.call-start = ((), (), s32[]{:S(2)}) async-start(), calls=%async_computation.13 | async-start | bytes 2654208 | tf_op jit(solution)/shard_map/reduce_scatter | solution.py:270
  445.3 2.0 copy-start.4
  445.3 677.6 %reduce-scatter.25.cloned.1.call-start = ((), (), s32[]{:S(2)}) async-start(), calls=%async_computation.17 | async-start | bytes 442368
  445.4 2.5 copy-start.17
  447.3 1.1 copy-start.21
  448.4 540.6 %copy-start.8 = (f32[256,768]{1,0:T(8,128)}, f32[256,768]{1,0:T(8,128)S(1)}, u32[]{:S(2)}) copy-start(f32[256,768]{1,0:T(8,128)S(1)} %convolution_add_fusion.1) | copy-start | bytes 2359300
  450.1 722.8 %all-reduce.14.cloned.1.call-start = ((), (), s32[]{:S(2)}) async-start(), calls=%async_computation.18 | async-start | bytes 3538944 | tf_op jit(solution)/shard_map/psum | solution.py:285
  584.6 476.3 %copy-start.31 = (u32[32]{0:T(128)S(1)}, u32[32]{0:T(128)}, u32[]{:S(2)}) copy-start(u32[32]{0:T(128)} %constant.150) | copy-start | bytes 388
  1060.9 121.9 %copy-start.1 = (bf16[768,768]{1,0:T(8,128)(2,1)S(1)}, bf16[768,768]{1,0:T(8,128)(2,1)}, u32[]{:S(2)}) copy-start(bf16[768,768]{1,0:T(8,128)(2,1)} %param.31) | copy-start | bytes 3538948
  1172.8 8.8 copy-start.18
Sparse Core Ops, SparseCore 0:
  12.3 63.1 all-gather.3
  78.3 59.0 all-gather.5
  233.5 206.3 reduce-scatter.10
  443.2 68.3 reduce-scatter.12
  515.0 67.9 reduce-scatter.18
  586.4 162.5 reduce-scatter.20
  752.6 162.5 reduce-scatter.22
  918.7 68.6 reduce-scatter.14
  990.9 68.2 reduce-scatter.16
  1062.3 60.4 reduce-scatter.24
  1126.8 45.9 all-reduce.13
where the time goes:
time: 1200 us; the launch traced here: 1190 us
  waiting for transfers between devices  910 us (76%)
  matrix products  128 us (11%)
  blocking collectives  63.5 us (5%)
  other arithmetic  55.4 us (5%)
  between operations  16.4 us (1%)
  local copies, waits for them, and re-layouts  15.9 us (1%)
    reduce_scatter x1, waiting for transfers between devices, local(): lax.psum_scatter(joined_all, 'blk', scatter_dimension=0, tiled=True)  179 us
    reduce_scatter x1, waiting for transfers between devices, local(): lax.psum_scatter(local_grads[10], 'blk', scatter_dimension=0, tiled=True)  164 us
    reduce_scatter x1, waiting for transfers between devices, local(): lax.psum_scatter(local_grads[12], 'blk', scatter_dimension=0, tiled=True)  164 us
    reduce_scatter x1, waiting for transfers between devices, local(): lax.psum_scatter(local_grads[4], 'blk', scatter_dimension=0, tiled=True)  70.2 us
    reduce_scatter x1, waiting for transfers between devices, local(): lax.psum_scatter(local_grads[3], 'blk', scatter_dimension=0, tiled=True)  70.1 us
    reduce_scatter x1, waiting for transfers between devices, local(): lax.psum_scatter(local_grads[6], 'blk', scatter_dimension=0, tiled=True)  69.7 us
    reduce_scatter x1, waiting for transfers between devices, local(): lax.psum_scatter(local_grads[1], 'blk', scatter_dimension=0, tiled=True)  61.5 us
    psum x1, waiting for transfers between devices, local(): lax.psum(shares[1].astype(jnp.bfloat16), 'grp').astype(jnp.float32)  38.1 us
  transfers between devices with their start and end apart: 11, of which 11 were waited for; matrix products, arithmetic and copies ran while one was open for 7% of the time, Pallas kernels for 0%

commit v1 on v0

v1 whole, which is shorter than its diff:
```python
import math

import jax
import jax.numpy as jnp
from jax import lax
from jax.sharding import PartitionSpec as P

HEADS = 12
HEAD_DIM = 64
TAB_MAX = 64
far_below = -1e30
BF = jnp.bfloat16
F32 = jnp.float32


def outer_sum(left, right):
    return lax.dot_general(left, right, (((0,), (0,)), ((), ())), preferred_element_type=F32)


def back_dot(left, right):
    return lax.dot_general(left, right, (((1,), (1,)), ((), ())), preferred_element_type=F32)


def fwd_dot(left, right):
    return jnp.dot(left, right, preferred_element_type=F32)


def norm_parts(values):
    centred = values - jnp.mean(values, axis=-1, keepdims=True)
    spread = jnp.mean(centred * centred, axis=-1, keepdims=True)
    inv = lax.rsqrt(spread + 1e-06)
    return centred * inv, inv


def norm_grad(grad, normed, inv, gain):
    scaled = grad * gain
    return inv * (
        scaled
        - jnp.mean(scaled, axis=-1, keepdims=True)
        - normed * jnp.mean(scaled * normed, axis=-1, keepdims=True)
    )


def local(
    tokens, seg_ids, turn_ids, prev_ids, answer_table, query_weight, query_bias,
    key_weight, value_weight, value_bias, out_weight, out_bias, norm_gain, norm_shift,
    up_weight, up_bias, down_weight, down_bias, final_gain, final_shift, cotangent,
):
    rows, width = tokens.shape
    blocks = lax.axis_size("blk")
    grps = lax.axis_size("grp")
    tab = TAB_MAX
    scale = HEAD_DIM ** (-0.5)
    f = lambda v: v.astype(F32)
    is_one = (prev_ids == 1)[:, None]
    answers = f(answer_table)
    resid_in = f(tokens) + jnp.where(is_one, answers[1][None], answers[0][None])
    layer_input = resid_in.astype(BF)
    flags = jnp.concatenate(
        [(seg_ids[:tab] == 0).astype(BF), jnp.zeros((128 - tab,), BF), prev_ids[:tab].astype(BF),
         jnp.zeros((width - 128 - tab,), BF)]
    )[None]
    payload = jnp.concatenate([layer_input[:tab], flags, jnp.zeros((7, width), BF)], axis=0)
    gathered = lax.all_gather(payload, "blk", axis=0, tiled=False)
    table_input = gathered[:, :tab].reshape(blocks * tab, width)
    table_open = gathered[:, tab, :tab].reshape(blocks * tab) > 0.5
    table_prev = gathered[:, tab, 128 : 128 + tab].reshape(blocks * tab)

    qkv_in = jnp.concatenate([table_input, layer_input], axis=0)
    queries = (fwd_dot(layer_input, query_weight) + f(query_bias)).astype(BF)
    keys = fwd_dot(qkv_in, key_weight).astype(BF)
    values = (fwd_dot(qkv_in, value_weight) + f(value_bias)).astype(BF)
    n_keys = keys.shape[0]
    own_open = (turn_ids[:, None] == turn_ids[None, :]) & (seg_ids != 0)[None, :]
    allowed = jnp.concatenate(
        [jnp.broadcast_to(table_open[None], (rows, blocks * tab)), own_open], axis=1
    )[None]
    qh = queries.reshape(rows, HEADS, HEAD_DIM)
    kh = keys.reshape(n_keys, HEADS, HEAD_DIM)
    vh = values.reshape(n_keys, HEADS, HEAD_DIM)
    scores = jnp.einsum("qhd,khd->hqk", qh, kh, preferred_element_type=F32) * scale
    scores = jnp.where(allowed, scores, far_below)
    top = jnp.max(scores, axis=-1, keepdims=True)
    weights = jnp.where(allowed, jnp.exp(scores - top), 0.0)
    prob_full = weights / jnp.sum(weights, axis=-1, keepdims=True)
    prob_low = prob_full.astype(BF)
    context = jnp.einsum("hqk,khd->qhd", prob_low, vh, preferred_element_type=F32)
    context_low = context.reshape(rows, width).astype(BF)

    first_in = resid_in + fwd_dot(context_low, out_weight) + f(out_bias)
    normed1, inv1 = norm_parts(first_in)
    middle = normed1 * f(norm_gain) + f(norm_shift)
    middle_low = middle.astype(BF)
    pre_act = fwd_dot(middle_low, up_weight) + f(up_bias)
    cdf = 0.5 * (1.0 + lax.erf(pre_act * (0.5**0.5)))
    act_low = (pre_act * cdf).astype(BF)
    gelu_slope = cdf + pre_act * jnp.exp(-0.5 * pre_act * pre_act) * (1.0 / math.sqrt(2 * math.pi))
    second_in = middle + fwd_dot(act_low, down_weight) + f(down_bias)
    normed2, inv2 = norm_parts(second_in)
    mixed = (normed2 * f(final_gain) + f(final_shift)).astype(BF)
    cot = f(cotangent)
    grad_final_sum = norm_grad(cot, normed2, inv2, f(final_gain))
    grad_ffn = grad_final_sum.astype(BF)
    grad_down_weight = outer_sum(act_low, grad_ffn).astype(BF)
    grad_pre = (back_dot(grad_ffn, down_weight) * gelu_slope).astype(BF)
    grad_up_weight = outer_sum(middle_low, grad_pre).astype(BF)

    def share(value):
        part = lax.psum_scatter(value, ("blk", "grp"), scatter_dimension=0, tiled=True)
        return f(lax.all_gather(part, "grp", axis=0, tiled=True))

    out_down = share(grad_down_weight)
    out_up = share(grad_up_weight)

    grad_middle = grad_final_sum + back_dot(grad_pre, up_weight)
    grad_mid_sum = norm_grad(grad_middle, normed1, inv1, f(norm_gain))
    grad_attn = grad_mid_sum.astype(BF)
    grad_out_weight = outer_sum(context_low, grad_attn).astype(BF)
    grad_context = back_dot(grad_attn, out_weight).astype(BF).reshape(rows, HEADS, HEAD_DIM)
    row_dot = jnp.einsum("qhd,qhd->hq", f(grad_context), context)
    grad_probs = jnp.einsum("qhd,khd->hqk", grad_context, vh, preferred_element_type=F32)
    grad_scores = (prob_full * (grad_probs - row_dot[..., None])).astype(BF)
    grad_queries = (
        (jnp.einsum("hqk,khd->qhd", grad_scores, kh, preferred_element_type=F32) * scale)
        .reshape(rows, width)
        .astype(BF)
    )
    grad_keys = (
        (jnp.einsum("hqk,qhd->khd", grad_scores, qh, preferred_element_type=F32) * scale)
        .reshape(n_keys, width)
        .astype(BF)
    )
    grad_values = (
        jnp.einsum("hqk,qhd->khd", prob_low, grad_context, preferred_element_type=F32)
        .reshape(n_keys, width)
        .astype(BF)
    )
    grad_kv_in = back_dot(grad_keys, key_weight) + back_dot(grad_values, value_weight)
    grad_table = grad_kv_in[: blocks * tab]
    table_share = lax.psum_scatter(grad_table.astype(BF), "blk", scatter_dimension=0, tiled=True)
    grad_query_weight = outer_sum(layer_input, grad_queries).astype(BF)
    grad_key_weight = outer_sum(qkv_in, grad_keys).astype(BF)
    grad_value_weight = outer_sum(qkv_in, grad_values).astype(BF)
    n_out = width // blocks
    stacked = jnp.stack(
        [grad_query_weight, grad_key_weight, grad_value_weight, grad_out_weight], axis=0
    ).reshape(4, blocks, grps, n_out // grps, width)
    stacked = jnp.transpose(stacked, (1, 2, 0, 3, 4)).reshape(blocks * grps * 4, n_out // grps, width)
    square = lax.psum_scatter(stacked, ("blk", "grp"), scatter_dimension=0, tiled=True)
    square = lax.all_gather(square, "grp", axis=1, tiled=True)

    grad_input_local = grad_mid_sum + back_dot(grad_queries, query_weight) + grad_kv_in[blocks * tab :]
    all_prev = jnp.concatenate([table_prev, prev_ids.astype(BF)])
    all_grads = jnp.concatenate([grad_table, grad_input_local], axis=0)
    total_sum = jnp.sum(all_grads, axis=0)
    one_sum = jnp.sum(jnp.where(all_prev[:, None] > 0.5, all_grads, 0.0), axis=0)
    column_sum = lambda v: jnp.sum(f(v), axis=0)
    vectors = jnp.stack(
        [
            total_sum - one_sum,
            one_sum,
            column_sum(grad_queries),
            column_sum(grad_values),
            column_sum(grad_attn),
            jnp.sum(grad_middle * normed1, axis=0),
            jnp.sum(grad_middle, axis=0),
            column_sum(grad_ffn),
            jnp.sum(cot * normed2, axis=0),
            jnp.sum(cot, axis=0),
        ]
        + list(column_sum(grad_pre).reshape(-1, width)),
        axis=0,
    )
    vectors = lax.psum(vectors, ("blk", "grp"))
    own = lax.axis_index("blk")
    mine = lax.dynamic_slice_in_dim(vectors[:10], own * n_out, n_out, 1)
    ff_out = up_weight.shape[1] // blocks
    up_bias_out = lax.dynamic_slice_in_dim(vectors[10:].reshape(-1), own * ff_out, ff_out, 0)
    grad_input = grad_input_local.at[:tab].add(f(table_share))
    return (
        mixed,
        grad_input,
        mine[:2],
        f(square[0]),
        mine[2],
        f(square[1]),
        f(square[2]),
        mine[3],
        f(square[3]),
        mine[4],
        mine[5],
        mine[6],
        out_up,
        up_bias_out,
        out_down,
        mine[7],
        mine[8],
        mine[9],
    )


def solution(mesh):
    both = ("grp", "blk")
    placed = (P(both, None), P(both), P(both), P(both)) + (P(),) * 16 + (P(both, None),)
    vec, mat = P("blk"), P("blk", None)
    return jax.shard_map(
        local,
        mesh=mesh,
        in_specs=placed,
        out_specs=(
            P(both, None), P(both, None), P(None, "blk"), mat, vec, mat, mat, vec, mat, vec,
            vec, vec, mat, vec, mat, vec, vec, vec,
        ),
        check_vma=False,
    )
```

time: 1200 us -> 524 us (0.44)
  waiting for transfers between devices: 910 us -> 299 us
  matrix products: 128 us -> 58.6 us
  blocking collectives: 63.5 us -> 97.3 us
  other arithmetic: 55.4 us -> 25.4 us
    reduce_scatter x7 -> x4, waiting for transfers between devices: 778 us -> 299 us  [the longest x2 196 us: share(): lax.psum_scatter(value, ('blk', 'grp'), scatter_dimension=0, tiled=True)]
    dot_general x13 -> x11, matrix products: 97.6 us -> 27.2 us  [the longest x6 11.7 us: fwd_dot(): return jnp.dot(left, right, preferred_element_type=F32)]
    all_gather x2 -> x0, waiting for transfers between devices: 69.4 us -> none  [the longest x1 36.7 us: local(): lax.all_gather(key_rows, 'blk', axis=0, tiled=True)]
    psum x1 -> x0, waiting for transfers between devices: 38.1 us -> none  [local(): lax.psum(shares[1].astype(jnp.bfloat16), 'grp').astype(jnp.float32)]
    unnamed x1 -> x0, blocking collectives: 35.4 us -> none
    all_gather x1 -> x4, blocking collectives: 22.3 us -> 57.1 us  [the longest x1 34.1 us: local(): gathered = lax.all_gather(payload, 'blk', axis=0, tiled=False)]
    psum x1, blocking collectives: 5.75 us -> 40.2 us  [local(): vectors = lax.psum(vectors, ('blk', 'grp'))]
    unnamed x12 -> x4, waiting for transfers between devices: 23.9 us -> 0.07 us
  transfers between devices with their start and end apart: 11 -> 4, of which waited for: 11 -> 3; matrix products, arithmetic and copies ran while one was open for 7% -> 8% of each run, Pallas kernels for 0% -> 0%
where the time goes in v1:
time: 524 us; the launch traced here: 523 us
  waiting for transfers between devices  299 us (57%)
  blocking collectives  97.3 us (19%)
  matrix products  58.6 us (11%)
  local copies, waits for them, and re-layouts  27.9 us (5%)
  other arithmetic  25.4 us (5%)
  between operations  14.8 us (3%)
    reduce_scatter x2, waiting for transfers between devices, share(): lax.psum_scatter(value, ('blk', 'grp'), scatter_dimension=0, tiled=True)  196 us
    reduce_scatter x1, waiting for transfers between devices, local(): lax.psum_scatter(stacked, ('blk', 'grp'), scatter_dimension=0, tiled=True)  103 us
    psum x1, blocking collectives, local(): vectors = lax.psum(vectors, ('blk', 'grp'))  40.2 us
    all_gather x1, blocking collectives, local(): gathered = lax.all_gather(payload, 'blk', axis=0, tiled=False)  34.1 us
    all_gather x2, blocking collectives, share(): return f(lax.all_gather(part, 'grp', axis=0, tiled=True))  15.4 us
    dot_general x6, matrix products, outer_sum(): lax.dot_general(left, right, (((0,), (0,)), ((), ())), preferred_element_...  13.9 us
    dot_general x6, matrix products, fwd_dot(): return jnp.dot(left, right, preferred_element_type=F32)  11.7 us
  transfers between devices with their start and end apart: 4, of which 3 were waited for; matrix products, arithmetic and copies ran while one was open for 8% of the time, Pallas kernels for 0%

profile of v1, /device:TPU:0, one launch (start us, length us, event | category | flops | bytes accessed | tf_op | source)
XLA Modules:
  0.0 523.3 jit_solution(8078548345063149485)
XLA Ops:
  8.9 1.2 broadcast_compare_fusion
  11.6 1.2 fusion.27
  13.0 34.1 %all-gather = bf16[576,768]{1,0:T(8,128)(2,1)S(1)} all-gather(bf16[72,768]{1,0:T(8,128)(2,1)S(1)} %maximum_maximum_fusion), channel_id=2, replica_groups=mesh['grp'=4,'blk'=8] {'blk'}, dimensions={0}, use_global_device_ids=true | all-gather | bytes 995328 | tf_op jit(solution)/shard_map/all_gather | solution.py:64
  47.0 1.2 slice_reduce_fusion
  51.5 1.2 fusion.15
  52.7 1.2 copy.45
  55.7 2.1 convolution_convert_fusion.7
  57.8 2.2 add_convert_fusion
  60.0 8.9 %fusion.44 = (f32[12,256]{1,0:T(8,128)S(1)}, f32[12,256,768]{2,1,0:T(8,128)}) fusion(pred[256,768]{1,0:T(8,128)(4,1)S(1)} %pad_add_fusion, bf16[256,12,64]{0,2,1:T(8,128)(2,1)S(1)} %bitcast.128, bf16[768,12,64]{0,2,1:T(8,128)(2,1)} %bitcast.134), kind=kOutput, calls=%fused_computation.128 | convolution fusion | flops 313787136 | bytes 11218944 | tf_op jit(solution)/shard_map/sub | solution.py:84
  68.9 4.3 fusion.6
  73.2 1.5 bitcast_convert_fusion
  76.6 4.0 multiply_convert_fusion.1
  80.7 1.5 fusion.46
  82.5 1.0 fusion.25
  83.5 1.7 convert_reduce_fusion.3
  85.2 3.0 convert_reduce_fusion
  88.2 2.2 multiply_reduce_fusion
  93.0 3.4 convert_reduce_fusion.1
  96.5 5.2 multiply_convert_fusion
  101.7 0.9 multiply_convert_fusion.2
  102.7 1.2 copy-done.2
  103.9 1.1 fusion.48
  105.6 1.1 convolution_add_fusion.1
  106.7 1.0 slice.162
  107.8 5.4 %convolution_convert_fusion.1 = bf16[768,3072]{1,0:T(8,128)(2,1)} fusion(bf16[256,3072]{1,0:T(8,128)(2,1)} %copy-done.19, f32[256,768]{1,0:T(8,128)} %copy-done.6, f32[768]{0:T(1024)S(1)} %convert_element_type.207, f32[768]{0:T(1024)S(1)} %convert_element_type.206, f32[256]{0:T(256)} %copy-done.36, f32[256]{0:T(256)} %copy-done.32), kind=kOutput, calls=%fused_computation.6 | convolution fusion | flops 1211301888 | bytes 7086080 | tf_op jit(solution)/shard_map/dot_general | solution.py:17
  113.3 4.4 convert_reduce_fusion.5
  119.5 1.1 convolution_convert_fusion.4
  120.8 1.1 convolution_convert_fusion.3
  122.6 2.8 copy.48
  125.4 5.3 %convolution_convert_fusion = bf16[3072,768]{1,0:T(8,128)(2,1)} fusion(bf16[256,3072]{1,0:T(8,128)(2,1)} %copy-done.10, f32[256,768]{1,0:T(8,128)} %copy-done.13), kind=kOutput, calls=%fused_computation.5 | convolution fusion | flops 1210515456 | bytes 7077888 | tf_op jit(solution)/shard_map/dot_general | solution.py:17
  130.8 1.3 concatenate.31
  132.1 1.3 stack.50
  133.4 1.3 stack.51
  134.6 1.3 stack.49
  139.1 1.3 stack.47
  140.3 1.3 stack.46
  141.6 1.3 stack.48
  147.5 40.2 %psum.7 = f32[14,768]{1,0:T(8,128)S(1)} all-reduce(f32[14,768]{1,0:T(8,128)S(1)} %stack.52), channel_id=1, replica_groups=mesh['grp'=4,'blk'=8] {'blk','grp'}, use_global_device_ids=true, to_apply=%region_23.24 | all-reduce | flops 10752 | bytes 86016 | tf_op jit(solution)/shard_map/psum | solution.py:174
  189.6 1.7 fusion.29
  191.3 92.6 %reduce-scatter.9.cloned.1.call-done = bf16[24,3072]{1,0:T(8,128)(2,1)} async-done(((bf16[768,3072]{1,0:T(8,128)(2,1)}), bf16[24,3072]{1,0:T(8,128)(2,1)}) %reduce-scatter.9.cloned.1.call-update) | async-done | bytes 147472 | tf_op jit(solution)/shard_map/reduce_scatter | solution.py:109
  284.0 7.7 %all_gather.18 = bf16[96,3072]{1,0:T(8,128)(2,1)S(1)} all-gather(bf16[24,3072]{1,0:T(8,128)(2,1)} %reduce-scatter.9.cloned.1.call-done), channel_id=1, replica_groups=mesh['grp'=4,'blk'=8] {'grp'}, dimensions={0}, use_global_device_ids=true | all-gather | bytes 737280 | tf_op jit(solution)/shard_map/all_gather | solution.py:110
  291.6 1.1 convert_element_type.250
  292.7 102.8 %reduce-scatter.7.cloned.1.call-done = bf16[4,24,768]{2,1,0:T(8,128)(2,1)} async-done(((bf16[128,24,768]{2,1,0:T(8,128)(2,1)}), bf16[4,24,768]{2,1,0:T(8,128)(2,1)}) %reduce-scatter.7.cloned.1.call-update) | async-done | bytes 147472 | tf_op jit(solution)/shard_map/reduce_scatter | solution.py:149
  395.6 7.7 %all_gather.17 = bf16[4,96,768]{2,1,0:T(8,128)(2,1)S(1)} all-gather(bf16[4,24,768]{2,1,0:T(8,128)(2,1)} %reduce-scatter.7.cloned.1.call-done), channel_id=1, replica_groups=mesh['grp'=4,'blk'=8] {'grp'}, dimensions={1}, use_global_device_ids=true | all-gather | bytes 737280 | tf_op jit(solution)/shard_map/all_gather | solution.py:150
  403.3 1.0 fusion.30
  404.3 103.6 %reduce-scatter.11.cloned.1.call-done = bf16[96,768]{1,0:T(8,128)(2,1)} async-done(((bf16[3072,768]{1,0:T(8,128)(2,1)}), bf16[96,768]{1,0:T(8,128)(2,1)}) %reduce-scatter.11.cloned.1.call-update) | async-done | bytes 147472 | tf_op jit(solution)/shard_map/reduce_scatter | solution.py:109
  507.9 7.7 %all_gather.19 = bf16[384,768]{1,0:T(8,128)(2,1)S(1)} all-gather(bf16[96,768]{1,0:T(8,128)(2,1)} %reduce-scatter.11.cloned.1.call-done), channel_id=1, replica_groups=mesh['grp'=4,'blk'=8] {'grp'}, dimensions={0}, use_global_device_ids=true | all-gather | bytes 737280 | tf_op jit(solution)/shard_map/all_gather | solution.py:110
  515.6 1.1 convert_element_type.252
  (213 shorter events, 25.7 us)
Async XLA Ops:
  7.2 48.4 %copy-start = (bf16[768,768]{1,0:T(8,128)(2,1)S(1)}, bf16[768,768]{1,0:T(8,128)(2,1)}, u32[]{:S(2)}) copy-start(bf16[768,768]{1,0:T(8,128)(2,1)} %param.30) | copy-start | bytes 3538948
  7.2 41.1 %copy-start.54 = (bf16[768]{0:T(1024)(128)(2,1)S(1)}, bf16[768]{0:T(1024)(128)(2,1)}, u32[]{:S(2)}) copy-start(bf16[768]{0:T(1024)(128)(2,1)} %param.35) | copy-start | bytes 4612
  7.2 41.1 %copy-start.55 = (bf16[768]{0:T(1024)(128)(2,1)S(1)}, bf16[768]{0:T(1024)(128)(2,1)}, u32[]{:S(2)}) copy-start(bf16[768]{0:T(1024)(128)(2,1)} %param.36) | copy-start | bytes 4612
  7.2 44.3 %copy-start.22 = (bf16[768,768]{1,0:T(8,128)(2,1)S(1)}, bf16[768,768]{1,0:T(8,128)(2,1)}, u32[]{:S(2)}) copy-start(bf16[768,768]{1,0:T(8,128)(2,1)} %param.28) | copy-start | bytes 3538948
  7.2 182.4 %reduce-scatter.5.cloned.1.call-start = ((), (), s32[]{:S(2)}) async-start(), calls=%async_computation.4 | async-start | bytes 884736 | tf_op jit(solution)/shard_map/reduce_scatter | solution.py:140
  7.3 41.0 %copy-start.56 = (bf16[768]{0:T(1024)(128)(2,1)S(1)}, bf16[768]{0:T(1024)(128)(2,1)}, u32[]{:S(2)}) copy-start(bf16[768]{0:T(1024)(128)(2,1)} %param.41) | copy-start | bytes 4612
  7.3 41.0 %copy-start.57 = (bf16[768]{0:T(1024)(128)(2,1)S(1)}, bf16[768]{0:T(1024)(128)(2,1)}, u32[]{:S(2)}) copy-start(bf16[768]{0:T(1024)(128)(2,1)} %param.29) | copy-start | bytes 4612
  7.3 41.1 %copy-start.58 = (bf16[768]{0:T(1024)(128)(2,1)S(1)}, bf16[768]{0:T(1024)(128)(2,1)}, u32[]{:S(2)}) copy-start(bf16[768]{0:T(1024)(128)(2,1)} %param.32) | copy-start | bytes 4612
  7.3 41.8 %copy-start.59 = (bf16[768]{0:T(1024)(128)(2,1)S(1)}, bf16[768]{0:T(1024)(128)(2,1)}, u32[]{:S(2)}) copy-start(bf16[768]{0:T(1024)(128)(2,1)} %param.34) | copy-start | bytes 4612
  7.3 42.4 %copy-start.60 = (bf16[768]{0:T(1024)(128)(2,1)S(1)}, bf16[768]{0:T(1024)(128)(2,1)}, u32[]{:S(2)}) copy-start(bf16[768]{0:T(1024)(128)(2,1)} %param.40) | copy-start | bytes 4612
  7.3 42.9 %copy-start.61 = (bf16[768]{0:T(1024)(128)(2,1)S(1)}, bf16[768]{0:T(1024)(128)(2,1)}, u32[]{:S(2)}) copy-start(bf16[768]{0:T(1024)(128)(2,1)} %param.42) | copy-start | bytes 4612
  7.3 43.5 %copy-start.50 = (bf16[3072]{0:T(1024)(128)(2,1)S(1)}, bf16[3072]{0:T(1024)(128)(2,1)}, u32[]{:S(2)}) copy-start(bf16[3072]{0:T(1024)(128)(2,1)} %param.38) | copy-start | bytes 18436
  8.2 2.6 copy-start.62
  8.9 38.2 %copy-start.63 = (pred[256]{0:T(512)(128)(4,1)}, pred[256]{0:T(512)(128)(4,1)S(1)}, u32[]{:S(2)}) copy-start(pred[256]{0:T(512)(128)(4,1)S(1)} %broadcast_compare_fusion.1) | copy-start | bytes 772
  11.6 35.5 %copy-start.33 = (f32[768]{0:T(1024)}, f32[768]{0:T(1024)S(1)}, u32[]{:S(2)}) copy-start(f32[768]{0:T(1024)S(1)} %get-tuple-element.39) | copy-start | bytes 9220
  12.7 45.1 %copy-start.14 = (bf16[256,768]{1,0:T(8,128)(2,1)}, bf16[256,768]{1,0:T(8,128)(2,1)S(1)}, u32[]{:S(2)}) copy-start(bf16[256,768]{1,0:T(8,128)(2,1)S(1)} %fusion.27) | copy-start | bytes 1179652
  48.3 9.5 %copy-start.29 = (bf16[8,64,768]{2,1,0:T(8,128)(2,1)}, bf16[8,64,768]{2,1,0:T(8,128)(2,1)S(1)}, u32[]{:S(2)}) copy-start(bf16[8,64,768]{2,1,0:T(8,128)(2,1)S(1)} %slice.128) | copy-start | bytes 2359300
  55.6 2.2 copy-start.20
  55.6 2.2 copy-start.53
  68.9 4.3 copy-start.24
  73.1 2.2 copy-start.1
  73.2 2.2 copy-start.26
  73.2 2.5 copy-start.31
  73.2 2.5 copy-start.34
  73.2 2.5 copy-start.52
  73.2 2.5 copy-start.64
  75.4 5.3 %copy-start.16 = (bf16[256,12,64]{0,2,1:T(8,128)(2,1)}, bf16[256,12,64]{0,2,1:T(8,128)(2,1)S(1)}, u32[]{:S(2)}) copy-start(bf16[256,12,64]{0,2,1:T(8,128)(2,1)S(1)} %get-tuple-element.67) | copy-start | bytes 1179652
  76.3 14.2 %copy-start.6 = (f32[256,768]{1,0:T(8,128)}, f32[256,768]{1,0:T(8,128)S(1)}, u32[]{:S(2)}) copy-start(f32[256,768]{1,0:T(8,128)S(1)} %get-tuple-element.70) | copy-start | bytes 2359300
  76.3 14.2 %copy-start.32 = (f32[256]{0:T(256)}, f32[256]{0:T(256)S(1)}, u32[]{:S(2)}) copy-start(f32[256]{0:T(256)S(1)} %broadcast_multiply_fusion.5) | copy-start | bytes 3076
  76.3 4.4 slice-start
  76.6 13.9 %copy-start.36 = (f32[256]{0:T(256)}, f32[256]{0:T(256)S(1)}, u32[]{:S(2)}) copy-start(f32[256]{0:T(256)S(1)} %add_rsqrt_fusion.1) | copy-start | bytes 3076
  76.6 4.1 copy-start.51
  76.6 4.1 slice-start.1
  80.7 2.8 copy-start.35
  83.5 4.7 slice-start.2
  85.2 3.0 copy-start.13
  85.2 3.0 slice-start.3
  88.2 2.3 copy-start.19
  92.9 3.5 copy-start.25
  96.4 8.7 %copy-start.7 = (bf16[12,64,768]{2,1,0:T(8,128)(2,1)}, bf16[12,64,768]{2,1,0:T(8,128)(2,1)S(1)}, u32[]{:S(2)}) copy-start(bf16[12,64,768]{2,1,0:T(8,128)(2,1)S(1)} %get-tuple-element.81) | copy-start | bytes 3538948
  101.7 2.2 copy-start.2
  107.7 176.2 %reduce-scatter.9.cloned.1.call-start = ((), (), s32[]{:S(2)}) async-start(), calls=%async_computation.6 | async-start | bytes 4866048 | tf_op jit(solution)/shard_map/reduce_scatter | solution.py:109
  113.2 282.4 %reduce-scatter.7.cloned.1.call-start = ((), (), s32[]{:S(2)}) async-start(), calls=%async_computation.5 | async-start | bytes 4866048 | tf_op jit(solution)/shard_map/reduce_scatter | solution.py:149
  113.3 4.4 copy-start.15
  113.3 5.0 copy-start.17
  117.7 3.0 copy-start.11
  117.7 1.8 copy-start.30
  125.4 382.5 %reduce-scatter.11.cloned.1.call-start = ((), (), s32[]{:S(2)}) async-start(), calls=%async_computation.7 | async-start | bytes 4866048 | tf_op jit(solution)/shard_map/reduce_scatter | solution.py:109
  (25 other events, 31.1 us)
Sparse Core Ops, SparseCore 0:
  107.9 63.5 reduce-scatter.4
  177.8 106.1 reduce-scatter.8
  289.4 106.0 reduce-scatter.6
  401.8 106.0 reduce-scatter.10

commit v2 on v1

v2 whole, which is shorter than its diff:
```python
import math

import jax
import jax.numpy as jnp
from jax import lax
from jax.experimental import pallas as pl
from jax.experimental.pallas import tpu as pltpu
from jax.sharding import PartitionSpec as P

HEADS = 12
HEAD_DIM = 64
TAB_MAX = 64
LANES = 256
far_below = -1e30
BF = jnp.bfloat16
F32 = jnp.float32
MIB = 1 << 20


def outer_sum(left, right):
    return lax.dot_general(left, right, (((0,), (0,)), ((), ())), preferred_element_type=F32)


def back_dot(left, right):
    return lax.dot_general(left, right, (((1,), (1,)), ((), ())), preferred_element_type=F32)


def fwd_dot(left, right):
    return jnp.dot(left, right, preferred_element_type=F32)


def norm_parts(values):
    centred = values - jnp.mean(values, axis=-1, keepdims=True)
    spread = jnp.mean(centred * centred, axis=-1, keepdims=True)
    inv = lax.rsqrt(spread + 1e-06)
    return centred * inv, inv


def norm_grad(grad, normed, inv, gain):
    scaled = grad * gain
    return inv * (
        scaled
        - jnp.mean(scaled, axis=-1, keepdims=True)
        - normed * jnp.mean(scaled * normed, axis=-1, keepdims=True)
    )


def head_lanes(shape, index):
    lane = lax.broadcasted_iota(jnp.int32, shape, len(shape) - 1)
    return (lane >= index * HEAD_DIM) & (lane < (index + 1) * HEAD_DIM)


def attend_kernel(
    table_ref, key_w_ref, value_w_ref, value_b_ref, q_ref, own_k_ref, own_v_ref, bias_ref,
    keys_ref, values_ref, prob_ref, context_ref,
):
    n_table = table_ref.shape[0]
    table = table_ref[...]
    keys_ref[:n_table] = fwd_dot(table, key_w_ref[...]).astype(BF)
    values_ref[:n_table] = (fwd_dot(table, value_w_ref[...]) + value_b_ref[...]).astype(BF)
    keys_ref[n_table:] = own_k_ref[...]
    values_ref[n_table:] = own_v_ref[...]
    queries = q_ref[...]
    context = jnp.zeros(context_ref.shape, F32)
    for h in range(LANES // HEAD_DIM):
        mask = head_lanes(queries.shape, h)
        picked = jnp.where(mask, queries, jnp.zeros_like(queries))
        scores = back_dot(picked, keys_ref[...]) + bias_ref[...]
        top = jnp.max(scores, axis=-1, keepdims=True)
        weights = jnp.exp(scores - top)
        prob = (weights * (1.0 / jnp.sum(weights, axis=-1, keepdims=True))).astype(BF)
        prob_ref[h] = prob
        context = jnp.where(mask, fwd_dot(prob, values_ref[...]), context)
    context_ref[...] = context


def attend(table, key_w, value_w, value_b, queries, own_k, own_v, bias):
    rows, width = queries.shape
    n_table = table.shape[0]
    n_keys = n_table + rows
    steps = width // LANES
    per = LANES // HEAD_DIM
    whole = lambda shape: pl.BlockSpec(shape, lambda i: (0, 0))
    lanes = lambda n: pl.BlockSpec((n, LANES), lambda i: (0, i))
    return pl.pallas_call(
        attend_kernel,
        grid=(steps,),
        in_specs=[
            whole((n_table, width)), lanes(width), lanes(width), lanes(1), lanes(rows), lanes(rows),
            lanes(rows), whole((rows, n_keys)),
        ],
        out_specs=[
            lanes(n_keys), lanes(n_keys), pl.BlockSpec((per, rows, n_keys), lambda i: (i, 0, 0)), lanes(rows),
        ],
        out_shape=[
            jax.ShapeDtypeStruct((n_keys, width), BF),
            jax.ShapeDtypeStruct((n_keys, width), BF),
            jax.ShapeDtypeStruct((HEADS, rows, n_keys), BF),
            jax.ShapeDtypeStruct((rows, width), F32),
        ],
        compiler_params=pltpu.CompilerParams(vmem_limit_bytes=56 * MIB),
        cost_estimate=pl.CostEstimate(
            flops=4 * width * (n_table * width + rows * n_keys), bytes_accessed=10 * MIB,
            transcendentals=HEADS * rows * n_keys,
        ),
    )(table, key_w, value_w, value_b, queries, own_k, own_v, bias)


def middle_kernel(
    resid_ref, context_ref, cot_ref, out_w_ref, up_w_ref, down_w_ref, vec_ref, up_b_ref,
    mixed_ref, context_low_ref, middle_low_ref, act_ref, grad_ffn_ref, grad_pre_ref, grad_attn_ref,
    grad_context_ref, grad_mid_ref, sums_ref, up_sum_ref, slope_ref, total_ref,
):
    hidden = up_w_ref.shape[1]
    tile = 512
    steps = hidden // tile
    out_b, norm_g, norm_s, down_b, final_g, final_s = (vec_ref[i : i + 1] for i in range(6))
    column = lambda v: jnp.sum(v, axis=0, keepdims=True)
    context_low = context_ref[...].astype(BF)
    context_low_ref[...] = context_low
    normed1, inv1 = norm_parts(resid_ref[...] + fwd_dot(context_low, out_w_ref[...]) + out_b)
    middle = normed1 * norm_g + norm_s
    middle_low_ref[...] = middle.astype(BF)
    total_ref[...] = middle + down_b

    def forward(i, carry):
        at = pl.ds(pl.multiple_of(i * tile, tile), tile)
        pre = fwd_dot(middle_low_ref[...], up_w_ref[:, at]) + up_b_ref[:, at]
        cdf = 0.5 * (1.0 + lax.erf(pre * (0.5**0.5)))
        act = (pre * cdf).astype(BF)
        act_ref[:, at] = act
        slope_ref[:, at] = cdf + pre * jnp.exp(-0.5 * pre * pre) * (1.0 / math.sqrt(2 * math.pi))
        total_ref[...] += fwd_dot(act, down_w_ref[at, :])
        return carry

    lax.fori_loop(0, steps, forward, 0)
    normed2, inv2 = norm_parts(total_ref[...])
    mixed_ref[...] = (normed2 * final_g + final_s).astype(BF)
    cot = cot_ref[...].astype(F32)
    grad_final = norm_grad(cot, normed2, inv2, final_g)
    grad_ffn = grad_final.astype(BF)
    grad_ffn_ref[...] = grad_ffn
    total_ref[...] = grad_final

    def backward(i, carry):
        at = pl.ds(pl.multiple_of(i * tile, tile), tile)
        grad_pre = (back_dot(grad_ffn_ref[...], down_w_ref[at, :]) * slope_ref[:, at]).astype(BF)
        grad_pre_ref[:, at] = grad_pre
        up_sum_ref[:, at] = column(grad_pre.astype(F32))
        total_ref[...] += back_dot(grad_pre, up_w_ref[:, at])
        return carry

    lax.fori_loop(0, steps, backward, 0)
    grad_middle = total_ref[...]
    grad_mid = norm_grad(grad_middle, normed1, inv1, norm_g)
    grad_mid_ref[...] = grad_mid
    grad_attn = grad_mid.astype(BF)
    grad_attn_ref[...] = grad_attn
    grad_context_ref[...] = back_dot(grad_attn, out_w_ref[...]).astype(BF)
    sums_ref[0:1] = column(grad_attn.astype(F32))
    sums_ref[1:2] = column(grad_middle * normed1)
    sums_ref[2:3] = column(grad_middle)
    sums_ref[3:4] = column(grad_ffn.astype(F32))
    sums_ref[4:5] = column(cot * normed2)
    sums_ref[5:6] = column(cot)
    sums_ref[6:8] = jnp.zeros((2, sums_ref.shape[1]), F32)


def middle_part(resid, context, cot, out_w, up_w, down_w, vecs, up_b):
    rows, width = resid.shape
    hidden = up_w.shape[1]
    vmem = pl.BlockSpec(memory_space=pltpu.VMEM)
    shape = lambda n, t: jax.ShapeDtypeStruct((rows, n), t)
    return pl.pallas_call(
        middle_kernel,
        in_specs=[vmem] * 8,
        out_specs=[vmem] * 11,
        out_shape=[
            shape(width, BF), shape(width, BF), shape(width, BF), shape(hidden, BF), shape(width, BF),
            shape(hidden, BF), shape(width, BF), shape(width, BF), shape(width, F32),
            jax.ShapeDtypeStruct((8, width), F32), jax.ShapeDtypeStruct((1, hidden), F32),
        ],
        scratch_shapes=[pltpu.VMEM((rows, hidden), F32), pltpu.VMEM((rows, width), F32)],
        compiler_params=pltpu.CompilerParams(vmem_limit_bytes=48 * MIB),
        cost_estimate=pl.CostEstimate(
            flops=4 * rows * width * (2 * hidden + width), bytes_accessed=24 * MIB, transcendentals=2 * rows * hidden
        ),
    )(resid, context, cot, out_w, up_w, down_w, vecs, up_b)


def attend_back_kernel(
    q_ref, keys_ref, values_ref, prob_ref, context_ref, grad_ref, *refs
):
    grad_q_ref, grad_k_ref, grad_v_ref = refs[-3:]
    grad = grad_ref[...]
    grad_f = grad.astype(F32)
    product = grad_f * context_ref[...]
    grad_t = grad_f.T.astype(BF)
    q_t = q_ref[...].astype(F32).T.astype(BF)
    grad_q = jnp.zeros(grad.shape, F32)
    for h in range(LANES // HEAD_DIM):
        mask = head_lanes(grad.shape, h)
        at = slice(h * HEAD_DIM, (h + 1) * HEAD_DIM)
        row_dot = jnp.sum(jnp.where(mask, product, 0.0), axis=-1, keepdims=True)
        grad_prob = back_dot(jnp.where(mask, grad, jnp.zeros_like(grad)), values_ref[...])
        prob = prob_ref[h]
        grad_score = (prob.astype(F32) * (grad_prob - row_dot)).astype(BF)
        grad_v_ref[at] = fwd_dot(grad_t[at], prob).astype(BF)
        grad_k_ref[at] = fwd_dot(q_t[at], grad_score).astype(BF)
        grad_q = jnp.where(mask, fwd_dot(grad_score, keys_ref[...]), grad_q)
    grad_q_ref[...] = (grad_q * HEAD_DIM**-0.5).astype(BF)


def attend_back(queries, keys, values, prob, context, grad_context, after):
    rows, width = queries.shape
    n_keys = keys.shape[0]
    per = LANES // HEAD_DIM
    lanes = lambda n: pl.BlockSpec((n, LANES), lambda i: (0, i))
    return pl.pallas_call(
        attend_back_kernel,
        grid=(width // LANES,),
        in_specs=[
            lanes(rows), lanes(n_keys), lanes(n_keys), pl.BlockSpec((per, rows, n_keys), lambda i: (i, 0, 0)),
            lanes(rows), lanes(rows),
        ]
        + [pl.BlockSpec(memory_space=pl.ANY)] * len(after),
        out_specs=[lanes(rows)] + [pl.BlockSpec((LANES, n_keys), lambda i: (i, 0))] * 2,
        out_shape=[
            jax.ShapeDtypeStruct((rows, width), BF),
            jax.ShapeDtypeStruct((width, n_keys), BF),
            jax.ShapeDtypeStruct((width, n_keys), BF),
        ],
        compiler_params=pltpu.CompilerParams(vmem_limit_bytes=48 * MIB),
        cost_estimate=pl.CostEstimate(
            flops=8 * rows * n_keys * width, bytes_accessed=12 * MIB, transcendentals=0
        ),
    )(queries, keys, values, prob, context, grad_context, *after)


def local(
    tokens, seg_ids, turn_ids, prev_ids, answer_table, query_weight, query_bias,
    key_weight, value_weight, value_bias, out_weight, out_bias, norm_gain, norm_shift,
    up_weight, up_bias, down_weight, down_bias, final_gain, final_shift, cotangent,
):
    rows, width = tokens.shape
    blocks = lax.axis_size("blk")
    grps = lax.axis_size("grp")
    tab = TAB_MAX
    scale = HEAD_DIM ** (-0.5)
    f = lambda v: v.astype(F32)
    is_one = (prev_ids == 1)[:, None]
    answers = f(answer_table)
    resid_in = f(tokens) + jnp.where(is_one, answers[1][None], answers[0][None])
    layer_input = resid_in.astype(BF)
    flags = jnp.concatenate(
        [(seg_ids[:tab] == 0).astype(BF), jnp.zeros((128 - tab,), BF), prev_ids[:tab].astype(BF),
         jnp.zeros((width - 128 - tab,), BF)]
    )[None]
    payload = jnp.concatenate([layer_input[:tab], flags, jnp.zeros((15, width), BF)], axis=0)
    gathered = lax.all_gather(payload, "blk", axis=0, tiled=False)
    table_input = gathered[:, :tab].reshape(blocks * tab, width)
    table_open = gathered[:, tab, :tab].reshape(blocks * tab) > 0.5
    table_prev = gathered[:, tab, 128 : 128 + tab].reshape(blocks * tab)

    qkv_in = jnp.concatenate([table_input, layer_input], axis=0)
    queries = ((fwd_dot(layer_input, query_weight) + f(query_bias)).astype(BF) * scale).astype(BF)
    own_keys = fwd_dot(layer_input, key_weight).astype(BF)
    own_values = (fwd_dot(layer_input, value_weight) + f(value_bias)).astype(BF)
    own_open = (turn_ids[:, None] == turn_ids[None, :]) & (seg_ids != 0)[None, :]
    bias = jnp.concatenate(
        [
            jnp.broadcast_to(jnp.where(table_open, 0.0, far_below)[None], (rows, blocks * tab)),
            jnp.where(own_open, 0.0, far_below),
        ],
        axis=1,
    )
    keys, values, prob, context = attend(
        table_input, key_weight, value_weight, f(value_bias)[None], queries, own_keys, own_values, bias
    )
    n_keys = keys.shape[0]
    vecs = jnp.stack(
        [f(v) for v in (out_bias, norm_gain, norm_shift, down_bias, final_gain, final_shift)] + [jnp.zeros((width,), F32)] * 2
    )
    (
        mixed, context_low, middle_low, act_low, grad_ffn, grad_pre, grad_attn, grad_context, grad_mid_sum,
        sums, up_sum,
    ) = middle_part(
        resid_in, context, cotangent, out_weight, up_weight, down_weight, vecs, f(up_bias)[None]
    )

    core_bit = lax.axis_index("grp") & 1
    x_bit = lax.axis_index("grp") >> 1
    own = lax.axis_index("blk")
    y_bit, z_own = own & 1, own >> 1
    planes = blocks // 2

    def swap_grp(value, mask):
        return lax.ppermute(value, "grp", [(i, i ^ mask) for i in range(grps)])

    def swap_blk(value, mask):
        return lax.ppermute(value, "blk", [(i, i ^ mask) for i in range(blocks)])

    def take(value, index, axis):
        return lax.dynamic_index_in_dim(value, index, axis, keepdims=False)

    def half(value, index):
        size = value.shape[1] // 2
        return lax.dynamic_slice_in_dim(value, index * size, size, 1)

    def add(first, second):
        return (f(first) + f(second)).astype(BF)

    def core_stage(lhs, rhs):
        sent = swap_grp(outer_sum(lhs, half(rhs, 1 - core_bit)).astype(BF), 1)
        return (outer_sum(lhs, half(rhs, core_bit)) + f(sent)).astype(BF)

    def y_split(value):
        return take(value, y_bit, 1), take(value, 1 - y_bit, 1)

    def y_stage(value):
        kept, sent = y_split(value)
        return add(kept, swap_blk(sent, 1))

    def z_stage(value):
        total = f(take(value, z_own, 0))
        for k in range(1, planes):
            total = total + f(swap_blk(take(value, z_own ^ k, 0), 2 * k))
        return total.astype(BF)

    def x_split(value, axis):
        return take(value, x_bit, axis), take(value, 1 - x_bit, axis)

    def join(value, other, bit, axis):
        first = jnp.where(bit == 0, value, other)
        second = jnp.where(bit == 0, other, value)
        return jnp.concatenate([first, second], axis=axis)

    n_out = width // blocks
    ff_out = up_weight.shape[1] // blocks
    half_width = width // 2

    down_part = core_stage(act_low, grad_ffn).reshape(planes, 2, ff_out, half_width)
    up_part = core_stage(middle_low, grad_pre).reshape(planes, 2, 2, n_out // 2, 2 * width)
    down_kept, down_sent = y_split(down_part)
    up_kept, up_sent = x_split(up_part, 2)
    grad_queries, grad_keys_t, grad_values_t = attend_back(
        queries, keys, values, prob, context, grad_context, (down_sent, up_sent)
    )
    down_part = add(down_kept, swap_blk(down_sent, 1)).reshape(planes, 2, ff_out // 2, half_width)
    down_kept, down_sent = x_split(down_part, 1)
    down_part = z_stage(add(down_kept, swap_grp(down_sent, 2)))
    down_part = join(down_part, swap_grp(down_part, 2), x_bit, 0)
    up_part = add(up_kept, swap_grp(up_sent, 2))
    up_part = z_stage(y_stage(up_part))
    up_part = join(up_part, swap_grp(up_part, 2), x_bit, 0)
    out_down = f(join(down_part, swap_grp(down_part, 1), core_bit, 1))
    out_up = f(join(up_part, swap_grp(up_part, 1), core_bit, 1))

    half_rows = lambda value, index: lax.dynamic_slice_in_dim(value, index * half_width, half_width, 0)
    mix = lambda left, right, dims: lax.dot_general(left, right, (dims, ((), ())), preferred_element_type=F32)
    grad_kv_in = mix(grad_keys_t, key_weight, ((0,), (1,))) + mix(grad_values_t, value_weight, ((0,), (1,)))
    grad_table = grad_kv_in[: blocks * tab]
    grad_input_local = grad_mid_sum + back_dot(grad_queries, query_weight) + grad_kv_in[blocks * tab :]
    all_prev = jnp.concatenate([table_prev, prev_ids.astype(BF)])
    all_grads = jnp.concatenate([grad_table, grad_input_local], axis=0)
    total_sum = jnp.sum(all_grads, axis=0, keepdims=True)
    one_sum = jnp.sum(jnp.where(all_prev[:, None] > 0.5, all_grads, 0.0), axis=0, keepdims=True)
    vectors = jnp.concatenate(
        [
            total_sum - one_sum,
            one_sum,
            jnp.sum(f(grad_queries), axis=0, keepdims=True),
            jnp.sum(f(grad_values_t), axis=1)[None],
            sums[:6],
            up_sum.reshape(-1, width),
            jnp.zeros((2, width), F32),
        ],
        axis=0,
    )
    n_vec = vectors.shape[0]

    def pack(value):
        high = value.astype(BF)
        return jnp.concatenate([high, (value - f(high)).astype(BF)], axis=0)

    def unpack(value):
        return f(value[:n_vec]) + f(value[n_vec:])

    def pair_half(index):
        return jnp.concatenate(
            [outer_sum(layer_input, half(grad_queries, index)), mix(qkv_in, half_rows(grad_keys_t, index), ((0,), (1,)))],
            axis=1,
        )

    def pair_half_two(index):
        return jnp.concatenate(
            [mix(qkv_in, half_rows(grad_values_t, index), ((0,), (1,))), outer_sum(context_low, half(grad_attn, index))],
            axis=1,
        )

    sent = swap_grp(jnp.concatenate([pair_half(1 - core_bit).astype(BF), pack(vectors)], axis=0), 1)
    first = (pair_half(core_bit) + f(sent[:width])).astype(BF)
    vectors = vectors + unpack(sent[width:])
    sent = swap_grp(pair_half_two(1 - core_bit).astype(BF), 1)
    second = (pair_half_two(core_bit) + f(sent)).astype(BF)

    first = first.reshape(planes, 2, 2, n_out // 2, width)
    second = jnp.concatenate(
        [second.reshape(planes, 2, n_out, width), grad_table.astype(BF).reshape(planes, 2, tab, width)], axis=2
    )
    rows_of = planes * n_out
    sent = swap_grp(
        jnp.concatenate([take(first, 1 - x_bit, 2).reshape(rows_of, width), pack(vectors)], axis=0), 2
    )
    first = add(take(first, x_bit, 2).reshape(rows_of, width), sent[:rows_of]).reshape(
        planes, 2, n_out // 2, width
    )
    vectors = vectors + unpack(sent[rows_of:])
    second = y_stage(second)
    rows_of = planes * n_out // 2
    sent = swap_blk(
        jnp.concatenate([take(first, 1 - y_bit, 1).reshape(rows_of, width), pack(vectors)], axis=0), 1
    )
    first = add(take(first, y_bit, 1).reshape(rows_of, width), sent[:rows_of]).reshape(
        planes, n_out // 2, width
    )
    vectors = vectors + unpack(sent[rows_of:])
    table_kept = second[:, n_out:]
    second = second[:, :n_out].reshape(planes, 2, n_out // 2, width)
    second_kept, second_sent = x_split(second, 1)
    second = add(second_kept, swap_grp(second_sent, 2))
    second = z_stage(jnp.concatenate([second, table_kept], axis=1))
    rows_of = n_out // 2
    total = f(take(first, z_own, 0))
    packed = pack(vectors)
    for k in range(1, planes):
        sent = swap_blk(jnp.concatenate([take(first, z_own ^ k, 0), packed], axis=0), 2 * k)
        total = total + f(sent[:rows_of])
        vectors = vectors + unpack(sent[rows_of:])
    first = total.astype(BF)
    table_share = second[rows_of:]
    both = jnp.concatenate([first, second[:rows_of]], axis=1)
    both = join(both, swap_grp(both, 2), x_bit, 0)
    other = swap_grp(both, 1)
    square = []
    for index in range(4):
        at = (slice(None), slice(index * half_width, (index + 1) * half_width))
        square.append(join(both[at], other[at], core_bit, 1))
    mine = lax.dynamic_slice_in_dim(vectors[:10], own * n_out, n_out, 1)
    up_bias_out = lax.dynamic_slice_in_dim(vectors[10:14].reshape(-1), own * ff_out, ff_out, 0)
    grad_input = grad_input_local.at[:tab].add(f(table_share))
    return (
        mixed,
        grad_input,
        mine[:2],
        f(square[0]),
        mine[2],
        f(square[1]),
        f(square[2]),
        mine[3],
        f(square[3]),
        mine[4],
        mine[5],
        mine[6],
        out_up,
        up_bias_out,
        out_down,
        mine[7],
        mine[8],
        mine[9],
    )


def solution(mesh):
    both = ("grp", "blk")
    placed = (P(both, None), P(both), P(both), P(both)) + (P(),) * 16 + (P(both, None),)
    vec, mat = P("blk"), P("blk", None)
    return jax.shard_map(
        local,
        mesh=mesh,
        in_specs=placed,
        out_specs=(
            P(both, None), P(both, None), P(None, "blk"), mat, vec, mat, mat, vec, mat, vec,
            vec, vec, mat, vec, mat, vec, vec, vec,
        ),
        check_vma=False,
    )
```

time: 524 us -> 232 us (0.44)
  waiting for transfers between devices: 299 us -> 45.2 us
  blocking collectives: 97.3 us -> 34.4 us
  Pallas kernels: 0 us -> 33.9 us
  starting transfers between devices: 0.16 us -> 32.9 us
  matrix products: 58.6 us -> 30.8 us
  between operations: 14.8 us -> 1.73 us
    reduce_scatter x4 -> x0, waiting for transfers between devices: 299 us -> none  [the longest x2 196 us: share(): lax.psum_scatter(value, ('blk', 'grp'), scatter_dimension=0, tiled=True)]
    ppermute x0 -> x30, waiting for transfers between devices: none -> 45.2 us  [the longest x16 27.7 us: swap_blk(): return lax.ppermute(value, 'blk', [(i, i ^ mask) for i in range(blocks)])]
    psum x1 -> x0, blocking collectives: 40.2 us -> none  [local(): vectors = lax.psum(vectors, ('blk', 'grp'))]
    pallas_call x0 -> x3, Pallas kernels: none -> 33.9 us  [the longest x1 16.5 us: middle_part(): pl.pallas_call(middle_kernel, in_specs=[vmem] * 8, out_specs=[vmem] * 11,...]
    ppermute x0 -> x30, starting transfers between devices: none -> 32.9 us  [the longest x16 24 us: swap_blk(): return lax.ppermute(value, 'blk', [(i, i ^ mask) for i in range(blocks)])]
    all_gather x3 -> x0, blocking collectives: 23.1 us -> none  [the longest x2 15.4 us: share(): return f(lax.all_gather(part, 'grp', axis=0, tiled=True))]
    another operation x14 -> x8, local copies, waits for them, and re-layouts: 12.1 us -> 0.68 us  [the longest x7 0.67 us: local(): jnp.stack([f(v) for v in (out_bias, norm_gain, norm_shift, down_bias, fin...]
    sub x1 -> x0, matrix products: 8.89 us -> none  [local(): weights = jnp.where(allowed, jnp.exp(scores - top), 0.0)]
  transfers between devices with their start and end apart: 4 -> 30, of which waited for: 3 -> 9; matrix products, arithmetic and copies ran while one was open for 8% -> 23% of each run, Pallas kernels for 0% -> 3%
where the time goes in v2:
time: 232 us; the launch traced here: 231 us
  waiting for transfers between devices  45.2 us (19%)
  blocking collectives  34.4 us (15%)
  Pallas kernels  33.9 us (15%)
  starting transfers between devices  32.9 us (14%)
  matrix products  30.8 us (13%)
  other arithmetic  28.3 us (12%)
  local copies, waits for them, and re-layouts  23.6 us (10%)
    all_gather x1, blocking collectives, local(): gathered = lax.all_gather(payload, 'blk', axis=0, tiled=False)  34.4 us
    ppermute x16, waiting for transfers between devices, swap_blk(): return lax.ppermute(value, 'blk', [(i, i ^ mask) for i in range(blocks)])  27.7 us
    ppermute x16, starting transfers between devices, swap_blk(): return lax.ppermute(value, 'blk', [(i, i ^ mask) for i in range(blocks)])  24 us
    dot_general x8, matrix products, outer_sum(): lax.dot_general(left, right, (((0,), (0,)), ((), ())), preferred_element_...  18.2 us
    ppermute x14, waiting for transfers between devices, swap_grp(): return lax.ppermute(value, 'grp', [(i, i ^ mask) for i in range(grps)])  17.4 us
    pallas_call x1, Pallas kernels, middle_part(): pl.pallas_call(middle_kernel, in_specs=[vmem] * 8, out_specs=[vmem] * 11,...  16.5 us
    unnamed x124, local copies, waits for them, and re-layouts  10.5 us
    pallas_call x1, Pallas kernels, attend(): pl.pallas_call(attend_kernel, grid=(steps,), in_specs=[whole((n_table, wi...  9.6 us
  transfers between devices with their start and end apart: 30, of which 9 were waited for; matrix products, arithmetic and copies ran while one was open for 23% of the time, Pallas kernels for 3%

profile of v2, /device:TPU:0, one launch (start us, length us, event | category | flops | bytes accessed | tf_op | source)
XLA Modules:
  0.0 230.8 jit_solution(7956242315988604044)
XLA Ops:
  2.9 1.2 fusion.81
  4.4 34.4 %all-gather = bf16[640,768]{1,0:T(8,128)(2,1)S(1)} all-gather(bf16[80,768]{1,0:T(8,128)(2,1)S(1)} %maximum_maximum_fusion), channel_id=2, replica_groups=mesh['grp'=4,'blk'=8] {'blk'}, dimensions={0}, use_global_device_ids=true | all-gather | bytes 1105920 | tf_op jit(solution)/shard_map/all_gather | solution.py:260
  40.8 2.5 %convolution_convert_fusion.6.own_k_ref = bf16[256,768]{1,0:T(8,128)(2,1)} fusion(bf16[256,768]{1,0:T(8,128)(2,1)S(1)} %get-tuple-element.104, bf16[768,768]{1,0:T(8,128)(2,1)} %key_w_ref.1), kind=kOutput, calls=%fused_computation.32 | convolution fusion | flops 302186496 | bytes 1966080 | tf_op jit(solution)/shard_map/dot_general | solution.py:29
  45.1 1.2 fusion.9.q_ref
  46.4 1.2 fusion.8.own_v_ref
  47.6 9.6 %shard_map.340 = (bf16[768,768]{1,0:T(8,128)(2,1)}, bf16[768,768]{1,0:T(8,128)(2,1)}, bf16[12,256,768]{2,1,0:T(8,128)(2,1)}, f32[256,768]{1,0:T(8,128)}) custom-call(bf16[512,768]{1,0:T(8,128)(2,1)} %bitcast.168, bf16[768,768]{1,0:T(8,128)(2,1)} %key_w_ref.1, bf16[768,768]{1,0:T(8,128)(2,1)} %value_w_ref.1, f32[1,768]{1,0:T(1,128)} %broadcast_in_dim.106.value_b_ref, ...), custom_call_target="tpu_custom_call" | custom-call | flops 1811939328 | bytes 10485760 | tf_op jit(solution)/shard_map/pallas_call | solution.py:85
  57.9 1.1 copy-done.3
  60.4 1.3 copy-done.16
  62.7 16.5 %shard_map.341 = (bf16[256,768]{1,0:T(8,128)(2,1)}, bf16[256,768]{1,0:T(8,128)(2,1)S(1)}, bf16[256,768]{1,0:T(8,128)(2,1)S(1)}, bf16[256,3072]{1,0:T(8,128)(2,1)...) custom-call(f32[256,768]{1,0:T(8,128)S(1)} %get-tuple-element.105.re, ...), custom_call_target="tpu_custom_call" | custom-call | flops 5435817984 | bytes 25165824 | tf_op jit(solution)/shard_map/pallas_call | solution.py:174
  79.2 4.2 %convolution_convert_fusion = bf16[3072,384]{1,0:T(8,128)(2,1)} fusion(bf16[256,3072]{1,0:T(8,128)(2,1)} %get-tuple-element.55, bf16[256,768]{1,0:T(8,128)(2,1)S(1)} %get-tuple-element.56, s32[]{:T(128)S(6)} %select_n.205), kind=kOutput, calls=%fused_computation.2 | convolution fusion | flops 605159424 | bytes 4128772 | tf_op jit(solution)/shard_map/dot_general | solution.py:21
  83.6 3.5 %convolution_convert_fusion.1 = bf16[768,1536]{1,0:T(8,128)(2,1)} fusion(bf16[256,768]{1,0:T(8,128)(2,1)S(1)} %get-tuple-element.57, bf16[256,3072]{1,0:T(8,128)(2,1)} %get-tuple-element.58, s32[]{:T(128)S(6)} %select_n.208), kind=kOutput, calls=%fused_computation.3 | convolution fusion | flops 605159424 | bytes 3538948 | tf_op jit(solution)/shard_map/dot_general | solution.py:21
  89.6 1.2 convolution_convert_fusion.5
  90.8 1.4 fusion.44
  92.3 2.7 %add_convert_fusion.1 = bf16[3072,384]{1,0:T(8,128)(2,1)S(1)} fusion(bf16[3072,384]{1,0:T(8,128)(2,1)} %collective-permute-done, bf16[256,3072]{1,0:T(8,128)(2,1)S(1)} %copy-done.20, bf16[256,768]{1,0:T(8,128)(2,1)S(1)} %copy-done.9, s32[]{:T(128)S(6)} %select_n.204), kind=kOutput, calls=%fused_computation.1 | convolution fusion | flops 607518720 | bytes 6488068 | tf_op jit(solution)/shard_map/dot_general | solution.py:21
  95.0 1.2 dynamic-slice_bitcast_fusion.1.refs_0_
  96.9 1.4 collective-permute-start.23
  98.3 2.5 %add_convert_fusion = bf16[768,1536]{1,0:T(8,128)(2,1)S(1)} fusion(bf16[768,1536]{1,0:T(8,128)(2,1)} %collective-permute-done.1, bf16[256,768]{1,0:T(8,128)(2,1)S(1)} %get-tuple-element.57, bf16[256,3072]{1,0:T(8,128)(2,1)S(1)} %copy-done.39, s32[]{:T(128)S(6)} %select_n.207), kind=kOutput, calls=%fused_computation | convolution fusion | flops 607518720 | bytes 5898244 | tf_op jit(solution)/shard_map/dot_general | solution.py:21
  100.9 1.2 dynamic-slice_bitcast_fusion.refs_1_
  102.7 1.5 collective-permute-start.16
  104.2 7.8 %shard_map.342 = (bf16[256,768]{1,0:T(8,128)(2,1)S(1)}, bf16[768,768]{1,0:T(8,128)(2,1)S(1)}, bf16[768,768]{1,0:T(8,128)(2,1)S(1)}) custom-call(bf16[256,768]{1,0:T(8,128)(2,1)S(1)} %copy-done.5, bf16[768,768]{1,0:T(8,128)(2,1)S(1)} %copy-done.2, bf16[768,768]{1,0:T(8,128)(2,1)} %get-tuple-element.52.values_ref, ...), custom_call_target="tpu_custom_call" | custom-call | flops 1207959552 | bytes 12582912 | tf_op jit(solution)/shard_map/pallas_call | solution.py:219
  113.7 1.6 convolution_convert_fusion.3
  115.4 1.2 convolution_convert_fusion.4
  116.9 1.1 convolution_add_fusion
  121.2 2.3 pad_maximum_fusion
  125.8 1.8 fusion.24
  128.3 1.4 fusion.40
  129.7 1.7 fusion.3
  133.5 1.6 fusion.4
  140.4 1.6 fusion.2
  143.2 5.7 %collective-permute-done.24 = bf16[4,192,384]{2,1,0:T(8,128)(2,1)} collective-permute-done((bf16[4,192,384]{2,1,0:T(8,128)(2,1)}, bf16[4,192,384]{2,1,0:T(8,128)(2,1)}, u32[]{:S(2)}, u32[]{:S(2)}) %collective-permute-start.24) | collective-permute-done | bytes 589856 | tf_op jit(solution)/shard_map/ppermute | solution.py:298
  149.0 1.2 fusion.10
  150.3 3.8 %collective-permute-start.26 = (bf16[192,384]{1,0:T(8,128)(2,1)S(1)}, bf16[192,384]{1,0:T(8,128)(2,1)S(1)}, u32[]{:S(2)}, u32[]{:S(2)}) collective-permute-start(bf16[192,384]{1,0:T(8,128)(2,1)S(1)} %get-tuple-element.88), channel_id=1, source_target_pairs={{0,4},{1,5},{2,6},{3,7},{4,0},{5,1},{6,2},{7,3},{8,12},{9,13},{10,... | collective-permute-start | bytes 442376 | tf_op jit(solution)/shard_map/ppermute | solution.py:301
  154.1 1.7 collective-permute-start.27
  155.8 1.2 fusion.11
  157.1 4.7 %collective-permute-done.9 = bf16[416,768]{1,0:T(8,128)(2,1)S(1)} collective-permute-done((bf16[416,768]{1,0:T(8,128)(2,1)S(1)}, bf16[416,768]{1,0:T(8,128)(2,1)S(1)}, u32[]{:S(2)}, u32[]{:S(2)}) %collective-permute-start.9) | collective-permute-done | bytes 639008 | tf_op jit(solution)/shard_map/ppermute | solution.py:298
  162.8 3.9 %collective-permute-start.19 = (bf16[48,1536]{1,0:T(8,128)(2,1)S(1)}, bf16[48,1536]{1,0:T(8,128)(2,1)S(1)}, u32[]{:S(2)}, u32[]{:S(2)}) collective-permute-start(bf16[48,1536]{1,0:T(8,128)(2,1)S(1)} %get-tuple-element.93), channel_id=1, source_target_pairs={{0,4},{1,5},{2,6},{3,7},{4,0},{5,1},{6,2},{7,3},{8,12},{9,13},{10,... | collective-permute-start | bytes 442376 | tf_op jit(solution)/shard_map/ppermute | solution.py:301
  169.1 7.9 %collective-permute-done.19 = bf16[48,1536]{1,0:T(8,128)(2,1)S(1)} collective-permute-done((bf16[48,1536]{1,0:T(8,128)(2,1)S(1)}, bf16[48,1536]{1,0:T(8,128)(2,1)S(1)}, u32[]{:S(2)}, u32[]{:S(2)}) %collective-permute-start.19) | collective-permute-done | bytes 147488 | tf_op jit(solution)/shard_map/ppermute | solution.py:301
  178.4 4.0 %collective-permute-done.21 = bf16[48,1536]{1,0:T(8,128)(2,1)S(1)} collective-permute-done((bf16[48,1536]{1,0:T(8,128)(2,1)S(1)}, bf16[48,1536]{1,0:T(8,128)(2,1)S(1)}, u32[]{:S(2)}, u32[]{:S(2)}) %collective-permute-start.21) | collective-permute-done | bytes 147488 | tf_op jit(solution)/shard_map/ppermute | solution.py:298
  182.7 2.7 %collective-permute-start.11 = (bf16[80,768]{1,0:T(8,128)(2,1)S(1)}, bf16[80,768]{1,0:T(8,128)(2,1)S(1)}, u32[]{:S(2)}, u32[]{:S(2)}) collective-permute-start(bf16[80,768]{1,0:T(8,128)(2,1)S(1)} %get-tuple-element.123), channel_id=1, source_target_pairs={{0,2},{1,3},{2,0},{3,1},{4,6},{5,7},{6,4},{7,5},{8,10},{9,11},{10,... | collective-permute-start | bytes 368648 | tf_op jit(solution)/shard_map/ppermute | solution.py:301
  186.4 1.4 collective-permute-start.13
  188.9 2.4 %collective-permute-done.11 = bf16[80,768]{1,0:T(8,128)(2,1)S(1)} collective-permute-done((bf16[80,768]{1,0:T(8,128)(2,1)S(1)}, bf16[80,768]{1,0:T(8,128)(2,1)S(1)}, u32[]{:S(2)}, u32[]{:S(2)}) %collective-permute-start.11) | collective-permute-done | bytes 122912 | tf_op jit(solution)/shard_map/ppermute | solution.py:301
  192.4 5.4 %collective-permute-done.12 = bf16[80,768]{1,0:T(8,128)(2,1)S(1)} collective-permute-done((bf16[80,768]{1,0:T(8,128)(2,1)S(1)}, bf16[80,768]{1,0:T(8,128)(2,1)S(1)}, u32[]{:S(2)}, u32[]{:S(2)}) %collective-permute-start.12) | collective-permute-done | bytes 122912 | tf_op jit(solution)/shard_map/ppermute | solution.py:301
  202.6 2.5 %collective-permute-start.5 = (bf16[112,768]{1,0:T(8,128)(2,1)S(1)}, bf16[112,768]{1,0:T(8,128)(2,1)S(1)}, u32[]{:S(2)}, u32[]{:S(2)}) collective-permute-start(bf16[112,768]{1,0:T(8,128)(2,1)S(1)} %get-tuple-element.81), channel_id=1, source_target_pairs={{0,2},{1,3},{2,0},{3,1},{4,6},{5,7},{6,4},{7,5},{8,10},{9,11},{10,... | collective-permute-start | bytes 516104 | tf_op jit(solution)/shard_map/ppermute | solution.py:301
  206.1 1.4 collective-permute-start.7
  208.7 2.6 %collective-permute-done.5 = bf16[112,768]{1,0:T(8,128)(2,1)S(1)} collective-permute-done((bf16[112,768]{1,0:T(8,128)(2,1)S(1)}, bf16[112,768]{1,0:T(8,128)(2,1)S(1)}, u32[]{:S(2)}, u32[]{:S(2)}) %collective-permute-start.5) | collective-permute-done | bytes 172064 | tf_op jit(solution)/shard_map/ppermute | solution.py:301
  211.3 9.4 %collective-permute-done.6 = bf16[112,768]{1,0:T(8,128)(2,1)S(1)} collective-permute-done((bf16[112,768]{1,0:T(8,128)(2,1)S(1)}, bf16[112,768]{1,0:T(8,128)(2,1)S(1)}, u32[]{:S(2)}, u32[]{:S(2)}) %collective-permute-start.6) | collective-permute-done | bytes 172064 | tf_op jit(solution)/shard_map/ppermute | solution.py:301
  223.0 3.0 %collective-permute-done.14 = bf16[48,1536]{1,0:T(8,128)(2,1)S(1)} collective-permute-done((bf16[48,1536]{1,0:T(8,128)(2,1)S(1)}, bf16[48,1536]{1,0:T(8,128)(2,1)S(1)}, u32[]{:S(2)}, u32[]{:S(2)}) %collective-permute-start.14) | collective-permute-done | bytes 147488 | tf_op jit(solution)/shard_map/ppermute | solution.py:298
  227.3 1.6 fusion.39
  (269 shorter events, 50.2 us)
Async XLA Ops:
  0.7 44.4 %copy-start = (bf16[768,768]{1,0:T(8,128)(2,1)S(1)}, bf16[768,768]{1,0:T(8,128)(2,1)}, u32[]{:S(2)}) copy-start(bf16[768,768]{1,0:T(8,128)(2,1)} %param.28) | copy-start | bytes 3538948
  0.7 3.4 %copy-start.61 = (s32[256]{0:T(256)S(1)}, s32[256]{0:T(256)}, u32[]{:S(2)}) copy-start(s32[256]{0:T(256)} %param.24) | copy-start | bytes 3076
  4.0 42.3 %copy-start.25 = (bf16[256,768]{1,0:T(8,128)(2,1)}, bf16[256,768]{1,0:T(8,128)(2,1)S(1)}, u32[]{:S(2)}) copy-start(bf16[256,768]{1,0:T(8,128)(2,1)S(1)} %get-tuple-element.104) | copy-start | bytes 1179652
  4.4 35.7 %copy-start.51 = (bf16[768]{0:T(1024)(128)(2,1)S(1)}, bf16[768]{0:T(1024)(128)(2,1)}, u32[]{:S(2)}) copy-start(bf16[768]{0:T(1024)(128)(2,1)} %param.32) | copy-start | bytes 4612
  4.4 36.4 %copy-start.54 = (bf16[768]{0:T(1024)(128)(2,1)S(1)}, bf16[768]{0:T(1024)(128)(2,1)}, u32[]{:S(2)}) copy-start(bf16[768]{0:T(1024)(128)(2,1)} %param.29) | copy-start | bytes 4612
  40.0 3.4 %copy-start.52 = (bf16[3072]{0:T(1024)(128)(2,1)S(1)}, bf16[3072]{0:T(1024)(128)(2,1)}, u32[]{:S(2)}) copy-start(bf16[3072]{0:T(1024)(128)(2,1)} %param.38) | copy-start | bytes 18436
  40.1 4.0 %copy-start.53 = (s32[256]{0:T(256)S(1)}, s32[256]{0:T(256)}, u32[]{:S(2)}) copy-start(s32[256]{0:T(256)} %param.25) | copy-start | bytes 3076
  79.2 4.3 %copy-start.6 = (bf16[256,768]{1,0:T(8,128)(2,1)}, bf16[256,768]{1,0:T(8,128)(2,1)S(1)}, u32[]{:S(2)}) copy-start(bf16[256,768]{1,0:T(8,128)(2,1)S(1)} %get-tuple-element.54.grad_ref) | copy-start | bytes 1179652
  79.2 4.3 %copy-start.8 = (bf16[256,768]{1,0:T(8,128)(2,1)}, bf16[256,768]{1,0:T(8,128)(2,1)S(1)}, u32[]{:S(2)}) copy-start(bf16[256,768]{1,0:T(8,128)(2,1)S(1)} %get-tuple-element.56) | copy-start | bytes 1179652
  79.2 4.3 %copy-start.10 = (bf16[256,768]{1,0:T(8,128)(2,1)}, bf16[256,768]{1,0:T(8,128)(2,1)S(1)}, u32[]{:S(2)}) copy-start(bf16[256,768]{1,0:T(8,128)(2,1)S(1)} %get-tuple-element.63) | copy-start | bytes 1179652
  79.2 4.3 %copy-start.13 = (f32[8,768]{1,0:T(8,128)}, f32[8,768]{1,0:T(8,128)S(1)}, u32[]{:S(2)}) copy-start(f32[8,768]{1,0:T(8,128)S(1)} %get-tuple-element.64) | copy-start | bytes 73732
  83.5 8.7 %collective-permute-start = (bf16[3072,384]{1,0:T(8,128)(2,1)}, bf16[3072,384]{1,0:T(8,128)(2,1)}, u32[]{:S(2)}, u32[]{:S(2)}) collective-permute-start(bf16[3072,384]{1,0:T(8,128)(2,1)} %convolution_convert_fusion), channel_id=1, source_target_pairs={{0,8},{8,0},{16,24},{24,16},{1,9},{9,1},{17,25},{25,17},{2,10},{10... | collective-permute-start | bytes 7077896 | tf_op jit(solution)/shard_map/ppermute | solution.py:298
  83.6 6.0 %copy-start.11 = (bf16[256,768]{1,0:T(8,128)(2,1)S(1)}, bf16[256,768]{1,0:T(8,128)(2,1)}, u32[]{:S(2)}) copy-start(bf16[256,768]{1,0:T(8,128)(2,1)} %copy-done.10) | copy-start | bytes 1179652
  87.1 11.2 %collective-permute-start.1 = (bf16[768,1536]{1,0:T(8,128)(2,1)}, bf16[768,1536]{1,0:T(8,128)(2,1)}, u32[]{:S(2)}, u32[]{:S(2)}) collective-permute-start(bf16[768,1536]{1,0:T(8,128)(2,1)} %convolution_convert_fusion.1), channel_id=1, source_target_pairs={{0,8},{8,0},{16,24},{24,16},{1,9},{9,1},{17,25},{25,17},{2,10},{10... | collective-permute-start | bytes 7077896 | tf_op jit(solution)/shard_map/ppermute | solution.py:298
  96.9 32.9 %collective-permute-start.23 = (bf16[4,384,384]{2,1,0:T(8,128)(2,1)}, bf16[4,384,384]{2,1,0:T(8,128)(2,1)}, u32[]{:S(2)}, u32[]{:S(2)}) collective-permute-start(bf16[4,384,384]{2,1,0:T(8,128)(2,1)} %dynamic-slice_bitcast_fusion.1.refs_0_), channel_id=1, source_target_pairs={{0,1},{1,0},{2,3},{3,2},{4,5},{5,4},{6,7},{7,6},{8,9},{9,8},{10,11... | collective-permute-start | bytes 3538952 | tf_op jit(solution)/shard_map/ppermute | solution.py:301
  98.3 5.8 %copy-start.7 = (bf16[256,768]{1,0:T(8,128)(2,1)S(1)}, bf16[256,768]{1,0:T(8,128)(2,1)}, u32[]{:S(2)}) copy-start(bf16[256,768]{1,0:T(8,128)(2,1)} %copy-done.6) | copy-start | bytes 1179652
  102.7 30.8 %collective-permute-start.16 = (bf16[4,2,48,1536]{3,2,1,0:T(8,128)(2,1)}, bf16[4,2,48,1536]{3,2,1,0:T(8,128)(2,1)}, u32[]{:S(2)}, u32[]{:S(2)}) collective-permute-start(bf16[4,2,48,1536]{3,2,1,0:T(8,128)(2,1)} %dynamic-slice_bitcast_fusion.refs_1_), channel_id=1, source_target_pairs={{0,16},{8,24},{16,0},{24,8},{1,17},{9,25},{17,1},{25,9},{2,18},{10... | collective-permute-start | bytes 3538952 | tf_op jit(solution)/shard_map/ppermute | solution.py:298
  104.2 7.9 %copy-start.42 = (bf16[768,768]{1,0:T(8,128)(2,1)S(1)}, bf16[768,768]{1,0:T(8,128)(2,1)}, u32[]{:S(2)}) copy-start(bf16[768,768]{1,0:T(8,128)(2,1)} %key_w_ref.1) | copy-start | bytes 3538948
  123.5 16.1 %collective-permute-start.8 = (bf16[800,768]{1,0:T(8,128)(2,1)}, bf16[800,768]{1,0:T(8,128)(2,1)}, u32[]{:S(2)}, u32[]{:S(2)}) collective-permute-start(bf16[800,768]{1,0:T(8,128)(2,1)} %pad_maximum_fusion), channel_id=1, source_target_pairs={{0,8},{8,0},{16,24},{24,16},{1,9},{9,1},{17,25},{25,17},{2,10},{10... | collective-permute-start | bytes 3686408 | tf_op jit(solution)/shard_map/ppermute | solution.py:298
  124.6 12.1 %collective-permute-start.2 = (bf16[768,768]{0,1:T(8,128)(2,1)S(1)}, bf16[768,768]{0,1:T(8,128)(2,1)S(1)}, u32[]{:S(2)}, u32[]{:S(2)}) collective-permute-start(bf16[768,768]{0,1:T(8,128)(2,1)S(1)} %pad_maximum_fusion.2), channel_id=1, source_target_pairs={{0,8},{8,0},{16,24},{24,16},{1,9},{9,1},{17,25},{25,17},{2,10},{10... | collective-permute-start | bytes 3538952 | tf_op jit(solution)/shard_map/ppermute | solution.py:298
  129.7 3.8 %copy-start.24 = (bf16[768,1536]{1,0:T(8,128)(2,1)S(1)}, bf16[768,1536]{1,0:T(8,128)(2,1)}, u32[]{:S(2)}) copy-start(bf16[768,1536]{1,0:T(8,128)(2,1)} %copy-done.23) | copy-start | bytes 7077892
  132.5 16.5 %collective-permute-start.24 = (bf16[4,192,384]{2,1,0:T(8,128)(2,1)}, bf16[4,192,384]{2,1,0:T(8,128)(2,1)}, u32[]{:S(2)}, u32[]{:S(2)}) collective-permute-start(bf16[4,192,384]{2,1,0:T(8,128)(2,1)} %dynamic-slice_bitcast_fusion.2), channel_id=1, source_target_pairs={{0,16},{8,24},{16,0},{24,8},{1,17},{9,25},{17,1},{25,9},{2,18},{10... | collective-permute-start | bytes 1769480 | tf_op jit(solution)/shard_map/ppermute | solution.py:298
  136.0 18.1 %collective-permute-start.17 = (bf16[4,48,1536]{2,1,0:T(8,128)(2,1)}, bf16[4,48,1536]{2,1,0:T(8,128)(2,1)}, u32[]{:S(2)}, u32[]{:S(2)}) collective-permute-start(bf16[4,48,1536]{2,1,0:T(8,128)(2,1)} %dynamic-slice_bitcast_fusion.3), channel_id=1, source_target_pairs={{0,1},{1,0},{2,3},{3,2},{4,5},{5,4},{6,7},{7,6},{8,9},{9,8},{10,11... | collective-permute-start | bytes 1769480 | tf_op jit(solution)/shard_map/ppermute | solution.py:301
  138.5 47.9 %collective-permute-start.3 = (bf16[4,160,768]{2,1,0:T(8,128)(2,1)S(1)}, bf16[4,160,768]{2,1,0:T(8,128)(2,1)S(1)}, u32[]{:S(2)}, u32[]{:S(2)}) collective-permute-start(bf16[4,160,768]{2,1,0:T(8,128)(2,1)S(1)} %fusion.14), channel_id=1, source_target_pairs={{0,1},{1,0},{2,3},{3,2},{4,5},{5,4},{6,7},{7,6},{8,9},{9,8},{10,11... | collective-permute-start | bytes 2949128 | tf_op jit(solution)/shard_map/ppermute | solution.py:301
  142.1 6.9 %copy-start.34 = (bf16[4,384,384]{2,1,0:T(8,128)(2,1)S(1)}, bf16[4,384,384]{2,1,0:T(8,128)(2,1)}, u32[]{:S(2)}) copy-start(bf16[4,384,384]{2,1,0:T(8,128)(2,1)} %copy-done.33) | copy-start | bytes 3538948
  142.1 13.7 %copy-start.32 = (bf16[4,2,48,1536]{3,2,1,0:T(8,128)(2,1)S(1)}, bf16[4,2,48,1536]{3,2,1,0:T(8,128)(2,1)}, u32[]{:S(2)}) copy-start(bf16[4,2,48,1536]{3,2,1,0:T(8,128)(2,1)} %copy-done.31) | copy-start | bytes 3538948
  142.2 19.6 %collective-permute-start.9 = (bf16[416,768]{1,0:T(8,128)(2,1)S(1)}, bf16[416,768]{1,0:T(8,128)(2,1)S(1)}, u32[]{:S(2)}, u32[]{:S(2)}) collective-permute-start(bf16[416,768]{1,0:T(8,128)(2,1)S(1)} %pad_maximum_fusion.4), channel_id=1, source_target_pairs={{0,16},{8,24},{16,0},{24,8},{1,17},{9,25},{17,1},{25,9},{2,18},{10... | collective-permute-start | bytes 1916936 | tf_op jit(solution)/shard_map/ppermute | solution.py:298
  150.2 12.5 %collective-permute-start.25 = (bf16[192,384]{1,0:T(8,128)(2,1)S(1)}, bf16[192,384]{1,0:T(8,128)(2,1)S(1)}, u32[]{:S(2)}, u32[]{:S(2)}) collective-permute-start(bf16[192,384]{1,0:T(8,128)(2,1)S(1)} %get-tuple-element.86), channel_id=1, source_target_pairs={{0,2},{1,3},{2,0},{3,1},{4,6},{5,7},{6,4},{7,5},{8,10},{9,11},{10,... | collective-permute-start | bytes 442376 | tf_op jit(solution)/shard_map/ppermute | solution.py:301
  150.3 16.3 %collective-permute-start.26 = (bf16[192,384]{1,0:T(8,128)(2,1)S(1)}, bf16[192,384]{1,0:T(8,128)(2,1)S(1)}, u32[]{:S(2)}, u32[]{:S(2)}) collective-permute-start(bf16[192,384]{1,0:T(8,128)(2,1)S(1)} %get-tuple-element.88), channel_id=1, source_target_pairs={{0,4},{1,5},{2,6},{3,7},{4,0},{5,1},{6,2},{7,3},{8,12},{9,13},{10,... | collective-permute-start | bytes 442376 | tf_op jit(solution)/shard_map/ppermute | solution.py:301
  154.1 13.1 %collective-permute-start.27 = (bf16[192,384]{1,0:T(8,128)(2,1)S(1)}, bf16[192,384]{1,0:T(8,128)(2,1)S(1)}, u32[]{:S(2)}, u32[]{:S(2)}) collective-permute-start(bf16[192,384]{1,0:T(8,128)(2,1)S(1)} %get-tuple-element.87), channel_id=1, source_target_pairs={{0,6},{1,7},{2,4},{3,5},{4,2},{5,3},{6,0},{7,1},{8,14},{9,15},{10,... | collective-permute-start | bytes 442376 | tf_op jit(solution)/shard_map/ppermute | solution.py:301
  161.7 6.3 %collective-permute-start.18 = (bf16[48,1536]{1,0:T(8,128)(2,1)S(1)}, bf16[48,1536]{1,0:T(8,128)(2,1)S(1)}, u32[]{:S(2)}, u32[]{:S(2)}) collective-permute-start(bf16[48,1536]{1,0:T(8,128)(2,1)S(1)} %get-tuple-element.91), channel_id=1, source_target_pairs={{0,2},{1,3},{2,0},{3,1},{4,6},{5,7},{6,4},{7,5},{8,10},{9,11},{10,... | collective-permute-start | bytes 442376 | tf_op jit(solution)/shard_map/ppermute | solution.py:301
  162.8 14.3 %collective-permute-start.19 = (bf16[48,1536]{1,0:T(8,128)(2,1)S(1)}, bf16[48,1536]{1,0:T(8,128)(2,1)S(1)}, u32[]{:S(2)}, u32[]{:S(2)}) collective-permute-start(bf16[48,1536]{1,0:T(8,128)(2,1)S(1)} %get-tuple-element.93), channel_id=1, source_target_pairs={{0,4},{1,5},{2,6},{3,7},{4,0},{5,1},{6,2},{7,3},{8,12},{9,13},{10,... | collective-permute-start | bytes 442376 | tf_op jit(solution)/shard_map/ppermute | solution.py:301
  166.7 10.4 %collective-permute-start.20 = (bf16[48,1536]{1,0:T(8,128)(2,1)S(1)}, bf16[48,1536]{1,0:T(8,128)(2,1)S(1)}, u32[]{:S(2)}, u32[]{:S(2)}) collective-permute-start(bf16[48,1536]{1,0:T(8,128)(2,1)S(1)} %get-tuple-element.92), channel_id=1, source_target_pairs={{0,6},{1,7},{2,4},{3,5},{4,2},{5,3},{6,0},{7,1},{8,14},{9,15},{10,... | collective-permute-start | bytes 442376 | tf_op jit(solution)/shard_map/ppermute | solution.py:301
  167.2 15.2 %collective-permute-start.10 = (bf16[224,768]{1,0:T(8,128)(2,1)S(1)}, bf16[224,768]{1,0:T(8,128)(2,1)S(1)}, u32[]{:S(2)}, u32[]{:S(2)}) collective-permute-start(bf16[224,768]{1,0:T(8,128)(2,1)S(1)} %pad_maximum_fusion.6), channel_id=1, source_target_pairs={{0,1},{1,0},{2,3},{3,2},{4,5},{5,4},{6,7},{7,6},{8,9},{9,8},{10,11... | collective-permute-start | bytes 1032200 | tf_op jit(solution)/shard_map/ppermute | solution.py:301
  168.0 10.2 %collective-permute-start.28 = (bf16[192,384]{1,0:T(8,128)(2,1)S(1)}, bf16[192,384]{1,0:T(8,128)(2,1)S(1)}, u32[]{:S(2)}, u32[]{:S(2)}) collective-permute-start(bf16[192,384]{1,0:T(8,128)(2,1)S(1)} %fusion.35), channel_id=1, source_target_pairs={{0,16},{8,24},{16,0},{24,8},{1,17},{9,25},{17,1},{25,9},{2,18},{10... | collective-permute-start | bytes 442376 | tf_op jit(solution)/shard_map/ppermute | solution.py:298
  177.1 5.2 %collective-permute-start.21 = (bf16[48,1536]{1,0:T(8,128)(2,1)S(1)}, bf16[48,1536]{1,0:T(8,128)(2,1)S(1)}, u32[]{:S(2)}, u32[]{:S(2)}) collective-permute-start(bf16[48,1536]{1,0:T(8,128)(2,1)S(1)} %fusion.38), channel_id=1, source_target_pairs={{0,16},{8,24},{16,0},{24,8},{1,17},{9,25},{17,1},{25,9},{2,18},{10... | collective-permute-start | bytes 442376 | tf_op jit(solution)/shard_map/ppermute | solution.py:298
  178.3 43.6 %collective-permute-start.29 = (bf16[384,384]{1,0:T(8,128)(2,1)S(1)}, bf16[384,384]{1,0:T(8,128)(2,1)}, u32[]{:S(2)}, u32[]{:S(2)}) collective-permute-start(bf16[384,384]{1,0:T(8,128)(2,1)S(1)} %pad_maximum_fusion.8), channel_id=1, source_target_pairs={{0,8},{8,0},{16,24},{24,16},{1,9},{9,1},{17,25},{25,17},{2,10},{10... | collective-permute-start | bytes 884744 | tf_op jit(solution)/shard_map/ppermute | solution.py:298
  182.4 19.0 %collective-permute-start.22 = (bf16[96,1536]{1,0:T(8,128)(2,1)S(1)}, bf16[96,1536]{1,0:T(8,128)(2,1)}, u32[]{:S(2)}, u32[]{:S(2)}) collective-permute-start(bf16[96,1536]{1,0:T(8,128)(2,1)S(1)} %pad_maximum_fusion.7), channel_id=1, source_target_pairs={{0,8},{8,0},{16,24},{24,16},{1,9},{9,1},{17,25},{25,17},{2,10},{10... | collective-permute-start | bytes 884744 | tf_op jit(solution)/shard_map/ppermute | solution.py:298
  182.7 8.7 %collective-permute-start.11 = (bf16[80,768]{1,0:T(8,128)(2,1)S(1)}, bf16[80,768]{1,0:T(8,128)(2,1)S(1)}, u32[]{:S(2)}, u32[]{:S(2)}) collective-permute-start(bf16[80,768]{1,0:T(8,128)(2,1)S(1)} %get-tuple-element.123), channel_id=1, source_target_pairs={{0,2},{1,3},{2,0},{3,1},{4,6},{5,7},{6,4},{7,5},{8,10},{9,11},{10,... | collective-permute-start | bytes 368648 | tf_op jit(solution)/shard_map/ppermute | solution.py:301
  185.4 12.4 %collective-permute-start.12 = (bf16[80,768]{1,0:T(8,128)(2,1)S(1)}, bf16[80,768]{1,0:T(8,128)(2,1)S(1)}, u32[]{:S(2)}, u32[]{:S(2)}) collective-permute-start(bf16[80,768]{1,0:T(8,128)(2,1)S(1)} %get-tuple-element.124), channel_id=1, source_target_pairs={{0,4},{1,5},{2,6},{3,7},{4,0},{5,1},{6,2},{7,3},{8,12},{9,13},{10,... | collective-permute-start | bytes 368648 | tf_op jit(solution)/shard_map/ppermute | solution.py:301
  186.4 11.4 %collective-permute-start.13 = (bf16[80,768]{1,0:T(8,128)(2,1)S(1)}, bf16[80,768]{1,0:T(8,128)(2,1)S(1)}, u32[]{:S(2)}, u32[]{:S(2)}) collective-permute-start(bf16[80,768]{1,0:T(8,128)(2,1)S(1)} %get-tuple-element.125), channel_id=1, source_target_pairs={{0,6},{1,7},{2,4},{3,5},{4,2},{5,3},{6,0},{7,1},{8,14},{9,15},{10,... | collective-permute-start | bytes 368648 | tf_op jit(solution)/shard_map/ppermute | solution.py:301
  191.4 6.5 %copy-start.46 = (bf16[80,768]{1,0:T(8,128)(2,1)}, bf16[80,768]{1,0:T(8,128)(2,1)S(1)}, u32[]{:S(2)}) copy-start(bf16[80,768]{1,0:T(8,128)(2,1)S(1)} %collective-permute-done.11) | copy-start | bytes 368644
  191.4 11.1 %collective-permute-start.4 = (bf16[4,48,768]{2,1,0:T(8,128)(2,1)}, bf16[4,48,768]{2,1,0:T(8,128)(2,1)S(1)}, u32[]{:S(2)}, u32[]{:S(2)}) collective-permute-start(bf16[4,48,768]{2,1,0:T(8,128)(2,1)} %dynamic-slice_bitcast_fusion.4), channel_id=1, source_target_pairs={{0,16},{8,24},{16,0},{24,8},{1,17},{9,25},{17,1},{25,9},{2,18},{10... | collective-permute-start | bytes 884744 | tf_op jit(solution)/shard_map/ppermute | solution.py:298
  202.6 8.6 %collective-permute-start.5 = (bf16[112,768]{1,0:T(8,128)(2,1)S(1)}, bf16[112,768]{1,0:T(8,128)(2,1)S(1)}, u32[]{:S(2)}, u32[]{:S(2)}) collective-permute-start(bf16[112,768]{1,0:T(8,128)(2,1)S(1)} %get-tuple-element.81), channel_id=1, source_target_pairs={{0,2},{1,3},{2,0},{3,1},{4,6},{5,7},{6,4},{7,5},{8,10},{9,11},{10,... | collective-permute-start | bytes 516104 | tf_op jit(solution)/shard_map/ppermute | solution.py:301
  205.1 15.5 %collective-permute-start.6 = (bf16[112,768]{1,0:T(8,128)(2,1)S(1)}, bf16[112,768]{1,0:T(8,128)(2,1)S(1)}, u32[]{:S(2)}, u32[]{:S(2)}) collective-permute-start(bf16[112,768]{1,0:T(8,128)(2,1)S(1)} %get-tuple-element.82), channel_id=1, source_target_pairs={{0,4},{1,5},{2,6},{3,7},{4,0},{5,1},{6,2},{7,3},{8,12},{9,13},{10,... | collective-permute-start | bytes 516104 | tf_op jit(solution)/shard_map/ppermute | solution.py:301
  206.1 14.5 %collective-permute-start.7 = (bf16[112,768]{1,0:T(8,128)(2,1)S(1)}, bf16[112,768]{1,0:T(8,128)(2,1)S(1)}, u32[]{:S(2)}, u32[]{:S(2)}) collective-permute-start(bf16[112,768]{1,0:T(8,128)(2,1)S(1)} %get-tuple-element.83), channel_id=1, source_target_pairs={{0,6},{1,7},{2,4},{3,5},{4,2},{5,3},{6,0},{7,1},{8,14},{9,15},{10,... | collective-permute-start | bytes 516104 | tf_op jit(solution)/shard_map/ppermute | solution.py:301
  220.8 5.2 %collective-permute-start.14 = (bf16[48,1536]{1,0:T(8,128)(2,1)S(1)}, bf16[48,1536]{1,0:T(8,128)(2,1)S(1)}, u32[]{:S(2)}, u32[]{:S(2)}) collective-permute-start(bf16[48,1536]{1,0:T(8,128)(2,1)S(1)} %pad_maximum_fusion.15), channel_id=1, source_target_pairs={{0,16},{8,24},{16,0},{24,8},{1,17},{9,25},{17,1},{25,9},{2,18},{10... | collective-permute-start | bytes 442376 | tf_op jit(solution)/shard_map/ppermute | solution.py:298
  226.1 2.8 %collective-permute-start.15 = (bf16[96,1536]{1,0:T(8,128)(2,1)S(1)}, bf16[96,1536]{1,0:T(8,128)(2,1)S(1)}, u32[]{:S(2)}, u32[]{:S(2)}) collective-permute-start(bf16[96,1536]{1,0:T(8,128)(2,1)S(1)} %pad_maximum_fusion.5), channel_id=1, source_target_pairs={{0,8},{8,0},{16,24},{24,16},{1,9},{9,1},{17,25},{25,17},{2,10},{10... | collective-permute-start | bytes 884744 | tf_op jit(solution)/shard_map/ppermute | solution.py:298
  (44 other events, 81.2 us)

commit v3 on v2

v3 whole, which is shorter than its diff:
```python
import math

import jax
import jax.numpy as jnp
from jax import lax
from jax.experimental import pallas as pl
from jax.experimental.pallas import tpu as pltpu
from jax.sharding import PartitionSpec as P

HEADS = 12
HEAD_DIM = 64
TAB_MAX = 64
LANES = 256
far_below = -1e30
BF = jnp.bfloat16
F32 = jnp.float32
MIB = 1 << 20


def outer_sum(left, right):
    return lax.dot_general(left, right, (((0,), (0,)), ((), ())), preferred_element_type=F32)


def back_dot(left, right):
    return lax.dot_general(left, right, (((1,), (1,)), ((), ())), preferred_element_type=F32)


def fwd_dot(left, right):
    return jnp.dot(left, right, preferred_element_type=F32)


def norm_parts(values):
    centred = values - jnp.mean(values, axis=-1, keepdims=True)
    spread = jnp.mean(centred * centred, axis=-1, keepdims=True)
    inv = lax.rsqrt(spread + 1e-06)
    return centred * inv, inv


def norm_grad(grad, normed, inv, gain):
    scaled = grad * gain
    return inv * (
        scaled
        - jnp.mean(scaled, axis=-1, keepdims=True)
        - normed * jnp.mean(scaled * normed, axis=-1, keepdims=True)
    )


def head_lanes(shape, index):
    lane = lax.broadcasted_iota(jnp.int32, shape, len(shape) - 1)
    return (lane >= index * HEAD_DIM) & (lane < (index + 1) * HEAD_DIM)


def column_of(row):
    return jnp.broadcast_to(row, (128, row.shape[1])).T[:, :1]


def entry_kernel(tokens_ref, seg_ref, prev_ref, answer_ref, payload_ref, input_ref):
    tab = TAB_MAX
    prev = prev_ref[...].astype(F32)[None]
    low = residual(tokens_ref, prev, answer_ref).astype(BF)
    input_ref[...] = low
    payload_ref[:tab] = low[:tab]
    payload_ref[tab:] = jnp.zeros((16, low.shape[1]), BF)
    lane = lax.broadcasted_iota(jnp.int32, (1, 128), 1)

    def twice(row):
        row = row[:, :128]
        return jnp.where(lane < tab, row, pltpu.roll(row, tab, 1))

    is_open = twice(jnp.where(seg_ref[...] == 0, 1.0, 0.0)[None])
    both = jnp.concatenate([is_open, twice(prev)], axis=1)
    payload_ref[tab:, :256] = jnp.broadcast_to(both, (16, 256)).astype(BF)


def residual(tokens_ref, prev, answer_ref):
    answers = answer_ref[...].astype(F32)
    return tokens_ref[...].astype(F32) + jnp.where(column_of(prev) == 1.0, answers[1:2], answers[0:1])


def entry(tokens, seg, prev, answers):
    rows, width = tokens.shape
    vmem = pl.BlockSpec(memory_space=pltpu.VMEM)
    return pl.pallas_call(
        entry_kernel,
        in_specs=[vmem] * 4,
        out_specs=[vmem] * 2,
        out_shape=[jax.ShapeDtypeStruct((TAB_MAX + 16, width), BF), jax.ShapeDtypeStruct((rows, width), BF)],
        compiler_params=pltpu.CompilerParams(vmem_limit_bytes=12 * MIB),
    )(tokens, seg, prev, answers)


def own_kernel(
    input_ref, query_w_ref, key_w_ref, value_w_ref, query_b_ref, value_b_ref, seg_ref, turn_ref,
    q_ref, k_ref, v_ref, bias_ref, value_row_ref,
):
    low = input_ref[...]
    query = fwd_dot(low, query_w_ref[...]) + query_b_ref[...].astype(F32)[None]
    q_ref[...] = (query.astype(BF).astype(F32) * HEAD_DIM**-0.5).astype(BF)
    k_ref[...] = fwd_dot(low, key_w_ref[...]).astype(BF)
    value_b = value_b_ref[...].astype(F32)[None]
    value_row_ref[...] = value_b
    v_ref[...] = (fwd_dot(low, value_w_ref[...]) + value_b).astype(BF)
    turn = turn_ref[...].astype(F32)[None]
    seg = seg_ref[...].astype(F32)[None]
    same = (column_of(turn) == turn) & (seg != 0.0)
    bias_ref[...] = jnp.where(same, 0.0, far_below)


def own_part(layer_input, query_w, key_w, value_w, query_b, value_b, seg, turn):
    rows, width = layer_input.shape
    vmem = pl.BlockSpec(memory_space=pltpu.VMEM)
    return pl.pallas_call(
        own_kernel,
        in_specs=[vmem] * 8,
        out_specs=[vmem] * 5,
        out_shape=[jax.ShapeDtypeStruct((rows, width), BF)] * 3
        + [jax.ShapeDtypeStruct((rows, rows), F32), jax.ShapeDtypeStruct((1, width), F32)],
        compiler_params=pltpu.CompilerParams(vmem_limit_bytes=20 * MIB),
        cost_estimate=pl.CostEstimate(flops=900_000_000, bytes_accessed=5 * MIB, transcendentals=0),
    )(layer_input, query_w, key_w, value_w, query_b, value_b, seg, turn)


def attend_kernel(
    input_ref, key_w_ref, value_w_ref, value_b_ref, q_ref, own_k_ref, own_v_ref, own_bias_ref, *refs
):
    *slots, keys_ref, values_ref, prob_ref, context_ref, x_t_ref, prev_ref, table_ref, bias_ref = refs
    n_table = table_ref.shape[0]
    tab = TAB_MAX

    @pl.when(pl.program_id(0) == 0)
    def _():
        lane = lax.broadcasted_iota(jnp.int32, (1, 128), 1)
        for i, slot in enumerate(slots):
            table_ref[i * tab : (i + 1) * tab] = slot[:tab]
        for i in range(0, len(slots), 2):
            marks = jnp.where(
                lax.broadcasted_iota(jnp.int32, (16, 256), 1) % 128 < tab,
                slots[i][tab:, :256].astype(F32), slots[i + 1][tab:, :256].astype(F32),
            )
            at = slice(i * tab, (i + 2) * tab)
            closed = jnp.where(marks[:1, :128] > 0.5, 0.0, far_below)
            bias_ref[:, at] = jnp.broadcast_to(closed, (bias_ref.shape[0], 128))
            prev_ref[:, at] = marks[:8, 128:]
        bias_ref[:, n_table:] = own_bias_ref[...]
        x_t_ref[:, :n_table] = table_ref[...].T
        x_t_ref[:, n_table:] = input_ref[...].T

    table = table_ref[...]
    keys_ref[:n_table] = fwd_dot(table, key_w_ref[...]).astype(BF)
    values_ref[:n_table] = (fwd_dot(table, value_w_ref[...]) + value_b_ref[...]).astype(BF)
    keys_ref[n_table:] = own_k_ref[...]
    values_ref[n_table:] = own_v_ref[...]
    queries = q_ref[...]
    context = jnp.zeros(context_ref.shape, F32)
    for h in range(queries.shape[1] // HEAD_DIM):
        mask = head_lanes(queries.shape, h)
        picked = jnp.where(mask, queries, jnp.zeros_like(queries))
        scores = back_dot(picked, keys_ref[...]) + bias_ref[...]
        top = jnp.max(scores, axis=-1, keepdims=True)
        weights = jnp.exp(scores - top)
        prob = (weights * (1.0 / jnp.sum(weights, axis=-1, keepdims=True))).astype(BF)
        prob_ref[h] = prob
        context = jnp.where(mask, fwd_dot(prob, values_ref[...]), context)
    context_ref[...] = context


def vmem_limit(n_keys, small):
    return (small if n_keys <= 1024 else 60) * MIB


def attend(slots, layer_input, key_w, value_w, value_b, queries, own_k, own_v, own_bias):
    rows, width = queries.shape
    n_table = len(slots) * TAB_MAX
    n_keys = n_table + rows
    group = LANES if n_keys <= 1024 else LANES // 2
    per = group // HEAD_DIM
    steady = {} if n_keys <= 1024 else {"pipeline_mode": pl.Buffered(1)}
    whole = lambda shape: pl.BlockSpec(shape, lambda i: (0, 0), **steady)
    lanes = lambda n: pl.BlockSpec((n, group), lambda i: (0, i))
    return pl.pallas_call(
        attend_kernel,
        grid=(width // group,),
        in_specs=[
            whole((rows, width)), lanes(width), lanes(width), lanes(1), lanes(rows), lanes(rows), lanes(rows),
            whole((rows, rows)),
        ]
        + [whole(slot.shape) for slot in slots],
        out_specs=[
            lanes(n_keys), lanes(n_keys), pl.BlockSpec((per, rows, n_keys), lambda i: (i, 0, 0)), lanes(rows),
            whole((width, n_keys)), whole((8, n_table)),
        ],
        out_shape=[
            jax.ShapeDtypeStruct((n_keys, width), BF),
            jax.ShapeDtypeStruct((n_keys, width), BF),
            jax.ShapeDtypeStruct((HEADS, rows, n_keys), BF),
            jax.ShapeDtypeStruct((rows, width), F32),
            jax.ShapeDtypeStruct((width, n_keys), BF),
            jax.ShapeDtypeStruct((8, n_table), F32),
        ],
        scratch_shapes=[pltpu.VMEM((n_table, width), BF), pltpu.VMEM((rows, n_keys), F32)],
        compiler_params=pltpu.CompilerParams(vmem_limit_bytes=vmem_limit(n_keys, 56)),
        cost_estimate=pl.CostEstimate(flops=100_000_000, bytes_accessed=1 * MIB, transcendentals=0),
    )(layer_input, key_w, value_w, value_b, queries, own_k, own_v, own_bias, *slots)


def middle_kernel(
    tokens_ref, prev_ref, answer_ref, context_ref, cot_ref, out_w_any, up_w_any, down_w_any, up_b_1d_ref, *refs
):
    biases, refs = refs[:6], refs[6:]
    mixed_ref, context_t_ref, middle_t_ref, act_t_ref, grad_ffn_ref, grad_pre_ref, grad_attn_ref = refs[:7]
    grad_context_ref, grad_mid_ref, sums_ref, up_sum_ref, slope_ref, total_ref, middle_low_ref = refs[7:14]
    out_w_ref, up_w_ref, down_w_ref, up_b_ref, sems = refs[14:]
    copies = [
        pltpu.make_async_copy(source, target, sems.at[i])
        for i, (source, target) in enumerate(
            ((out_w_any, out_w_ref), (up_w_any, up_w_ref), (down_w_any, down_w_ref))
        )
    ]
    for copy in copies:
        copy.start()
    hidden = up_w_ref.shape[1]
    tile = 512
    steps = hidden // tile
    out_b, norm_g, norm_s, down_b, final_g, final_s = (ref[...].astype(F32)[None] for ref in biases)
    up_b_ref[...] = up_b_1d_ref[...].astype(F32)[None]
    resid = residual(tokens_ref, prev_ref[...].astype(F32)[None], answer_ref)
    column = lambda v: jnp.sum(v, axis=0, keepdims=True)
    context_low = context_ref[...].astype(BF)
    context_t_ref[...] = context_low.T
    copies[0].wait()
    normed1, inv1 = norm_parts(resid + fwd_dot(context_low, out_w_ref[...]) + out_b)
    middle = normed1 * norm_g + norm_s
    middle_low = middle.astype(BF)
    middle_low_ref[...] = middle_low
    middle_t_ref[...] = middle_low.T
    total_ref[...] = middle + down_b
    copies[1].wait()
    copies[2].wait()

    def forward(i, carry):
        at = pl.ds(pl.multiple_of(i * tile, tile), tile)
        pre = fwd_dot(middle_low_ref[...], up_w_ref[:, at]) + up_b_ref[:, at]
        cdf = 0.5 * (1.0 + lax.erf(pre * (0.5**0.5)))
        act = (pre * cdf).astype(BF)
        act_t_ref[at, :] = act.T
        slope_ref[:, at] = cdf + pre * jnp.exp(-0.5 * pre * pre) * (1.0 / math.sqrt(2 * math.pi))
        total_ref[...] += fwd_dot(act, down_w_ref[at, :])
        return carry

    lax.fori_loop(0, steps, forward, 0)
    normed2, inv2 = norm_parts(total_ref[...])
    mixed_ref[...] = (normed2 * final_g + final_s).astype(BF)
    cot = cot_ref[...].astype(F32)
    grad_final = norm_grad(cot, normed2, inv2, final_g)
    grad_ffn = grad_final.astype(BF)
    grad_ffn_ref[...] = grad_ffn
    total_ref[...] = grad_final

    def backward(i, carry):
        at = pl.ds(pl.multiple_of(i * tile, tile), tile)
        grad_pre = (back_dot(grad_ffn_ref[...], down_w_ref[at, :]) * slope_ref[:, at]).astype(BF)
        grad_pre_ref[:, at] = grad_pre
        up_sum_ref[:, at] = column(grad_pre.astype(F32))
        total_ref[...] += back_dot(grad_pre, up_w_ref[:, at])
        return carry

    lax.fori_loop(0, steps, backward, 0)
    grad_middle = total_ref[...]
    grad_mid = norm_grad(grad_middle, normed1, inv1, norm_g)
    grad_mid_ref[...] = grad_mid
    grad_attn = grad_mid.astype(BF)
    grad_attn_ref[...] = grad_attn
    grad_context_ref[...] = back_dot(grad_attn, out_w_ref[...]).astype(BF)
    sums_ref[0:1] = column(grad_attn.astype(F32))
    sums_ref[1:2] = column(grad_middle * normed1)
    sums_ref[2:3] = column(grad_middle)
    sums_ref[3:4] = column(grad_ffn.astype(F32))
    sums_ref[4:5] = column(cot * normed2)
    sums_ref[5:6] = column(cot)
    sums_ref[6:8] = jnp.zeros((2, sums_ref.shape[1]), F32)


def middle_part(tokens, prev, answers, context, cot, out_w, up_w, down_w, up_b, *biases):
    rows, width = tokens.shape
    hidden = up_w.shape[1]
    vmem = pl.BlockSpec(memory_space=pltpu.VMEM)
    shape = lambda n, t: jax.ShapeDtypeStruct((rows, n), t)
    turned = lambda n: jax.ShapeDtypeStruct((n, rows), BF)
    return pl.pallas_call(
        middle_kernel,
        in_specs=[vmem] * 5 + [pl.BlockSpec(memory_space=pl.ANY)] * 3 + [vmem] * 7,
        out_specs=[vmem] * 11,
        out_shape=[
            shape(width, BF), turned(width), turned(width), turned(hidden), shape(width, BF),
            shape(hidden, BF), shape(width, BF), shape(width, BF), shape(width, F32),
            jax.ShapeDtypeStruct((8, width), F32), jax.ShapeDtypeStruct((1, hidden), F32),
        ],
        scratch_shapes=[
            pltpu.VMEM((rows, hidden), F32), pltpu.VMEM((rows, width), F32), pltpu.VMEM((rows, width), BF),
            pltpu.VMEM(out_w.shape, BF), pltpu.VMEM(up_w.shape, BF), pltpu.VMEM(down_w.shape, BF),
            pltpu.VMEM((1, hidden), F32), pltpu.SemaphoreType.DMA((3,)),
        ],
        compiler_params=pltpu.CompilerParams(vmem_limit_bytes=56 * MIB),
        cost_estimate=pl.CostEstimate(
            flops=4 * rows * width * (2 * hidden + width), bytes_accessed=24 * MIB, transcendentals=2 * rows * hidden
        ),
    )(tokens, prev, answers, context, cot, out_w, up_w, down_w, up_b, *biases)


def attend_back_kernel(
    q_ref, keys_ref, values_ref, prob_ref, context_ref, grad_ref, *refs
):
    grad_q_ref, grad_k_ref, grad_v_ref = refs[-3:]
    grad = grad_ref[...]
    grad_f = grad.astype(F32)
    product = grad_f * context_ref[...]
    grad_t = grad_f.T.astype(BF)
    q_t = q_ref[...].astype(F32).T.astype(BF)
    grad_q = jnp.zeros(grad.shape, F32)
    for h in range(grad.shape[1] // HEAD_DIM):
        mask = head_lanes(grad.shape, h)
        at = slice(h * HEAD_DIM, (h + 1) * HEAD_DIM)
        row_dot = jnp.sum(jnp.where(mask, product, 0.0), axis=-1, keepdims=True)
        grad_prob = back_dot(jnp.where(mask, grad, jnp.zeros_like(grad)), values_ref[...])
        prob = prob_ref[h]
        grad_score = (prob.astype(F32) * (grad_prob - row_dot)).astype(BF)
        grad_v_ref[at] = fwd_dot(grad_t[at], prob).astype(BF)
        grad_k_ref[at] = fwd_dot(q_t[at], grad_score).astype(BF)
        grad_q = jnp.where(mask, fwd_dot(grad_score, keys_ref[...]), grad_q)
    grad_q_ref[...] = (grad_q * HEAD_DIM**-0.5).astype(BF)


def attend_back(queries, keys, values, prob, context, grad_context, after):
    rows, width = queries.shape
    n_keys = keys.shape[0]
    group = LANES if n_keys <= 1024 else LANES // 2
    per = group // HEAD_DIM
    lanes = lambda n: pl.BlockSpec((n, group), lambda i: (0, i))
    return pl.pallas_call(
        attend_back_kernel,
        grid=(width // group,),
        in_specs=[
            lanes(rows), lanes(n_keys), lanes(n_keys), pl.BlockSpec((per, rows, n_keys), lambda i: (i, 0, 0)),
            lanes(rows), lanes(rows),
        ]
        + [pl.BlockSpec(memory_space=pl.ANY)] * len(after),
        out_specs=[lanes(rows)] + [pl.BlockSpec((group, n_keys), lambda i: (i, 0))] * 2,
        out_shape=[
            jax.ShapeDtypeStruct((rows, width), BF),
            jax.ShapeDtypeStruct((width, n_keys), BF),
            jax.ShapeDtypeStruct((width, n_keys), BF),
        ],
        compiler_params=pltpu.CompilerParams(vmem_limit_bytes=vmem_limit(n_keys, 20)),
        cost_estimate=pl.CostEstimate(flops=100_000_000, bytes_accessed=1 * MIB, transcendentals=0),
    )(queries, keys, values, prob, context, grad_context, *after)


def core_lanes(pos_ref, own, size):
    core = pos_ref[0] if own else 1 - pos_ref[0]
    return pl.ds(pl.multiple_of(core * size, 128), size)


def down_values(own, pos_ref, act_t_ref, context_t_ref, grad_ffn_ref, grad_attn_ref, blocks, store):
    half = grad_ffn_ref.shape[1] // 2
    at = core_lanes(pos_ref, own, half)
    grad_ffn = grad_ffn_ref[:, at]
    size = act_t_ref.shape[0] // blocks
    for b in range(blocks):
        store(b, 0, fwd_dot(act_t_ref[b * size : (b + 1) * size], grad_ffn))
    out = fwd_dot(context_t_ref[...], grad_attn_ref[:, at])
    small = out.shape[0] // blocks
    for b in range(blocks):
        store(b, size, out[b * small : (b + 1) * small])


def up_values(own, pos_ref, middle_t_ref, grad_pre_ref, blocks, store):
    half = grad_pre_ref.shape[1] // 2
    piece = middle_t_ref.shape[0] // 2
    small = middle_t_ref.shape[0] // blocks
    core = pos_ref[0] if own else 1 - pos_ref[0]
    for p in range(half // piece):
        at = pl.ds(pl.multiple_of(core * half + p * piece, 128), piece)
        value = fwd_dot(middle_t_ref[...], grad_pre_ref[:, at])
        for b in range(blocks):
            store(b, p * small, value[b * small : (b + 1) * small])


def qkv_values(own, pos_ref, x_t_ref, grad_q_ref, grad_k_ref, grad_v_ref, blocks, store):
    half = grad_q_ref.shape[1] // 2
    n_table = x_t_ref.shape[1] - grad_q_ref.shape[0]
    small = x_t_ref.shape[0] // blocks
    at = core_lanes(pos_ref, own, half)
    core = pos_ref[0] if own else 1 - pos_ref[0]
    rows = pl.ds(pl.multiple_of(core * half, 128), half)
    values = (
        fwd_dot(x_t_ref[:, n_table:], grad_q_ref[:, at]),
        back_dot(x_t_ref[...], grad_k_ref[rows, :]),
        back_dot(x_t_ref[...], grad_v_ref[rows, :]),
    )
    for i, value in enumerate(values):
        for b in range(blocks):
            store(b, i * small, value[b * small : (b + 1) * small])


def send_kernel(make, n_in, blocks, *refs):
    pos_ref, out_ref = refs[0], refs[-1]

    def store(b, first, value):
        out_ref[b, first : first + value.shape[0]] = value.astype(BF)

    make(False, pos_ref, *refs[1 : 1 + n_in], blocks, store)


def pick(bit, first, second):
    return jnp.where(bit == 0, first, second)


def keep_down_kernel(
    blocks, pos_ref, act_t_ref, context_t_ref, grad_ffn_ref, grad_attn_ref, got_ref,
    kept_ref, sent_ref, z_kept_ref, z_sent_ref,
):
    small = context_t_ref.shape[0] // blocks
    held = {}

    def z_store(b, first, value):
        y, low_z, high_z = b % 2, b // 2 % 2, b // 4
        if low_z == 0:
            held[b, first] = value
        else:
            rows = slice((high_z * 2 + y) * 2 * small + first, (high_z * 2 + y) * 2 * small + first + small)
            pair = (held[b - 2, first], value)
            z_kept_ref[rows] = pick(pos_ref[3], *pair)
            z_sent_ref[rows] = pick(pos_ref[3], *pair[::-1])

    def store(b, first, value):
        value = (value + got_ref[b, first : first + value.shape[0]].astype(F32)).astype(BF)
        if first == 0:
            part = (value.shape[0] - small) // 2
            low, high = value[small : small + part], value[small + part :]
            rows = slice(b * part, (b + 1) * part)
            kept_ref[rows] = pick(pos_ref[1], low, high)
            sent_ref[rows] = pick(pos_ref[1], high, low)
            z_store(b, 0, value[:small])
        else:
            z_store(b, small, value)

    down_values(True, pos_ref, act_t_ref, context_t_ref, grad_ffn_ref, grad_attn_ref, blocks, store)


def keep_up_kernel(blocks, pos_ref, middle_t_ref, grad_pre_ref, got_ref, *outs):
    kept_ref, sent_ref = outs[:2]
    size = grad_pre_ref.shape[1] // blocks
    held = {}

    def store(b, first, value):
        rows = slice(first, first + value.shape[0])
        value = (value + got_ref[b, rows].astype(F32)).astype(BF)
        if b % 2 == 0:
            held[0] = value
        else:
            rows = slice(b // 2 * size + first, b // 2 * size + first + value.shape[0])
            kept_ref[rows] = pick(pos_ref[2], held[0], value)
            sent_ref[rows] = pick(pos_ref[2], value, held[0])

    up_values(True, pos_ref, middle_t_ref, grad_pre_ref, blocks, store)


def pack(value):
    high = value.astype(BF)
    return jnp.concatenate([high, (value - high.astype(F32)).astype(BF)], axis=0)


def unpack(value):
    half = value.shape[0] // 2
    return value[:half].astype(F32) + value[half:].astype(F32)


def keep_qkv_kernel(
    blocks, pos_ref, x_t_ref, grad_q_ref, grad_k_ref, grad_v_ref, got_ref, table_ref, vec_ref, vec_got_ref, *outs
):
    first_kept_ref, first_sent_ref, kept_ref, sent_ref, vec_out_ref = outs
    small = x_t_ref.shape[0] // blocks
    planes = blocks // 2
    held = {}

    def store(b, first, value):
        value = (value + got_ref[b, first : first + small].astype(F32)).astype(BF)
        held[b, first] = value
        if first == small:
            query = held.pop((b, 0))
            rows = slice(b * small, (b + 1) * small)
            first_kept_ref[rows] = pick(pos_ref[1], query, value)
            first_sent_ref[rows] = pick(pos_ref[1], value, query)
        if first == 2 * small and b % 2 == 1:
            rows = slice(b // 2 * small, (b // 2 + 1) * small)
            kept_ref[rows] = pick(pos_ref[2], held[b - 1, first], value)
            sent_ref[rows] = pick(pos_ref[2], value, held[b - 1, first])

    qkv_values(True, pos_ref, x_t_ref, grad_q_ref, grad_k_ref, grad_v_ref, blocks, store)
    vec = vec_ref[...] + unpack(vec_got_ref[...])
    vec_out_ref[...] = vec
    first_sent_ref[blocks * small :] = pack(vec)
    sent_ref[planes * small :] = table_ref[...]


def inputs_kernel(
    blocks, grad_q_ref, grad_k_ref, grad_v_ref, query_w_ref, key_w_ref, value_w_ref, grad_mid_ref, prev_ref,
    table_prev_ref, sums_ref, up_sum_ref, *refs
):
    table_kept_ref, table_sent_ref, grad_ref, vec_ref, packed_ref = refs[-5:]
    tab = TAB_MAX
    n_table = blocks * tab
    rows, width = grad_q_ref.shape
    half = width // 2
    own = fwd_dot(key_w_ref[...], grad_k_ref[:, n_table:]) + fwd_dot(value_w_ref[...], grad_v_ref[:, n_table:])
    grad = grad_mid_ref[...] + back_dot(grad_q_ref[...], query_w_ref[...]) + own.T
    grad_ref[...] = grad
    is_one = column_of(prev_ref[...].astype(F32)[None]) == 1.0
    one_sum = jnp.sum(jnp.where(is_one, grad, 0.0), axis=0, keepdims=True)
    zero_sum = jnp.sum(jnp.where(is_one, 0.0, grad), axis=0, keepdims=True)
    step = min(n_table, 512)
    row = lax.broadcasted_iota(jnp.int32, (8, step), 0)
    for first in range(0, n_table, step):
        at = slice(first, first + step)
        part = (fwd_dot(key_w_ref[...], grad_k_ref[:, at]) + fwd_dot(value_w_ref[...], grad_v_ref[:, at])).astype(BF)
        marks = table_prev_ref[:, at]
        marks = jnp.where(row == 0, marks, 1.0 - marks).astype(BF)
        table_sums = back_dot(marks, part)
        one_sum += table_sums[0:1]
        zero_sum += table_sums[1:2]
        for j in range(step // 128):
            pair = part[:, j * 128 : (j + 1) * 128].T
            slot = first // 128 + j
            for k, ref in enumerate((table_kept_ref, table_sent_ref)):
                for side in range(2):
                    ref[(slot * 2 + side) * tab : (slot * 2 + side + 1) * tab] = pair[
                        k * tab : (k + 1) * tab, side * half : (side + 1) * half
                    ]
    ones = jnp.ones((8, grad_v_ref.shape[1]), BF)
    lines = [
        zero_sum,
        one_sum,
        jnp.sum(grad_q_ref[...].astype(F32), axis=0, keepdims=True),
        back_dot(ones, grad_v_ref[...])[0:1],
    ]
    lines += [sums_ref[i : i + 1] for i in range(6)]
    lines += [up_sum_ref[:, i * width : (i + 1) * width] for i in range(up_sum_ref.shape[1] // width)]
    vec_ref[...] = jnp.zeros(vec_ref.shape, F32)
    for i, line in enumerate(lines):
        for side in range(2):
            vec_ref[side * 16 + i : side * 16 + i + 1] = line[:, side * half : (side + 1) * half]
    packed_ref[...] = pack(vec_ref[...])


def input_grads(blocks, grad_q, grad_k, grad_v, query_w, key_w, value_w, grad_mid, prev, table_prev, sums, up_sum, after):
    rows, width = grad_q.shape
    n_half = blocks * TAB_MAX
    vmem = pl.BlockSpec(memory_space=pltpu.VMEM)
    args = (grad_q, grad_k, grad_v, query_w, key_w, value_w, grad_mid, prev, table_prev, sums, up_sum)
    return pl.pallas_call(
        lambda *refs: inputs_kernel(blocks, *refs),
        in_specs=[vmem] * len(args) + [pl.BlockSpec(memory_space=pl.ANY)] * len(after),
        out_specs=[vmem] * 5,
        out_shape=[
            jax.ShapeDtypeStruct((n_half, width // 2), BF),
            jax.ShapeDtypeStruct((n_half, width // 2), BF),
            jax.ShapeDtypeStruct((rows, width), F32),
            jax.ShapeDtypeStruct((32, width // 2), F32),
            jax.ShapeDtypeStruct((64, width // 2), BF),
        ],
        compiler_params=pltpu.CompilerParams(vmem_limit_bytes=(20 if blocks <= 8 else 56) * MIB),
        cost_estimate=pl.CostEstimate(flops=100_000_000, bytes_accessed=1 * MIB, transcendentals=0),
    )(*args, *after)


def combine(pos, items, after=()):
    width = items[0][1].shape[1]
    gots, shapes, heights, places = [], [], {}, []
    for kind, kept, got, first, outer, inner, bit, message in items:
        if not any(got is g for g in gots):
            gots.append(got)
        rows = kept.shape[0] if kind != "part" else outer * inner
        shapes.append(jax.ShapeDtypeStruct((rows, width), kept.dtype))
        if message is not None:
            places.append(heights.get(message, 0))
            heights[message] = places[-1] + (2 * rows if kind == "vec" else rows)
        else:
            places.append(None)
    sizes = [heights[m] for m in sorted(heights)]
    shapes += [jax.ShapeDtypeStruct((n, width), BF) for n in sizes]
    which = [next(i for i, g in enumerate(gots) if g is item[2]) for item in items]

    def body(pos_ref, *refs):
        kept_refs, refs = refs[: len(items)], refs[len(items) :]
        got_refs, refs = refs[: len(gots)], refs[len(gots) + len(after) :]
        out_refs, sent_refs = refs[: len(items)], refs[len(items) :]
        for i, (kind, _, _, first, outer, inner, bit, message) in enumerate(items):
            kept_ref, got_ref, out_ref = kept_refs[i], got_refs[which[i]], out_refs[i]
            n = kept_ref.shape[0]
            if kind == "vec":
                total = kept_ref[...] + unpack(got_ref[first : first + 2 * n])
                out_ref[...] = total
                if message is not None:
                    sent_refs[message][places[i] : places[i] + 2 * n] = pack(total)
            elif kind == "sum":
                total = kept_ref[...].astype(F32) + got_ref[first : first + n].astype(F32)
                out_ref[...] = total.astype(BF)
            else:
                for o in range(outer):
                    halves = []
                    for side in range(2):
                        at = (2 * o + side) * inner
                        total = kept_ref[at : at + inner].astype(F32)
                        total = total + got_ref[first + at : first + at + inner].astype(F32)
                        halves.append(total.astype(BF))
                    rows = slice(places[i] + o * inner, places[i] + (o + 1) * inner)
                    if bit is None:
                        out_ref[o * inner : (o + 1) * inner], sent_refs[message][rows] = halves
                    else:
                        out_ref[o * inner : (o + 1) * inner] = pick(pos_ref[bit], *halves)
                        sent_refs[message][rows] = pick(pos_ref[bit], *halves[::-1])

    vmem = pl.BlockSpec(memory_space=pltpu.VMEM)
    results = pl.pallas_call(
        body,
        in_specs=[pl.BlockSpec(memory_space=pltpu.SMEM)]
        + [vmem] * (len(items) + len(gots))
        + [pl.BlockSpec(memory_space=pl.ANY)] * len(after),
        out_specs=[vmem] * len(shapes),
        out_shape=shapes,
        compiler_params=pltpu.CompilerParams(vmem_limit_bytes=16 * MIB),
        cost_estimate=pl.CostEstimate(flops=1_000_000, bytes_accessed=1 * MIB, transcendentals=0),
    )(pos, *[item[1] for item in items], *gots, *after)
    return results[: len(items)], results[len(items) :]


def packet_call(kernel, shapes, pos, args, after=(), scratch=(), wide=()):
    smem, vmem = pl.BlockSpec(memory_space=pltpu.SMEM), pl.BlockSpec(memory_space=pltpu.VMEM)
    outs = [jax.ShapeDtypeStruct(shape, BF) for shape in shapes]
    outs += [jax.ShapeDtypeStruct(shape, F32) for shape in wide]

    def body(*refs):
        n = 1 + len(args)
        kernel(*refs[:n], *refs[n + len(after) :])

    return pl.pallas_call(
        body,
        in_specs=[smem] + [vmem] * len(args) + [pl.BlockSpec(memory_space=pl.ANY)] * len(after),
        out_specs=[vmem] * len(outs),
        out_shape=outs,
        scratch_shapes=list(scratch),
        compiler_params=pltpu.CompilerParams(vmem_limit_bytes=20 * MIB),
        cost_estimate=pl.CostEstimate(flops=100_000_000, bytes_accessed=1 * MIB, transcendentals=0),
    )(pos, *args, *after)


def local(
    tokens, seg_ids, turn_ids, prev_ids, answer_table, query_weight, query_bias,
    key_weight, value_weight, value_bias, out_weight, out_bias, norm_gain, norm_shift,
    up_weight, up_bias, down_weight, down_bias, final_gain, final_shift, cotangent,
):
    rows, width = tokens.shape
    blocks = lax.axis_size("blk")
    grps = lax.axis_size("grp")
    tab = TAB_MAX
    scale = HEAD_DIM ** (-0.5)
    f = lambda v: v.astype(F32)
    core_bit = lax.axis_index("grp") & 1
    x_bit = lax.axis_index("grp") >> 1
    own = lax.axis_index("blk")
    planes = blocks // 2
    n_out = width // blocks
    ff_out = up_weight.shape[1] // blocks
    half_width = width // 2
    n_table = blocks * tab
    pos = jnp.stack([core_bit, x_bit, own & 1, (own >> 1) & 1, own >> 2]).astype(jnp.int32)

    def swap_grp(value, mask):
        return lax.ppermute(value, "grp", [(i, i ^ mask) for i in range(grps)])

    def swap_blk(value, mask):
        return lax.ppermute(value, "blk", [(i, i ^ mask) for i in range(blocks)])

    payload, layer_input = entry(tokens, seg_ids, prev_ids, answer_table)
    slots = [payload] + [None] * (blocks - 1)
    for k in range(1, planes):
        slots[2 * k] = swap_blk(payload, 2 * k)
    slots[1] = swap_blk(payload, 1)
    for k in range(1, planes):
        slots[2 * k + 1] = swap_blk(slots[2 * k], 1)
    queries, own_keys, own_values, own_bias, value_row = own_part(
        layer_input, query_weight, key_weight, value_weight, query_bias, value_bias, seg_ids, turn_ids
    )
    keys, values, prob, context, x_t, table_prev = attend(
        slots, layer_input, key_weight, value_weight, value_row, queries, own_keys, own_values, own_bias
    )
    (
        mixed, context_t, middle_t, act_t, grad_ffn, grad_pre, grad_attn, grad_context, grad_mid_sum,
        sums, up_sum,
    ) = middle_part(
        tokens, prev_ids, answer_table, context, cotangent, out_weight, up_weight, down_weight, up_bias,
        out_bias, norm_gain, norm_shift, down_bias, final_gain, final_shift,
    )
    down_args = (act_t, context_t, grad_ffn, grad_attn)
    up_args = (middle_t, grad_pre)
    part = (ff_out - n_out) // 2
    back_args = (queries, keys, values, prob, context, grad_context)
    input_args = (query_weight, key_weight, value_weight, grad_mid_sum, prev_ids, table_prev, sums, up_sum)

    if blocks == 8 and n_out % 32 == 0:
        flat = lambda rows: (rows, half_width)
        (sent,) = packet_call(
            lambda *refs: send_kernel(down_values, 4, blocks, *refs),
            [(blocks, ff_out + n_out, half_width)], pos, down_args,
        )
        down_got = swap_grp(sent, 1)
        (sent,) = packet_call(
            lambda *refs: send_kernel(up_values, 2, blocks, *refs),
            [(blocks, ff_out, half_width)], pos, up_args, after=(sent,),
        )
        up_got = swap_grp(sent, 1)
        down_kept, down_sent, z_kept, z_sent = packet_call(
            lambda *refs: keep_down_kernel(blocks, *refs),
            [flat(blocks * part)] * 2 + [flat(8 * n_out)] * 2, pos, down_args + (down_got,), after=(sent,),
        )
        down_got = swap_grp(down_sent, 2)
        z_got = swap_blk(z_sent, 2)
        up_kept, up_sent = packet_call(
            lambda *refs: keep_up_kernel(blocks, *refs),
            [flat(planes * ff_out)] * 2, pos, up_args + (up_got,), after=(down_sent,),
        )
        up_got = swap_blk(up_sent, 1)
        grad_queries, grad_keys_t, grad_values_t = attend_back(*back_args, (down_sent, up_sent, z_sent))
        qkv_args = (x_t, grad_queries, grad_keys_t, grad_values_t)
        (qkv_sent,) = packet_call(
            lambda *refs: send_kernel(qkv_values, 4, blocks, *refs),
            [(blocks, 3 * n_out, half_width)], pos, qkv_args,
        )
        qkv_got = swap_grp(qkv_sent, 1)
        table_kept, table_sent, grad_input_local, vectors, packed = input_grads(
            blocks, grad_queries, grad_keys_t, grad_values_t, *input_args, (qkv_sent,)
        )
        vec_got = swap_grp(packed, 1)
        (z_kept,), (z_sent,) = combine(pos, [("part", z_kept, z_got, 0, 1, 4 * n_out, 4, 0)], after=(table_sent,))
        z_got = swap_blk(z_sent, 4)
        n_first, n_value, n_rows = blocks * n_out, planes * n_out, blocks * tab
        first_kept, first_sent, value_kept, value_sent, vectors = packet_call(
            lambda *refs: keep_qkv_kernel(blocks, *refs),
            [flat(n_first), flat(n_first + 64), flat(n_value), flat(n_value + n_rows)],
            pos, qkv_args + (qkv_got, table_sent, vectors, vec_got), wide=[flat(32)], after=(z_sent,),
        )
        first_got = swap_grp(first_sent, 2)
        value_got = swap_blk(value_sent, 1)
        (down_kept,), (down_sent,) = combine(
            pos, [("part", down_kept, down_got, 0, 2, 2 * part, 3, 0)], after=(value_sent,)
        )
        down_got = swap_blk(down_sent, 2)
        (up_kept,), (up_sent,) = combine(
            pos, [("part", up_kept, up_got, 0, planes, ff_out // 2, 1, 0)], after=(down_sent,)
        )
        up_got = swap_grp(up_sent, 2)
        (first_kept, vectors), (first_sent,) = combine(
            pos,
            [
                ("part", first_kept, first_got, 0, planes, n_out, 2, 0),
                ("vec", vectors, first_got, n_first, 0, 0, None, 0),
            ],
            after=(up_sent,),
        )
        first_got = swap_blk(first_sent, 1)
        (value_kept, table_kept), (value_sent, table_sent) = combine(
            pos,
            [
                ("part", value_kept, value_got, 0, planes, n_out // 2, 1, 0),
                ("part", table_kept, value_got, n_value, 2, 2 * tab, None, 1),
            ],
            after=(first_sent,),
        )
        value_got = swap_grp(value_sent, 2)
        table_got = swap_blk(table_sent, 2)
        (down_kept, z_kept), (down_sent,) = combine(
            pos,
            [
                ("part", down_kept, down_got, 0, 2, part, 2, 0),
                ("part", z_kept, z_got, 0, 1, 2 * n_out, 2, 0),
            ],
            after=(value_sent,),
        )
        down_got = swap_blk(down_sent, 1)
        (up_kept,), (up_sent,) = combine(
            pos, [("part", up_kept, up_got, 0, 2, ff_out // 2, 3, 0)], after=(down_sent,)
        )
        up_got = swap_blk(up_sent, 2)
        (first_kept, value_kept, vectors), (first_sent,) = combine(
            pos,
            [
                ("part", first_kept, first_got, 0, 2, n_out, 3, 0),
                ("part", value_kept, value_got, 0, 2, n_out // 2, 3, 0),
                ("vec", vectors, first_got, n_value, 0, 0, None, 0),
            ],
            after=(up_sent,),
        )
        first_got = swap_blk(first_sent, 2)
        n_down = 2 * part
        (down_kept, z_kept, up_kept), (down_sent, z_sent) = combine(
            pos,
            [
                ("part", down_kept, down_got, 0, 1, part, 4, 0),
                ("part", z_kept, down_got, n_down, 1, n_out, 1, 1),
                ("part", up_kept, up_got, 0, 1, ff_out // 2, 4, 0),
            ],
            after=(first_sent,),
        )
        down_got = swap_blk(down_sent, 4)
        z_got = swap_grp(z_sent, 2)
        (first_kept, value_kept, table_kept, vectors), (first_sent,) = combine(
            pos,
            [
                ("part", first_kept, first_got, 0, 1, n_out, 4, 0),
                ("part", value_kept, first_got, 2 * n_out, 1, n_out // 2, 4, 0),
                ("part", table_kept, table_got, 0, 1, 2 * tab, None, 0),
                ("vec", vectors, first_got, 3 * n_out, 0, 0, None, 0),
            ],
            after=(down_sent,),
        )
        first_got = swap_blk(first_sent, 4)
        (down_part, up_part, z_part), _ = combine(
            pos,
            [
                ("sum", down_kept, down_got, 0, 0, 0, None, None),
                ("sum", up_kept, down_got, part, 0, 0, None, None),
                ("sum", z_kept, z_got, 0, 0, 0, None, None),
            ],
            after=(first_sent,),
        )
        n_small = n_out + n_out // 2
        (first_part, value_part, table_part, vectors), _ = combine(
            pos,
            [
                ("sum", first_kept, first_got, 0, 0, 0, None, None),
                ("sum", value_kept, first_got, n_out, 0, 0, None, None),
                ("sum", table_kept, first_got, n_small, 0, 0, None, None),
                ("vec", vectors, first_got, n_small + 2 * tab, 0, 0, None, None),
            ],
            after=(down_part,),
        )

        def whole(value):
            other = swap_grp(value, 2)
            return pick(x_bit, value, other), pick(x_bit, other, value)

        low, high = whole(jnp.concatenate([down_part, up_part, z_part], axis=0))
        at_up, at_z = part, part + ff_out // 2
        big = jnp.concatenate(
            [low[:at_up], high[:at_up], low[at_up:at_z], high[at_up:at_z], low[at_z:], high[at_z:]], axis=0
        )
        low, high = whole(jnp.concatenate([first_part, value_part], axis=0))
        square = jnp.concatenate([low[:n_out], high[:n_out], low[n_out:], high[n_out:]], axis=0)
        down_rows, up_rows, z_rows = big[: 2 * part], big[2 * at_up : 2 * at_z], big[2 * at_z :]
        table_share = f(table_part)
    else:
        lanes = lambda value, index: lax.dynamic_slice_in_dim(value, index * (value.shape[1] // 2), value.shape[1] // 2, 1)
        rows_of = lambda value, index: lax.dynamic_slice_in_dim(value, index * (value.shape[0] // 2), value.shape[0] // 2, 0)
        blocked = lambda value: value.reshape(blocks, value.shape[0] // blocks, value.shape[1])
        grad_queries, grad_keys_t, grad_values_t = attend_back(*back_args, ())
        table_kept, table_sent, grad_input_local, vectors, packed = input_grads(
            blocks, grad_queries, grad_keys_t, grad_values_t, *input_args, ()
        )

        def packet(index):
            up = blocked(fwd_dot(middle_t, lanes(grad_pre, index)))
            return jnp.concatenate(
                [
                    blocked(fwd_dot(x_t[:, n_table:], lanes(grad_queries, index))),
                    blocked(back_dot(x_t, rows_of(grad_keys_t, index))),
                    blocked(back_dot(x_t, rows_of(grad_values_t, index))),
                    blocked(fwd_dot(context_t, lanes(grad_attn, index))),
                ]
                + [up[:, :, i : i + half_width] for i in range(0, up.shape[2], half_width)]
                + [blocked(fwd_dot(act_t, lanes(grad_ffn, index)))],
                axis=1,
            )

        total = (packet(core_bit) + f(swap_grp(packet(1 - core_bit).astype(BF), 1))).astype(BF)
        total = lax.psum_scatter(total, "blk", scatter_dimension=0, tiled=False)
        total = (f(total) + f(swap_grp(total, 2))).astype(BF)
        at = 4 * n_out
        square = total[: 3 * n_out]
        up_rows = total[at : at + ff_out]
        down_all = total[at + ff_out :]
        z_rows = jnp.concatenate([down_all[:n_out], total[3 * n_out : at]], axis=0)
        down_rows = down_all[n_out:]
        table_rows = jnp.stack([blocked_half.reshape(planes, 2 * tab, half_width) for blocked_half in (table_kept, table_sent)], axis=1)
        table_rows = table_rows.reshape(blocks, 2 * tab, half_width)
        table_rows = jnp.take(table_rows, jnp.arange(blocks) ^ own, axis=0)
        table_share = f(lax.psum_scatter(table_rows, "blk", scatter_dimension=0, tiled=False))
        vectors = lax.psum(vectors, ("blk", "grp"))
        big = jnp.concatenate([down_rows, up_rows, z_rows], axis=0)

    def both_cores(value):
        other = swap_grp(value, 1)
        return f(pick(core_bit, value, other)), f(pick(core_bit, other, value))

    sides = both_cores(big)
    n_down = ff_out - n_out
    at_z = n_down + ff_out
    out_up = jnp.concatenate(
        [side[i : i + n_out] for side in sides for i in range(n_down, at_z, n_out)], axis=1
    )
    out_down = jnp.concatenate(
        [
            jnp.concatenate([side[at_z : at_z + n_out] for side in sides], axis=1),
            jnp.concatenate([side[:n_down] for side in sides], axis=1),
        ],
        axis=0,
    )
    out_out = jnp.concatenate([side[at_z + n_out :] for side in sides], axis=1)
    square = jnp.concatenate(both_cores(square), axis=1)
    table_share = jnp.concatenate([table_share[:tab], table_share[tab:]], axis=1)
    vectors = jnp.concatenate([vectors[:16], vectors[16:]], axis=1)
    mine = lax.dynamic_slice_in_dim(vectors[:10], own * n_out, n_out, 1)
    up_bias_out = lax.dynamic_slice_in_dim(vectors[10:14].reshape(-1), own * ff_out, ff_out, 0)
    grad_input = grad_input_local.at[:tab].add(table_share)
    return (
        mixed,
        grad_input,
        mine[:2],
        square[:n_out],
        mine[2],
        square[n_out : 2 * n_out],
        square[2 * n_out :],
        mine[3],
        out_out,
        mine[4],
        mine[5],
        mine[6],
        out_up,
        up_bias_out,
        out_down,
        mine[7],
        mine[8],
        mine[9],
    )


def solution(mesh):
    both = ("grp", "blk")
    placed = (P(both, None), P(both), P(both), P(both)) + (P(),) * 16 + (P(both, None),)
    vec, mat = P("blk"), P("blk", None)
    return jax.shard_map(
        local,
        mesh=mesh,
        in_specs=placed,
        out_specs=(
            P(both, None), P(both, None), P(None, "blk"), mat, vec, mat, mat, vec, mat, vec,
            vec, vec, mat, vec, mat, vec, vec, vec,
        ),
        check_vma=False,
    )
```

time: 232 us -> 194 us (0.84)
  blocking collectives: 34.4 us -> 0 us
  waiting for transfers between devices: 45.2 us -> 76.1 us
  matrix products: 30.8 us -> 0 us
  Pallas kernels: 33.9 us -> 58.1 us
  other arithmetic: 28.3 us -> 4.43 us
  local copies, waits for them, and re-layouts: 23.6 us -> 20.7 us
    all_gather x1 -> x0, blocking collectives: 34.4 us -> none  [local(): gathered = lax.all_gather(payload, 'blk', axis=0, tiled=False)]
    dot_general x18 -> x0, matrix products: 30.8 us -> none  [the longest x8 18.2 us: outer_sum(): lax.dot_general(left, right, (((0,), (0,)), ((), ())), preferred_element_...]
    ppermute x16 -> x19, waiting for transfers between devices: 27.7 us -> 57.4 us  [swap_blk(): return lax.ppermute(value, 'blk', [(i, i ^ mask) for i in range(blocks)])]
    pallas_call x3 -> x24, Pallas kernels: 33.9 us -> 58.1 us  [the longest x1 17.2 us: middle_part(): pl.pallas_call(middle_kernel, in_specs=[vmem] * 5 + [pl.BlockSpec(memory_...]
    convert_element_type x20 -> x0, other arithmetic: 12.2 us -> none  [the longest x8 6.36 us: add(): return (f(first) + f(second)).astype(BF)]
    unnamed x124 -> x114, local copies, waits for them, and re-layouts: 10.5 us -> 18.6 us
    squeeze x8 -> x0, local copies, waits for them, and re-layouts: 5.07 us -> none  [take(): return lax.dynamic_index_in_dim(value, index, axis, keepdims=False)]
    convert_element_type x7 -> x1, other arithmetic: 4.61 us -> 0.18 us  [local(): f = lambda v: v.astype(F32)]
  transfers between devices with their start and end apart: 30 -> 32, of which waited for: 9 -> 17; matrix products, arithmetic and copies ran while one was open for 23% -> 2% of each run, Pallas kernels for 3% -> 10%
where the time goes in v3:
time: 194 us
  waiting for transfers between devices  76.1 us (39%)
  Pallas kernels  58.1 us (30%)
  starting transfers between devices  32.9 us (17%)
  local copies, waits for them, and re-layouts  20.7 us (11%)
  other arithmetic  4.43 us (2%)
    ppermute x19, waiting for transfers between devices, swap_blk(): return lax.ppermute(value, 'blk', [(i, i ^ mask) for i in range(blocks)])  57.4 us
    ppermute x19, starting transfers between devices, swap_blk(): return lax.ppermute(value, 'blk', [(i, i ^ mask) for i in range(blocks)])  25.7 us
    ppermute x13, waiting for transfers between devices, swap_grp(): return lax.ppermute(value, 'grp', [(i, i ^ mask) for i in range(grps)])  18.7 us
    unnamed x114, local copies, waits for them, and re-layouts  18.6 us
    pallas_call x1, Pallas kernels, middle_part(): pl.pallas_call(middle_kernel, in_specs=[vmem] * 5 + [pl.BlockSpec(memory_...  17.2 us
    pallas_call x6, Pallas kernels, packet_call(): pl.pallas_call(body, in_specs=[smem] + [vmem] * len(args) + [pl.BlockSpec...  10.9 us
    pallas_call x1, Pallas kernels, attend(): pl.pallas_call(attend_kernel, grid=(width // group,), in_specs=[whole((ro...  10.3 us
    pallas_call x12, Pallas kernels, combine(): pl.pallas_call(body, in_specs=[pl.BlockSpec(memory_space=pltpu.SMEM)] + [...  8.78 us
  transfers between devices with their start and end apart: 32, of which 17 were waited for; matrix products, arithmetic and copies ran while one was open for 2% of the time, Pallas kernels for 10%

profile of v3, /device:TPU:0, one launch (start us, length us, event | category | flops | bytes accessed | tf_op | source)
XLA Modules:
  0.0 193.7 jit_solution(2289509090870593753)
XLA Ops:
  4.0 3.1 %collective-permute-start.1 = (bf16[80,768]{1,0:T(8,128)(2,1)S(1)}, bf16[80,768]{1,0:T(8,128)(2,1)S(1)}, u32[]{:S(2)}, u32[]{:S(2)}) collective-permute-start(bf16[80,768]{1,0:T(8,128)(2,1)S(1)} %get-tuple-element.118.refs_0_), channel_id=1, source_target_pairs={{0,2},{1,3},{2,0},{3,1},{4,6},{5,7},{6,4},{7,5},{8,10},{9,11},{10,... | collective-permute-start | bytes 368648 | tf_op jit(solution)/shard_map/ppermute | solution.py:682
  7.0 2.6 %collective-permute-start.3 = (bf16[80,768]{1,0:T(8,128)(2,1)S(1)}, bf16[80,768]{1,0:T(8,128)(2,1)S(1)}, u32[]{:S(2)}, u32[]{:S(2)}) collective-permute-start(bf16[80,768]{1,0:T(8,128)(2,1)S(1)} %get-tuple-element.118.refs_0_), channel_id=1, source_target_pairs={{0,4},{1,5},{2,6},{3,7},{4,0},{5,1},{6,2},{7,3},{8,12},{9,13},{10,... | collective-permute-start | bytes 368648 | tf_op jit(solution)/shard_map/ppermute | solution.py:682
  9.6 1.7 collective-permute-start
  11.7 1.7 collective-permute-start.2
  13.4 5.9 %collective-permute-done.3.refs_4_ = bf16[80,768]{1,0:T(8,128)(2,1)S(1)} collective-permute-done((bf16[80,768]{1,0:T(8,128)(2,1)S(1)}, bf16[80,768]{1,0:T(8,128)(2,1)S(1)}, u32[]{:S(2)}, u32[]{:S(2)}) %collective-permute-start.3) | collective-permute-done | bytes 122912 | tf_op jit(solution)/shard_map/ppermute | solution.py:682
  19.4 1.5 collective-permute-start.4
  21.5 1.3 copy-done
  22.8 1.3 copy-done.2
  24.0 1.3 copy-done.7
  28.0 1.1 shard_map.341
  32.9 10.3 %shard_map.342 = (bf16[768,768]{1,0:T(8,128)(2,1)}, bf16[768,768]{1,0:T(8,128)(2,1)}, bf16[12,256,768]{2,1,0:T(8,128)(2,1)}, f32[256,768]{1,0:T(8,128)}, bf16[768,768]{1,0:T(8,128)(2,1)}, /*index=5*/f32[8,512]{1,0:T(8,128)}) custom-call(bf16[256,768]{1,0:T(8,128)(2,1)} %copy-done.17, bf16[768,768]{1,0:T(8,128)(2,1)} %refs_4_.3, bf16[768,768]{1,0:T(8,128)(2,1)} %refs_5_.3, ...), custom_call_target="tpu_custom_call" | custom-call | flops 100000000 | bytes 1048576 | tf_op jit(solution)/shard_map/pallas_call | solution.py:180
  43.2 17.2 %shard_map.343 = (bf16[256,768]{1,0:T(8,128)(2,1)}, bf16[768,256]{1,0:T(8,128)(2,1)}, bf16[768,256]{1,0:T(8,128)(2,1)}, bf16[3072,256]{1,0:T(8,128)(2,1)}, bf16[...) custom-call(bf16[256,768]{1,0:T(8,128)(2,1)} %tokens_ref.3, ...), custom_call_target="tpu_custom_call" | custom-call | flops 5435817984 | bytes 25165824 | tf_op jit(solution)/shard_map/pallas_call | solution.py:289
  60.4 1.4 copy-done.5
  64.8 1.7 shard_map.344.refs_3_
  66.7 1.5 shard_map.345.refs_6_
  68.8 3.2 %collective-permute-done.7.refs_5_ = bf16[8,480,384]{2,1,0:T(8,128)(2,1)S(1)} collective-permute-done((bf16[8,480,384]{2,1,0:T(8,128)(2,1)S(1)}, bf16[8,480,384]{2,1,0:T(8,128)(2,1)S(1)}, u32[]{:S(2)}, u32[]{:S(2)}) %collective-permute-start.7) | collective-permute-done | bytes 2949152 | tf_op jit(solution)/shard_map/ppermute | solution.py:679
  72.0 1.8 shard_map.346
  73.8 1.6 collective-permute-done.8.refs_3_
  75.4 1.6 shard_map.347
  77.4 6.2 %shard_map.348 = (bf16[256,768]{1,0:T(8,128)(2,1)S(1)}, bf16[768,768]{1,0:T(8,128)(2,1)S(1)}, bf16[768,768]{1,0:T(8,128)(2,1)S(1)}) custom-call(bf16[256,768]{1,0:T(8,128)(2,1)S(1)} %copy-done.15, bf16[768,768]{1,0:T(8,128)(2,1)S(1)} %copy-done.18, bf16[768,768]{1,0:T(8,128)(2,1)S(1)} %copy-done.19, bf16[12,256,768]{2,1,0:T(8,128)(2,1)S(1)} %bitcast.22, ...), custom_call_target="tpu_custom_call" | custom-call | flops 100000000 | bytes 1048576 | tf_op jit(solution)/shard_map/pallas_call | solution.py:339
  83.7 2.1 %shard_map.349.refs_11_ = bf16[8,288,384]{2,1,0:T(8,128)(2,1)S(1)} custom-call(s32[5]{0:T(128)S(1)} %stack.23.refs_0_.pos_ref, bf16[768,768]{1,0:T(8,128)(2,1)S(1)} %copy-done.6, bf16[256,768]{1,0:T(8,128)(2,1)S(1)} %get-tuple-element.134.refs_2_.refs_0_, bf16[768,768]{1,0:T(8,128)(2,1)S(1)} %get-tuple-element.135.refs_3_.refs_1_, ...), custom_call_target="tpu_custom_call" | custom-call | flops 100000000 | bytes 1048576 | tf_op jit(solution)/shard_map/pallas_call | solution.py:646
  86.1 1.5 collective-permute-start.13
  87.6 1.5 collective-permute-start.14
  89.5 3.4 %shard_map.350 = (bf16[512,384]{1,0:T(8,128)(2,1)S(1)}, bf16[512,384]{1,0:T(8,128)(2,1)S(1)}, f32[256,768]{1,0:T(8,128)}, f32[32,384]{1,0:T(8,128)S(1)}, bf16[64,384]{1,0:T(8,128)(2,1)S(1)}) custom-call(bf16[256,768]{1,0:T(8,128)(2,1)S(1)} %get-tuple-element.134.refs_2_.refs_0_, bf16[768,768]{1,0:T(8,128)(2,1)S(1)} %get-tuple-element.135.refs_3_.refs_1_, ...), custom_call_target="tpu_custom_call" | custom-call | flops 100000000 | bytes 1048576 | tf_op jit(solution)/shard_map/pallas_call | solution.py:560
  92.9 11.2 %collective-permute-done.11.refs_1_ = bf16[768,384]{1,0:T(8,128)(2,1)S(1)} collective-permute-done((bf16[768,384]{1,0:T(8,128)(2,1)S(1)}, bf16[768,384]{1,0:T(8,128)(2,1)S(1)}, u32[]{:S(2)}, u32[]{:S(2)}) %collective-permute-start.11) | collective-permute-done | bytes 589856 | tf_op jit(solution)/shard_map/ppermute | solution.py:682
  104.9 2.2 %shard_map.352 = (bf16[768,384]{1,0:T(8,128)(2,1)S(1)}, bf16[832,384]{1,0:T(8,128)(2,1)S(1)}, bf16[384,384]{1,0:T(8,128)(2,1)S(1)}, bf16[896,384]{1,0:T(8,128)(2,1)S(1)}, f32[32,384]{1,0:T(8,128)S(1)}) custom-call(s32[5]{0:T(128)S(1)} %stack.23.refs_0_.pos_ref, bf16[768,768]{1,0:T(8,128)(2,1)S(1)} %copy-done.6, ...), custom_call_target="tpu_custom_call" | custom-call | flops 100000000 | bytes 1048576 | tf_op jit(solution)/shard_map/pallas_call | solution.py:646
  108.2 1.3 collective-permute-done.14.refs_1_
  110.3 4.5 %collective-permute-done.13.refs_1_ = bf16[1536,384]{1,0:T(8,128)(2,1)S(1)} collective-permute-done((bf16[1536,384]{1,0:T(8,128)(2,1)S(1)}, bf16[1536,384]{1,0:T(8,128)(2,1)S(1)}, u32[]{:S(2)}, u32[]{:S(2)}) %collective-permute-start.13) | collective-permute-done | bytes 1179680 | tf_op jit(solution)/shard_map/ppermute | solution.py:682
  115.8 1.6 collective-permute-start.18
  117.3 1.4 collective-permute-start.19
  118.7 1.6 collective-permute-start.20
  120.3 4.7 %collective-permute-done.12.refs_2_ = bf16[832,384]{1,0:T(8,128)(2,1)S(1)} collective-permute-done((bf16[832,384]{1,0:T(8,128)(2,1)S(1)}, bf16[832,384]{1,0:T(8,128)(2,1)S(1)}, u32[]{:S(2)}, u32[]{:S(2)}) %collective-permute-start.12) | collective-permute-done | bytes 639008 | tf_op jit(solution)/shard_map/ppermute | solution.py:679
  125.7 3.4 %collective-permute-done.15.refs_2_ = bf16[896,384]{1,0:T(8,128)(2,1)S(1)} collective-permute-done((bf16[896,384]{1,0:T(8,128)(2,1)S(1)}, bf16[896,384]{1,0:T(8,128)(2,1)S(1)}, u32[]{:S(2)}, u32[]{:S(2)}) %collective-permute-start.15) | collective-permute-done | bytes 688160 | tf_op jit(solution)/shard_map/ppermute | solution.py:682
  129.8 3.6 %collective-permute-done.20.refs_3_ = bf16[384,384]{1,0:T(8,128)(2,1)S(1)} collective-permute-done((bf16[384,384]{1,0:T(8,128)(2,1)S(1)}, bf16[384,384]{1,0:T(8,128)(2,1)S(1)}, u32[]{:S(2)}, u32[]{:S(2)}) %collective-permute-start.20) | collective-permute-done | bytes 294944 | tf_op jit(solution)/shard_map/ppermute | solution.py:682
  133.3 1.1 collective-permute-done.19.refs_2_
  135.2 1.6 collective-permute-start.23
  138.1 2.4 %collective-permute-start.24 = (bf16[384,384]{1,0:T(8,128)(2,1)S(1)}, bf16[384,384]{1,0:T(8,128)(2,1)S(1)}, u32[]{:S(2)}, u32[]{:S(2)}) collective-permute-start(bf16[384,384]{1,0:T(8,128)(2,1)S(1)} %get-tuple-element.167.refs_5_), channel_id=1, source_target_pairs={{0,2},{1,3},{2,0},{3,1},{4,6},{5,7},{6,4},{7,5},{8,10},{9,11},{10,... | collective-permute-start | bytes 884744 | tf_op jit(solution)/shard_map/ppermute | solution.py:682
  141.0 4.6 %collective-permute-done.17.refs_4_ = bf16[192,384]{1,0:T(8,128)(2,1)S(1)} collective-permute-done((bf16[192,384]{1,0:T(8,128)(2,1)S(1)}, bf16[192,384]{1,0:T(8,128)(2,1)S(1)}, u32[]{:S(2)}, u32[]{:S(2)}) %collective-permute-start.17) | collective-permute-done | bytes 147488 | tf_op jit(solution)/shard_map/ppermute | solution.py:679
  145.6 6.3 %collective-permute-done.16.refs_3_ = bf16[448,384]{1,0:T(8,128)(2,1)S(1)} collective-permute-done((bf16[448,384]{1,0:T(8,128)(2,1)S(1)}, bf16[448,384]{1,0:T(8,128)(2,1)S(1)}, u32[]{:S(2)}, u32[]{:S(2)}) %collective-permute-start.16) | collective-permute-done | bytes 344096 | tf_op jit(solution)/shard_map/ppermute | solution.py:682
  152.6 1.5 collective-permute-start.21
  154.9 1.5 collective-permute-start.26
  157.4 11.3 %collective-permute-done.22.refs_5_ = bf16[256,384]{1,0:T(8,128)(2,1)S(1)} collective-permute-done((bf16[256,384]{1,0:T(8,128)(2,1)S(1)}, bf16[256,384]{1,0:T(8,128)(2,1)S(1)}, u32[]{:S(2)}, u32[]{:S(2)}) %collective-permute-start.22) | collective-permute-done | bytes 196640 | tf_op jit(solution)/shard_map/ppermute | solution.py:682
  171.7 9.9 %collective-permute-done.25.refs_4_ = bf16[336,384]{1,0:T(8,128)(2,1)S(1)} collective-permute-done((bf16[336,384]{1,0:T(8,128)(2,1)S(1)}, bf16[336,384]{1,0:T(8,128)(2,1)S(1)}, u32[]{:S(2)}, u32[]{:S(2)}) %collective-permute-start.25) | collective-permute-done | bytes 258080 | tf_op jit(solution)/shard_map/ppermute | solution.py:682
  183.5 1.6 fusion
  185.8 1.9 collective-permute-done.28
  189.3 1.3 collective-permute-done.29
  191.2 1.2 fusion.3
  192.6 1.1 maximum_maximum_fusion
  (185 shorter events, 33.1 us)
Async XLA Ops:
  3.9 25.2 %copy-start.17 = (bf16[256,768]{1,0:T(8,128)(2,1)}, bf16[256,768]{1,0:T(8,128)(2,1)S(1)}, u32[]{:S(2)}) copy-start(bf16[256,768]{1,0:T(8,128)(2,1)S(1)} %get-tuple-element.112.input_ref) | copy-start | bytes 1179652
  3.9 25.2 %copy-start.27 = (bf16[80,768]{1,0:T(8,128)(2,1)}, bf16[80,768]{1,0:T(8,128)(2,1)S(1)}, u32[]{:S(2)}) copy-start(bf16[80,768]{1,0:T(8,128)(2,1)S(1)} %get-tuple-element.118.refs_0_) | copy-start | bytes 368644
  4.0 7.7 %collective-permute-start.1 = (bf16[80,768]{1,0:T(8,128)(2,1)S(1)}, bf16[80,768]{1,0:T(8,128)(2,1)S(1)}, u32[]{:S(2)}, u32[]{:S(2)}) collective-permute-start(bf16[80,768]{1,0:T(8,128)(2,1)S(1)} %get-tuple-element.118.refs_0_), channel_id=1, source_target_pairs={{0,2},{1,3},{2,0},{3,1},{4,6},{5,7},{6,4},{7,5},{8,10},{9,11},{10,... | collective-permute-start | bytes 368648 | tf_op jit(solution)/shard_map/ppermute | solution.py:682
  7.0 12.3 %collective-permute-start.3 = (bf16[80,768]{1,0:T(8,128)(2,1)S(1)}, bf16[80,768]{1,0:T(8,128)(2,1)S(1)}, u32[]{:S(2)}, u32[]{:S(2)}) collective-permute-start(bf16[80,768]{1,0:T(8,128)(2,1)S(1)} %get-tuple-element.118.refs_0_), channel_id=1, source_target_pairs={{0,4},{1,5},{2,6},{3,7},{4,0},{5,1},{6,2},{7,3},{8,12},{9,13},{10,... | collective-permute-start | bytes 368648 | tf_op jit(solution)/shard_map/ppermute | solution.py:682
  9.6 11.2 %collective-permute-start.5 = (bf16[80,768]{1,0:T(8,128)(2,1)S(1)}, bf16[80,768]{1,0:T(8,128)(2,1)S(1)}, u32[]{:S(2)}, u32[]{:S(2)}) collective-permute-start(bf16[80,768]{1,0:T(8,128)(2,1)S(1)} %get-tuple-element.118.refs_0_), channel_id=1, source_target_pairs={{0,6},{1,7},{2,4},{3,5},{4,2},{5,3},{6,0},{7,1},{8,14},{9,15},{10,... | collective-permute-start | bytes 368648 | tf_op jit(solution)/shard_map/ppermute | solution.py:682
  9.6 22.5 %collective-permute-start = (bf16[80,768]{1,0:T(8,128)(2,1)S(1)}, bf16[80,768]{1,0:T(8,128)(2,1)S(1)}, u32[]{:S(2)}, u32[]{:S(2)}) collective-permute-start(bf16[80,768]{1,0:T(8,128)(2,1)S(1)} %get-tuple-element.118.refs_0_), channel_id=1, source_target_pairs={{0,1},{1,0},{2,3},{3,2},{4,5},{5,4},{6,7},{7,6},{8,9},{9,8},{10,11... | collective-permute-start | bytes 368648 | tf_op jit(solution)/shard_map/ppermute | solution.py:682
  11.7 17.4 %copy-start.40 = (bf16[80,768]{1,0:T(8,128)(2,1)}, bf16[80,768]{1,0:T(8,128)(2,1)S(1)}, u32[]{:S(2)}) copy-start(bf16[80,768]{1,0:T(8,128)(2,1)S(1)} %collective-permute-done.1.refs_2_) | copy-start | bytes 368644
  11.7 20.4 %collective-permute-start.2 = (bf16[80,768]{1,0:T(8,128)(2,1)S(1)}, bf16[80,768]{1,0:T(8,128)(2,1)S(1)}, u32[]{:S(2)}, u32[]{:S(2)}) collective-permute-start(bf16[80,768]{1,0:T(8,128)(2,1)S(1)} %collective-permute-done.1.refs_2_), channel_id=1, source_target_pairs={{0,1},{1,0},{2,3},{3,2},{4,5},{5,4},{6,7},{7,6},{8,9},{9,8},{10,11... | collective-permute-start | bytes 368648 | tf_op jit(solution)/shard_map/ppermute | solution.py:682
  19.4 9.8 %copy-start.41 = (bf16[80,768]{1,0:T(8,128)(2,1)}, bf16[80,768]{1,0:T(8,128)(2,1)S(1)}, u32[]{:S(2)}) copy-start(bf16[80,768]{1,0:T(8,128)(2,1)S(1)} %collective-permute-done.3.refs_4_) | copy-start | bytes 368644
  19.4 12.8 %collective-permute-start.4 = (bf16[80,768]{1,0:T(8,128)(2,1)S(1)}, bf16[80,768]{1,0:T(8,128)(2,1)S(1)}, u32[]{:S(2)}, u32[]{:S(2)}) collective-permute-start(bf16[80,768]{1,0:T(8,128)(2,1)S(1)} %collective-permute-done.3.refs_4_), channel_id=1, source_target_pairs={{0,1},{1,0},{2,3},{3,2},{4,5},{5,4},{6,7},{7,6},{8,9},{9,8},{10,11... | collective-permute-start | bytes 368648 | tf_op jit(solution)/shard_map/ppermute | solution.py:682
  20.9 8.3 %copy-start.42 = (bf16[80,768]{1,0:T(8,128)(2,1)}, bf16[80,768]{1,0:T(8,128)(2,1)S(1)}, u32[]{:S(2)}) copy-start(bf16[80,768]{1,0:T(8,128)(2,1)S(1)} %collective-permute-done.5.refs_6_) | copy-start | bytes 368644
  20.9 11.3 %collective-permute-start.6 = (bf16[80,768]{1,0:T(8,128)(2,1)S(1)}, bf16[80,768]{1,0:T(8,128)(2,1)S(1)}, u32[]{:S(2)}, u32[]{:S(2)}) collective-permute-start(bf16[80,768]{1,0:T(8,128)(2,1)S(1)} %collective-permute-done.5.refs_6_), channel_id=1, source_target_pairs={{0,1},{1,0},{2,3},{3,2},{4,5},{5,4},{6,7},{7,6},{8,9},{9,8},{10,11... | collective-permute-start | bytes 368648 | tf_op jit(solution)/shard_map/ppermute | solution.py:682
  66.5 5.4 %collective-permute-start.7 = (bf16[8,480,384]{2,1,0:T(8,128)(2,1)S(1)}, bf16[8,480,384]{2,1,0:T(8,128)(2,1)S(1)}, u32[]{:S(2)}, u32[]{:S(2)}) collective-permute-start(bf16[8,480,384]{2,1,0:T(8,128)(2,1)S(1)} %shard_map.344.refs_3_), channel_id=1, source_target_pairs={{0,8},{8,0},{16,24},{24,16},{1,9},{9,1},{17,25},{25,17},{2,10},{10... | collective-permute-start | bytes 8847368 | tf_op jit(solution)/shard_map/ppermute | solution.py:679
  66.7 10.3 %slice-start = ((s8[4718592]{0:T(1024)(128)(4,1)}), s8[4194304]{0:T(1024)(128)(4,1)S(1)}, s32[]{:S(2)}) async-start(s8[4718592]{0:T(1024)(128)(4,1)} %bitcast.21), calls=%async_computation | async-start | bytes 8388608
  68.2 8.7 %slice-start.1 = ((s8[4718592]{0:T(1024)(128)(4,1)}), s8[524288]{0:T(1024)(128)(4,1)S(1)}, s32[]{:S(2)}) async-start(s8[4718592]{0:T(1024)(128)(4,1)} %bitcast.21), calls=%async_computation.1 | async-start | bytes 1048576
  68.2 7.1 %collective-permute-start.8 = (bf16[8,384,384]{2,1,0:T(8,128)(2,1)S(1)}, bf16[8,384,384]{2,1,0:T(8,128)(2,1)S(1)}, u32[]{:S(2)}, u32[]{:S(2)}) collective-permute-start(bf16[8,384,384]{2,1,0:T(8,128)(2,1)S(1)} %shard_map.345.refs_6_), channel_id=1, source_target_pairs={{0,8},{8,0},{16,24},{24,16},{1,9},{9,1},{17,25},{25,17},{2,10},{10... | collective-permute-start | bytes 7077896 | tf_op jit(solution)/shard_map/ppermute | solution.py:679
  77.4 6.2 %copy-start.6 = (bf16[768,768]{1,0:T(8,128)(2,1)S(1)}, bf16[768,768]{1,0:T(8,128)(2,1)}, u32[]{:S(2)}) copy-start(bf16[768,768]{1,0:T(8,128)(2,1)} %get-tuple-element.141.refs_1_) | copy-start | bytes 3538948
  83.6 5.8 %copy-start.1 = (bf16[768,768]{1,0:T(8,128)(2,1)S(1)}, bf16[768,768]{1,0:T(8,128)(2,1)}, u32[]{:S(2)}) copy-start(bf16[768,768]{1,0:T(8,128)(2,1)} %refs_4_.3) | copy-start | bytes 3538948
  83.6 5.8 %copy-start.3 = (bf16[768,768]{1,0:T(8,128)(2,1)S(1)}, bf16[768,768]{1,0:T(8,128)(2,1)}, u32[]{:S(2)}) copy-start(bf16[768,768]{1,0:T(8,128)(2,1)} %refs_5_.3) | copy-start | bytes 3538948
  83.6 5.8 %copy-start.8 = (bf16[768,768]{1,0:T(8,128)(2,1)S(1)}, bf16[768,768]{1,0:T(8,128)(2,1)}, u32[]{:S(2)}) copy-start(bf16[768,768]{1,0:T(8,128)(2,1)} %refs_3_.3) | copy-start | bytes 3538948
  83.7 5.8 %copy-start.20 = (f32[256,768]{1,0:T(8,128)S(1)}, f32[256,768]{1,0:T(8,128)}, u32[]{:S(2)}) copy-start(f32[256,768]{1,0:T(8,128)} %get-tuple-element.137.refs_6_) | copy-start | bytes 2359300
  83.7 5.8 %copy-start.28 = (f32[8,768]{1,0:T(8,128)S(1)}, f32[8,768]{1,0:T(8,128)}, u32[]{:S(2)}) copy-start(f32[8,768]{1,0:T(8,128)} %get-tuple-element.139.refs_9_) | copy-start | bytes 73732
  83.7 5.8 %copy-start.29 = (f32[8,512]{1,0:T(8,128)S(1)}, f32[8,512]{1,0:T(8,128)}, u32[]{:S(2)}) copy-start(f32[8,512]{1,0:T(8,128)} %get-tuple-element.138.refs_8_) | copy-start | bytes 49156
  83.7 5.8 %copy-start.30 = (f32[1,3072]{1,0:T(1,128)S(1)}, f32[1,3072]{1,0:T(1,128)}, u32[]{:S(2)}) copy-start(f32[1,3072]{1,0:T(1,128)} %get-tuple-element.140.refs_10_) | copy-start | bytes 36868
  83.7 5.8 %copy-start.32 = (s32[256]{0:T(256)S(1)}, s32[256]{0:T(256)}, u32[]{:S(2)}) copy-start(s32[256]{0:T(256)} %refs_7_.1) | copy-start | bytes 3076
  85.9 19.0 %collective-permute-start.9 = (bf16[8,288,384]{2,1,0:T(8,128)(2,1)S(1)}, bf16[8,288,384]{2,1,0:T(8,128)(2,1)S(1)}, u32[]{:S(2)}, u32[]{:S(2)}) collective-permute-start(bf16[8,288,384]{2,1,0:T(8,128)(2,1)S(1)} %shard_map.349.refs_11_), channel_id=1, source_target_pairs={{0,8},{8,0},{16,24},{24,16},{1,9},{9,1},{17,25},{25,17},{2,10},{10... | collective-permute-start | bytes 5308424 | tf_op jit(solution)/shard_map/ppermute | solution.py:679
  86.1 28.8 %collective-permute-start.13 = (bf16[1536,384]{1,0:T(8,128)(2,1)S(1)}, bf16[1536,384]{1,0:T(8,128)(2,1)S(1)}, u32[]{:S(2)}, u32[]{:S(2)}) collective-permute-start(bf16[1536,384]{1,0:T(8,128)(2,1)S(1)} %get-tuple-element.132.refs_1_), channel_id=1, source_target_pairs={{0,1},{1,0},{2,3},{3,2},{4,5},{5,4},{6,7},{7,6},{8,9},{9,8},{10,11... | collective-permute-start | bytes 3538952 | tf_op jit(solution)/shard_map/ppermute | solution.py:682
  87.6 21.9 %collective-permute-start.14 = (bf16[1152,384]{1,0:T(8,128)(2,1)S(1)}, bf16[1152,384]{1,0:T(8,128)(2,1)S(1)}, u32[]{:S(2)}, u32[]{:S(2)}) collective-permute-start(bf16[1152,384]{1,0:T(8,128)(2,1)S(1)} %get-tuple-element.131.refs_4_.refs_0_), channel_id=1, source_target_pairs={{0,16},{8,24},{16,0},{24,8},{1,17},{9,25},{17,1},{25,9},{2,18},{10... | collective-permute-start | bytes 2654216 | tf_op jit(solution)/shard_map/ppermute | solution.py:679
  89.1 15.0 %collective-permute-start.11 = (bf16[768,384]{1,0:T(8,128)(2,1)S(1)}, bf16[768,384]{1,0:T(8,128)(2,1)S(1)}, u32[]{:S(2)}, u32[]{:S(2)}) collective-permute-start(bf16[768,384]{1,0:T(8,128)(2,1)S(1)} %get-tuple-element.133.refs_2_), channel_id=1, source_target_pairs={{0,2},{1,3},{2,0},{3,1},{4,6},{5,7},{6,4},{7,5},{8,10},{9,11},{10,... | collective-permute-start | bytes 1769480 | tf_op jit(solution)/shard_map/ppermute | solution.py:682
  92.9 11.9 %collective-permute-start.10 = (bf16[64,384]{1,0:T(8,128)(2,1)S(1)}, bf16[64,384]{1,0:T(8,128)(2,1)S(1)}, u32[]{:S(2)}, u32[]{:S(2)}) collective-permute-start(bf16[64,384]{1,0:T(8,128)(2,1)S(1)} %get-tuple-element.145), channel_id=1, source_target_pairs={{0,8},{8,0},{16,24},{24,16},{1,9},{9,1},{17,25},{25,17},{2,10},{10... | collective-permute-start | bytes 147464 | tf_op jit(solution)/shard_map/ppermute | solution.py:679
  107.1 22.0 %collective-permute-start.15 = (bf16[896,384]{1,0:T(8,128)(2,1)S(1)}, bf16[896,384]{1,0:T(8,128)(2,1)S(1)}, u32[]{:S(2)}, u32[]{:S(2)}) collective-permute-start(bf16[896,384]{1,0:T(8,128)(2,1)S(1)} %get-tuple-element.153.refs_2_), channel_id=1, source_target_pairs={{0,1},{1,0},{2,3},{3,2},{4,5},{5,4},{6,7},{7,6},{8,9},{9,8},{10,11... | collective-permute-start | bytes 2064392 | tf_op jit(solution)/shard_map/ppermute | solution.py:682
  107.6 17.3 %collective-permute-start.12 = (bf16[832,384]{1,0:T(8,128)(2,1)S(1)}, bf16[832,384]{1,0:T(8,128)(2,1)S(1)}, u32[]{:S(2)}, u32[]{:S(2)}) collective-permute-start(bf16[832,384]{1,0:T(8,128)(2,1)S(1)} %get-tuple-element.150), channel_id=1, source_target_pairs={{0,16},{8,24},{16,0},{24,8},{1,17},{9,25},{17,1},{25,9},{2,18},{10... | collective-permute-start | bytes 1916936 | tf_op jit(solution)/shard_map/ppermute | solution.py:679
  115.8 21.6 %collective-permute-start.18 = (bf16[768,384]{1,0:T(8,128)(2,1)S(1)}, bf16[768,384]{1,0:T(8,128)(2,1)S(1)}, u32[]{:S(2)}, u32[]{:S(2)}) collective-permute-start(bf16[768,384]{1,0:T(8,128)(2,1)S(1)} %get-tuple-element.155.refs_3_), channel_id=1, source_target_pairs={{0,16},{8,24},{16,0},{24,8},{1,17},{9,25},{17,1},{25,9},{2,18},{10... | collective-permute-start | bytes 1769480 | tf_op jit(solution)/shard_map/ppermute | solution.py:679
  117.3 17.1 %collective-permute-start.19 = (bf16[576,384]{1,0:T(8,128)(2,1)S(1)}, bf16[576,384]{1,0:T(8,128)(2,1)S(1)}, u32[]{:S(2)}, u32[]{:S(2)}) collective-permute-start(bf16[576,384]{1,0:T(8,128)(2,1)S(1)} %get-tuple-element.154.refs_2_), channel_id=1, source_target_pairs={{0,2},{1,3},{2,0},{3,1},{4,6},{5,7},{6,4},{7,5},{8,10},{9,11},{10,... | collective-permute-start | bytes 1327112 | tf_op jit(solution)/shard_map/ppermute | solution.py:682
  118.7 14.6 %collective-permute-start.20 = (bf16[384,384]{1,0:T(8,128)(2,1)S(1)}, bf16[384,384]{1,0:T(8,128)(2,1)S(1)}, u32[]{:S(2)}, u32[]{:S(2)}) collective-permute-start(bf16[384,384]{1,0:T(8,128)(2,1)S(1)} %get-tuple-element.147.refs_9_), channel_id=1, source_target_pairs={{0,4},{1,5},{2,6},{3,7},{4,0},{5,1},{6,2},{7,3},{8,12},{9,13},{10,... | collective-permute-start | bytes 884744 | tf_op jit(solution)/shard_map/ppermute | solution.py:682
  135.2 18.9 %collective-permute-start.23 = (bf16[480,384]{1,0:T(8,128)(2,1)S(1)}, bf16[480,384]{1,0:T(8,128)(2,1)S(1)}, u32[]{:S(2)}, u32[]{:S(2)}) collective-permute-start(bf16[480,384]{1,0:T(8,128)(2,1)S(1)} %get-tuple-element.166.refs_2_), channel_id=1, source_target_pairs={{0,1},{1,0},{2,3},{3,2},{4,5},{5,4},{6,7},{7,6},{8,9},{9,8},{10,11... | collective-permute-start | bytes 1105928 | tf_op jit(solution)/shard_map/ppermute | solution.py:682
  136.8 15.1 %collective-permute-start.16 = (bf16[448,384]{1,0:T(8,128)(2,1)S(1)}, bf16[448,384]{1,0:T(8,128)(2,1)S(1)}, u32[]{:S(2)}, u32[]{:S(2)}) collective-permute-start(bf16[448,384]{1,0:T(8,128)(2,1)S(1)} %get-tuple-element.159.refs_3_), channel_id=1, source_target_pairs={{0,1},{1,0},{2,3},{3,2},{4,5},{5,4},{6,7},{7,6},{8,9},{9,8},{10,11... | collective-permute-start | bytes 1032200 | tf_op jit(solution)/shard_map/ppermute | solution.py:682
  138.1 16.1 %collective-permute-start.24 = (bf16[384,384]{1,0:T(8,128)(2,1)S(1)}, bf16[384,384]{1,0:T(8,128)(2,1)S(1)}, u32[]{:S(2)}, u32[]{:S(2)}) collective-permute-start(bf16[384,384]{1,0:T(8,128)(2,1)S(1)} %get-tuple-element.167.refs_5_), channel_id=1, source_target_pairs={{0,2},{1,3},{2,0},{3,1},{4,6},{5,7},{6,4},{7,5},{8,10},{9,11},{10,... | collective-permute-start | bytes 884744 | tf_op jit(solution)/shard_map/ppermute | solution.py:682
  140.5 5.1 %collective-permute-start.17 = (bf16[192,384]{1,0:T(8,128)(2,1)S(1)}, bf16[192,384]{1,0:T(8,128)(2,1)S(1)}, u32[]{:S(2)}, u32[]{:S(2)}) collective-permute-start(bf16[192,384]{1,0:T(8,128)(2,1)S(1)} %get-tuple-element.162.refs_4_), channel_id=1, source_target_pairs={{0,16},{8,24},{16,0},{24,8},{1,17},{9,25},{17,1},{25,9},{2,18},{10... | collective-permute-start | bytes 442376 | tf_op jit(solution)/shard_map/ppermute | solution.py:679
  152.6 16.0 %collective-permute-start.21 = (bf16[352,384]{1,0:T(8,128)(2,1)S(1)}, bf16[352,384]{1,0:T(8,128)(2,1)S(1)}, u32[]{:S(2)}, u32[]{:S(2)}) collective-permute-start(bf16[352,384]{1,0:T(8,128)(2,1)S(1)} %get-tuple-element.172.refs_5_), channel_id=1, source_target_pairs={{0,2},{1,3},{2,0},{3,1},{4,6},{5,7},{6,4},{7,5},{8,10},{9,11},{10,... | collective-permute-start | bytes 811016 | tf_op jit(solution)/shard_map/ppermute | solution.py:682
  154.9 15.5 %collective-permute-start.26 = (bf16[336,384]{1,0:T(8,128)(2,1)S(1)}, bf16[336,384]{1,0:T(8,128)(2,1)S(1)}, u32[]{:S(2)}, u32[]{:S(2)}) collective-permute-start(bf16[336,384]{1,0:T(8,128)(2,1)S(1)} %get-tuple-element.177.refs_6_), channel_id=1, source_target_pairs={{0,4},{1,5},{2,6},{3,7},{4,0},{5,1},{6,2},{7,3},{8,12},{9,13},{10,... | collective-permute-start | bytes 774152 | tf_op jit(solution)/shard_map/ppermute | solution.py:682
  156.4 12.3 %collective-permute-start.22 = (bf16[256,384]{1,0:T(8,128)(2,1)S(1)}, bf16[256,384]{1,0:T(8,128)(2,1)S(1)}, u32[]{:S(2)}, u32[]{:S(2)}) collective-permute-start(bf16[256,384]{1,0:T(8,128)(2,1)S(1)} %get-tuple-element.173), channel_id=1, source_target_pairs={{0,2},{1,3},{2,0},{3,1},{4,6},{5,7},{6,4},{7,5},{8,10},{9,11},{10,... | collective-permute-start | bytes 589832 | tf_op jit(solution)/shard_map/ppermute | solution.py:682
  156.9 13.6 %collective-permute-start.27 = (bf16[96,384]{1,0:T(8,128)(2,1)S(1)}, bf16[96,384]{1,0:T(8,128)(2,1)S(1)}, u32[]{:S(2)}, u32[]{:S(2)}) collective-permute-start(bf16[96,384]{1,0:T(8,128)(2,1)S(1)} %get-tuple-element.186), channel_id=1, source_target_pairs={{0,16},{8,24},{16,0},{24,8},{1,17},{9,25},{17,1},{25,9},{2,18},{10... | collective-permute-start | bytes 221192 | tf_op jit(solution)/shard_map/ppermute | solution.py:679
  169.3 12.3 %collective-permute-start.25 = (bf16[336,384]{1,0:T(8,128)(2,1)S(1)}, bf16[336,384]{1,0:T(8,128)(2,1)S(1)}, u32[]{:S(2)}, u32[]{:S(2)}) collective-permute-start(bf16[336,384]{1,0:T(8,128)(2,1)S(1)} %get-tuple-element.182.refs_5_), channel_id=1, source_target_pairs={{0,4},{1,5},{2,6},{3,7},{4,0},{5,1},{6,2},{7,3},{8,12},{9,13},{10,... | collective-permute-start | bytes 774152 | tf_op jit(solution)/shard_map/ppermute | solution.py:682
  171.1 16.7 %collective-permute-start.30 = (bf16[432,384]{1,0:T(8,128)(2,1)S(1)}, bf16[432,384]{1,0:T(8,128)(2,1)S(1)}, u32[]{:S(2)}, u32[]{:S(2)}) collective-permute-start(bf16[432,384]{1,0:T(8,128)(2,1)S(1)} %constant_dynamic-update-slice_fusion.2), channel_id=1, source_target_pairs={{0,16},{8,24},{16,0},{24,8},{1,17},{9,25},{17,1},{25,9},{2,18},{10... | collective-permute-start | bytes 995336 | tf_op jit(solution)/shard_map/ppermute | solution.py:679
  182.9 4.8 %collective-permute-start.28 = (bf16[144,384]{1,0:T(8,128)(2,1)S(1)}, bf16[144,384]{1,0:T(8,128)(2,1)S(1)}, u32[]{:S(2)}, u32[]{:S(2)}) collective-permute-start(bf16[144,384]{1,0:T(8,128)(2,1)S(1)} %constant_dynamic-update-slice_fusion), channel_id=1, source_target_pairs={{0,16},{8,24},{16,0},{24,8},{1,17},{9,25},{17,1},{25,9},{2,18},{10... | collective-permute-start | bytes 331784 | tf_op jit(solution)/shard_map/ppermute | solution.py:679
  188.1 2.7 %collective-permute-start.31 = (bf16[864,384]{1,0:T(8,128)(2,1)S(1)}, bf16[864,384]{1,0:T(8,128)(2,1)S(1)}, u32[]{:S(2)}, u32[]{:S(2)}) collective-permute-start(bf16[864,384]{1,0:T(8,128)(2,1)S(1)} %slice_dynamic-update-slice_fusion.12), channel_id=1, source_target_pairs={{0,8},{8,0},{16,24},{24,16},{1,9},{9,1},{17,25},{25,17},{2,10},{10... | collective-permute-start | bytes 1990664 | tf_op jit(solution)/shard_map/ppermute | solution.py:679
  188.2 2.4 %collective-permute-start.29 = (bf16[288,384]{1,0:T(8,128)(2,1)S(1)}, bf16[288,384]{1,0:T(8,128)(2,1)S(1)}, u32[]{:S(2)}, u32[]{:S(2)}) collective-permute-start(bf16[288,384]{1,0:T(8,128)(2,1)S(1)} %pad_maximum_fusion.1), channel_id=1, source_target_pairs={{0,8},{8,0},{16,24},{24,16},{1,9},{9,1},{17,25},{25,17},{2,10},{10... | collective-permute-start | bytes 663560 | tf_op jit(solution)/shard_map/ppermute | solution.py:679
  (34 other events, 44.9 us)

commit v4 on v3

--- a/solution.py
+++ b/solution.py
@@ -15,6 +15,9 @@
 BF = jnp.bfloat16
 F32 = jnp.float32
 MIB = 1 << 20
+LONG = pl.CostEstimate(flops=40_000_000_000, bytes_accessed=MIB, transcendentals=0)
+SHORT = pl.CostEstimate(flops=100000000, bytes_accessed=MIB, transcendentals=0)
+HBM = pl.BlockSpec(memory_space=pltpu.HBM)
 
 
 def outer_sum(left, right):
@@ -54,8 +57,19 @@
     return jnp.broadcast_to(row, (128, row.shape[1])).T[:, :1]
 
 
-def entry_kernel(tokens_ref, seg_ref, prev_ref, answer_ref, payload_ref, input_ref):
+def start_copies(sources, targets, sems):
+    copies = [pltpu.make_async_copy(a, b, sems.at[i]) for i, (a, b) in enumerate(zip(sources, targets))]
+    for copy in copies:
+        copy.start()
+    return copies
+
+
+def entry_kernel(tokens_any, seg_any, prev_any, answer_any, payload_ref, input_ref, *scratch):
     tab = TAB_MAX
+    *held, sems = scratch
+    for copy in start_copies((tokens_any, seg_any, prev_any, answer_any), held, sems):
+        copy.wait()
+    tokens_ref, seg_ref, prev_ref, answer_ref = held
     prev = prev_ref[...].astype(F32)[None]
     low = residual(tokens_ref, prev, answer_ref).astype(BF)
     input_ref[...] = low
@@ -82,17 +96,24 @@
     vmem = pl.BlockSpec(memory_space=pltpu.VMEM)
     return pl.pallas_call(
         entry_kernel,
-        in_specs=[vmem] * 4,
+        in_specs=[HBM] * 4,
         out_specs=[vmem] * 2,
         out_shape=[jax.ShapeDtypeStruct((TAB_MAX + 16, width), BF), jax.ShapeDtypeStruct((rows, width), BF)],
-        compiler_params=pltpu.CompilerParams(vmem_limit_bytes=12 * MIB),
+        scratch_shapes=[pltpu.VMEM(v.shape, v.dtype) for v in (tokens, seg, prev, answers)]
+        + [pltpu.SemaphoreType.DMA((4,))],
+        compiler_params=pltpu.CompilerParams(vmem_limit_bytes=60 * MIB),
     )(tokens, seg, prev, answers)
 
 
 def own_kernel(
-    input_ref, query_w_ref, key_w_ref, value_w_ref, query_b_ref, value_b_ref, seg_ref, turn_ref,
-    q_ref, k_ref, v_ref, bias_ref, value_row_ref,
+    input_ref, query_w_any, key_w_any, value_w_any, query_b_any, value_b_any, seg_any, turn_any,
+    q_ref, k_ref, v_ref, bias_ref, value_row_ref, *scratch
 ):
+    *held, sems = scratch
+    query_w_ref, key_w_ref, value_w_ref, query_b_ref, value_b_ref, seg_ref, turn_ref = held
+    sources = (query_w_any, key_w_any, value_w_any, query_b_any, value_b_any, seg_any, turn_any)
+    for copy in start_copies(sources, held, sems):
+        copy.wait()
     low = input_ref[...]
     query = fwd_dot(low, query_w_ref[...]) + query_b_ref[...].astype(F32)[None]
     q_ref[...] = (query.astype(BF).astype(F32) * HEAD_DIM**-0.5).astype(BF)
@@ -111,21 +132,26 @@
     vmem = pl.BlockSpec(memory_space=pltpu.VMEM)
     return pl.pallas_call(
         own_kernel,
-        in_specs=[vmem] * 8,
+        in_specs=[vmem] + [HBM] * 7,
         out_specs=[vmem] * 5,
         out_shape=[jax.ShapeDtypeStruct((rows, width), BF)] * 3
         + [jax.ShapeDtypeStruct((rows, rows), F32), jax.ShapeDtypeStruct((1, width), F32)],
-        compiler_params=pltpu.CompilerParams(vmem_limit_bytes=20 * MIB),
-        cost_estimate=pl.CostEstimate(flops=900_000_000, bytes_accessed=5 * MIB, transcendentals=0),
+        scratch_shapes=[
+            pltpu.VMEM(v.shape, v.dtype) for v in (query_w, key_w, value_w, query_b, value_b, seg, turn)
+        ]
+        + [pltpu.SemaphoreType.DMA((7,))],
+        compiler_params=pltpu.CompilerParams(vmem_limit_bytes=60 * MIB),
+        cost_estimate=pl.CostEstimate(flops=100000000, bytes_accessed=MIB, transcendentals=0),
     )(layer_input, query_w, key_w, value_w, query_b, value_b, seg, turn)
 
 
 def attend_kernel(
-    input_ref, key_w_ref, value_w_ref, value_b_ref, q_ref, own_k_ref, own_v_ref, own_bias_ref, *refs
+    views, input_ref, key_w_ref, value_w_ref, value_b_ref, q_ref, own_k_ref, own_v_ref, own_bias_ref, *refs
 ):
-    *slots, keys_ref, values_ref, prob_ref, context_ref, x_t_ref, prev_ref, table_ref, bias_ref = refs
+    *parts, keys_ref, values_ref, prob_ref, context_ref, x_t_ref, prev_ref, table_ref, bias_ref = refs
     n_table = table_ref.shape[0]
     tab = TAB_MAX
+    slots = [parts[part].at[first : first + tab + 16] for part, first in views]
 
     @pl.when(pl.program_id(0) == 0)
     def _():
@@ -168,9 +194,9 @@
     return (small if n_keys <= 1024 else 60) * MIB
 
 
-def attend(slots, layer_input, key_w, value_w, value_b, queries, own_k, own_v, own_bias):
+def attend(parts, views, layer_input, key_w, value_w, value_b, queries, own_k, own_v, own_bias):
     rows, width = queries.shape
-    n_table = len(slots) * TAB_MAX
+    n_table = len(views) * TAB_MAX
     n_keys = n_table + rows
     group = LANES if n_keys <= 1024 else LANES // 2
     per = group // HEAD_DIM
@@ -178,13 +204,13 @@
     whole = lambda shape: pl.BlockSpec(shape, lambda i: (0, 0), **steady)
     lanes = lambda n: pl.BlockSpec((n, group), lambda i: (0, i))
     return pl.pallas_call(
-        attend_kernel,
+        lambda *refs: attend_kernel(views, *refs),
         grid=(width // group,),
         in_specs=[
             whole((rows, width)), lanes(width), lanes(width), lanes(1), lanes(rows), lanes(rows), lanes(rows),
             whole((rows, rows)),
         ]
-        + [whole(slot.shape) for slot in slots],
+        + [whole(part.shape) for part in parts],
         out_specs=[
             lanes(n_keys), lanes(n_keys), pl.BlockSpec((per, rows, n_keys), lambda i: (i, 0, 0)), lanes(rows),
             whole((width, n_keys)), whole((8, n_table)),
@@ -198,47 +224,56 @@
             jax.ShapeDtypeStruct((8, n_table), F32),
         ],
         scratch_shapes=[pltpu.VMEM((n_table, width), BF), pltpu.VMEM((rows, n_keys), F32)],
-        compiler_params=pltpu.CompilerParams(vmem_limit_bytes=vmem_limit(n_keys, 56)),
-        cost_estimate=pl.CostEstimate(flops=100_000_000, bytes_accessed=1 * MIB, transcendentals=0),
-    )(layer_input, key_w, value_w, value_b, queries, own_k, own_v, own_bias, *slots)
+        compiler_params=pltpu.CompilerParams(vmem_limit_bytes=vmem_limit(n_keys, 60)),
+        cost_estimate=pl.CostEstimate(flops=100000000, bytes_accessed=MIB, transcendentals=0),
+    )(layer_input, key_w, value_w, value_b, queries, own_k, own_v, own_bias, *parts)
 
 
 def middle_kernel(
-    tokens_ref, prev_ref, answer_ref, context_ref, cot_ref, out_w_any, up_w_any, down_w_any, up_b_1d_ref, *refs
+    packets, pos_ref, tokens_ref, prev_ref, answer_ref, context_ref, cot_ref, out_w_any, up_w_any, down_w_any,
+    up_b_1d_ref, *refs
 ):
     biases, refs = refs[:6], refs[6:]
-    mixed_ref, context_t_ref, middle_t_ref, act_t_ref, grad_ffn_ref, grad_pre_ref, grad_attn_ref = refs[:7]
-    grad_context_ref, grad_mid_ref, sums_ref, up_sum_ref, slope_ref, total_ref, middle_low_ref = refs[7:14]
-    out_w_ref, up_w_ref, down_w_ref, up_b_ref, sems = refs[14:]
-    copies = [
-        pltpu.make_async_copy(source, target, sems.at[i])
-        for i, (source, target) in enumerate(
-            ((out_w_any, out_w_ref), (up_w_any, up_w_ref), (down_w_any, down_w_ref))
-        )
-    ]
-    for copy in copies:
-        copy.start()
-    hidden = up_w_ref.shape[1]
-    tile = 512
+    mixed_ref, grad_context_ref, grad_mid_ref, sums_ref, up_sum_ref = refs[:5]
+    refs = refs[5:]
+    if packets:
+        anys, refs = refs[:5], refs[5:]
+    context_t_ref, middle_t_ref, act_t_ref, grad_ffn_ref, grad_pre_ref, grad_attn_ref = refs[:6]
+    slope_ref, total_ref, middle_low_ref, out_w_ref, up_w_ref, down_w_ref, up_b_ref, sems = refs[6:14]
+    width, hidden = up_w_ref.shape
+    tile = width
     steps = hidden // tile
+
+    def tile_copies(i):
+        at = pl.ds(pl.multiple_of(i * tile, tile), tile)
+        return (
+            pltpu.make_async_copy(up_w_any.at[:, at], up_w_ref.at[:, at], sems.at[2 * i + 1]),
+            pltpu.make_async_copy(down_w_any.at[at, :], down_w_ref.at[at, :], sems.at[2 * i + 2]),
+        )
+
+    out_copy = pltpu.make_async_copy(out_w_any, out_w_ref, sems.at[0])
+    out_copy.start()
+    for i in range(steps):
+        for copy in tile_copies(i):
+            copy.start()
     out_b, norm_g, norm_s, down_b, final_g, final_s = (ref[...].astype(F32)[None] for ref in biases)
     up_b_ref[...] = up_b_1d_ref[...].astype(F32)[None]
     resid = residual(tokens_ref, prev_ref[...].astype(F32)[None], answer_ref)
     column = lambda v: jnp.sum(v, axis=0, keepdims=True)
     context_low = context_ref[...].astype(BF)
     context_t_ref[...] = context_low.T
-    copies[0].wait()
+    out_copy.wait()
     normed1, inv1 = norm_parts(resid + fwd_dot(context_low, out_w_ref[...]) + out_b)
     middle = normed1 * norm_g + norm_s
     middle_low = middle.astype(BF)
     middle_low_ref[...] = middle_low
     middle_t_ref[...] = middle_low.T
     total_ref[...] = middle + down_b
-    copies[1].wait()
-    copies[2].wait()
 
     def forward(i, carry):
         at = pl.ds(pl.multiple_of(i * tile, tile), tile)
+        for copy in tile_copies(i):
+            copy.wait()
         pre = fwd_dot(middle_low_ref[...], up_w_ref[:, at]) + up_b_ref[:, at]
         cdf = 0.5 * (1.0 + lax.erf(pre * (0.5**0.5)))
         act = (pre * cdf).astype(BF)
@@ -264,12 +299,61 @@
         total_ref[...] += back_dot(grad_pre, up_w_ref[:, at])
         return carry
 
-    lax.fori_loop(0, steps, backward, 0)
+    copies = []
+    if packets:
+        blocks = packets
+        sent_ref, down_own_ref, z_own_ref, up_sent_ref, up_own_ref, out_sems = refs[14:]
+        half = width // 2
+        small, size = width // blocks, hidden // blocks
+        first_rows = 2 * small // 3
+        z_rows, rows = first_rows + small, size - first_rows
+        core = pos_ref[0]
+        n_down = blocks * rows
+
+        def leave(source, target):
+            copy = pltpu.make_async_copy(source, target, out_sems.at[len(copies)])
+            copy.start()
+            copies.append(copy)
+
+        def lanes_of(own):
+            return pl.ds(pl.multiple_of((core if own else 1 - core) * half, 128), half)
+
+        for own, down_ref, first_z, z_ref in ((False, sent_ref, n_down, sent_ref), (True, down_own_ref, 0, z_own_ref)):
+            part = grad_ffn_ref[:, lanes_of(own)]
+            for b in range(blocks):
+                value = fwd_dot(act_t_ref[b * size : (b + 1) * size], part).astype(BF)
+                down_ref[b * rows : (b + 1) * rows] = value[first_rows:]
+                z_ref[first_z + b * z_rows : first_z + b * z_rows + first_rows] = value[:first_rows]
+            leave(down_ref.at[:n_down], (anys[1] if own else anys[0].at[:n_down]))
+        for i in range(steps):
+            t = lax.rem(2 * (1 - core) + i, steps)
+            backward(t, 0)
+            value = fwd_dot(middle_t_ref[...], grad_pre_ref[:, pl.ds(pl.multiple_of(t * tile, tile), tile)]).astype(BF)
+            target = up_sent_ref if i < steps // 2 else up_own_ref
+            for b in range(blocks):
+                for q in range(2):
+                    first = b * size + (2 * (i % (steps // 2)) + q) * small
+                    target[first : first + small] = value[b * small : (b + 1) * small, q * half : (q + 1) * half]
+            if i == steps // 2 - 1:
+                leave(up_sent_ref, anys[3])
+        leave(up_own_ref, anys[4])
+    else:
+        lax.fori_loop(0, steps, backward, 0)
     grad_middle = total_ref[...]
     grad_mid = norm_grad(grad_middle, normed1, inv1, norm_g)
     grad_mid_ref[...] = grad_mid
     grad_attn = grad_mid.astype(BF)
     grad_attn_ref[...] = grad_attn
+    if packets:
+        for own, first_z, z_ref in ((False, n_down, sent_ref), (True, 0, z_own_ref)):
+            value = fwd_dot(context_t_ref[...], grad_attn_ref[:, lanes_of(own)]).astype(BF)
+            for b in range(blocks):
+                first = first_z + b * z_rows + first_rows
+                z_ref[first : first + small] = value[b * small : (b + 1) * small]
+            if own:
+                leave(z_own_ref, anys[2])
+            else:
+                leave(sent_ref.at[n_down:], anys[0].at[n_down:])
     grad_context_ref[...] = back_dot(grad_attn, out_w_ref[...]).astype(BF)
     sums_ref[0:1] = column(grad_attn.astype(F32))
     sums_ref[1:2] = column(grad_middle * normed1)
@@ -278,33 +362,48 @@
     sums_ref[4:5] = column(cot * normed2)
     sums_ref[5:6] = column(cot)
     sums_ref[6:8] = jnp.zeros((2, sums_ref.shape[1]), F32)
-
-
-def middle_part(tokens, prev, answers, context, cot, out_w, up_w, down_w, up_b, *biases):
+    for copy in copies:
+        copy.wait()
+
+
+def middle_part(packets, pos, tokens, prev, answers, context, cot, out_w, up_w, down_w, up_b, *biases):
     rows, width = tokens.shape
     hidden = up_w.shape[1]
-    vmem = pl.BlockSpec(memory_space=pltpu.VMEM)
+    half = width // 2
+    vmem, away = pl.BlockSpec(memory_space=pltpu.VMEM), pl.BlockSpec(memory_space=pl.ANY)
     shape = lambda n, t: jax.ShapeDtypeStruct((rows, n), t)
     turned = lambda n: jax.ShapeDtypeStruct((n, rows), BF)
+    inner = [turned(width), turned(width), turned(hidden), shape(width, BF), shape(hidden, BF), shape(width, BF)]
+    held = lambda shapes: [pltpu.VMEM(v.shape, v.dtype) for v in shapes]
+    outs = [
+        shape(width, BF), shape(width, BF), shape(width, F32), jax.ShapeDtypeStruct((8, width), F32),
+        jax.ShapeDtypeStruct((1, hidden), F32),
+    ]
+    scratch = [
+        pltpu.VMEM((rows, hidden), F32), pltpu.VMEM((rows, width), F32), pltpu.VMEM((rows, width), BF),
+        pltpu.VMEM(out_w.shape, BF), pltpu.VMEM(up_w.shape, BF), pltpu.VMEM(down_w.shape, BF),
+        pltpu.VMEM((1, hidden), F32), pltpu.SemaphoreType.DMA((1 + 2 * (hidden // width),)),
+    ]
+    specs = [vmem] * 5
+    if packets:
+        first_rows = 2 * width // 3
+        z_rows, down_rows = first_rows + width, hidden - first_rows
+        packed = [
+            jax.ShapeDtypeStruct((n, half), BF) for n in (down_rows + z_rows, down_rows, z_rows, hidden, hidden)
+        ]
+        scratch = held(inner) + scratch + held(packed) + [pltpu.SemaphoreType.DMA((6,))]
+        outs, specs = outs + packed, specs + [away] * 5
+    else:
+        outs, specs = outs + inner, specs + [vmem] * 6
     return pl.pallas_call(
-        middle_kernel,
-        in_specs=[vmem] * 5 + [pl.BlockSpec(memory_space=pl.ANY)] * 3 + [vmem] * 7,
-        out_specs=[vmem] * 11,
-        out_shape=[
-            shape(width, BF), turned(width), turned(width), turned(hidden), shape(width, BF),
-            shape(hidden, BF), shape(width, BF), shape(width, BF), shape(width, F32),
-            jax.ShapeDtypeStruct((8, width), F32), jax.ShapeDtypeStruct((1, hidden), F32),
-        ],
-        scratch_shapes=[
-            pltpu.VMEM((rows, hidden), F32), pltpu.VMEM((rows, width), F32), pltpu.VMEM((rows, width), BF),
-            pltpu.VMEM(out_w.shape, BF), pltpu.VMEM(up_w.shape, BF), pltpu.VMEM(down_w.shape, BF),
-            pltpu.VMEM((1, hidden), F32), pltpu.SemaphoreType.DMA((3,)),
-        ],
-        compiler_params=pltpu.CompilerParams(vmem_limit_bytes=56 * MIB),
-        cost_estimate=pl.CostEstimate(
-            flops=4 * rows * width * (2 * hidden + width), bytes_accessed=24 * MIB, transcendentals=2 * rows * hidden
-        ),
-    )(tokens, prev, answers, context, cot, out_w, up_w, down_w, up_b, *biases)
+        lambda *refs: middle_kernel(packets, *refs),
+        in_specs=[pl.BlockSpec(memory_space=pltpu.SMEM)] + [vmem] * 5 + [HBM] * 3 + [vmem] * 7,
+        out_specs=specs,
+        out_shape=outs,
+        scratch_shapes=scratch,
+        compiler_params=pltpu.CompilerParams(vmem_limit_bytes=60 * MIB),
+        cost_estimate=pl.CostEstimate(flops=100000000, bytes_accessed=MIB, transcendentals=0),
+    )(pos, tokens, prev, answers, context, cot, out_w, up_w, down_w, up_b, *biases)
 
 
 def attend_back_kernel(
@@ -350,39 +449,14 @@
             jax.ShapeDtypeStruct((width, n_keys), BF),
             jax.ShapeDtypeStruct((width, n_keys), BF),
         ],
-        compiler_params=pltpu.CompilerParams(vmem_limit_bytes=vmem_limit(n_keys, 20)),
-        cost_estimate=pl.CostEstimate(flops=100_000_000, bytes_accessed=1 * MIB, transcendentals=0),
+        compiler_params=pltpu.CompilerParams(vmem_limit_bytes=vmem_limit(n_keys, 60)),
+        cost_estimate=LONG,
     )(queries, keys, values, prob, context, grad_context, *after)
 
 
 def core_lanes(pos_ref, own, size):
     core = pos_ref[0] if own else 1 - pos_ref[0]
     return pl.ds(pl.multiple_of(core * size, 128), size)
-
-
-def down_values(own, pos_ref, act_t_ref, context_t_ref, grad_ffn_ref, grad_attn_ref, blocks, store):
-    half = grad_ffn_ref.shape[1] // 2
-    at = core_lanes(pos_ref, own, half)
-    grad_ffn = grad_ffn_ref[:, at]
-    size = act_t_ref.shape[0] // blocks
-    for b in range(blocks):
-        store(b, 0, fwd_dot(act_t_ref[b * size : (b + 1) * size], grad_ffn))
-    out = fwd_dot(context_t_ref[...], grad_attn_ref[:, at])
-    small = out.shape[0] // blocks
-    for b in range(blocks):
-        store(b, size, out[b * small : (b + 1) * small])
-
-
-def up_values(own, pos_ref, middle_t_ref, grad_pre_ref, blocks, store):
-    half = grad_pre_ref.shape[1] // 2
-    piece = middle_t_ref.shape[0] // 2
-    small = middle_t_ref.shape[0] // blocks
-    core = pos_ref[0] if own else 1 - pos_ref[0]
-    for p in range(half // piece):
-        at = pl.ds(pl.multiple_of(core * half + p * piece, 128), piece)
-        value = fwd_dot(middle_t_ref[...], grad_pre_ref[:, at])
-        for b in range(blocks):
-            store(b, p * small, value[b * small : (b + 1) * small])
 
 
 def qkv_values(own, pos_ref, x_t_ref, grad_q_ref, grad_k_ref, grad_v_ref, blocks, store):
@@ -415,70 +489,10 @@
     return jnp.where(bit == 0, first, second)
 
 
-def keep_down_kernel(
-    blocks, pos_ref, act_t_ref, context_t_ref, grad_ffn_ref, grad_attn_ref, got_ref,
-    kept_ref, sent_ref, z_kept_ref, z_sent_ref,
+def keep_qkv_kernel(
+    blocks, pos_ref, x_t_ref, grad_q_ref, grad_k_ref, grad_v_ref, got_ref, table_ref, vec_ref, *outs
 ):
-    small = context_t_ref.shape[0] // blocks
-    held = {}
-
-    def z_store(b, first, value):
-        y, low_z, high_z = b % 2, b // 2 % 2, b // 4
-        if low_z == 0:
-            held[b, first] = value
-        else:
-            rows = slice((high_z * 2 + y) * 2 * small + first, (high_z * 2 + y) * 2 * small + first + small)
-            pair = (held[b - 2, first], value)
-            z_kept_ref[rows] = pick(pos_ref[3], *pair)
-            z_sent_ref[rows] = pick(pos_ref[3], *pair[::-1])
-
-    def store(b, first, value):
-        value = (value + got_ref[b, first : first + value.shape[0]].astype(F32)).astype(BF)
-        if first == 0:
-            part = (value.shape[0] - small) // 2
-            low, high = value[small : small + part], value[small + part :]
-            rows = slice(b * part, (b + 1) * part)
-            kept_ref[rows] = pick(pos_ref[1], low, high)
-            sent_ref[rows] = pick(pos_ref[1], high, low)
-            z_store(b, 0, value[:small])
-        else:
-            z_store(b, small, value)
-
-    down_values(True, pos_ref, act_t_ref, context_t_ref, grad_ffn_ref, grad_attn_ref, blocks, store)
-
-
-def keep_up_kernel(blocks, pos_ref, middle_t_ref, grad_pre_ref, got_ref, *outs):
-    kept_ref, sent_ref = outs[:2]
-    size = grad_pre_ref.shape[1] // blocks
-    held = {}
-
-    def store(b, first, value):
-        rows = slice(first, first + value.shape[0])
-        value = (value + got_ref[b, rows].astype(F32)).astype(BF)
-        if b % 2 == 0:
-            held[0] = value
-        else:
-            rows = slice(b // 2 * size + first, b // 2 * size + first + value.shape[0])
-            kept_ref[rows] = pick(pos_ref[2], held[0], value)
-            sent_ref[rows] = pick(pos_ref[2], value, held[0])
-
-    up_values(True, pos_ref, middle_t_ref, grad_pre_ref, blocks, store)
-
-
-def pack(value):
-    high = value.astype(BF)
-    return jnp.concatenate([high, (value - high.astype(F32)).astype(BF)], axis=0)
-
-
-def unpack(value):
-    half = value.shape[0] // 2
-    return value[:half].astype(F32) + value[half:].astype(F32)
-
-
-def keep_qkv_kernel(
-    blocks, pos_ref, x_t_ref, grad_q_ref, grad_k_ref, grad_v_ref, got_ref, table_ref, vec_ref, vec_got_ref, *outs
-):
-    first_kept_ref, first_sent_ref, kept_ref, sent_ref, vec_out_ref = outs
+    first_kept_ref, first_sent_ref, kept_ref, sent_ref = outs
     small = x_t_ref.shape[0] // blocks
     planes = blocks // 2
     held = {}
@@ -497,9 +511,7 @@
             sent_ref[rows] = pick(pos_ref[2], value, held[b - 1, first])
 
     qkv_values(True, pos_ref, x_t_ref, grad_q_ref, grad_k_ref, grad_v_ref, blocks, store)
-    vec = vec_ref[...] + unpack(vec_got_ref[...])
-    vec_out_ref[...] = vec
-    first_sent_ref[blocks * small :] = pack(vec)
+    first_sent_ref[blocks * small :] = vec_ref[...].astype(BF)
     sent_ref[planes * small :] = table_ref[...]
 
 
@@ -507,7 +519,7 @@
     blocks, grad_q_ref, grad_k_ref, grad_v_ref, query_w_ref, key_w_ref, value_w_ref, grad_mid_ref, prev_ref,
     table_prev_ref, sums_ref, up_sum_ref, *refs
 ):
-    table_kept_ref, table_sent_ref, grad_ref, vec_ref, packed_ref = refs[-5:]
+    table_kept_ref, table_sent_ref, grad_ref, vec_ref = refs[-4:]
     tab = TAB_MAX
     n_table = blocks * tab
     rows, width = grad_q_ref.shape
@@ -549,7 +561,6 @@
     for i, line in enumerate(lines):
         for side in range(2):
             vec_ref[side * 16 + i : side * 16 + i + 1] = line[:, side * half : (side + 1) * half]
-    packed_ref[...] = pack(vec_ref[...])
 
 
 def input_grads(blocks, grad_q, grad_k, grad_v, query_w, key_w, value_w, grad_mid, prev, table_prev, sums, up_sum, after):
@@ -560,16 +571,15 @@
     return pl.pallas_call(
         lambda *refs: inputs_kernel(blocks, *refs),
         in_specs=[vmem] * len(args) + [pl.BlockSpec(memory_space=pl.ANY)] * len(after),
-        out_specs=[vmem] * 5,
+        out_specs=[vmem] * 4,
         out_shape=[
             jax.ShapeDtypeStruct((n_half, width // 2), BF),
             jax.ShapeDtypeStruct((n_half, width // 2), BF),
             jax.ShapeDtypeStruct((rows, width), F32),
             jax.ShapeDtypeStruct((32, width // 2), F32),
-            jax.ShapeDtypeStruct((64, width // 2), BF),
         ],
         compiler_params=pltpu.CompilerParams(vmem_limit_bytes=(20 if blocks <= 8 else 56) * MIB),
-        cost_estimate=pl.CostEstimate(flops=100_000_000, bytes_accessed=1 * MIB, transcendentals=0),
+        cost_estimate=LONG,
     )(*args, *after)
 
 
@@ -577,34 +587,42 @@
     width = items[0][1].shape[1]
     gots, shapes, heights, places = [], [], {}, []
     for kind, kept, got, first, outer, inner, bit, message in items:
-        if not any(got is g for g in gots):
+        if got is not None and not any(got is g for g in gots):
             gots.append(got)
         rows = kept.shape[0] if kind != "part" else outer * inner
-        shapes.append(jax.ShapeDtypeStruct((rows, width), kept.dtype))
+        if kind != "copy":
+            shapes.append(jax.ShapeDtypeStruct((rows, width), kept.dtype))
         if message is not None:
             places.append(heights.get(message, 0))
-            heights[message] = places[-1] + (2 * rows if kind == "vec" else rows)
+            heights[message] = places[-1] + rows
         else:
             places.append(None)
     sizes = [heights[m] for m in sorted(heights)]
     shapes += [jax.ShapeDtypeStruct((n, width), BF) for n in sizes]
-    which = [next(i for i, g in enumerate(gots) if g is item[2]) for item in items]
+    which = [next((i for i, g in enumerate(gots) if g is item[2]), None) for item in items]
+    n_outs = sum(item[0] != "copy" for item in items)
 
     def body(pos_ref, *refs):
         kept_refs, refs = refs[: len(items)], refs[len(items) :]
         got_refs, refs = refs[: len(gots)], refs[len(gots) + len(after) :]
-        out_refs, sent_refs = refs[: len(items)], refs[len(items) :]
+        out_refs, sent_refs = list(refs[:n_outs]), refs[n_outs:]
         for i, (kind, _, _, first, outer, inner, bit, message) in enumerate(items):
-            kept_ref, got_ref, out_ref = kept_refs[i], got_refs[which[i]], out_refs[i]
+            kept_ref = kept_refs[i]
             n = kept_ref.shape[0]
+            if kind == "copy":
+                sent_refs[message][places[i] : places[i] + n] = kept_ref[...]
+                continue
+            got_ref, out_ref = got_refs[which[i]], out_refs.pop(0)
             if kind == "vec":
-                total = kept_ref[...] + unpack(got_ref[first : first + 2 * n])
+                total = kept_ref[...] + got_ref[first : first + n].astype(F32)
                 out_ref[...] = total
                 if message is not None:
-                    sent_refs[message][places[i] : places[i] + 2 * n] = pack(total)
+                    sent_refs[message][places[i] : places[i] + n] = total.astype(BF)
             elif kind == "sum":
                 total = kept_ref[...].astype(F32) + got_ref[first : first + n].astype(F32)
                 out_ref[...] = total.astype(BF)
+                if message is not None:
+                    sent_refs[message][places[i] : places[i] + n] = total.astype(BF)
             else:
                 for o in range(outer):
                     halves = []
@@ -629,12 +647,12 @@
         out_specs=[vmem] * len(shapes),
         out_shape=shapes,
         compiler_params=pltpu.CompilerParams(vmem_limit_bytes=16 * MIB),
-        cost_estimate=pl.CostEstimate(flops=1_000_000, bytes_accessed=1 * MIB, transcendentals=0),
+        cost_estimate=LONG,
     )(pos, *[item[1] for item in items], *gots, *after)
-    return results[: len(items)], results[len(items) :]
-
-
-def packet_call(kernel, shapes, pos, args, after=(), scratch=(), wide=()):
+    return results[:n_outs], results[n_outs:]
+
+
+def packet_call(kernel, shapes, pos, args, after=(), scratch=(), wide=(), cost=LONG):
     smem, vmem = pl.BlockSpec(memory_space=pltpu.SMEM), pl.BlockSpec(memory_space=pltpu.VMEM)
     outs = [jax.ShapeDtypeStruct(shape, BF) for shape in shapes]
     outs += [jax.ShapeDtypeStruct(shape, F32) for shape in wide]
@@ -650,7 +668,7 @@
         out_shape=outs,
         scratch_shapes=list(scratch),
         compiler_params=pltpu.CompilerParams(vmem_limit_bytes=20 * MIB),
-        cost_estimate=pl.CostEstimate(flops=100_000_000, bytes_accessed=1 * MIB, transcendentals=0),
+        cost_estimate=cost,
     )(pos, *args, *after)
 
 
@@ -691,63 +709,56 @@
     queries, own_keys, own_values, own_bias, value_row = own_part(
         layer_input, query_weight, key_weight, value_weight, query_bias, value_bias, seg_ids, turn_ids
     )
+    views = [(i, 0) for i in range(blocks)]
     keys, values, prob, context, x_t, table_prev = attend(
-        slots, layer_input, key_weight, value_weight, value_row, queries, own_keys, own_values, own_bias
+        slots, views, layer_input, key_weight, value_weight, value_row, queries, own_keys, own_values, own_bias
     )
-    (
-        mixed, context_t, middle_t, act_t, grad_ffn, grad_pre, grad_attn, grad_context, grad_mid_sum,
-        sums, up_sum,
-    ) = middle_part(
-        tokens, prev_ids, answer_table, context, cotangent, out_weight, up_weight, down_weight, up_bias,
+    packets = blocks if blocks == 8 and n_out % 32 == 0 else 0
+    mixed, grad_context, grad_mid_sum, sums, up_sum, *made = middle_part(
+        packets, pos, tokens, prev_ids, answer_table, context, cotangent, out_weight, up_weight, down_weight, up_bias,
         out_bias, norm_gain, norm_shift, down_bias, final_gain, final_shift,
     )
-    down_args = (act_t, context_t, grad_ffn, grad_attn)
-    up_args = (middle_t, grad_pre)
-    part = (ff_out - n_out) // 2
+    first_rows = 2 * n_out // 3
+    part, z_rows = (ff_out - first_rows) // 2, n_out + first_rows
     back_args = (queries, keys, values, prob, context, grad_context)
     input_args = (query_weight, key_weight, value_weight, grad_mid_sum, prev_ids, table_prev, sums, up_sum)
 
-    if blocks == 8 and n_out % 32 == 0:
+    if packets:
         flat = lambda rows: (rows, half_width)
-        (sent,) = packet_call(
-            lambda *refs: send_kernel(down_values, 4, blocks, *refs),
-            [(blocks, ff_out + n_out, half_width)], pos, down_args,
-        )
-        down_got = swap_grp(sent, 1)
-        (sent,) = packet_call(
-            lambda *refs: send_kernel(up_values, 2, blocks, *refs),
-            [(blocks, ff_out, half_width)], pos, up_args, after=(sent,),
-        )
-        up_got = swap_grp(sent, 1)
-        down_kept, down_sent, z_kept, z_sent = packet_call(
-            lambda *refs: keep_down_kernel(blocks, *refs),
-            [flat(blocks * part)] * 2 + [flat(8 * n_out)] * 2, pos, down_args + (down_got,), after=(sent,),
+        down_sent, down_kept, z_kept, up_sent, up_kept = made
+        down_got = swap_grp(down_sent, 1)
+        up_got = swap_grp(up_sent, 1)
+        grad_queries, grad_keys_t, grad_values_t = attend_back(*back_args, ())
+        (down_kept, z_kept), (down_sent, z_sent) = combine(
+            pos,
+            [
+                ("part", down_kept, down_got, 0, blocks, part, 1, 0),
+                ("part", z_kept, down_got, 2 * blocks * part, 2, 2 * z_rows, 3, 1),
+            ],
+            after=(grad_queries,),
         )
         down_got = swap_grp(down_sent, 2)
         z_got = swap_blk(z_sent, 2)
-        up_kept, up_sent = packet_call(
-            lambda *refs: keep_up_kernel(blocks, *refs),
-            [flat(planes * ff_out)] * 2, pos, up_args + (up_got,), after=(down_sent,),
+        (up_kept,), (up_sent,) = combine(
+            pos, [("part", up_kept, up_got, 0, planes, ff_out, 2, 0)], after=(down_sent,)
         )
         up_got = swap_blk(up_sent, 1)
-        grad_queries, grad_keys_t, grad_values_t = attend_back(*back_args, (down_sent, up_sent, z_sent))
         qkv_args = (x_t, grad_queries, grad_keys_t, grad_values_t)
         (qkv_sent,) = packet_call(
             lambda *refs: send_kernel(qkv_values, 4, blocks, *refs),
-            [(blocks, 3 * n_out, half_width)], pos, qkv_args,
+            [(blocks, 3 * n_out, half_width)], pos, qkv_args, after=(up_sent,),
         )
         qkv_got = swap_grp(qkv_sent, 1)
-        table_kept, table_sent, grad_input_local, vectors, packed = input_grads(
+        table_kept, table_sent, grad_input_local, vectors = input_grads(
             blocks, grad_queries, grad_keys_t, grad_values_t, *input_args, (qkv_sent,)
         )
-        vec_got = swap_grp(packed, 1)
-        (z_kept,), (z_sent,) = combine(pos, [("part", z_kept, z_got, 0, 1, 4 * n_out, 4, 0)], after=(table_sent,))
+        (z_kept,), (z_sent,) = combine(pos, [("part", z_kept, z_got, 0, 1, 2 * z_rows, 4, 0)], after=(table_sent,))
         z_got = swap_blk(z_sent, 4)
         n_first, n_value, n_rows = blocks * n_out, planes * n_out, blocks * tab
-        first_kept, first_sent, value_kept, value_sent, vectors = packet_call(
+        first_kept, first_sent, value_kept, value_sent = packet_call(
             lambda *refs: keep_qkv_kernel(blocks, *refs),
-            [flat(n_first), flat(n_first + 64), flat(n_value), flat(n_value + n_rows)],
-            pos, qkv_args + (qkv_got, table_sent, vectors, vec_got), wide=[flat(32)], after=(z_sent,),
+            [flat(n_first), flat(n_first + 32), flat(n_value), flat(n_value + n_rows)],
+            pos, qkv_args + (qkv_got, table_sent, vectors), after=(z_sent,),
         )
         first_got = swap_grp(first_sent, 2)
         value_got = swap_blk(value_sent, 1)
@@ -759,60 +770,56 @@
             pos, [("part", up_kept, up_got, 0, planes, ff_out // 2, 1, 0)], after=(down_sent,)
         )
         up_got = swap_grp(up_sent, 2)
-        (first_kept, vectors), (first_sent,) = combine(
+        (first_kept, vectors, z_kept), (first_sent,) = combine(
             pos,
             [
                 ("part", first_kept, first_got, 0, planes, n_out, 2, 0),
                 ("vec", vectors, first_got, n_first, 0, 0, None, 0),
+                ("part", z_kept, z_got, 0, 1, z_rows, 2, 0),
             ],
             after=(up_sent,),
         )
         first_got = swap_blk(first_sent, 1)
+        (down_kept,), (down_sent,) = combine(
+            pos, [("part", down_kept, down_got, 0, 1, 2 * part, 4, 0)], after=(first_sent,)
+        )
+        down_got = swap_blk(down_sent, 4)
         (value_kept, table_kept), (value_sent, table_sent) = combine(
             pos,
             [
                 ("part", value_kept, value_got, 0, planes, n_out // 2, 1, 0),
                 ("part", table_kept, value_got, n_value, 2, 2 * tab, None, 1),
             ],
-            after=(first_sent,),
+            after=(down_sent,),
         )
         value_got = swap_grp(value_sent, 2)
         table_got = swap_blk(table_sent, 2)
-        (down_kept, z_kept), (down_sent,) = combine(
+        (down_kept, up_kept), (down_sent, up_sent) = combine(
             pos,
             [
-                ("part", down_kept, down_got, 0, 2, part, 2, 0),
-                ("part", z_kept, z_got, 0, 1, 2 * n_out, 2, 0),
+                ("part", down_kept, down_got, 0, 1, part, 2, 0),
+                ("part", up_kept, up_got, 0, 2, ff_out // 2, 3, 1),
             ],
             after=(value_sent,),
         )
         down_got = swap_blk(down_sent, 1)
-        (up_kept,), (up_sent,) = combine(
-            pos, [("part", up_kept, up_got, 0, 2, ff_out // 2, 3, 0)], after=(down_sent,)
-        )
         up_got = swap_blk(up_sent, 2)
-        (first_kept, value_kept, vectors), (first_sent,) = combine(
+        (first_kept, value_kept, vectors, z_kept), (first_sent, z_sent) = combine(
             pos,
             [
                 ("part", first_kept, first_got, 0, 2, n_out, 3, 0),
                 ("part", value_kept, value_got, 0, 2, n_out // 2, 3, 0),
                 ("vec", vectors, first_got, n_value, 0, 0, None, 0),
+                ("part", z_kept, first_got, n_value + 32, 1, z_rows // 2, 1, 1),
             ],
             after=(up_sent,),
         )
         first_got = swap_blk(first_sent, 2)
-        n_down = 2 * part
-        (down_kept, z_kept, up_kept), (down_sent, z_sent) = combine(
-            pos,
-            [
-                ("part", down_kept, down_got, 0, 1, part, 4, 0),
-                ("part", z_kept, down_got, n_down, 1, n_out, 1, 1),
-                ("part", up_kept, up_got, 0, 1, ff_out // 2, 4, 0),
-            ],
-            after=(first_sent,),
-        )
-        down_got = swap_blk(down_sent, 4)
         z_got = swap_grp(z_sent, 2)
+        (up_kept,), (up_sent,) = combine(
+            pos, [("part", up_kept, up_got, 0, 1, ff_out // 2, 4, 0)], after=(first_sent,)
+        )
+        up_got = swap_blk(up_sent, 4)
         (first_kept, value_kept, table_kept, vectors), (first_sent,) = combine(
             pos,
             [
@@ -821,17 +828,20 @@
                 ("part", table_kept, table_got, 0, 1, 2 * tab, None, 0),
                 ("vec", vectors, first_got, 3 * n_out, 0, 0, None, 0),
             ],
-            after=(down_sent,),
+            after=(up_sent,),
         )
         first_got = swap_blk(first_sent, 4)
-        (down_part, up_part, z_part), _ = combine(
+        early, (early_sent,) = combine(
             pos,
             [
-                ("sum", down_kept, down_got, 0, 0, 0, None, None),
-                ("sum", up_kept, down_got, part, 0, 0, None, None),
-                ("sum", z_kept, z_got, 0, 0, 0, None, None),
+                ("sum", down_kept, down_got, 0, 0, 0, None, 0),
+                ("sum", z_kept, z_got, 0, 0, 0, None, 0),
             ],
             after=(first_sent,),
+        )
+        early_got = swap_grp(early_sent, 2)
+        (up_part,), _ = combine(
+            pos, [("sum", up_kept, up_got, 0, 0, 0, None, None)], after=(early_sent,)
         )
         n_small = n_out + n_out // 2
         (first_part, value_part, table_part, vectors), _ = combine(
@@ -842,28 +852,32 @@
                 ("sum", table_kept, first_got, n_small, 0, 0, None, None),
                 ("vec", vectors, first_got, n_small + 2 * tab, 0, 0, None, None),
             ],
-            after=(down_part,),
-        )
-
-        def whole(value):
-            other = swap_grp(value, 2)
+            after=(up_part,),
+        )
+
+        def whole(value, other):
             return pick(x_bit, value, other), pick(x_bit, other, value)
 
-        low, high = whole(jnp.concatenate([down_part, up_part, z_part], axis=0))
-        at_up, at_z = part, part + ff_out // 2
-        big = jnp.concatenate(
-            [low[:at_up], high[:at_up], low[at_up:at_z], high[at_up:at_z], low[at_z:], high[at_z:]], axis=0
-        )
-        low, high = whole(jnp.concatenate([first_part, value_part], axis=0))
-        square = jnp.concatenate([low[:n_out], high[:n_out], low[n_out:], high[n_out:]], axis=0)
-        down_rows, up_rows, z_rows = big[: 2 * part], big[2 * at_up : 2 * at_z], big[2 * at_z :]
+        low, high = whole(early_sent, early_got)
+        early = jnp.concatenate([low[:part], high[:part], low[part:], high[part:]], axis=0)
+        up_rows = jnp.concatenate(whole(up_part, swap_grp(up_part, 2)), axis=0)
+        square = jnp.concatenate([first_part, value_part], axis=0)
+        near_core = swap_grp(jnp.concatenate([square, vectors.astype(BF)], axis=0), 1)
+        near, far = (square, swap_grp(square, 2)), (near_core[:n_small], swap_grp(square, 3))
+        vectors = vectors + f(near_core[n_small:])
+        sides = []
+        for value, other in (near, far):
+            low, high = pick(x_bit, value, other), pick(x_bit, other, value)
+            sides.append(jnp.concatenate([low[:n_out], high[:n_out], low[n_out:], high[n_out:]], axis=0))
+        square = (f(pick(core_bit, *sides)), f(pick(core_bit, *sides[::-1])))
         table_share = f(table_part)
     else:
+        context_t, middle_t, act_t, grad_ffn, grad_pre, grad_attn = made
         lanes = lambda value, index: lax.dynamic_slice_in_dim(value, index * (value.shape[1] // 2), value.shape[1] // 2, 1)
         rows_of = lambda value, index: lax.dynamic_slice_in_dim(value, index * (value.shape[0] // 2), value.shape[0] // 2, 0)
         blocked = lambda value: value.reshape(blocks, value.shape[0] // blocks, value.shape[1])
         grad_queries, grad_keys_t, grad_values_t = attend_back(*back_args, ())
-        table_kept, table_sent, grad_input_local, vectors, packed = input_grads(
+        table_kept, table_sent, grad_input_local, vectors = input_grads(
             blocks, grad_queries, grad_keys_t, grad_values_t, *input_args, ()
         )
 
@@ -888,34 +902,32 @@
         square = total[: 3 * n_out]
         up_rows = total[at : at + ff_out]
         down_all = total[at + ff_out :]
-        z_rows = jnp.concatenate([down_all[:n_out], total[3 * n_out : at]], axis=0)
-        down_rows = down_all[n_out:]
+        z_rows = jnp.concatenate([down_all[:first_rows], total[3 * n_out : at]], axis=0)
+        down_rows = down_all[first_rows:]
         table_rows = jnp.stack([blocked_half.reshape(planes, 2 * tab, half_width) for blocked_half in (table_kept, table_sent)], axis=1)
         table_rows = table_rows.reshape(blocks, 2 * tab, half_width)
         table_rows = jnp.take(table_rows, jnp.arange(blocks) ^ own, axis=0)
         table_share = f(lax.psum_scatter(table_rows, "blk", scatter_dimension=0, tiled=False))
         vectors = lax.psum(vectors, ("blk", "grp"))
-        big = jnp.concatenate([down_rows, up_rows, z_rows], axis=0)
+        early = jnp.concatenate([down_rows, z_rows], axis=0)
 
     def both_cores(value):
         other = swap_grp(value, 1)
         return f(pick(core_bit, value, other)), f(pick(core_bit, other, value))
 
-    sides = both_cores(big)
-    n_down = ff_out - n_out
-    at_z = n_down + ff_out
-    out_up = jnp.concatenate(
-        [side[i : i + n_out] for side in sides for i in range(n_down, at_z, n_out)], axis=1
-    )
+    sides = both_cores(up_rows)
+    out_up = jnp.concatenate([side[i : i + n_out] for side in sides for i in range(0, ff_out, n_out)], axis=1)
+    sides = both_cores(early)
+    at_z = ff_out - first_rows
     out_down = jnp.concatenate(
         [
-            jnp.concatenate([side[at_z : at_z + n_out] for side in sides], axis=1),
-            jnp.concatenate([side[:n_down] for side in sides], axis=1),
+            jnp.concatenate([side[at_z : at_z + first_rows] for side in sides], axis=1),
+            jnp.concatenate([side[:at_z] for side in sides], axis=1),
         ],
         axis=0,
     )
-    out_out = jnp.concatenate([side[at_z + n_out :] for side in sides], axis=1)
-    square = jnp.concatenate(both_cores(square), axis=1)
+    out_out = jnp.concatenate([side[at_z + first_rows :] for side in sides], axis=1)
+    square = jnp.concatenate(square if packets else both_cores(square), axis=1)
     table_share = jnp.concatenate([table_share[:tab], table_share[tab:]], axis=1)
     vectors = jnp.concatenate([vectors[:16], vectors[16:]], axis=1)
     mine = lax.dynamic_slice_in_dim(vectors[:10], own * n_out, n_out, 1)

time: 194 us -> 170 us (0.88)
  waiting for transfers between devices: 76.1 us -> 53.1 us
  local copies, waits for them, and re-layouts: 20.7 us -> 8.1 us
  Pallas kernels: 58.1 us -> 70.4 us
    ppermute x19 -> x20, waiting for transfers between devices: 57.4 us -> 37.9 us  [swap_blk(): return lax.ppermute(value, 'blk', [(i, i ^ mask) for i in range(blocks)])]
    unnamed x114 -> x58, local copies, waits for them, and re-layouts: 18.6 us -> 5.46 us
    pallas_call x12 -> x15, Pallas kernels: 8.78 us -> 17.6 us  [combine(): pl.pallas_call(body, in_specs=[pl.BlockSpec(memory_space=pltpu.SMEM)] + [...]
    pallas_call x4, Pallas kernels: 28.8 us -> 35.4 us  [the longest x1 18.2 us: middle_part(): pl.pallas_call(lambda *refs: middle_kernel(packets, *refs), in_specs=[pl....]
    pallas_call x6 -> x2, Pallas kernels: 10.9 us -> 5.17 us  [packet_call(): pl.pallas_call(body, in_specs=[smem] + [vmem] * len(args) + [pl.BlockSpec...]
    ppermute x13 -> x15, waiting for transfers between devices: 18.7 us -> 15.1 us  [swap_grp(): return lax.ppermute(value, 'grp', [(i, i ^ mask) for i in range(grps)])]
    ppermute x19 -> x20, starting transfers between devices: 25.7 us -> 22.8 us  [swap_blk(): return lax.ppermute(value, 'blk', [(i, i ^ mask) for i in range(blocks)])]
    pallas_call x1, Pallas kernels: 6.17 us -> 8.43 us  [attend_back(): pl.pallas_call(attend_back_kernel, grid=(width // group,), in_specs=[lane...]
  transfers between devices with their start and end apart: 32 -> 35, of which waited for: 17 -> 18; matrix products, arithmetic and copies ran while one was open for 2% -> 3% of each run, Pallas kernels for 10% -> 23%
where the time goes in v4:
time: 170 us
  Pallas kernels  70.4 us (41%)
  waiting for transfers between devices  53.1 us (31%)
  starting transfers between devices  32.3 us (19%)
  local copies, waits for them, and re-layouts  8.1 us (5%)
  other arithmetic  4.4 us (3%)
    ppermute x20, waiting for transfers between devices, swap_blk(): return lax.ppermute(value, 'blk', [(i, i ^ mask) for i in range(blocks)])  37.9 us
    ppermute x20, starting transfers between devices, swap_blk(): return lax.ppermute(value, 'blk', [(i, i ^ mask) for i in range(blocks)])  22.8 us
    pallas_call x1, Pallas kernels, middle_part(): pl.pallas_call(lambda *refs: middle_kernel(packets, *refs), in_specs=[pl....  18.2 us
    pallas_call x15, Pallas kernels, combine(): pl.pallas_call(body, in_specs=[pl.BlockSpec(memory_space=pltpu.SMEM)] + [...  17.6 us
    ppermute x15, waiting for transfers between devices, swap_grp(): return lax.ppermute(value, 'grp', [(i, i ^ mask) for i in range(grps)])  15.1 us
    pallas_call x1, Pallas kernels, attend(): pl.pallas_call(lambda *refs: attend_kernel(views, *refs), grid=(width //...  10.3 us
    ppermute x15, starting transfers between devices, swap_grp(): return lax.ppermute(value, 'grp', [(i, i ^ mask) for i in range(grps)])  9.41 us
    pallas_call x1, Pallas kernels, attend_back(): pl.pallas_call(attend_back_kernel, grid=(width // group,), in_specs=[lane...  8.43 us
  transfers between devices with their start and end apart: 35, of which 18 were waited for; matrix products, arithmetic and copies ran while one was open for 3% of the time, Pallas kernels for 23%

profile of v4, /device:TPU:0, one launch (start us, length us, event | category | flops | bytes accessed | tf_op | source)
XLA Modules:
  0.0 169.7 jit_solution(7376811715088065068)
XLA Ops:
  0.7 2.0 %shard_map.340 = (bf16[80,768]{1,0:T(8,128)(2,1)}, bf16[256,768]{1,0:T(8,128)(2,1)}) custom-call(bf16[256,768]{1,0:T(8,128)(2,1)} %refs_1_.3, s32[256]{0:T(256)} %seg_any.3, s32[256]{0:T(256)} %refs_7_.3, bf16[2,768]{1,0:T(2,128)(2,1)} %refs_3_.2), custom_call_target="tpu_custom_call" | custom-call | tf_op jit(solution)/shard_map/pallas_call | solution.py:97
  2.7 3.1 %collective-permute-start.1 = (bf16[80,768]{1,0:T(8,128)(2,1)}, bf16[80,768]{1,0:T(8,128)(2,1)S(1)}, u32[]{:S(2)}, u32[]{:S(2)}) collective-permute-start(bf16[80,768]{1,0:T(8,128)(2,1)} %get-tuple-element.114.refs_8_), channel_id=1, source_target_pairs={{0,2},{1,3},{2,0},{3,1},{4,6},{5,7},{6,4},{7,5},{8,10},{9,11},{10,... | collective-permute-start | bytes 368648 | tf_op jit(solution)/shard_map/ppermute | solution.py:700
  5.8 2.6 %collective-permute-start.3 = (bf16[80,768]{1,0:T(8,128)(2,1)}, bf16[80,768]{1,0:T(8,128)(2,1)S(1)}, u32[]{:S(2)}, u32[]{:S(2)}) collective-permute-start(bf16[80,768]{1,0:T(8,128)(2,1)} %get-tuple-element.114.refs_8_), channel_id=1, source_target_pairs={{0,4},{1,5},{2,6},{3,7},{4,0},{5,1},{6,2},{7,3},{8,12},{9,13},{10,... | collective-permute-start | bytes 368648 | tf_op jit(solution)/shard_map/ppermute | solution.py:700
  8.4 1.7 %collective-permute-start = (bf16[80,768]{1,0:T(8,128)(2,1)}, bf16[80,768]{1,0:T(8,128)(2,1)S(1)}, u32[]{:S(2)}, u32[]{:S(2)}) collective-permute-start(bf16[80,768]{1,0:T(8,128)(2,1)} %get-tuple-element.114.refs_8_), channel_id=1, source_target_pairs={{0,1},{1,0},{2,3},{3,2},{4,5},{5,4},{6,7},{7,6},{8,9},{9,8},{10,11... | collective-permute-start | bytes 368648 | tf_op jit(solution)/shard_map/ppermute | solution.py:700
  10.7 1.7 %collective-permute-start.2 = (bf16[80,768]{1,0:T(8,128)(2,1)S(1)}, bf16[80,768]{1,0:T(8,128)(2,1)S(1)}, u32[]{:S(2)}, u32[]{:S(2)}) collective-permute-start(bf16[80,768]{1,0:T(8,128)(2,1)S(1)} %collective-permute-done.1.refs_10_), channel_id=1, source_target_pairs={{0,1},{1,0},{2,3},{3,2},{4,5},{5,4},{6,7},{7,6},{8,9},{9,8},{10,11... | collective-permute-start | bytes 368648 | tf_op jit(solution)/shard_map/ppermute | solution.py:700
  12.4 5.9 %collective-permute-done.3.refs_12_ = bf16[80,768]{1,0:T(8,128)(2,1)S(1)} collective-permute-done((bf16[80,768]{1,0:T(8,128)(2,1)}, bf16[80,768]{1,0:T(8,128)(2,1)S(1)}, u32[]{:S(2)}, u32[]{:S(2)}) %collective-permute-start.3) | collective-permute-done | bytes 122912 | tf_op jit(solution)/shard_map/ppermute | solution.py:700
  18.3 1.5 collective-permute-start.4
  21.0 4.9 %shard_map.341 = (bf16[256,768]{1,0:T(8,128)(2,1)}, bf16[256,768]{1,0:T(8,128)(2,1)}, bf16[256,768]{1,0:T(8,128)(2,1)}, f32[256,256]{1,0:T(8,128)}, f32[1,768]{1,0:T(1,128)}) custom-call(bf16[256,768]{1,0:T(8,128)(2,1)} %get-tuple-element.108.input_ref.refs_0_, bf16[768,768]{1,0:T(8,128)(2,1)} %refs_3_.3, bf16[768,768]{1,0:T(8,128)(2,1)} %refs_4_.1, ...), custom_call_target="tpu_custom_call" | custom-call | flops 100000000 | bytes 1048576 | tf_op jit(solution)/shard_map/pallas_call | solution.py:133
  26.7 10.3 %shard_map.342 = (bf16[768,768]{1,0:T(8,128)(2,1)}, bf16[768,768]{1,0:T(8,128)(2,1)}, bf16[12,256,768]{2,1,0:T(8,128)(2,1)}, f32[256,768]{1,0:T(8,128)}, bf16[768,768]{1,0:T(8,128)(2,1)}, /*index=5*/f32[8,512]{1,0:T(8,128)}) custom-call(bf16[256,768]{1,0:T(8,128)(2,1)} %get-tuple-element.108.input_ref.refs_0_, bf16[768,768]{1,0:T(8,128)(2,1)} %refs_4_.1, ...), custom_call_target="tpu_custom_call" | custom-call | flops 100000000 | bytes 1048576 | tf_op jit(solution)/shard_map/pallas_call | solution.py:206
  37.0 18.2 %shard_map.343 = (bf16[256,768]{1,0:T(8,128)(2,1)}, bf16[256,768]{1,0:T(8,128)(2,1)}, f32[256,768]{1,0:T(8,128)}, f32[8,768]{1,0:T(8,128)}, f32[1,3072]{1,0:T(1,...) custom-call(s32[5]{0:T(128)} %stack.23.refs_0_.pos_ref, ...), custom_call_target="tpu_custom_call" | custom-call | flops 100000000 | bytes 1048576 | tf_op jit(solution)/shard_map/pallas_call | solution.py:398
  55.8 8.4 %shard_map.344 = (bf16[256,768]{1,0:T(8,128)(2,1)}, bf16[768,768]{1,0:T(8,128)(2,1)}, bf16[768,768]{1,0:T(8,128)(2,1)}) custom-call(bf16[256,768]{1,0:T(8,128)(2,1)} %get-tuple-element.110.refs_4_.q_ref, bf16[768,768]{1,0:T(8,128)(2,1)} %get-tuple-element.117.keys_ref, bf16[768,768]{1,0:T(8,128)(2,1)} %get-tuple-element.118.values_ref, ...), custom_call_target="tpu_custom_call" | custom-call | flops 40000000000 | bytes 1048576 | tf_op jit(solution)/shard_map/pallas_call | solution.py:438
  64.2 1.5 copy-done.6
  65.8 1.2 copy-done.8
  67.0 1.0 copy-done.15
  68.0 2.1 %shard_map.345 = (bf16[1280,384]{1,0:T(8,128)(2,1)S(1)}, bf16[640,384]{1,0:T(8,128)(2,1)S(1)}, bf16[1280,384]{1,0:T(8,128)(2,1)}, bf16[640,384]{1,0:T(8,128)(2,1)S(1)}) custom-call(s32[5]{0:T(128)S(1)} %copy-done.4, bf16[2560,384]{1,0:T(8,128)(2,1)S(1)} %copy-done.6, bf16[1280,384]{1,0:T(8,128)(2,1)S(1)} %copy-done.8, ...), custom_call_target="tpu_custom_call" | custom-call | flops 40000000000 | bytes 1048576 | tf_op jit(solution)/shard_map/pallas_call | solution.py:642
  70.1 1.4 collective-permute-start.10
  71.5 1.5 collective-permute-start.14
  73.0 3.5 %shard_map.346 = (bf16[1536,384]{1,0:T(8,128)(2,1)S(1)}, bf16[1536,384]{1,0:T(8,128)(2,1)}) custom-call(s32[5]{0:T(128)S(1)} %copy-done.4, bf16[3072,384]{1,0:T(8,128)(2,1)S(1)} %copy-done.5, bf16[3072,384]{1,0:T(8,128)(2,1)} %collective-permute-done.7.refs_1_, bf16[1280,384]{1,0:T(8,128)(2,1)} %get-tuple-element.134.refs_2_), custom_call_target="tpu_custom_call" | custom-call | flops 40000000000 | bytes 1048576 | tf_op jit(solution)/shard_map/pallas_call | solution.py:642
  77.1 2.1 %shard_map.347.refs_11_ = bf16[8,288,384]{2,1,0:T(8,128)(2,1)S(1)} custom-call(s32[5]{0:T(128)S(1)} %copy-done.4, bf16[768,768]{1,0:T(8,128)(2,1)S(1)} %copy-done.7, bf16[256,768]{1,0:T(8,128)(2,1)S(1)} %copy-done.16, bf16[768,768]{1,0:T(8,128)(2,1)S(1)} %copy-done.13, bf16[768,768]{1,0:T(8,128)(2,1)S(1)} %copy-done.14, ...), custom_call_target="tpu_custom_call" | custom-call | flops 40000000000 | bytes 1048576 | tf_op jit(solution)/shard_map/pallas_call | solution.py:664
  79.4 3.8 %shard_map.348 = (bf16[512,384]{1,0:T(8,128)(2,1)S(1)}, bf16[512,384]{1,0:T(8,128)(2,1)S(1)}, f32[256,768]{1,0:T(8,128)}, f32[32,384]{1,0:T(8,128)S(1)}) custom-call(bf16[256,768]{1,0:T(8,128)(2,1)S(1)} %copy-done.16, bf16[768,768]{1,0:T(8,128)(2,1)S(1)} %copy-done.13, bf16[768,768]{1,0:T(8,128)(2,1)S(1)} %copy-done.14, bf16[768,768]{1,0:T(8,128)(2,1)S(1)} %copy-done.2, ...), custom_call_target="tpu_custom_call" | custom-call | flops 40000000000 | bytes 1048576 | tf_op jit(solution)/shard_map/pallas_call | solution.py:571
  84.1 2.5 %collective-permute-start.12 = (bf16[320,384]{1,0:T(8,128)(2,1)S(1)}, bf16[320,384]{1,0:T(8,128)(2,1)S(1)}, u32[]{:S(2)}, u32[]{:S(2)}) collective-permute-start(bf16[320,384]{1,0:T(8,128)(2,1)S(1)} %get-tuple-element.141.refs_8_), channel_id=1, source_target_pairs={{0,4},{1,5},{2,6},{3,7},{4,0},{5,1},{6,2},{7,3},{8,12},{9,13},{10,... | collective-permute-start | bytes 737288 | tf_op jit(solution)/shard_map/ppermute | solution.py:700
  86.5 3.0 %shard_map.350 = (bf16[768,384]{1,0:T(8,128)(2,1)S(1)}, bf16[800,384]{1,0:T(8,128)(2,1)S(1)}, bf16[384,384]{1,0:T(8,128)(2,1)S(1)}, bf16[896,384]{1,0:T(8,128)(2,1)}) custom-call(s32[5]{0:T(128)S(1)} %copy-done.4, bf16[768,768]{1,0:T(8,128)(2,1)S(1)} %copy-done.7, bf16[256,768]{1,0:T(8,128)(2,1)S(1)} %copy-done.16, bf16[768,768]{1,0:T(8,128)(2,1)S(1)} %copy-done.13, ...), custom_call_target="tpu_custom_call" | custom-call | flops 40000000000 | bytes 1048576 | tf_op jit(solution)/shard_map/pallas_call | solution.py:664
  89.6 1.5 collective-permute-start.11
  91.5 4.9 %collective-permute-done.14.refs_1_ = bf16[1280,384]{1,0:T(8,128)(2,1)} collective-permute-done((bf16[1280,384]{1,0:T(8,128)(2,1)}, bf16[1280,384]{1,0:T(8,128)(2,1)}, u32[]{:S(2)}, u32[]{:S(2)}) %collective-permute-start.14) | collective-permute-done | bytes 983072 | tf_op jit(solution)/shard_map/ppermute | solution.py:697
  96.4 1.5 shard_map.351
  98.7 7.0 %collective-permute-done.13.refs_1_ = bf16[1536,384]{1,0:T(8,128)(2,1)} collective-permute-done((bf16[1536,384]{1,0:T(8,128)(2,1)}, bf16[1536,384]{1,0:T(8,128)(2,1)}, u32[]{:S(2)}, u32[]{:S(2)}) %collective-permute-start.13) | collective-permute-done | bytes 1179680 | tf_op jit(solution)/shard_map/ppermute | solution.py:700
  105.7 1.7 shard_map.352
  108.0 1.4 collective-permute-done.11.refs_3_
  111.5 2.6 %collective-permute-start.19 = (bf16[320,384]{1,0:T(8,128)(2,1)S(1)}, bf16[320,384]{1,0:T(8,128)(2,1)S(1)}, u32[]{:S(2)}, u32[]{:S(2)}) collective-permute-start(bf16[320,384]{1,0:T(8,128)(2,1)S(1)} %get-tuple-element.155.refs_3_), channel_id=1, source_target_pairs={{0,4},{1,5},{2,6},{3,7},{4,0},{5,1},{6,2},{7,3},{8,12},{9,13},{10,... | collective-permute-start | bytes 737288 | tf_op jit(solution)/shard_map/ppermute | solution.py:700
  114.1 6.3 %collective-permute-done.15.refs_2_ = bf16[896,384]{1,0:T(8,128)(2,1)} collective-permute-done((bf16[896,384]{1,0:T(8,128)(2,1)}, bf16[896,384]{1,0:T(8,128)(2,1)}, u32[]{:S(2)}, u32[]{:S(2)}) %collective-permute-start.15) | collective-permute-done | bytes 688160 | tf_op jit(solution)/shard_map/ppermute | solution.py:700
  120.4 1.3 shard_map.355
  124.3 1.0 collective-permute-start.23
  125.9 1.0 collective-permute-done.18.refs_5_
  126.9 2.7 %collective-permute-done.17.refs_4_ = bf16[576,384]{1,0:T(8,128)(2,1)S(1)} collective-permute-done((bf16[576,384]{1,0:T(8,128)(2,1)S(1)}, bf16[576,384]{1,0:T(8,128)(2,1)S(1)}, u32[]{:S(2)}, u32[]{:S(2)}) %collective-permute-start.17) | collective-permute-done | bytes 442400 | tf_op jit(solution)/shard_map/ppermute | solution.py:700
  131.0 7.0 %collective-permute-done.23.refs_1_ = bf16[384,384]{1,0:T(8,128)(2,1)S(1)} collective-permute-done((bf16[384,384]{1,0:T(8,128)(2,1)S(1)}, bf16[384,384]{1,0:T(8,128)(2,1)S(1)}, u32[]{:S(2)}, u32[]{:S(2)}) %collective-permute-start.23) | collective-permute-done | bytes 294944 | tf_op jit(solution)/shard_map/ppermute | solution.py:700
  138.7 2.2 %collective-permute-done.21.refs_4_ = bf16[320,384]{1,0:T(8,128)(2,1)S(1)} collective-permute-done((bf16[320,384]{1,0:T(8,128)(2,1)S(1)}, bf16[320,384]{1,0:T(8,128)(2,1)S(1)}, u32[]{:S(2)}, u32[]{:S(2)}) %collective-permute-start.21) | collective-permute-done | bytes 245792 | tf_op jit(solution)/shard_map/ppermute | solution.py:700
  141.6 1.2 shard_map.360
  142.9 2.0 %collective-permute-done.25.refs_1_ = bf16[192,384]{1,0:T(8,128)(2,1)S(1)} collective-permute-done((bf16[192,384]{1,0:T(8,128)(2,1)S(1)}, bf16[192,384]{1,0:T(8,128)(2,1)S(1)}, u32[]{:S(2)}, u32[]{:S(2)}) %collective-permute-start.25) | collective-permute-done | bytes 147488 | tf_op jit(solution)/shard_map/ppermute | solution.py:700
  145.5 1.6 collective-permute-start.33
  147.6 3.1 %collective-permute-done.33 = bf16[192,384]{1,0:T(8,128)(2,1)S(1)} collective-permute-done((bf16[192,384]{1,0:T(8,128)(2,1)S(1)}, bf16[192,384]{1,0:T(8,128)(2,1)S(1)}, u32[]{:S(2)}, u32[]{:S(2)}) %collective-permute-start.33) | collective-permute-done | bytes 147488 | tf_op jit(solution)/shard_map/ppermute | solution.py:697
  150.8 1.8 %collective-permute-done.31 = bf16[240,384]{1,0:T(8,128)(2,1)S(1)} collective-permute-done((bf16[240,384]{1,0:T(8,128)(2,1)S(1)}, bf16[240,384]{1,0:T(8,128)(2,1)S(1)}, u32[]{:S(2)}, u32[]{:S(2)}) %collective-permute-start.31) | collective-permute-done | bytes 184352 | tf_op jit(solution)/shard_map/ppermute | solution.py:697
  152.9 3.6 %collective-permute-done.24.refs_4_ = bf16[304,384]{1,0:T(8,128)(2,1)S(1)} collective-permute-done((bf16[304,384]{1,0:T(8,128)(2,1)S(1)}, bf16[304,384]{1,0:T(8,128)(2,1)S(1)}, u32[]{:S(2)}, u32[]{:S(2)}) %collective-permute-start.24) | collective-permute-done | bytes 233504 | tf_op jit(solution)/shard_map/ppermute | solution.py:700
  157.1 1.6 collective-permute-start.29
  159.4 1.6 fusion
  161.1 1.1 collective-permute-done.29
  162.3 1.7 %collective-permute-done.30 = bf16[144,384]{1,0:T(8,128)(2,1)S(1)} collective-permute-done((bf16[144,384]{1,0:T(8,128)(2,1)S(1)}, bf16[144,384]{1,0:T(8,128)(2,1)S(1)}, u32[]{:S(2)}, u32[]{:S(2)}) %collective-permute-start.30) | collective-permute-done | bytes 110624 | tf_op jit(solution)/shard_map/ppermute | solution.py:697
  167.5 1.0 fusion.1
  168.6 1.1 maximum_maximum_fusion
  (149 shorter events, 20.5 us)
Async XLA Ops:
  2.7 8.0 %collective-permute-start.1 = (bf16[80,768]{1,0:T(8,128)(2,1)}, bf16[80,768]{1,0:T(8,128)(2,1)S(1)}, u32[]{:S(2)}, u32[]{:S(2)}) collective-permute-start(bf16[80,768]{1,0:T(8,128)(2,1)} %get-tuple-element.114.refs_8_), channel_id=1, source_target_pairs={{0,2},{1,3},{2,0},{3,1},{4,6},{5,7},{6,4},{7,5},{8,10},{9,11},{10,... | collective-permute-start | bytes 368648 | tf_op jit(solution)/shard_map/ppermute | solution.py:700
  5.8 12.5 %collective-permute-start.3 = (bf16[80,768]{1,0:T(8,128)(2,1)}, bf16[80,768]{1,0:T(8,128)(2,1)S(1)}, u32[]{:S(2)}, u32[]{:S(2)}) collective-permute-start(bf16[80,768]{1,0:T(8,128)(2,1)} %get-tuple-element.114.refs_8_), channel_id=1, source_target_pairs={{0,4},{1,5},{2,6},{3,7},{4,0},{5,1},{6,2},{7,3},{8,12},{9,13},{10,... | collective-permute-start | bytes 368648 | tf_op jit(solution)/shard_map/ppermute | solution.py:700
  8.4 11.5 %collective-permute-start.5 = (bf16[80,768]{1,0:T(8,128)(2,1)}, bf16[80,768]{1,0:T(8,128)(2,1)S(1)}, u32[]{:S(2)}, u32[]{:S(2)}) collective-permute-start(bf16[80,768]{1,0:T(8,128)(2,1)} %get-tuple-element.114.refs_8_), channel_id=1, source_target_pairs={{0,6},{1,7},{2,4},{3,5},{4,2},{5,3},{6,0},{7,1},{8,14},{9,15},{10,... | collective-permute-start | bytes 368648 | tf_op jit(solution)/shard_map/ppermute | solution.py:700
  8.4 17.5 %collective-permute-start = (bf16[80,768]{1,0:T(8,128)(2,1)}, bf16[80,768]{1,0:T(8,128)(2,1)S(1)}, u32[]{:S(2)}, u32[]{:S(2)}) collective-permute-start(bf16[80,768]{1,0:T(8,128)(2,1)} %get-tuple-element.114.refs_8_), channel_id=1, source_target_pairs={{0,1},{1,0},{2,3},{3,2},{4,5},{5,4},{6,7},{7,6},{8,9},{9,8},{10,11... | collective-permute-start | bytes 368648 | tf_op jit(solution)/shard_map/ppermute | solution.py:700
  10.7 15.2 %copy-start.17 = (bf16[80,768]{1,0:T(8,128)(2,1)}, bf16[80,768]{1,0:T(8,128)(2,1)S(1)}, u32[]{:S(2)}) copy-start(bf16[80,768]{1,0:T(8,128)(2,1)S(1)} %collective-permute-done.1.refs_10_) | copy-start | bytes 368644
  10.7 15.3 %collective-permute-start.2 = (bf16[80,768]{1,0:T(8,128)(2,1)S(1)}, bf16[80,768]{1,0:T(8,128)(2,1)S(1)}, u32[]{:S(2)}, u32[]{:S(2)}) collective-permute-start(bf16[80,768]{1,0:T(8,128)(2,1)S(1)} %collective-permute-done.1.refs_10_), channel_id=1, source_target_pairs={{0,1},{1,0},{2,3},{3,2},{4,5},{5,4},{6,7},{7,6},{8,9},{9,8},{10,11... | collective-permute-start | bytes 368648 | tf_op jit(solution)/shard_map/ppermute | solution.py:700
  18.3 7.6 %copy-start.18 = (bf16[80,768]{1,0:T(8,128)(2,1)}, bf16[80,768]{1,0:T(8,128)(2,1)S(1)}, u32[]{:S(2)}) copy-start(bf16[80,768]{1,0:T(8,128)(2,1)S(1)} %collective-permute-done.3.refs_12_) | copy-start | bytes 368644
  18.3 7.6 %collective-permute-start.4 = (bf16[80,768]{1,0:T(8,128)(2,1)S(1)}, bf16[80,768]{1,0:T(8,128)(2,1)S(1)}, u32[]{:S(2)}, u32[]{:S(2)}) collective-permute-start(bf16[80,768]{1,0:T(8,128)(2,1)S(1)} %collective-permute-done.3.refs_12_), channel_id=1, source_target_pairs={{0,1},{1,0},{2,3},{3,2},{4,5},{5,4},{6,7},{7,6},{8,9},{9,8},{10,11... | collective-permute-start | bytes 368648 | tf_op jit(solution)/shard_map/ppermute | solution.py:700
  19.8 6.1 %copy-start.19 = (bf16[80,768]{1,0:T(8,128)(2,1)}, bf16[80,768]{1,0:T(8,128)(2,1)S(1)}, u32[]{:S(2)}) copy-start(bf16[80,768]{1,0:T(8,128)(2,1)S(1)} %collective-permute-done.5.refs_14_) | copy-start | bytes 368644
  19.8 6.1 %collective-permute-start.6 = (bf16[80,768]{1,0:T(8,128)(2,1)S(1)}, bf16[80,768]{1,0:T(8,128)(2,1)S(1)}, u32[]{:S(2)}, u32[]{:S(2)}) collective-permute-start(bf16[80,768]{1,0:T(8,128)(2,1)S(1)} %collective-permute-done.5.refs_14_), channel_id=1, source_target_pairs={{0,1},{1,0},{2,3},{3,2},{4,5},{5,4},{6,7},{7,6},{8,9},{9,8},{10,11... | collective-permute-start | bytes 368648 | tf_op jit(solution)/shard_map/ppermute | solution.py:700
  55.2 9.0 %collective-permute-start.8 = (bf16[3840,384]{1,0:T(8,128)(2,1)}, bf16[3840,384]{1,0:T(8,128)(2,1)S(1)}, u32[]{:S(2)}, u32[]{:S(2)}) collective-permute-start(bf16[3840,384]{1,0:T(8,128)(2,1)} %get-tuple-element.133), channel_id=1, source_target_pairs={{0,8},{8,0},{16,24},{24,16},{1,9},{9,1},{17,25},{25,17},{2,10},{10... | collective-permute-start | bytes 8847368 | tf_op jit(solution)/shard_map/ppermute | solution.py:697
  55.3 17.7 %collective-permute-start.7 = (bf16[3072,384]{1,0:T(8,128)(2,1)}, bf16[3072,384]{1,0:T(8,128)(2,1)}, u32[]{:S(2)}, u32[]{:S(2)}) collective-permute-start(bf16[3072,384]{1,0:T(8,128)(2,1)} %get-tuple-element.130), channel_id=1, source_target_pairs={{0,8},{8,0},{16,24},{24,16},{1,9},{9,1},{17,25},{25,17},{2,10},{10... | collective-permute-start | bytes 7077896 | tf_op jit(solution)/shard_map/ppermute | solution.py:697
  55.7 8.5 %copy-start.4 = (s32[5]{0:T(128)S(1)}, s32[5]{0:T(128)}, u32[]{:S(2)}) copy-start(s32[5]{0:T(128)} %stack.23.refs_0_.pos_ref) | copy-start | bytes 64
  67.9 5.0 %copy-start.5 = (bf16[3072,384]{1,0:T(8,128)(2,1)S(1)}, bf16[3072,384]{1,0:T(8,128)(2,1)}, u32[]{:S(2)}) copy-start(bf16[3072,384]{1,0:T(8,128)(2,1)} %get-tuple-element.129.refs_0_) | copy-start | bytes 7077892
  70.1 13.3 %collective-permute-start.10 = (bf16[640,384]{1,0:T(8,128)(2,1)S(1)}, bf16[640,384]{1,0:T(8,128)(2,1)S(1)}, u32[]{:S(2)}, u32[]{:S(2)}) collective-permute-start(bf16[640,384]{1,0:T(8,128)(2,1)S(1)} %get-tuple-element.140), channel_id=1, source_target_pairs={{0,2},{1,3},{2,0},{3,1},{4,6},{5,7},{6,4},{7,5},{8,10},{9,11},{10,... | collective-permute-start | bytes 1474568 | tf_op jit(solution)/shard_map/ppermute | solution.py:700
  71.5 25.0 %collective-permute-start.14 = (bf16[1280,384]{1,0:T(8,128)(2,1)}, bf16[1280,384]{1,0:T(8,128)(2,1)}, u32[]{:S(2)}, u32[]{:S(2)}) collective-permute-start(bf16[1280,384]{1,0:T(8,128)(2,1)} %get-tuple-element.134.refs_2_), channel_id=1, source_target_pairs={{0,16},{8,24},{16,0},{24,8},{1,17},{9,25},{17,1},{25,9},{2,18},{10... | collective-permute-start | bytes 2949128 | tf_op jit(solution)/shard_map/ppermute | solution.py:697
  73.0 4.0 %copy-start.7 = (bf16[768,768]{1,0:T(8,128)(2,1)S(1)}, bf16[768,768]{1,0:T(8,128)(2,1)}, u32[]{:S(2)}) copy-start(bf16[768,768]{1,0:T(8,128)(2,1)} %get-tuple-element.128.refs_1_) | copy-start | bytes 3538948
  73.0 4.0 %copy-start.13 = (bf16[768,768]{1,0:T(8,128)(2,1)S(1)}, bf16[768,768]{1,0:T(8,128)(2,1)}, u32[]{:S(2)}) copy-start(bf16[768,768]{1,0:T(8,128)(2,1)} %get-tuple-element.122.refs_3_.refs_1_) | copy-start | bytes 3538948
  73.0 4.0 %copy-start.14 = (bf16[768,768]{1,0:T(8,128)(2,1)S(1)}, bf16[768,768]{1,0:T(8,128)(2,1)}, u32[]{:S(2)}) copy-start(bf16[768,768]{1,0:T(8,128)(2,1)} %get-tuple-element.123.refs_4_.refs_2_) | copy-start | bytes 3538948
  73.0 4.0 %copy-start.16 = (bf16[256,768]{1,0:T(8,128)(2,1)S(1)}, bf16[256,768]{1,0:T(8,128)(2,1)}, u32[]{:S(2)}) copy-start(bf16[256,768]{1,0:T(8,128)(2,1)} %get-tuple-element.121.refs_3_.refs_2_.refs_0_) | copy-start | bytes 1179652
  76.5 29.2 %collective-permute-start.13 = (bf16[1536,384]{1,0:T(8,128)(2,1)}, bf16[1536,384]{1,0:T(8,128)(2,1)}, u32[]{:S(2)}, u32[]{:S(2)}) collective-permute-start(bf16[1536,384]{1,0:T(8,128)(2,1)} %get-tuple-element.135.refs_5_), channel_id=1, source_target_pairs={{0,1},{1,0},{2,3},{3,2},{4,5},{5,4},{6,7},{7,6},{8,9},{9,8},{10,11... | collective-permute-start | bytes 3538952 | tf_op jit(solution)/shard_map/ppermute | solution.py:700
  77.0 2.3 %copy-start = (bf16[768,768]{1,0:T(8,128)(2,1)S(1)}, bf16[768,768]{1,0:T(8,128)(2,1)}, u32[]{:S(2)}) copy-start(bf16[768,768]{1,0:T(8,128)(2,1)} %refs_4_.1) | copy-start | bytes 3538948
  77.0 2.3 %copy-start.1 = (bf16[768,768]{1,0:T(8,128)(2,1)S(1)}, bf16[768,768]{1,0:T(8,128)(2,1)}, u32[]{:S(2)}) copy-start(bf16[768,768]{1,0:T(8,128)(2,1)} %refs_5_.3) | copy-start | bytes 3538948
  77.0 2.3 %copy-start.2 = (bf16[768,768]{1,0:T(8,128)(2,1)S(1)}, bf16[768,768]{1,0:T(8,128)(2,1)}, u32[]{:S(2)}) copy-start(bf16[768,768]{1,0:T(8,128)(2,1)} %refs_3_.3) | copy-start | bytes 3538948
  77.0 2.3 %copy-start.3 = (s32[256]{0:T(256)S(1)}, s32[256]{0:T(256)}, u32[]{:S(2)}) copy-start(s32[256]{0:T(256)} %refs_7_.3) | copy-start | bytes 3076
  79.2 7.3 %collective-permute-start.9 = (bf16[8,288,384]{2,1,0:T(8,128)(2,1)S(1)}, bf16[8,288,384]{2,1,0:T(8,128)(2,1)S(1)}, u32[]{:S(2)}, u32[]{:S(2)}) collective-permute-start(bf16[8,288,384]{2,1,0:T(8,128)(2,1)S(1)} %shard_map.347.refs_11_), channel_id=1, source_target_pairs={{0,8},{8,0},{16,24},{24,16},{1,9},{9,1},{17,25},{25,17},{2,10},{10... | collective-permute-start | bytes 5308424 | tf_op jit(solution)/shard_map/ppermute | solution.py:697
  84.1 23.9 %collective-permute-start.12 = (bf16[320,384]{1,0:T(8,128)(2,1)S(1)}, bf16[320,384]{1,0:T(8,128)(2,1)S(1)}, u32[]{:S(2)}, u32[]{:S(2)}) collective-permute-start(bf16[320,384]{1,0:T(8,128)(2,1)S(1)} %get-tuple-element.141.refs_8_), channel_id=1, source_target_pairs={{0,4},{1,5},{2,6},{3,7},{4,0},{5,1},{6,2},{7,3},{8,12},{9,13},{10,... | collective-permute-start | bytes 737288 | tf_op jit(solution)/shard_map/ppermute | solution.py:700
  89.6 19.8 %collective-permute-start.11 = (bf16[800,384]{1,0:T(8,128)(2,1)S(1)}, bf16[800,384]{1,0:T(8,128)(2,1)S(1)}, u32[]{:S(2)}, u32[]{:S(2)}) collective-permute-start(bf16[800,384]{1,0:T(8,128)(2,1)S(1)} %get-tuple-element.144), channel_id=1, source_target_pairs={{0,16},{8,24},{16,0},{24,8},{1,17},{9,25},{17,1},{25,9},{2,18},{10... | collective-permute-start | bytes 1843208 | tf_op jit(solution)/shard_map/ppermute | solution.py:697
  91.0 29.4 %collective-permute-start.15 = (bf16[896,384]{1,0:T(8,128)(2,1)}, bf16[896,384]{1,0:T(8,128)(2,1)}, u32[]{:S(2)}, u32[]{:S(2)}) collective-permute-start(bf16[896,384]{1,0:T(8,128)(2,1)} %get-tuple-element.147.refs_2_), channel_id=1, source_target_pairs={{0,1},{1,0},{2,3},{3,2},{4,5},{5,4},{6,7},{7,6},{8,9},{9,8},{10,11... | collective-permute-start | bytes 2064392 | tf_op jit(solution)/shard_map/ppermute | solution.py:700
  98.0 12.8 %collective-permute-start.16 = (bf16[640,384]{1,0:T(8,128)(2,1)S(1)}, bf16[640,384]{1,0:T(8,128)(2,1)S(1)}, u32[]{:S(2)}, u32[]{:S(2)}) collective-permute-start(bf16[640,384]{1,0:T(8,128)(2,1)S(1)} %get-tuple-element.148.refs_2_), channel_id=1, source_target_pairs={{0,2},{1,3},{2,0},{3,1},{4,6},{5,7},{6,4},{7,5},{8,10},{9,11},{10,... | collective-permute-start | bytes 1474568 | tf_op jit(solution)/shard_map/ppermute | solution.py:700
  107.4 15.6 %collective-permute-start.20 = (bf16[768,384]{1,0:T(8,128)(2,1)S(1)}, bf16[768,384]{1,0:T(8,128)(2,1)S(1)}, u32[]{:S(2)}, u32[]{:S(2)}) collective-permute-start(bf16[768,384]{1,0:T(8,128)(2,1)S(1)} %get-tuple-element.149.refs_5_), channel_id=1, source_target_pairs={{0,16},{8,24},{16,0},{24,8},{1,17},{9,25},{17,1},{25,9},{2,18},{10... | collective-permute-start | bytes 1769480 | tf_op jit(solution)/shard_map/ppermute | solution.py:697
  110.2 19.5 %collective-permute-start.17 = (bf16[576,384]{1,0:T(8,128)(2,1)S(1)}, bf16[576,384]{1,0:T(8,128)(2,1)S(1)}, u32[]{:S(2)}, u32[]{:S(2)}) collective-permute-start(bf16[576,384]{1,0:T(8,128)(2,1)S(1)} %get-tuple-element.154.refs_2_), channel_id=1, source_target_pairs={{0,1},{1,0},{2,3},{3,2},{4,5},{5,4},{6,7},{7,6},{8,9},{9,8},{10,11... | collective-permute-start | bytes 1327112 | tf_op jit(solution)/shard_map/ppermute | solution.py:700
  111.5 11.9 %collective-permute-start.19 = (bf16[320,384]{1,0:T(8,128)(2,1)S(1)}, bf16[320,384]{1,0:T(8,128)(2,1)S(1)}, u32[]{:S(2)}, u32[]{:S(2)}) collective-permute-start(bf16[320,384]{1,0:T(8,128)(2,1)S(1)} %get-tuple-element.155.refs_3_), channel_id=1, source_target_pairs={{0,4},{1,5},{2,6},{3,7},{4,0},{5,1},{6,2},{7,3},{8,12},{9,13},{10,... | collective-permute-start | bytes 737288 | tf_op jit(solution)/shard_map/ppermute | solution.py:700
  121.7 5.2 %collective-permute-start.18 = (bf16[192,384]{1,0:T(8,128)(2,1)S(1)}, bf16[192,384]{1,0:T(8,128)(2,1)S(1)}, u32[]{:S(2)}, u32[]{:S(2)}) collective-permute-start(bf16[192,384]{1,0:T(8,128)(2,1)S(1)} %get-tuple-element.159.refs_4_), channel_id=1, source_target_pairs={{0,16},{8,24},{16,0},{24,8},{1,17},{9,25},{17,1},{25,9},{2,18},{10... | collective-permute-start | bytes 442376 | tf_op jit(solution)/shard_map/ppermute | solution.py:697
  122.3 16.4 %collective-permute-start.22 = (bf16[256,384]{1,0:T(8,128)(2,1)S(1)}, bf16[256,384]{1,0:T(8,128)(2,1)S(1)}, u32[]{:S(2)}, u32[]{:S(2)}) collective-permute-start(bf16[256,384]{1,0:T(8,128)(2,1)S(1)} %get-tuple-element.168), channel_id=1, source_target_pairs={{0,2},{1,3},{2,0},{3,1},{4,6},{5,7},{6,4},{7,5},{8,10},{9,11},{10,... | collective-permute-start | bytes 589832 | tf_op jit(solution)/shard_map/ppermute | solution.py:700
  124.3 13.7 %collective-permute-start.23 = (bf16[384,384]{1,0:T(8,128)(2,1)S(1)}, bf16[384,384]{1,0:T(8,128)(2,1)S(1)}, u32[]{:S(2)}, u32[]{:S(2)}) collective-permute-start(bf16[384,384]{1,0:T(8,128)(2,1)S(1)} %get-tuple-element.162.refs_6_), channel_id=1, source_target_pairs={{0,2},{1,3},{2,0},{3,1},{4,6},{5,7},{6,4},{7,5},{8,10},{9,11},{10,... | collective-permute-start | bytes 884744 | tf_op jit(solution)/shard_map/ppermute | solution.py:700
  125.3 16.4 %collective-permute-start.26 = (bf16[160,384]{1,0:T(8,128)(2,1)S(1)}, bf16[160,384]{1,0:T(8,128)(2,1)S(1)}, u32[]{:S(2)}, u32[]{:S(2)}) collective-permute-start(bf16[160,384]{1,0:T(8,128)(2,1)S(1)} %get-tuple-element.179), channel_id=1, source_target_pairs={{0,1},{1,0},{2,3},{3,2},{4,5},{5,4},{6,7},{7,6},{8,9},{9,8},{10,11... | collective-permute-start | bytes 368648 | tf_op jit(solution)/shard_map/ppermute | solution.py:700
  130.4 10.5 %collective-permute-start.21 = (bf16[320,384]{1,0:T(8,128)(2,1)S(1)}, bf16[320,384]{1,0:T(8,128)(2,1)S(1)}, u32[]{:S(2)}, u32[]{:S(2)}) collective-permute-start(bf16[320,384]{1,0:T(8,128)(2,1)S(1)} %get-tuple-element.167.refs_2_), channel_id=1, source_target_pairs={{0,2},{1,3},{2,0},{3,1},{4,6},{5,7},{6,4},{7,5},{8,10},{9,11},{10,... | collective-permute-start | bytes 737288 | tf_op jit(solution)/shard_map/ppermute | solution.py:700
  130.9 10.7 %collective-permute-start.27 = (bf16[80,384]{1,0:T(8,128)(2,1)S(1)}, bf16[80,384]{1,0:T(8,128)(2,1)S(1)}, u32[]{:S(2)}, u32[]{:S(2)}) collective-permute-start(bf16[80,384]{1,0:T(8,128)(2,1)S(1)} %get-tuple-element.180), channel_id=1, source_target_pairs={{0,16},{8,24},{16,0},{24,8},{1,17},{9,25},{17,1},{25,9},{2,18},{10... | collective-permute-start | bytes 184328 | tf_op jit(solution)/shard_map/ppermute | solution.py:697
  138.7 6.2 %collective-permute-start.25 = (bf16[192,384]{1,0:T(8,128)(2,1)S(1)}, bf16[192,384]{1,0:T(8,128)(2,1)S(1)}, u32[]{:S(2)}, u32[]{:S(2)}) collective-permute-start(bf16[192,384]{1,0:T(8,128)(2,1)S(1)} %get-tuple-element.170.refs_6_), channel_id=1, source_target_pairs={{0,4},{1,5},{2,6},{3,7},{4,0},{5,1},{6,2},{7,3},{8,12},{9,13},{10,... | collective-permute-start | bytes 442376 | tf_op jit(solution)/shard_map/ppermute | solution.py:700
  145.5 5.2 %collective-permute-start.33 = (bf16[192,384]{1,0:T(8,128)(2,1)S(1)}, bf16[192,384]{1,0:T(8,128)(2,1)S(1)}, u32[]{:S(2)}, u32[]{:S(2)}) collective-permute-start(bf16[192,384]{1,0:T(8,128)(2,1)S(1)} %shard_map.361.refs_5_), channel_id=1, source_target_pairs={{0,16},{8,24},{16,0},{24,8},{1,17},{9,25},{17,1},{25,9},{2,18},{10... | collective-permute-start | bytes 442376 | tf_op jit(solution)/shard_map/ppermute | solution.py:697
  147.1 5.6 %collective-permute-start.31 = (bf16[240,384]{1,0:T(8,128)(2,1)S(1)}, bf16[240,384]{1,0:T(8,128)(2,1)S(1)}, u32[]{:S(2)}, u32[]{:S(2)}) collective-permute-start(bf16[240,384]{1,0:T(8,128)(2,1)S(1)} %get-tuple-element.181.refs_2_), channel_id=1, source_target_pairs={{0,16},{8,24},{16,0},{24,8},{1,17},{9,25},{17,1},{25,9},{2,18},{10... | collective-permute-start | bytes 552968 | tf_op jit(solution)/shard_map/ppermute | solution.py:697
  147.6 8.9 %collective-permute-start.24 = (bf16[304,384]{1,0:T(8,128)(2,1)S(1)}, bf16[304,384]{1,0:T(8,128)(2,1)S(1)}, u32[]{:S(2)}, u32[]{:S(2)}) collective-permute-start(bf16[304,384]{1,0:T(8,128)(2,1)S(1)} %get-tuple-element.175.refs_4_), channel_id=1, source_target_pairs={{0,4},{1,5},{2,6},{3,7},{4,0},{5,1},{6,2},{7,3},{8,12},{9,13},{10,... | collective-permute-start | bytes 700424 | tf_op jit(solution)/shard_map/ppermute | solution.py:700
  150.8 15.4 %collective-permute-start.34 = (bf16[384,384]{1,0:T(8,128)(2,1)S(1)}, bf16[384,384]{1,0:T(8,128)(2,1)S(1)}, u32[]{:S(2)}, u32[]{:S(2)}) collective-permute-start(bf16[384,384]{1,0:T(8,128)(2,1)S(1)} %pad_maximum_fusion.2), channel_id=1, source_target_pairs={{0,8},{8,0},{16,24},{24,16},{1,9},{9,1},{17,25},{25,17},{2,10},{10... | collective-permute-start | bytes 884744 | tf_op jit(solution)/shard_map/ppermute | solution.py:697
  152.8 13.6 %collective-permute-start.32 = (bf16[480,384]{1,0:T(8,128)(2,1)S(1)}, bf16[480,384]{1,0:T(8,128)(2,1)S(1)}, u32[]{:S(2)}, u32[]{:S(2)}) collective-permute-start(bf16[480,384]{1,0:T(8,128)(2,1)S(1)} %pad_maximum_fusion), channel_id=1, source_target_pairs={{0,8},{8,0},{16,24},{24,16},{1,9},{9,1},{17,25},{25,17},{2,10},{10... | collective-permute-start | bytes 1105928 | tf_op jit(solution)/shard_map/ppermute | solution.py:697
  157.1 5.1 %collective-permute-start.29 = (bf16[144,384]{1,0:T(8,128)(2,1)S(1)}, bf16[144,384]{1,0:T(8,128)(2,1)S(1)}, u32[]{:S(2)}, u32[]{:S(2)}) collective-permute-start(bf16[144,384]{1,0:T(8,128)(2,1)S(1)} %constant_dynamic-update-slice_fusion), channel_id=1, source_target_pairs={{0,16},{8,24},{16,0},{24,8},{1,17},{9,25},{17,1},{25,9},{2,18},{10... | collective-permute-start | bytes 331784 | tf_op jit(solution)/shard_map/ppermute | solution.py:697
  158.7 5.3 %collective-permute-start.30 = (bf16[144,384]{1,0:T(8,128)(2,1)S(1)}, bf16[144,384]{1,0:T(8,128)(2,1)S(1)}, u32[]{:S(2)}, u32[]{:S(2)}) collective-permute-start(bf16[144,384]{1,0:T(8,128)(2,1)S(1)} %constant_dynamic-update-slice_fusion), channel_id=1, source_target_pairs={{0,24},{8,16},{16,8},{24,0},{1,25},{9,17},{17,9},{25,1},{2,26},{10... | collective-permute-start | bytes 331784 | tf_op jit(solution)/shard_map/ppermute | solution.py:697
  158.7 5.3 %collective-permute-start.28 = (bf16[176,384]{1,0:T(8,128)(2,1)S(1)}, bf16[176,384]{1,0:T(8,128)(2,1)S(1)}, u32[]{:S(2)}, u32[]{:S(2)}) collective-permute-start(bf16[176,384]{1,0:T(8,128)(2,1)S(1)} %pad_maximum_fusion.5), channel_id=1, source_target_pairs={{0,8},{8,0},{16,24},{24,16},{1,9},{9,1},{17,25},{25,17},{2,10},{10... | collective-permute-start | bytes 405512 | tf_op jit(solution)/shard_map/ppermute | solution.py:697
  (12 other events, 16.7 us)

commit v5 on v4

--- a/solution.py
+++ b/solution.py
@@ -245,7 +245,7 @@
     steps = hidden // tile
 
     def tile_copies(i):
-        at = pl.ds(pl.multiple_of(i * tile, tile), tile)
+        at = pl.ds(i * tile, tile)
         return (
             pltpu.make_async_copy(up_w_any.at[:, at], up_w_ref.at[:, at], sems.at[2 * i + 1]),
             pltpu.make_async_copy(down_w_any.at[at, :], down_w_ref.at[at, :], sems.at[2 * i + 2]),
@@ -270,8 +270,8 @@
     middle_t_ref[...] = middle_low.T
     total_ref[...] = middle + down_b
 
-    def forward(i, carry):
-        at = pl.ds(pl.multiple_of(i * tile, tile), tile)
+    def forward(i):
+        at = pl.ds(i * tile, tile)
         for copy in tile_copies(i):
             copy.wait()
         pre = fwd_dot(middle_low_ref[...], up_w_ref[:, at]) + up_b_ref[:, at]
@@ -280,9 +280,9 @@
         act_t_ref[at, :] = act.T
         slope_ref[:, at] = cdf + pre * jnp.exp(-0.5 * pre * pre) * (1.0 / math.sqrt(2 * math.pi))
         total_ref[...] += fwd_dot(act, down_w_ref[at, :])
-        return carry
-
-    lax.fori_loop(0, steps, forward, 0)
+
+    for i in range(steps):
+        forward(i)
     normed2, inv2 = norm_parts(total_ref[...])
     mixed_ref[...] = (normed2 * final_g + final_s).astype(BF)
     cot = cot_ref[...].astype(F32)
@@ -713,6 +713,26 @@
     keys, values, prob, context, x_t, table_prev = attend(
         slots, views, layer_input, key_weight, value_weight, value_row, queries, own_keys, own_values, own_bias
     )
+    first_rows = 2 * n_out // 3
+    def both_cores(value):
+        other = swap_grp(value, 1)
+        return f(pick(core_bit, value, other)), f(pick(core_bit, other, value))
+
+    def big_outputs(up_rows, early):
+        sides = both_cores(up_rows)
+        out_up = jnp.concatenate([side[i : i + n_out] for side in sides for i in range(0, ff_out, n_out)], axis=1)
+        sides = both_cores(early)
+        at_z = ff_out - first_rows
+        out_down = jnp.concatenate(
+            [
+                jnp.concatenate([side[at_z : at_z + first_rows] for side in sides], axis=1),
+                jnp.concatenate([side[:at_z] for side in sides], axis=1),
+            ],
+            axis=0,
+        )
+        out_out = jnp.concatenate([side[at_z + first_rows :] for side in sides], axis=1)
+        return out_up, out_down, out_out
+
     packets = blocks if blocks == 8 and n_out % 32 == 0 else 0
     mixed, grad_context, grad_mid_sum, sums, up_sum, *made = middle_part(
         packets, pos, tokens, prev_ids, answer_table, context, cotangent, out_weight, up_weight, down_weight, up_bias,
@@ -843,6 +863,13 @@
         (up_part,), _ = combine(
             pos, [("sum", up_kept, up_got, 0, 0, 0, None, None)], after=(early_sent,)
         )
+        def whole(value, other):
+            return pick(x_bit, value, other), pick(x_bit, other, value)
+
+        low, high = whole(early_sent, early_got)
+        early = jnp.concatenate([low[:part], high[:part], low[part:], high[part:]], axis=0)
+        up_rows = jnp.concatenate(whole(up_part, swap_grp(up_part, 2)), axis=0)
+        out_up, out_down, out_out = big_outputs(up_rows, early)
         n_small = n_out + n_out // 2
         (first_part, value_part, table_part, vectors), _ = combine(
             pos,
@@ -852,15 +879,9 @@
                 ("sum", table_kept, first_got, n_small, 0, 0, None, None),
                 ("vec", vectors, first_got, n_small + 2 * tab, 0, 0, None, None),
             ],
-            after=(up_part,),
-        )
-
-        def whole(value, other):
-            return pick(x_bit, value, other), pick(x_bit, other, value)
-
-        low, high = whole(early_sent, early_got)
-        early = jnp.concatenate([low[:part], high[:part], low[part:], high[part:]], axis=0)
-        up_rows = jnp.concatenate(whole(up_part, swap_grp(up_part, 2)), axis=0)
+            after=(out_up, out_down),
+        )
+
         square = jnp.concatenate([first_part, value_part], axis=0)
         near_core = swap_grp(jnp.concatenate([square, vectors.astype(BF)], axis=0), 1)
         near, far = (square, swap_grp(square, 2)), (near_core[:n_small], swap_grp(square, 3))
@@ -910,23 +931,8 @@
         table_share = f(lax.psum_scatter(table_rows, "blk", scatter_dimension=0, tiled=False))
         vectors = lax.psum(vectors, ("blk", "grp"))
         early = jnp.concatenate([down_rows, z_rows], axis=0)
-
-    def both_cores(value):
-        other = swap_grp(value, 1)
-        return f(pick(core_bit, value, other)), f(pick(core_bit, other, value))
-
-    sides = both_cores(up_rows)
-    out_up = jnp.concatenate([side[i : i + n_out] for side in sides for i in range(0, ff_out, n_out)], axis=1)
-    sides = both_cores(early)
-    at_z = ff_out - first_rows
-    out_down = jnp.concatenate(
-        [
-            jnp.concatenate([side[at_z : at_z + first_rows] for side in sides], axis=1),
-            jnp.concatenate([side[:at_z] for side in sides], axis=1),
-        ],
-        axis=0,
-    )
-    out_out = jnp.concatenate([side[at_z + first_rows :] for side in sides], axis=1)
+        out_up, out_down, out_out = big_outputs(up_rows, early)
+
     square = jnp.concatenate(square if packets else both_cores(square), axis=1)
     table_share = jnp.concatenate([table_share[:tab], table_share[tab:]], axis=1)
     vectors = jnp.concatenate([vectors[:16], vectors[16:]], axis=1)

time: 170 us -> 168 us (0.988)
    ppermute x20, waiting for transfers between devices: 37.9 us -> 35.6 us  [swap_blk(): return lax.ppermute(value, 'blk', [(i, i ^ mask) for i in range(blocks)])]
    unnamed x58 -> x60, local copies, waits for them, and re-layouts: 5.46 us -> 3.44 us
  transfers between devices with their start and end apart: 35 -> 35, of which waited for: 18 -> 18; matrix products, arithmetic and copies ran while one was open for 3% -> 2% of each run, Pallas kernels for 23% -> 23%
where the time goes in v5:
time: 168 us
  Pallas kernels  70.2 us (42%)
  waiting for transfers between devices  52 us (31%)
  starting transfers between devices  33.8 us (20%)
  local copies, waits for them, and re-layouts  7 us (4%)
  other arithmetic  3.1 us (2%)
    ppermute x20, waiting for transfers between devices, swap_blk(): return lax.ppermute(value, 'blk', [(i, i ^ mask) for i in range(blocks)])  35.6 us
    ppermute x20, starting transfers between devices, swap_blk(): return lax.ppermute(value, 'blk', [(i, i ^ mask) for i in range(blocks)])  23 us
    pallas_call x1, Pallas kernels, middle_part(): pl.pallas_call(lambda *refs: middle_kernel(packets, *refs), in_specs=[pl....  17.8 us
    pallas_call x15, Pallas kernels, combine(): pl.pallas_call(body, in_specs=[pl.BlockSpec(memory_space=pltpu.SMEM)] + [...  17.6 us
    ppermute x15, waiting for transfers between devices, swap_grp(): return lax.ppermute(value, 'grp', [(i, i ^ mask) for i in range(grps)])  16.4 us
    ppermute x15, starting transfers between devices, swap_grp(): return lax.ppermute(value, 'grp', [(i, i ^ mask) for i in range(grps)])  10.8 us
    pallas_call x1, Pallas kernels, attend(): pl.pallas_call(lambda *refs: attend_kernel(views, *refs), grid=(width //...  10.4 us
    pallas_call x1, Pallas kernels, attend_back(): pl.pallas_call(attend_back_kernel, grid=(width // group,), in_specs=[lane...  8.53 us
  transfers between devices with their start and end apart: 35, of which 18 were waited for; matrix products, arithmetic and copies ran while one was open for 2% of the time, Pallas kernels for 23%

profile of v5, /device:TPU:0, one launch (start us, length us, event | category | flops | bytes accessed | tf_op | source)
XLA Modules:
  0.0 167.6 jit_solution(3951783886410780510)
XLA Ops:
  0.7 2.0 %shard_map.340 = (bf16[80,768]{1,0:T(8,128)(2,1)}, bf16[256,768]{1,0:T(8,128)(2,1)}) custom-call(bf16[256,768]{1,0:T(8,128)(2,1)} %refs_1_.3, s32[256]{0:T(256)} %seg_any.3, s32[256]{0:T(256)} %refs_7_.3, bf16[2,768]{1,0:T(2,128)(2,1)} %refs_3_.2), custom_call_target="tpu_custom_call" | custom-call | tf_op jit(solution)/shard_map/pallas_call | solution.py:97
  2.7 3.1 %collective-permute-start.1 = (bf16[80,768]{1,0:T(8,128)(2,1)}, bf16[80,768]{1,0:T(8,128)(2,1)S(1)}, u32[]{:S(2)}, u32[]{:S(2)}) collective-permute-start(bf16[80,768]{1,0:T(8,128)(2,1)} %get-tuple-element.114.refs_8_), channel_id=1, source_target_pairs={{0,2},{1,3},{2,0},{3,1},{4,6},{5,7},{6,4},{7,5},{8,10},{9,11},{10,... | collective-permute-start | bytes 368648 | tf_op jit(solution)/shard_map/ppermute | solution.py:700
  5.8 2.6 %collective-permute-start.3 = (bf16[80,768]{1,0:T(8,128)(2,1)}, bf16[80,768]{1,0:T(8,128)(2,1)S(1)}, u32[]{:S(2)}, u32[]{:S(2)}) collective-permute-start(bf16[80,768]{1,0:T(8,128)(2,1)} %get-tuple-element.114.refs_8_), channel_id=1, source_target_pairs={{0,4},{1,5},{2,6},{3,7},{4,0},{5,1},{6,2},{7,3},{8,12},{9,13},{10,... | collective-permute-start | bytes 368648 | tf_op jit(solution)/shard_map/ppermute | solution.py:700
  8.4 1.7 %collective-permute-start = (bf16[80,768]{1,0:T(8,128)(2,1)}, bf16[80,768]{1,0:T(8,128)(2,1)S(1)}, u32[]{:S(2)}, u32[]{:S(2)}) collective-permute-start(bf16[80,768]{1,0:T(8,128)(2,1)} %get-tuple-element.114.refs_8_), channel_id=1, source_target_pairs={{0,1},{1,0},{2,3},{3,2},{4,5},{5,4},{6,7},{7,6},{8,9},{9,8},{10,11... | collective-permute-start | bytes 368648 | tf_op jit(solution)/shard_map/ppermute | solution.py:700
  10.7 1.7 %collective-permute-start.2 = (bf16[80,768]{1,0:T(8,128)(2,1)S(1)}, bf16[80,768]{1,0:T(8,128)(2,1)S(1)}, u32[]{:S(2)}, u32[]{:S(2)}) collective-permute-start(bf16[80,768]{1,0:T(8,128)(2,1)S(1)} %collective-permute-done.1.refs_10_), channel_id=1, source_target_pairs={{0,1},{1,0},{2,3},{3,2},{4,5},{5,4},{6,7},{7,6},{8,9},{9,8},{10,11... | collective-permute-start | bytes 368648 | tf_op jit(solution)/shard_map/ppermute | solution.py:700
  12.4 5.9 %collective-permute-done.3.refs_12_ = bf16[80,768]{1,0:T(8,128)(2,1)S(1)} collective-permute-done((bf16[80,768]{1,0:T(8,128)(2,1)}, bf16[80,768]{1,0:T(8,128)(2,1)S(1)}, u32[]{:S(2)}, u32[]{:S(2)}) %collective-permute-start.3) | collective-permute-done | bytes 122912 | tf_op jit(solution)/shard_map/ppermute | solution.py:700
  18.3 1.5 collective-permute-start.4
  21.0 4.9 %shard_map.341 = (bf16[256,768]{1,0:T(8,128)(2,1)}, bf16[256,768]{1,0:T(8,128)(2,1)}, bf16[256,768]{1,0:T(8,128)(2,1)}, f32[256,256]{1,0:T(8,128)}, f32[1,768]{1,0:T(1,128)}) custom-call(bf16[256,768]{1,0:T(8,128)(2,1)} %get-tuple-element.108.input_ref.refs_0_, bf16[768,768]{1,0:T(8,128)(2,1)} %refs_3_.3, bf16[768,768]{1,0:T(8,128)(2,1)} %refs_4_.1, ...), custom_call_target="tpu_custom_call" | custom-call | flops 100000000 | bytes 1048576 | tf_op jit(solution)/shard_map/pallas_call | solution.py:133
  26.7 10.4 %shard_map.342 = (bf16[768,768]{1,0:T(8,128)(2,1)}, bf16[768,768]{1,0:T(8,128)(2,1)}, bf16[12,256,768]{2,1,0:T(8,128)(2,1)}, f32[256,768]{1,0:T(8,128)}, bf16[768,768]{1,0:T(8,128)(2,1)}, /*index=5*/f32[8,512]{1,0:T(8,128)}) custom-call(bf16[256,768]{1,0:T(8,128)(2,1)} %get-tuple-element.108.input_ref.refs_0_, bf16[768,768]{1,0:T(8,128)(2,1)} %refs_4_.1, ...), custom_call_target="tpu_custom_call" | custom-call | flops 100000000 | bytes 1048576 | tf_op jit(solution)/shard_map/pallas_call | solution.py:206
  37.1 17.8 %shard_map.343 = (bf16[256,768]{1,0:T(8,128)(2,1)}, bf16[256,768]{1,0:T(8,128)(2,1)}, f32[256,768]{1,0:T(8,128)}, f32[8,768]{1,0:T(8,128)}, f32[1,3072]{1,0:T(1,...) custom-call(s32[5]{0:T(128)} %stack.23.refs_0_.pos_ref, ...), custom_call_target="tpu_custom_call" | custom-call | flops 100000000 | bytes 1048576 | tf_op jit(solution)/shard_map/pallas_call | solution.py:398
  55.5 8.5 %shard_map.344 = (bf16[256,768]{1,0:T(8,128)(2,1)}, bf16[768,768]{1,0:T(8,128)(2,1)}, bf16[768,768]{1,0:T(8,128)(2,1)}) custom-call(bf16[256,768]{1,0:T(8,128)(2,1)} %get-tuple-element.110.refs_4_.q_ref, bf16[768,768]{1,0:T(8,128)(2,1)} %get-tuple-element.117.keys_ref, bf16[768,768]{1,0:T(8,128)(2,1)} %get-tuple-element.118.values_ref, ...), custom_call_target="tpu_custom_call" | custom-call | flops 40000000000 | bytes 1048576 | tf_op jit(solution)/shard_map/pallas_call | solution.py:438
  64.1 1.5 copy-done.8
  65.6 1.0 copy-done.17
  66.6 3.5 %shard_map.345 = (bf16[1280,384]{1,0:T(8,128)(2,1)S(1)}, bf16[640,384]{1,0:T(8,128)(2,1)S(1)}, bf16[1280,384]{1,0:T(8,128)(2,1)}, bf16[640,384]{1,0:T(8,128)(2,1)S(1)}) custom-call(s32[5]{0:T(128)S(1)} %copy-done.6, bf16[2560,384]{1,0:T(8,128)(2,1)S(1)} %copy-done.8, bf16[1280,384]{1,0:T(8,128)(2,1)S(1)} %copy-done.10, ...), custom_call_target="tpu_custom_call" | custom-call | flops 40000000000 | bytes 1048576 | tf_op jit(solution)/shard_map/pallas_call | solution.py:642
  70.1 1.4 collective-permute-start.10
  71.5 1.5 collective-permute-start.14
  73.0 2.2 %shard_map.346 = (bf16[1536,384]{1,0:T(8,128)(2,1)S(1)}, bf16[1536,384]{1,0:T(8,128)(2,1)}) custom-call(s32[5]{0:T(128)S(1)} %copy-done.6, bf16[3072,384]{1,0:T(8,128)(2,1)S(1)} %copy-done.7, bf16[3072,384]{1,0:T(8,128)(2,1)S(1)} %collective-permute-done.7.refs_1_, bf16[1280,384]{1,0:T(8,128)(2,1)} %get-tuple-element.134.refs_2_), custom_call_target="tpu_custom_call" | custom-call | flops 40000000000 | bytes 1048576 | tf_op jit(solution)/shard_map/pallas_call | solution.py:642
  75.8 2.1 %shard_map.347.refs_11_ = bf16[8,288,384]{2,1,0:T(8,128)(2,1)S(1)} custom-call(s32[5]{0:T(128)S(1)} %copy-done.6, bf16[768,768]{1,0:T(8,128)(2,1)S(1)} %copy-done.9, bf16[256,768]{1,0:T(8,128)(2,1)S(1)} %copy-done.18, bf16[768,768]{1,0:T(8,128)(2,1)S(1)} %copy-done.15, bf16[768,768]{1,0:T(8,128)(2,1)S(1)} %copy-done.16, ...), custom_call_target="tpu_custom_call" | custom-call | flops 40000000000 | bytes 1048576 | tf_op jit(solution)/shard_map/pallas_call | solution.py:664
  78.1 3.8 %shard_map.348 = (bf16[512,384]{1,0:T(8,128)(2,1)S(1)}, bf16[512,384]{1,0:T(8,128)(2,1)S(1)}, f32[256,768]{1,0:T(8,128)}, f32[32,384]{1,0:T(8,128)S(1)}) custom-call(bf16[256,768]{1,0:T(8,128)(2,1)S(1)} %copy-done.18, bf16[768,768]{1,0:T(8,128)(2,1)S(1)} %copy-done.15, bf16[768,768]{1,0:T(8,128)(2,1)S(1)} %copy-done.16, bf16[768,768]{1,0:T(8,128)(2,1)S(1)} %copy-done.3, ...), custom_call_target="tpu_custom_call" | custom-call | flops 40000000000 | bytes 1048576 | tf_op jit(solution)/shard_map/pallas_call | solution.py:571
  81.9 1.5 collective-permute-done.10.refs_1_
  84.1 2.4 %collective-permute-start.12 = (bf16[320,384]{1,0:T(8,128)(2,1)S(1)}, bf16[320,384]{1,0:T(8,128)(2,1)S(1)}, u32[]{:S(2)}, u32[]{:S(2)}) collective-permute-start(bf16[320,384]{1,0:T(8,128)(2,1)S(1)} %get-tuple-element.141.refs_8_), channel_id=1, source_target_pairs={{0,4},{1,5},{2,6},{3,7},{4,0},{5,1},{6,2},{7,3},{8,12},{9,13},{10,... | collective-permute-start | bytes 737288 | tf_op jit(solution)/shard_map/ppermute | solution.py:700
  86.5 3.1 %shard_map.350 = (bf16[768,384]{1,0:T(8,128)(2,1)S(1)}, bf16[800,384]{1,0:T(8,128)(2,1)S(1)}, bf16[384,384]{1,0:T(8,128)(2,1)S(1)}, bf16[896,384]{1,0:T(8,128)(2,1)}) custom-call(s32[5]{0:T(128)S(1)} %copy-done.6, bf16[768,768]{1,0:T(8,128)(2,1)S(1)} %copy-done.9, bf16[256,768]{1,0:T(8,128)(2,1)S(1)} %copy-done.18, bf16[768,768]{1,0:T(8,128)(2,1)S(1)} %copy-done.15, ...), custom_call_target="tpu_custom_call" | custom-call | flops 40000000000 | bytes 1048576 | tf_op jit(solution)/shard_map/pallas_call | solution.py:664
  89.6 1.5 collective-permute-start.11
  91.6 4.9 %collective-permute-done.14.refs_1_ = bf16[1280,384]{1,0:T(8,128)(2,1)} collective-permute-done((bf16[1280,384]{1,0:T(8,128)(2,1)}, bf16[1280,384]{1,0:T(8,128)(2,1)}, u32[]{:S(2)}, u32[]{:S(2)}) %collective-permute-start.14) | collective-permute-done | bytes 983072 | tf_op jit(solution)/shard_map/ppermute | solution.py:697
  96.4 1.5 shard_map.351
  98.7 5.7 %collective-permute-done.13.refs_1_ = bf16[1536,384]{1,0:T(8,128)(2,1)} collective-permute-done((bf16[1536,384]{1,0:T(8,128)(2,1)}, bf16[1536,384]{1,0:T(8,128)(2,1)}, u32[]{:S(2)}, u32[]{:S(2)}) %collective-permute-start.13) | collective-permute-done | bytes 1179680 | tf_op jit(solution)/shard_map/ppermute | solution.py:700
  104.4 1.6 shard_map.352
  106.7 2.8 %collective-permute-done.11.refs_3_ = bf16[800,384]{1,0:T(8,128)(2,1)S(1)} collective-permute-done((bf16[800,384]{1,0:T(8,128)(2,1)S(1)}, bf16[800,384]{1,0:T(8,128)(2,1)S(1)}, u32[]{:S(2)}, u32[]{:S(2)}) %collective-permute-start.11) | collective-permute-done | bytes 614432 | tf_op jit(solution)/shard_map/ppermute | solution.py:697
  111.6 2.6 %collective-permute-start.19 = (bf16[320,384]{1,0:T(8,128)(2,1)S(1)}, bf16[320,384]{1,0:T(8,128)(2,1)S(1)}, u32[]{:S(2)}, u32[]{:S(2)}) collective-permute-start(bf16[320,384]{1,0:T(8,128)(2,1)S(1)} %get-tuple-element.155.refs_3_), channel_id=1, source_target_pairs={{0,4},{1,5},{2,6},{3,7},{4,0},{5,1},{6,2},{7,3},{8,12},{9,13},{10,... | collective-permute-start | bytes 737288 | tf_op jit(solution)/shard_map/ppermute | solution.py:700
  114.2 4.9 %collective-permute-done.15.refs_2_ = bf16[896,384]{1,0:T(8,128)(2,1)} collective-permute-done((bf16[896,384]{1,0:T(8,128)(2,1)}, bf16[896,384]{1,0:T(8,128)(2,1)}, u32[]{:S(2)}, u32[]{:S(2)}) %collective-permute-start.15) | collective-permute-done | bytes 688160 | tf_op jit(solution)/shard_map/ppermute | solution.py:700
  119.1 1.3 shard_map.355
  121.7 1.8 %collective-permute-done.19.refs_2_ = bf16[320,384]{1,0:T(8,128)(2,1)S(1)} collective-permute-done((bf16[320,384]{1,0:T(8,128)(2,1)S(1)}, bf16[320,384]{1,0:T(8,128)(2,1)S(1)}, u32[]{:S(2)}, u32[]{:S(2)}) %collective-permute-start.19) | collective-permute-done | bytes 245792 | tf_op jit(solution)/shard_map/ppermute | solution.py:700
  124.4 1.6 collective-permute-start.26
  126.0 2.0 %collective-permute-done.17.refs_4_ = bf16[576,384]{1,0:T(8,128)(2,1)S(1)} collective-permute-done((bf16[576,384]{1,0:T(8,128)(2,1)S(1)}, bf16[576,384]{1,0:T(8,128)(2,1)S(1)}, u32[]{:S(2)}, u32[]{:S(2)}) %collective-permute-start.17) | collective-permute-done | bytes 442400 | tf_op jit(solution)/shard_map/ppermute | solution.py:700
  128.7 1.5 collective-permute-start.27
  130.2 5.0 %collective-permute-done.23.refs_1_ = bf16[384,384]{1,0:T(8,128)(2,1)S(1)} collective-permute-done((bf16[384,384]{1,0:T(8,128)(2,1)S(1)}, bf16[384,384]{1,0:T(8,128)(2,1)S(1)}, u32[]{:S(2)}, u32[]{:S(2)}) %collective-permute-start.23) | collective-permute-done | bytes 294944 | tf_op jit(solution)/shard_map/ppermute | solution.py:700
  136.6 4.4 %collective-permute-done.21.refs_4_ = bf16[320,384]{1,0:T(8,128)(2,1)S(1)} collective-permute-done((bf16[320,384]{1,0:T(8,128)(2,1)S(1)}, bf16[320,384]{1,0:T(8,128)(2,1)S(1)}, u32[]{:S(2)}, u32[]{:S(2)}) %collective-permute-start.21) | collective-permute-done | bytes 245792 | tf_op jit(solution)/shard_map/ppermute | solution.py:700
  141.6 1.2 shard_map.360
  142.9 1.1 collective-permute-done.25.refs_1_
  144.5 1.6 collective-permute-start.28
  146.6 3.2 %collective-permute-done.28 = bf16[192,384]{1,0:T(8,128)(2,1)S(1)} collective-permute-done((bf16[192,384]{1,0:T(8,128)(2,1)S(1)}, bf16[192,384]{1,0:T(8,128)(2,1)S(1)}, u32[]{:S(2)}, u32[]{:S(2)}) %collective-permute-start.28) | collective-permute-done | bytes 147488 | tf_op jit(solution)/shard_map/ppermute | solution.py:697
  150.0 1.8 %collective-permute-done.30 = bf16[240,384]{1,0:T(8,128)(2,1)S(1)} collective-permute-done((bf16[240,384]{1,0:T(8,128)(2,1)S(1)}, bf16[240,384]{1,0:T(8,128)(2,1)S(1)}, u32[]{:S(2)}, u32[]{:S(2)}) %collective-permute-start.30) | collective-permute-done | bytes 184352 | tf_op jit(solution)/shard_map/ppermute | solution.py:697
  152.3 1.4 collective-permute-done.31
  154.1 2.8 %collective-permute-done.24.refs_4_ = bf16[304,384]{1,0:T(8,128)(2,1)S(1)} collective-permute-done((bf16[304,384]{1,0:T(8,128)(2,1)S(1)}, bf16[304,384]{1,0:T(8,128)(2,1)S(1)}, u32[]{:S(2)}, u32[]{:S(2)}) %collective-permute-start.24) | collective-permute-done | bytes 233504 | tf_op jit(solution)/shard_map/ppermute | solution.py:700
  157.6 1.6 collective-permute-start.33
  159.9 1.6 fusion
  162.7 1.8 %collective-permute-done.34 = bf16[144,384]{1,0:T(8,128)(2,1)S(1)} collective-permute-done((bf16[144,384]{1,0:T(8,128)(2,1)S(1)}, bf16[144,384]{1,0:T(8,128)(2,1)S(1)}, u32[]{:S(2)}, u32[]{:S(2)}) %collective-permute-start.34) | collective-permute-done | bytes 110624 | tf_op jit(solution)/shard_map/ppermute | solution.py:697
  166.0 0.9 fusion.1
  (152 shorter events, 19.7 us)
Async XLA Ops:
  2.7 8.0 %collective-permute-start.1 = (bf16[80,768]{1,0:T(8,128)(2,1)}, bf16[80,768]{1,0:T(8,128)(2,1)S(1)}, u32[]{:S(2)}, u32[]{:S(2)}) collective-permute-start(bf16[80,768]{1,0:T(8,128)(2,1)} %get-tuple-element.114.refs_8_), channel_id=1, source_target_pairs={{0,2},{1,3},{2,0},{3,1},{4,6},{5,7},{6,4},{7,5},{8,10},{9,11},{10,... | collective-permute-start | bytes 368648 | tf_op jit(solution)/shard_map/ppermute | solution.py:700
  5.8 12.5 %collective-permute-start.3 = (bf16[80,768]{1,0:T(8,128)(2,1)}, bf16[80,768]{1,0:T(8,128)(2,1)S(1)}, u32[]{:S(2)}, u32[]{:S(2)}) collective-permute-start(bf16[80,768]{1,0:T(8,128)(2,1)} %get-tuple-element.114.refs_8_), channel_id=1, source_target_pairs={{0,4},{1,5},{2,6},{3,7},{4,0},{5,1},{6,2},{7,3},{8,12},{9,13},{10,... | collective-permute-start | bytes 368648 | tf_op jit(solution)/shard_map/ppermute | solution.py:700
  8.4 11.5 %collective-permute-start.5 = (bf16[80,768]{1,0:T(8,128)(2,1)}, bf16[80,768]{1,0:T(8,128)(2,1)S(1)}, u32[]{:S(2)}, u32[]{:S(2)}) collective-permute-start(bf16[80,768]{1,0:T(8,128)(2,1)} %get-tuple-element.114.refs_8_), channel_id=1, source_target_pairs={{0,6},{1,7},{2,4},{3,5},{4,2},{5,3},{6,0},{7,1},{8,14},{9,15},{10,... | collective-permute-start | bytes 368648 | tf_op jit(solution)/shard_map/ppermute | solution.py:700
  8.4 17.5 %collective-permute-start = (bf16[80,768]{1,0:T(8,128)(2,1)}, bf16[80,768]{1,0:T(8,128)(2,1)S(1)}, u32[]{:S(2)}, u32[]{:S(2)}) collective-permute-start(bf16[80,768]{1,0:T(8,128)(2,1)} %get-tuple-element.114.refs_8_), channel_id=1, source_target_pairs={{0,1},{1,0},{2,3},{3,2},{4,5},{5,4},{6,7},{7,6},{8,9},{9,8},{10,11... | collective-permute-start | bytes 368648 | tf_op jit(solution)/shard_map/ppermute | solution.py:700
  10.7 15.2 %copy-start.19 = (bf16[80,768]{1,0:T(8,128)(2,1)}, bf16[80,768]{1,0:T(8,128)(2,1)S(1)}, u32[]{:S(2)}) copy-start(bf16[80,768]{1,0:T(8,128)(2,1)S(1)} %collective-permute-done.1.refs_10_) | copy-start | bytes 368644
  10.7 15.2 %collective-permute-start.2 = (bf16[80,768]{1,0:T(8,128)(2,1)S(1)}, bf16[80,768]{1,0:T(8,128)(2,1)S(1)}, u32[]{:S(2)}, u32[]{:S(2)}) collective-permute-start(bf16[80,768]{1,0:T(8,128)(2,1)S(1)} %collective-permute-done.1.refs_10_), channel_id=1, source_target_pairs={{0,1},{1,0},{2,3},{3,2},{4,5},{5,4},{6,7},{7,6},{8,9},{9,8},{10,11... | collective-permute-start | bytes 368648 | tf_op jit(solution)/shard_map/ppermute | solution.py:700
  18.3 7.5 %copy-start.20 = (bf16[80,768]{1,0:T(8,128)(2,1)}, bf16[80,768]{1,0:T(8,128)(2,1)S(1)}, u32[]{:S(2)}) copy-start(bf16[80,768]{1,0:T(8,128)(2,1)S(1)} %collective-permute-done.3.refs_12_) | copy-start | bytes 368644
  18.3 7.6 %collective-permute-start.4 = (bf16[80,768]{1,0:T(8,128)(2,1)S(1)}, bf16[80,768]{1,0:T(8,128)(2,1)S(1)}, u32[]{:S(2)}, u32[]{:S(2)}) collective-permute-start(bf16[80,768]{1,0:T(8,128)(2,1)S(1)} %collective-permute-done.3.refs_12_), channel_id=1, source_target_pairs={{0,1},{1,0},{2,3},{3,2},{4,5},{5,4},{6,7},{7,6},{8,9},{9,8},{10,11... | collective-permute-start | bytes 368648 | tf_op jit(solution)/shard_map/ppermute | solution.py:700
  19.8 6.0 %copy-start.21 = (bf16[80,768]{1,0:T(8,128)(2,1)}, bf16[80,768]{1,0:T(8,128)(2,1)S(1)}, u32[]{:S(2)}) copy-start(bf16[80,768]{1,0:T(8,128)(2,1)S(1)} %collective-permute-done.5.refs_14_) | copy-start | bytes 368644
  19.8 6.1 %collective-permute-start.6 = (bf16[80,768]{1,0:T(8,128)(2,1)S(1)}, bf16[80,768]{1,0:T(8,128)(2,1)S(1)}, u32[]{:S(2)}, u32[]{:S(2)}) collective-permute-start(bf16[80,768]{1,0:T(8,128)(2,1)S(1)} %collective-permute-done.5.refs_14_), channel_id=1, source_target_pairs={{0,1},{1,0},{2,3},{3,2},{4,5},{5,4},{6,7},{7,6},{8,9},{9,8},{10,11... | collective-permute-start | bytes 368648 | tf_op jit(solution)/shard_map/ppermute | solution.py:700
  54.9 9.2 %collective-permute-start.8 = (bf16[3840,384]{1,0:T(8,128)(2,1)}, bf16[3840,384]{1,0:T(8,128)(2,1)}, u32[]{:S(2)}, u32[]{:S(2)}) collective-permute-start(bf16[3840,384]{1,0:T(8,128)(2,1)} %get-tuple-element.133), channel_id=1, source_target_pairs={{0,8},{8,0},{16,24},{24,16},{1,9},{9,1},{17,25},{25,17},{2,10},{10... | collective-permute-start | bytes 8847368 | tf_op jit(solution)/shard_map/ppermute | solution.py:697
  55.0 18.0 %collective-permute-start.7 = (bf16[3072,384]{1,0:T(8,128)(2,1)}, bf16[3072,384]{1,0:T(8,128)(2,1)S(1)}, u32[]{:S(2)}, u32[]{:S(2)}) collective-permute-start(bf16[3072,384]{1,0:T(8,128)(2,1)} %get-tuple-element.130), channel_id=1, source_target_pairs={{0,8},{8,0},{16,24},{24,16},{1,9},{9,1},{17,25},{25,17},{2,10},{10... | collective-permute-start | bytes 7077896 | tf_op jit(solution)/shard_map/ppermute | solution.py:697
  55.5 8.6 %copy-start.6 = (s32[5]{0:T(128)S(1)}, s32[5]{0:T(128)}, u32[]{:S(2)}) copy-start(s32[5]{0:T(128)} %stack.23.refs_0_.pos_ref) | copy-start | bytes 64
  55.5 8.6 %copy-start.10 = (bf16[1280,384]{1,0:T(8,128)(2,1)S(1)}, bf16[1280,384]{1,0:T(8,128)(2,1)}, u32[]{:S(2)}) copy-start(bf16[1280,384]{1,0:T(8,128)(2,1)} %get-tuple-element.132.refs_1_) | copy-start | bytes 2949124
  66.6 6.3 %copy-start.7 = (bf16[3072,384]{1,0:T(8,128)(2,1)S(1)}, bf16[3072,384]{1,0:T(8,128)(2,1)}, u32[]{:S(2)}) copy-start(bf16[3072,384]{1,0:T(8,128)(2,1)} %get-tuple-element.129.refs_0_) | copy-start | bytes 7077892
  70.1 13.3 %collective-permute-start.10 = (bf16[640,384]{1,0:T(8,128)(2,1)S(1)}, bf16[640,384]{1,0:T(8,128)(2,1)S(1)}, u32[]{:S(2)}, u32[]{:S(2)}) collective-permute-start(bf16[640,384]{1,0:T(8,128)(2,1)S(1)} %get-tuple-element.140), channel_id=1, source_target_pairs={{0,2},{1,3},{2,0},{3,1},{4,6},{5,7},{6,4},{7,5},{8,10},{9,11},{10,... | collective-permute-start | bytes 1474568 | tf_op jit(solution)/shard_map/ppermute | solution.py:700
  71.5 25.0 %collective-permute-start.14 = (bf16[1280,384]{1,0:T(8,128)(2,1)}, bf16[1280,384]{1,0:T(8,128)(2,1)}, u32[]{:S(2)}, u32[]{:S(2)}) collective-permute-start(bf16[1280,384]{1,0:T(8,128)(2,1)} %get-tuple-element.134.refs_2_), channel_id=1, source_target_pairs={{0,16},{8,24},{16,0},{24,8},{1,17},{9,25},{17,1},{25,9},{2,18},{10... | collective-permute-start | bytes 2949128 | tf_op jit(solution)/shard_map/ppermute | solution.py:697
  73.0 2.7 %copy-start.9 = (bf16[768,768]{1,0:T(8,128)(2,1)S(1)}, bf16[768,768]{1,0:T(8,128)(2,1)}, u32[]{:S(2)}) copy-start(bf16[768,768]{1,0:T(8,128)(2,1)} %get-tuple-element.128.refs_1_) | copy-start | bytes 3538948
  73.0 2.7 %copy-start.15 = (bf16[768,768]{1,0:T(8,128)(2,1)S(1)}, bf16[768,768]{1,0:T(8,128)(2,1)}, u32[]{:S(2)}) copy-start(bf16[768,768]{1,0:T(8,128)(2,1)} %get-tuple-element.122.refs_3_.refs_1_) | copy-start | bytes 3538948
  73.0 2.7 %copy-start.16 = (bf16[768,768]{1,0:T(8,128)(2,1)S(1)}, bf16[768,768]{1,0:T(8,128)(2,1)}, u32[]{:S(2)}) copy-start(bf16[768,768]{1,0:T(8,128)(2,1)} %get-tuple-element.123.refs_4_.refs_2_) | copy-start | bytes 3538948
  73.0 2.7 %copy-start.18 = (bf16[256,768]{1,0:T(8,128)(2,1)S(1)}, bf16[256,768]{1,0:T(8,128)(2,1)}, u32[]{:S(2)}) copy-start(bf16[256,768]{1,0:T(8,128)(2,1)} %get-tuple-element.121.refs_3_.refs_2_.refs_0_) | copy-start | bytes 1179652
  75.2 29.2 %collective-permute-start.13 = (bf16[1536,384]{1,0:T(8,128)(2,1)}, bf16[1536,384]{1,0:T(8,128)(2,1)}, u32[]{:S(2)}, u32[]{:S(2)}) collective-permute-start(bf16[1536,384]{1,0:T(8,128)(2,1)} %get-tuple-element.135.refs_5_), channel_id=1, source_target_pairs={{0,1},{1,0},{2,3},{3,2},{4,5},{5,4},{6,7},{7,6},{8,9},{9,8},{10,11... | collective-permute-start | bytes 3538952 | tf_op jit(solution)/shard_map/ppermute | solution.py:700
  75.7 2.3 %copy-start = (bf16[768,768]{1,0:T(8,128)(2,1)S(1)}, bf16[768,768]{1,0:T(8,128)(2,1)}, u32[]{:S(2)}) copy-start(bf16[768,768]{1,0:T(8,128)(2,1)} %refs_4_.1) | copy-start | bytes 3538948
  77.9 8.6 %collective-permute-start.9 = (bf16[8,288,384]{2,1,0:T(8,128)(2,1)S(1)}, bf16[8,288,384]{2,1,0:T(8,128)(2,1)S(1)}, u32[]{:S(2)}, u32[]{:S(2)}) collective-permute-start(bf16[8,288,384]{2,1,0:T(8,128)(2,1)S(1)} %shard_map.347.refs_11_), channel_id=1, source_target_pairs={{0,8},{8,0},{16,24},{24,16},{1,9},{9,1},{17,25},{25,17},{2,10},{10... | collective-permute-start | bytes 5308424 | tf_op jit(solution)/shard_map/ppermute | solution.py:697
  84.1 22.6 %collective-permute-start.12 = (bf16[320,384]{1,0:T(8,128)(2,1)S(1)}, bf16[320,384]{1,0:T(8,128)(2,1)S(1)}, u32[]{:S(2)}, u32[]{:S(2)}) collective-permute-start(bf16[320,384]{1,0:T(8,128)(2,1)S(1)} %get-tuple-element.141.refs_8_), channel_id=1, source_target_pairs={{0,4},{1,5},{2,6},{3,7},{4,0},{5,1},{6,2},{7,3},{8,12},{9,13},{10,... | collective-permute-start | bytes 737288 | tf_op jit(solution)/shard_map/ppermute | solution.py:700
  89.6 19.9 %collective-permute-start.11 = (bf16[800,384]{1,0:T(8,128)(2,1)S(1)}, bf16[800,384]{1,0:T(8,128)(2,1)S(1)}, u32[]{:S(2)}, u32[]{:S(2)}) collective-permute-start(bf16[800,384]{1,0:T(8,128)(2,1)S(1)} %get-tuple-element.144), channel_id=1, source_target_pairs={{0,16},{8,24},{16,0},{24,8},{1,17},{9,25},{17,1},{25,9},{2,18},{10... | collective-permute-start | bytes 1843208 | tf_op jit(solution)/shard_map/ppermute | solution.py:697
  91.1 28.1 %collective-permute-start.15 = (bf16[896,384]{1,0:T(8,128)(2,1)}, bf16[896,384]{1,0:T(8,128)(2,1)}, u32[]{:S(2)}, u32[]{:S(2)}) collective-permute-start(bf16[896,384]{1,0:T(8,128)(2,1)} %get-tuple-element.147.refs_2_), channel_id=1, source_target_pairs={{0,1},{1,0},{2,3},{3,2},{4,5},{5,4},{6,7},{7,6},{8,9},{9,8},{10,11... | collective-permute-start | bytes 2064392 | tf_op jit(solution)/shard_map/ppermute | solution.py:700
  98.0 12.9 %collective-permute-start.16 = (bf16[640,384]{1,0:T(8,128)(2,1)S(1)}, bf16[640,384]{1,0:T(8,128)(2,1)S(1)}, u32[]{:S(2)}, u32[]{:S(2)}) collective-permute-start(bf16[640,384]{1,0:T(8,128)(2,1)S(1)} %get-tuple-element.148.refs_2_), channel_id=1, source_target_pairs={{0,2},{1,3},{2,0},{3,1},{4,6},{5,7},{6,4},{7,5},{8,10},{9,11},{10,... | collective-permute-start | bytes 1474568 | tf_op jit(solution)/shard_map/ppermute | solution.py:700
  106.0 15.7 %collective-permute-start.20 = (bf16[768,384]{1,0:T(8,128)(2,1)S(1)}, bf16[768,384]{1,0:T(8,128)(2,1)S(1)}, u32[]{:S(2)}, u32[]{:S(2)}) collective-permute-start(bf16[768,384]{1,0:T(8,128)(2,1)S(1)} %get-tuple-element.149.refs_5_), channel_id=1, source_target_pairs={{0,16},{8,24},{16,0},{24,8},{1,17},{9,25},{17,1},{25,9},{2,18},{10... | collective-permute-start | bytes 1769480 | tf_op jit(solution)/shard_map/ppermute | solution.py:697
  110.3 17.6 %collective-permute-start.17 = (bf16[576,384]{1,0:T(8,128)(2,1)S(1)}, bf16[576,384]{1,0:T(8,128)(2,1)S(1)}, u32[]{:S(2)}, u32[]{:S(2)}) collective-permute-start(bf16[576,384]{1,0:T(8,128)(2,1)S(1)} %get-tuple-element.154.refs_2_), channel_id=1, source_target_pairs={{0,1},{1,0},{2,3},{3,2},{4,5},{5,4},{6,7},{7,6},{8,9},{9,8},{10,11... | collective-permute-start | bytes 1327112 | tf_op jit(solution)/shard_map/ppermute | solution.py:700
  111.6 11.9 %collective-permute-start.19 = (bf16[320,384]{1,0:T(8,128)(2,1)S(1)}, bf16[320,384]{1,0:T(8,128)(2,1)S(1)}, u32[]{:S(2)}, u32[]{:S(2)}) collective-permute-start(bf16[320,384]{1,0:T(8,128)(2,1)S(1)} %get-tuple-element.155.refs_3_), channel_id=1, source_target_pairs={{0,4},{1,5},{2,6},{3,7},{4,0},{5,1},{6,2},{7,3},{8,12},{9,13},{10,... | collective-permute-start | bytes 737288 | tf_op jit(solution)/shard_map/ppermute | solution.py:700
  120.4 5.5 %collective-permute-start.18 = (bf16[192,384]{1,0:T(8,128)(2,1)S(1)}, bf16[192,384]{1,0:T(8,128)(2,1)S(1)}, u32[]{:S(2)}, u32[]{:S(2)}) collective-permute-start(bf16[192,384]{1,0:T(8,128)(2,1)S(1)} %get-tuple-element.159.refs_4_), channel_id=1, source_target_pairs={{0,16},{8,24},{16,0},{24,8},{1,17},{9,25},{17,1},{25,9},{2,18},{10... | collective-permute-start | bytes 442376 | tf_op jit(solution)/shard_map/ppermute | solution.py:697
  121.0 15.5 %collective-permute-start.22 = (bf16[256,384]{1,0:T(8,128)(2,1)S(1)}, bf16[256,384]{1,0:T(8,128)(2,1)S(1)}, u32[]{:S(2)}, u32[]{:S(2)}) collective-permute-start(bf16[256,384]{1,0:T(8,128)(2,1)S(1)} %get-tuple-element.168), channel_id=1, source_target_pairs={{0,2},{1,3},{2,0},{3,1},{4,6},{5,7},{6,4},{7,5},{8,10},{9,11},{10,... | collective-permute-start | bytes 589832 | tf_op jit(solution)/shard_map/ppermute | solution.py:700
  124.3 10.9 %collective-permute-start.23 = (bf16[384,384]{1,0:T(8,128)(2,1)S(1)}, bf16[384,384]{1,0:T(8,128)(2,1)S(1)}, u32[]{:S(2)}, u32[]{:S(2)}) collective-permute-start(bf16[384,384]{1,0:T(8,128)(2,1)S(1)} %get-tuple-element.162.refs_6_), channel_id=1, source_target_pairs={{0,2},{1,3},{2,0},{3,1},{4,6},{5,7},{6,4},{7,5},{8,10},{9,11},{10,... | collective-permute-start | bytes 884744 | tf_op jit(solution)/shard_map/ppermute | solution.py:700
  124.4 17.2 %collective-permute-start.26 = (bf16[160,384]{1,0:T(8,128)(2,1)S(1)}, bf16[160,384]{1,0:T(8,128)(2,1)S(1)}, u32[]{:S(2)}, u32[]{:S(2)}) collective-permute-start(bf16[160,384]{1,0:T(8,128)(2,1)S(1)} %get-tuple-element.179), channel_id=1, source_target_pairs={{0,1},{1,0},{2,3},{3,2},{4,5},{5,4},{6,7},{7,6},{8,9},{9,8},{10,11... | collective-permute-start | bytes 368648 | tf_op jit(solution)/shard_map/ppermute | solution.py:700
  128.6 12.3 %collective-permute-start.21 = (bf16[320,384]{1,0:T(8,128)(2,1)S(1)}, bf16[320,384]{1,0:T(8,128)(2,1)S(1)}, u32[]{:S(2)}, u32[]{:S(2)}) collective-permute-start(bf16[320,384]{1,0:T(8,128)(2,1)S(1)} %get-tuple-element.167.refs_2_), channel_id=1, source_target_pairs={{0,2},{1,3},{2,0},{3,1},{4,6},{5,7},{6,4},{7,5},{8,10},{9,11},{10,... | collective-permute-start | bytes 737288 | tf_op jit(solution)/shard_map/ppermute | solution.py:700
  128.7 12.9 %collective-permute-start.27 = (bf16[80,384]{1,0:T(8,128)(2,1)S(1)}, bf16[80,384]{1,0:T(8,128)(2,1)S(1)}, u32[]{:S(2)}, u32[]{:S(2)}) collective-permute-start(bf16[80,384]{1,0:T(8,128)(2,1)S(1)} %get-tuple-element.180), channel_id=1, source_target_pairs={{0,16},{8,24},{16,0},{24,8},{1,17},{9,25},{17,1},{25,9},{2,18},{10... | collective-permute-start | bytes 184328 | tf_op jit(solution)/shard_map/ppermute | solution.py:697
  135.8 8.1 %collective-permute-start.25 = (bf16[192,384]{1,0:T(8,128)(2,1)S(1)}, bf16[192,384]{1,0:T(8,128)(2,1)S(1)}, u32[]{:S(2)}, u32[]{:S(2)}) collective-permute-start(bf16[192,384]{1,0:T(8,128)(2,1)S(1)} %get-tuple-element.170.refs_6_), channel_id=1, source_target_pairs={{0,4},{1,5},{2,6},{3,7},{4,0},{5,1},{6,2},{7,3},{8,12},{9,13},{10,... | collective-permute-start | bytes 442376 | tf_op jit(solution)/shard_map/ppermute | solution.py:700
  144.5 5.3 %collective-permute-start.28 = (bf16[192,384]{1,0:T(8,128)(2,1)S(1)}, bf16[192,384]{1,0:T(8,128)(2,1)S(1)}, u32[]{:S(2)}, u32[]{:S(2)}) collective-permute-start(bf16[192,384]{1,0:T(8,128)(2,1)S(1)} %shard_map.361), channel_id=1, source_target_pairs={{0,16},{8,24},{16,0},{24,8},{1,17},{9,25},{17,1},{25,9},{2,18},{10... | collective-permute-start | bytes 442376 | tf_op jit(solution)/shard_map/ppermute | solution.py:697
  146.1 5.7 %collective-permute-start.30 = (bf16[240,384]{1,0:T(8,128)(2,1)S(1)}, bf16[240,384]{1,0:T(8,128)(2,1)S(1)}, u32[]{:S(2)}, u32[]{:S(2)}) collective-permute-start(bf16[240,384]{1,0:T(8,128)(2,1)S(1)} %get-tuple-element.181.refs_2_), channel_id=1, source_target_pairs={{0,16},{8,24},{16,0},{24,8},{1,17},{9,25},{17,1},{25,9},{2,18},{10... | collective-permute-start | bytes 552968 | tf_op jit(solution)/shard_map/ppermute | solution.py:697
  146.6 10.3 %collective-permute-start.24 = (bf16[304,384]{1,0:T(8,128)(2,1)S(1)}, bf16[304,384]{1,0:T(8,128)(2,1)S(1)}, u32[]{:S(2)}, u32[]{:S(2)}) collective-permute-start(bf16[304,384]{1,0:T(8,128)(2,1)S(1)} %get-tuple-element.175.refs_4_), channel_id=1, source_target_pairs={{0,4},{1,5},{2,6},{3,7},{4,0},{5,1},{6,2},{7,3},{8,12},{9,13},{10,... | collective-permute-start | bytes 700424 | tf_op jit(solution)/shard_map/ppermute | solution.py:700
  149.9 2.1 %collective-permute-start.29 = (bf16[384,384]{1,0:T(8,128)(2,1)S(1)}, bf16[384,384]{1,0:T(8,128)(2,1)S(1)}, u32[]{:S(2)}, u32[]{:S(2)}) collective-permute-start(bf16[384,384]{1,0:T(8,128)(2,1)S(1)} %pad_maximum_fusion.1), channel_id=1, source_target_pairs={{0,8},{8,0},{16,24},{24,16},{1,9},{9,1},{17,25},{25,17},{2,10},{10... | collective-permute-start | bytes 884744 | tf_op jit(solution)/shard_map/ppermute | solution.py:697
  152.0 1.8 %collective-permute-start.31 = (bf16[480,384]{1,0:T(8,128)(2,1)S(1)}, bf16[480,384]{1,0:T(8,128)(2,1)S(1)}, u32[]{:S(2)}, u32[]{:S(2)}) collective-permute-start(bf16[480,384]{1,0:T(8,128)(2,1)S(1)} %pad_maximum_fusion), channel_id=1, source_target_pairs={{0,8},{8,0},{16,24},{24,16},{1,9},{9,1},{17,25},{25,17},{2,10},{10... | collective-permute-start | bytes 1105928 | tf_op jit(solution)/shard_map/ppermute | solution.py:697
  152.3 4.6 %copy-start.4 = (f32[96,3072]{1,0:T(8,128)}, f32[96,3072]{1,0:T(8,128)S(1)}, u32[]{:S(2)}) copy-start(f32[96,3072]{1,0:T(8,128)S(1)} %slice_dynamic-update-slice_fusion.refs_5_) | copy-start | bytes 3538948
  154.1 3.4 %copy-start.2 = (f32[384,768]{1,0:T(8,128)}, f32[384,768]{1,0:T(8,128)S(1)}, u32[]{:S(2)}) copy-start(f32[384,768]{1,0:T(8,128)S(1)} %maximum_maximum_fusion.refs_6_) | copy-start | bytes 3538948
  157.6 5.1 %collective-permute-start.33 = (bf16[144,384]{1,0:T(8,128)(2,1)S(1)}, bf16[144,384]{1,0:T(8,128)(2,1)S(1)}, u32[]{:S(2)}, u32[]{:S(2)}) collective-permute-start(bf16[144,384]{1,0:T(8,128)(2,1)S(1)} %constant_dynamic-update-slice_fusion), channel_id=1, source_target_pairs={{0,16},{8,24},{16,0},{24,8},{1,17},{9,25},{17,1},{25,9},{2,18},{10... | collective-permute-start | bytes 331784 | tf_op jit(solution)/shard_map/ppermute | solution.py:697
  159.2 5.3 %collective-permute-start.34 = (bf16[144,384]{1,0:T(8,128)(2,1)S(1)}, bf16[144,384]{1,0:T(8,128)(2,1)S(1)}, u32[]{:S(2)}, u32[]{:S(2)}) collective-permute-start(bf16[144,384]{1,0:T(8,128)(2,1)S(1)} %constant_dynamic-update-slice_fusion), channel_id=1, source_target_pairs={{0,24},{8,16},{16,8},{24,0},{1,25},{9,17},{17,9},{25,1},{2,26},{10... | collective-permute-start | bytes 331784 | tf_op jit(solution)/shard_map/ppermute | solution.py:697
  159.2 5.3 %collective-permute-start.32 = (bf16[176,384]{1,0:T(8,128)(2,1)S(1)}, bf16[176,384]{1,0:T(8,128)(2,1)S(1)}, u32[]{:S(2)}, u32[]{:S(2)}) collective-permute-start(bf16[176,384]{1,0:T(8,128)(2,1)S(1)} %pad_maximum_fusion.5), channel_id=1, source_target_pairs={{0,8},{8,0},{16,24},{24,16},{1,9},{9,1},{17,25},{25,17},{2,10},{10... | collective-permute-start | bytes 405512 | tf_op jit(solution)/shard_map/ppermute | solution.py:697
  (13 other events, 21.4 us)

commit v6 on v5

--- a/solution.py
+++ b/solution.py
@@ -449,7 +449,7 @@
             jax.ShapeDtypeStruct((width, n_keys), BF),
             jax.ShapeDtypeStruct((width, n_keys), BF),
         ],
-        compiler_params=pltpu.CompilerParams(vmem_limit_bytes=vmem_limit(n_keys, 60)),
+        compiler_params=pltpu.CompilerParams(vmem_limit_bytes=vmem_limit(n_keys, 54)),
         cost_estimate=LONG,
     )(queries, keys, values, prob, context, grad_context, *after)
 
@@ -790,12 +790,11 @@
             pos, [("part", up_kept, up_got, 0, planes, ff_out // 2, 1, 0)], after=(down_sent,)
         )
         up_got = swap_grp(up_sent, 2)
-        (first_kept, vectors, z_kept), (first_sent,) = combine(
+        (first_kept, vectors), (first_sent,) = combine(
             pos,
             [
                 ("part", first_kept, first_got, 0, planes, n_out, 2, 0),
                 ("vec", vectors, first_got, n_first, 0, 0, None, 0),
-                ("part", z_kept, z_got, 0, 1, z_rows, 2, 0),
             ],
             after=(up_sent,),
         )
@@ -814,32 +813,37 @@
         )
         value_got = swap_grp(value_sent, 2)
         table_got = swap_blk(table_sent, 2)
-        (down_kept, up_kept), (down_sent, up_sent) = combine(
+        (down_kept, z_kept, up_kept), (down_sent, up_sent) = combine(
             pos,
             [
                 ("part", down_kept, down_got, 0, 1, part, 2, 0),
+                ("part", z_kept, z_got, 0, 1, z_rows, 2, 0),
                 ("part", up_kept, up_got, 0, 2, ff_out // 2, 3, 1),
             ],
             after=(value_sent,),
         )
         down_got = swap_blk(down_sent, 1)
         up_got = swap_blk(up_sent, 2)
-        (first_kept, value_kept, vectors, z_kept), (first_sent, z_sent) = combine(
+        (first_kept, value_kept, vectors), (first_sent,) = combine(
             pos,
             [
                 ("part", first_kept, first_got, 0, 2, n_out, 3, 0),
                 ("part", value_kept, value_got, 0, 2, n_out // 2, 3, 0),
                 ("vec", vectors, first_got, n_value, 0, 0, None, 0),
-                ("part", z_kept, first_got, n_value + 32, 1, z_rows // 2, 1, 1),
             ],
             after=(up_sent,),
         )
         first_got = swap_blk(first_sent, 2)
+        (up_kept, z_kept), (up_sent, z_sent) = combine(
+            pos,
+            [
+                ("part", up_kept, up_got, 0, 1, ff_out // 2, 4, 0),
+                ("part", z_kept, down_got, part, 1, z_rows // 2, 1, 1),
+            ],
+            after=(first_sent,),
+        )
+        up_got = swap_blk(up_sent, 4)
         z_got = swap_grp(z_sent, 2)
-        (up_kept,), (up_sent,) = combine(
-            pos, [("part", up_kept, up_got, 0, 1, ff_out // 2, 4, 0)], after=(first_sent,)
-        )
-        up_got = swap_blk(up_sent, 4)
         (first_kept, value_kept, table_kept, vectors), (first_sent,) = combine(
             pos,
             [

time: 168 us -> 167 us (level)
  waiting for transfers between devices: 52 us -> 47.7 us
  starting transfers between devices: 33.8 us -> 35.6 us
    ppermute x20, waiting for transfers between devices: 35.6 us -> 33.1 us  [swap_blk(): return lax.ppermute(value, 'blk', [(i, i ^ mask) for i in range(blocks)])]
    ppermute x15, waiting for transfers between devices: 16.4 us -> 14.6 us  [swap_grp(): return lax.ppermute(value, 'grp', [(i, i ^ mask) for i in range(grps)])]
  transfers between devices with their start and end apart: 35 -> 35, of which waited for: 18 -> 17; matrix products, arithmetic and copies ran while one was open for 2% -> 2% of each run, Pallas kernels for 23% -> 23%
where the time goes in v6:
time: 167 us; the launch traced here: 165 us
  Pallas kernels  70.1 us (42%)
  waiting for transfers between devices  47.7 us (29%)
  starting transfers between devices  35.6 us (21%)
  local copies, waits for them, and re-layouts  7 us (4%)
  other arithmetic  3.1 us (2%)
    ppermute x20, waiting for transfers between devices, swap_blk(): return lax.ppermute(value, 'blk', [(i, i ^ mask) for i in range(blocks)])  33.1 us
    ppermute x20, starting transfers between devices, swap_blk(): return lax.ppermute(value, 'blk', [(i, i ^ mask) for i in range(blocks)])  24.7 us
    pallas_call x1, Pallas kernels, middle_part(): pl.pallas_call(lambda *refs: middle_kernel(packets, *refs), in_specs=[pl....  17.8 us
    pallas_call x15, Pallas kernels, combine(): pl.pallas_call(body, in_specs=[pl.BlockSpec(memory_space=pltpu.SMEM)] + [...  17.3 us
    ppermute x15, waiting for transfers between devices, swap_grp(): return lax.ppermute(value, 'grp', [(i, i ^ mask) for i in range(grps)])  14.6 us
    ppermute x15, starting transfers between devices, swap_grp(): return lax.ppermute(value, 'grp', [(i, i ^ mask) for i in range(grps)])  10.9 us
    pallas_call x1, Pallas kernels, attend(): pl.pallas_call(lambda *refs: attend_kernel(views, *refs), grid=(width //...  10.4 us
    pallas_call x1, Pallas kernels, attend_back(): pl.pallas_call(attend_back_kernel, grid=(width // group,), in_specs=[lane...  8.55 us
  transfers between devices with their start and end apart: 35, of which 17 were waited for; matrix products, arithmetic and copies ran while one was open for 2% of the time, Pallas kernels for 23%

profile of v6, /device:TPU:0, one launch (start us, length us, event | category | flops | bytes accessed | tf_op | source)
XLA Modules:
  0.0 164.9 jit_solution(1632904195695193077)
XLA Ops:
  0.7 2.0 %shard_map.340 = (bf16[80,768]{1,0:T(8,128)(2,1)}, bf16[256,768]{1,0:T(8,128)(2,1)}) custom-call(bf16[256,768]{1,0:T(8,128)(2,1)} %refs_1_.3, s32[256]{0:T(256)} %seg_any.3, s32[256]{0:T(256)} %refs_7_.3, bf16[2,768]{1,0:T(2,128)(2,1)} %refs_3_.2), custom_call_target="tpu_custom_call" | custom-call | tf_op jit(solution)/shard_map/pallas_call | solution.py:97
  2.7 3.1 %collective-permute-start.1 = (bf16[80,768]{1,0:T(8,128)(2,1)}, bf16[80,768]{1,0:T(8,128)(2,1)S(1)}, u32[]{:S(2)}, u32[]{:S(2)}) collective-permute-start(bf16[80,768]{1,0:T(8,128)(2,1)} %get-tuple-element.114.refs_8_), channel_id=1, source_target_pairs={{0,2},{1,3},{2,0},{3,1},{4,6},{5,7},{6,4},{7,5},{8,10},{9,11},{10,... | collective-permute-start | bytes 368648 | tf_op jit(solution)/shard_map/ppermute | solution.py:700
  5.8 2.6 %collective-permute-start.3 = (bf16[80,768]{1,0:T(8,128)(2,1)}, bf16[80,768]{1,0:T(8,128)(2,1)S(1)}, u32[]{:S(2)}, u32[]{:S(2)}) collective-permute-start(bf16[80,768]{1,0:T(8,128)(2,1)} %get-tuple-element.114.refs_8_), channel_id=1, source_target_pairs={{0,4},{1,5},{2,6},{3,7},{4,0},{5,1},{6,2},{7,3},{8,12},{9,13},{10,... | collective-permute-start | bytes 368648 | tf_op jit(solution)/shard_map/ppermute | solution.py:700
  8.4 1.7 %collective-permute-start = (bf16[80,768]{1,0:T(8,128)(2,1)}, bf16[80,768]{1,0:T(8,128)(2,1)S(1)}, u32[]{:S(2)}, u32[]{:S(2)}) collective-permute-start(bf16[80,768]{1,0:T(8,128)(2,1)} %get-tuple-element.114.refs_8_), channel_id=1, source_target_pairs={{0,1},{1,0},{2,3},{3,2},{4,5},{5,4},{6,7},{7,6},{8,9},{9,8},{10,11... | collective-permute-start | bytes 368648 | tf_op jit(solution)/shard_map/ppermute | solution.py:700
  10.7 1.7 %collective-permute-start.2 = (bf16[80,768]{1,0:T(8,128)(2,1)S(1)}, bf16[80,768]{1,0:T(8,128)(2,1)S(1)}, u32[]{:S(2)}, u32[]{:S(2)}) collective-permute-start(bf16[80,768]{1,0:T(8,128)(2,1)S(1)} %collective-permute-done.1.refs_10_), channel_id=1, source_target_pairs={{0,1},{1,0},{2,3},{3,2},{4,5},{5,4},{6,7},{7,6},{8,9},{9,8},{10,11... | collective-permute-start | bytes 368648 | tf_op jit(solution)/shard_map/ppermute | solution.py:700
  12.4 5.9 %collective-permute-done.3.refs_12_ = bf16[80,768]{1,0:T(8,128)(2,1)S(1)} collective-permute-done((bf16[80,768]{1,0:T(8,128)(2,1)}, bf16[80,768]{1,0:T(8,128)(2,1)S(1)}, u32[]{:S(2)}, u32[]{:S(2)}) %collective-permute-start.3) | collective-permute-done | bytes 122912 | tf_op jit(solution)/shard_map/ppermute | solution.py:700
  18.3 1.5 collective-permute-start.4
  21.0 4.9 %shard_map.341 = (bf16[256,768]{1,0:T(8,128)(2,1)}, bf16[256,768]{1,0:T(8,128)(2,1)}, bf16[256,768]{1,0:T(8,128)(2,1)}, f32[256,256]{1,0:T(8,128)}, f32[1,768]{1,0:T(1,128)}) custom-call(bf16[256,768]{1,0:T(8,128)(2,1)} %get-tuple-element.108.input_ref.refs_0_, bf16[768,768]{1,0:T(8,128)(2,1)} %refs_3_.3, bf16[768,768]{1,0:T(8,128)(2,1)} %refs_4_.1, ...), custom_call_target="tpu_custom_call" | custom-call | flops 100000000 | bytes 1048576 | tf_op jit(solution)/shard_map/pallas_call | solution.py:133
  26.7 10.4 %shard_map.342 = (bf16[768,768]{1,0:T(8,128)(2,1)}, bf16[768,768]{1,0:T(8,128)(2,1)}, bf16[12,256,768]{2,1,0:T(8,128)(2,1)}, f32[256,768]{1,0:T(8,128)}, bf16[768,768]{1,0:T(8,128)(2,1)}, /*index=5*/f32[8,512]{1,0:T(8,128)}) custom-call(bf16[256,768]{1,0:T(8,128)(2,1)} %get-tuple-element.108.input_ref.refs_0_, bf16[768,768]{1,0:T(8,128)(2,1)} %refs_4_.1, ...), custom_call_target="tpu_custom_call" | custom-call | flops 100000000 | bytes 1048576 | tf_op jit(solution)/shard_map/pallas_call | solution.py:206
  37.1 17.8 %shard_map.343 = (bf16[256,768]{1,0:T(8,128)(2,1)}, bf16[256,768]{1,0:T(8,128)(2,1)}, f32[256,768]{1,0:T(8,128)}, f32[8,768]{1,0:T(8,128)}, f32[1,3072]{1,0:T(1,...) custom-call(s32[5]{0:T(128)} %stack.23.refs_0_.pos_ref, ...), custom_call_target="tpu_custom_call" | custom-call | flops 100000000 | bytes 1048576 | tf_op jit(solution)/shard_map/pallas_call | solution.py:398
  55.6 8.6 %shard_map.344 = (bf16[256,768]{1,0:T(8,128)(2,1)}, bf16[768,768]{1,0:T(8,128)(2,1)}, bf16[768,768]{1,0:T(8,128)(2,1)}) custom-call(bf16[256,768]{1,0:T(8,128)(2,1)} %get-tuple-element.110.refs_4_.q_ref, bf16[768,768]{1,0:T(8,128)(2,1)} %get-tuple-element.117.keys_ref, bf16[768,768]{1,0:T(8,128)(2,1)} %get-tuple-element.118.values_ref, ...), custom_call_target="tpu_custom_call" | custom-call | flops 40000000000 | bytes 1048576 | tf_op jit(solution)/shard_map/pallas_call | solution.py:438
  64.2 1.5 copy-done.8
  66.7 2.1 %shard_map.345 = (bf16[1280,384]{1,0:T(8,128)(2,1)S(1)}, bf16[640,384]{1,0:T(8,128)(2,1)S(1)}, bf16[1280,384]{1,0:T(8,128)(2,1)}, bf16[640,384]{1,0:T(8,128)(2,1)S(1)}) custom-call(s32[5]{0:T(128)S(1)} %copy-done.6, bf16[2560,384]{1,0:T(8,128)(2,1)S(1)} %copy-done.8, bf16[1280,384]{1,0:T(8,128)(2,1)S(1)} %copy-done.10, ...), custom_call_target="tpu_custom_call" | custom-call | flops 40000000000 | bytes 1048576 | tf_op jit(solution)/shard_map/pallas_call | solution.py:642
  68.8 1.4 collective-permute-start.10
  70.2 1.5 collective-permute-start.13
  71.7 2.2 %shard_map.346 = (bf16[1536,384]{1,0:T(8,128)(2,1)S(1)}, bf16[1536,384]{1,0:T(8,128)(2,1)}) custom-call(s32[5]{0:T(128)S(1)} %copy-done.6, bf16[3072,384]{1,0:T(8,128)(2,1)S(1)} %copy-done.7, bf16[3072,384]{1,0:T(8,128)(2,1)S(1)} %collective-permute-done.7.refs_1_, bf16[1280,384]{1,0:T(8,128)(2,1)} %get-tuple-element.134.refs_2_), custom_call_target="tpu_custom_call" | custom-call | flops 40000000000 | bytes 1048576 | tf_op jit(solution)/shard_map/pallas_call | solution.py:642
  74.5 2.1 %shard_map.347.refs_11_ = bf16[8,288,384]{2,1,0:T(8,128)(2,1)S(1)} custom-call(s32[5]{0:T(128)S(1)} %copy-done.6, bf16[768,768]{1,0:T(8,128)(2,1)S(1)} %copy-done.9, bf16[256,768]{1,0:T(8,128)(2,1)S(1)} %copy-done.18, bf16[768,768]{1,0:T(8,128)(2,1)S(1)} %copy-done.15, bf16[768,768]{1,0:T(8,128)(2,1)S(1)} %copy-done.16, ...), custom_call_target="tpu_custom_call" | custom-call | flops 40000000000 | bytes 1048576 | tf_op jit(solution)/shard_map/pallas_call | solution.py:664
  76.8 3.8 %shard_map.348 = (bf16[512,384]{1,0:T(8,128)(2,1)S(1)}, bf16[512,384]{1,0:T(8,128)(2,1)S(1)}, f32[256,768]{1,0:T(8,128)}, f32[32,384]{1,0:T(8,128)S(1)}) custom-call(bf16[256,768]{1,0:T(8,128)(2,1)S(1)} %copy-done.18, bf16[768,768]{1,0:T(8,128)(2,1)S(1)} %copy-done.15, bf16[768,768]{1,0:T(8,128)(2,1)S(1)} %copy-done.16, bf16[768,768]{1,0:T(8,128)(2,1)S(1)} %copy-done.3, ...), custom_call_target="tpu_custom_call" | custom-call | flops 40000000000 | bytes 1048576 | tf_op jit(solution)/shard_map/pallas_call | solution.py:571
  80.6 1.4 collective-permute-done.10.refs_1_
  82.0 1.4 shard_map.349
  83.4 2.4 %collective-permute-start.19 = (bf16[320,384]{1,0:T(8,128)(2,1)}, bf16[320,384]{1,0:T(8,128)(2,1)}, u32[]{:S(2)}, u32[]{:S(2)}) collective-permute-start(bf16[320,384]{1,0:T(8,128)(2,1)} %get-tuple-element.141.refs_8_), channel_id=1, source_target_pairs={{0,4},{1,5},{2,6},{3,7},{4,0},{5,1},{6,2},{7,3},{8,12},{9,13},{10,... | collective-permute-start | bytes 737288 | tf_op jit(solution)/shard_map/ppermute | solution.py:700
  85.7 3.1 %shard_map.350 = (bf16[768,384]{1,0:T(8,128)(2,1)S(1)}, bf16[800,384]{1,0:T(8,128)(2,1)S(1)}, bf16[384,384]{1,0:T(8,128)(2,1)S(1)}, bf16[896,384]{1,0:T(8,128)(2,1)}) custom-call(s32[5]{0:T(128)S(1)} %copy-done.6, bf16[768,768]{1,0:T(8,128)(2,1)S(1)} %copy-done.9, bf16[256,768]{1,0:T(8,128)(2,1)S(1)} %copy-done.18, bf16[768,768]{1,0:T(8,128)(2,1)S(1)} %copy-done.15, ...), custom_call_target="tpu_custom_call" | custom-call | flops 40000000000 | bytes 1048576 | tf_op jit(solution)/shard_map/pallas_call | solution.py:664
  88.8 1.5 collective-permute-start.11
  90.8 4.3 %collective-permute-done.13.refs_1_ = bf16[1280,384]{1,0:T(8,128)(2,1)} collective-permute-done((bf16[1280,384]{1,0:T(8,128)(2,1)}, bf16[1280,384]{1,0:T(8,128)(2,1)}, u32[]{:S(2)}, u32[]{:S(2)}) %collective-permute-start.13) | collective-permute-done | bytes 983072 | tf_op jit(solution)/shard_map/ppermute | solution.py:697
  95.1 1.5 shard_map.351
  97.4 5.7 %collective-permute-done.12.refs_1_ = bf16[1536,384]{1,0:T(8,128)(2,1)} collective-permute-done((bf16[1536,384]{1,0:T(8,128)(2,1)}, bf16[1536,384]{1,0:T(8,128)(2,1)}, u32[]{:S(2)}, u32[]{:S(2)}) %collective-permute-start.12) | collective-permute-done | bytes 1179680 | tf_op jit(solution)/shard_map/ppermute | solution.py:700
  103.1 1.7 %shard_map.352 = (bf16[768,384]{1,0:T(8,128)(2,1)S(1)}, bf16[768,384]{1,0:T(8,128)(2,1)S(1)}) custom-call(s32[5]{0:T(128)S(1)} %copy-done.6, bf16[1536,384]{1,0:T(8,128)(2,1)S(1)} %get-tuple-element.144.refs_0_, bf16[1536,384]{1,0:T(8,128)(2,1)} %collective-permute-done.12.refs_1_, bf16[640,384]{1,0:T(8,128)(2,1)S(1)} %get-tuple-element.147.refs_2_), custom_call_target="tpu_custom_call" | custom-call | flops 40000000000 | bytes 1048576 | tf_op jit(solution)/shard_map/pallas_call | solution.py:642
  105.4 2.8 %collective-permute-done.11.refs_2_ = bf16[800,384]{1,0:T(8,128)(2,1)S(1)} collective-permute-done((bf16[800,384]{1,0:T(8,128)(2,1)S(1)}, bf16[800,384]{1,0:T(8,128)(2,1)S(1)}, u32[]{:S(2)}, u32[]{:S(2)}) %collective-permute-start.11) | collective-permute-done | bytes 614432 | tf_op jit(solution)/shard_map/ppermute | solution.py:697
  110.2 2.6 %collective-permute-start.18 = (bf16[320,384]{1,0:T(8,128)(2,1)S(1)}, bf16[320,384]{1,0:T(8,128)(2,1)S(1)}, u32[]{:S(2)}, u32[]{:S(2)}) collective-permute-start(bf16[320,384]{1,0:T(8,128)(2,1)S(1)} %get-tuple-element.154.refs_3_), channel_id=1, source_target_pairs={{0,4},{1,5},{2,6},{3,7},{4,0},{5,1},{6,2},{7,3},{8,12},{9,13},{10,... | collective-permute-start | bytes 737288 | tf_op jit(solution)/shard_map/ppermute | solution.py:700
  112.9 5.0 %collective-permute-done.14.refs_2_ = bf16[896,384]{1,0:T(8,128)(2,1)} collective-permute-done((bf16[896,384]{1,0:T(8,128)(2,1)}, bf16[896,384]{1,0:T(8,128)(2,1)}, u32[]{:S(2)}, u32[]{:S(2)}) %collective-permute-start.14) | collective-permute-done | bytes 688160 | tf_op jit(solution)/shard_map/ppermute | solution.py:700
  117.8 1.3 shard_map.355
  120.4 1.5 collective-permute-done.18.refs_3_
  122.0 1.3 shard_map.356
  123.3 1.6 collective-permute-start.24
  125.6 2.0 %collective-permute-start.21 = (bf16[320,384]{1,0:T(8,128)(2,1)S(1)}, bf16[320,384]{1,0:T(8,128)(2,1)S(1)}, u32[]{:S(2)}, u32[]{:S(2)}) collective-permute-start(bf16[320,384]{1,0:T(8,128)(2,1)S(1)} %get-tuple-element.166.refs_4_), channel_id=1, source_target_pairs={{0,2},{1,3},{2,0},{3,1},{4,6},{5,7},{6,4},{7,5},{8,10},{9,11},{10,... | collective-permute-start | bytes 737288 | tf_op jit(solution)/shard_map/ppermute | solution.py:700
  127.6 2.6 %collective-permute-done.24.refs_3_.refs_2_ = bf16[320,384]{1,0:T(8,128)(2,1)S(1)} collective-permute-done((bf16[320,384]{1,0:T(8,128)(2,1)S(1)}, bf16[320,384]{1,0:T(8,128)(2,1)S(1)}, u32[]{:S(2)}, u32[]{:S(2)}) %collective-permute-start.24) | collective-permute-done | bytes 245792 | tf_op jit(solution)/shard_map/ppermute | solution.py:700
  130.2 3.5 %collective-permute-done.23.refs_2_ = bf16[384,384]{1,0:T(8,128)(2,1)S(1)} collective-permute-done((bf16[384,384]{1,0:T(8,128)(2,1)S(1)}, bf16[384,384]{1,0:T(8,128)(2,1)S(1)}, u32[]{:S(2)}, u32[]{:S(2)}) %collective-permute-start.23) | collective-permute-done | bytes 294944 | tf_op jit(solution)/shard_map/ppermute | solution.py:700
  134.4 1.6 collective-permute-start.27
  136.5 2.7 %collective-permute-done.21.refs_4_ = bf16[320,384]{1,0:T(8,128)(2,1)S(1)} collective-permute-done((bf16[320,384]{1,0:T(8,128)(2,1)S(1)}, bf16[320,384]{1,0:T(8,128)(2,1)S(1)}, u32[]{:S(2)}, u32[]{:S(2)}) %collective-permute-start.21) | collective-permute-done | bytes 245792 | tf_op jit(solution)/shard_map/ppermute | solution.py:700
  139.9 1.2 shard_map.360
  141.1 1.9 %collective-permute-done.26.refs_1_ = bf16[192,384]{1,0:T(8,128)(2,1)S(1)} collective-permute-done((bf16[192,384]{1,0:T(8,128)(2,1)S(1)}, bf16[192,384]{1,0:T(8,128)(2,1)S(1)}, u32[]{:S(2)}, u32[]{:S(2)}) %collective-permute-start.26) | collective-permute-done | bytes 147488 | tf_op jit(solution)/shard_map/ppermute | solution.py:700
  143.6 1.3 collective-permute-start.28
  145.7 3.1 %collective-permute-done.28 = bf16[192,384]{1,0:T(8,128)(2,1)S(1)} collective-permute-done((bf16[192,384]{1,0:T(8,128)(2,1)S(1)}, bf16[192,384]{1,0:T(8,128)(2,1)S(1)}, u32[]{:S(2)}, u32[]{:S(2)}) %collective-permute-start.28) | collective-permute-done | bytes 147488 | tf_op jit(solution)/shard_map/ppermute | solution.py:697
  149.0 1.8 %collective-permute-done.30 = bf16[240,384]{1,0:T(8,128)(2,1)S(1)} collective-permute-done((bf16[240,384]{1,0:T(8,128)(2,1)S(1)}, bf16[240,384]{1,0:T(8,128)(2,1)S(1)}, u32[]{:S(2)}, u32[]{:S(2)}) %collective-permute-start.30) | collective-permute-done | bytes 184352 | tf_op jit(solution)/shard_map/ppermute | solution.py:697
  151.3 1.4 collective-permute-done.31
  153.1 2.2 %collective-permute-done.25.refs_4_ = bf16[304,384]{1,0:T(8,128)(2,1)S(1)} collective-permute-done((bf16[304,384]{1,0:T(8,128)(2,1)S(1)}, bf16[304,384]{1,0:T(8,128)(2,1)S(1)}, u32[]{:S(2)}, u32[]{:S(2)}) %collective-permute-start.25) | collective-permute-done | bytes 233504 | tf_op jit(solution)/shard_map/ppermute | solution.py:700
  156.7 1.5 collective-permute-start.32
  158.2 1.6 fusion
  (152 shorter events, 20.9 us)
Async XLA Ops:
  2.7 8.0 %collective-permute-start.1 = (bf16[80,768]{1,0:T(8,128)(2,1)}, bf16[80,768]{1,0:T(8,128)(2,1)S(1)}, u32[]{:S(2)}, u32[]{:S(2)}) collective-permute-start(bf16[80,768]{1,0:T(8,128)(2,1)} %get-tuple-element.114.refs_8_), channel_id=1, source_target_pairs={{0,2},{1,3},{2,0},{3,1},{4,6},{5,7},{6,4},{7,5},{8,10},{9,11},{10,... | collective-permute-start | bytes 368648 | tf_op jit(solution)/shard_map/ppermute | solution.py:700
  5.8 12.5 %collective-permute-start.3 = (bf16[80,768]{1,0:T(8,128)(2,1)}, bf16[80,768]{1,0:T(8,128)(2,1)S(1)}, u32[]{:S(2)}, u32[]{:S(2)}) collective-permute-start(bf16[80,768]{1,0:T(8,128)(2,1)} %get-tuple-element.114.refs_8_), channel_id=1, source_target_pairs={{0,4},{1,5},{2,6},{3,7},{4,0},{5,1},{6,2},{7,3},{8,12},{9,13},{10,... | collective-permute-start | bytes 368648 | tf_op jit(solution)/shard_map/ppermute | solution.py:700
  8.4 11.5 %collective-permute-start.5 = (bf16[80,768]{1,0:T(8,128)(2,1)}, bf16[80,768]{1,0:T(8,128)(2,1)S(1)}, u32[]{:S(2)}, u32[]{:S(2)}) collective-permute-start(bf16[80,768]{1,0:T(8,128)(2,1)} %get-tuple-element.114.refs_8_), channel_id=1, source_target_pairs={{0,6},{1,7},{2,4},{3,5},{4,2},{5,3},{6,0},{7,1},{8,14},{9,15},{10,... | collective-permute-start | bytes 368648 | tf_op jit(solution)/shard_map/ppermute | solution.py:700
  8.4 17.5 %collective-permute-start = (bf16[80,768]{1,0:T(8,128)(2,1)}, bf16[80,768]{1,0:T(8,128)(2,1)S(1)}, u32[]{:S(2)}, u32[]{:S(2)}) collective-permute-start(bf16[80,768]{1,0:T(8,128)(2,1)} %get-tuple-element.114.refs_8_), channel_id=1, source_target_pairs={{0,1},{1,0},{2,3},{3,2},{4,5},{5,4},{6,7},{7,6},{8,9},{9,8},{10,11... | collective-permute-start | bytes 368648 | tf_op jit(solution)/shard_map/ppermute | solution.py:700
  10.7 15.2 %copy-start.19 = (bf16[80,768]{1,0:T(8,128)(2,1)}, bf16[80,768]{1,0:T(8,128)(2,1)S(1)}, u32[]{:S(2)}) copy-start(bf16[80,768]{1,0:T(8,128)(2,1)S(1)} %collective-permute-done.1.refs_10_) | copy-start | bytes 368644
  10.7 15.3 %collective-permute-start.2 = (bf16[80,768]{1,0:T(8,128)(2,1)S(1)}, bf16[80,768]{1,0:T(8,128)(2,1)S(1)}, u32[]{:S(2)}, u32[]{:S(2)}) collective-permute-start(bf16[80,768]{1,0:T(8,128)(2,1)S(1)} %collective-permute-done.1.refs_10_), channel_id=1, source_target_pairs={{0,1},{1,0},{2,3},{3,2},{4,5},{5,4},{6,7},{7,6},{8,9},{9,8},{10,11... | collective-permute-start | bytes 368648 | tf_op jit(solution)/shard_map/ppermute | solution.py:700
  18.3 7.5 %copy-start.20 = (bf16[80,768]{1,0:T(8,128)(2,1)}, bf16[80,768]{1,0:T(8,128)(2,1)S(1)}, u32[]{:S(2)}) copy-start(bf16[80,768]{1,0:T(8,128)(2,1)S(1)} %collective-permute-done.3.refs_12_) | copy-start | bytes 368644
  18.3 7.6 %collective-permute-start.4 = (bf16[80,768]{1,0:T(8,128)(2,1)S(1)}, bf16[80,768]{1,0:T(8,128)(2,1)S(1)}, u32[]{:S(2)}, u32[]{:S(2)}) collective-permute-start(bf16[80,768]{1,0:T(8,128)(2,1)S(1)} %collective-permute-done.3.refs_12_), channel_id=1, source_target_pairs={{0,1},{1,0},{2,3},{3,2},{4,5},{5,4},{6,7},{7,6},{8,9},{9,8},{10,11... | collective-permute-start | bytes 368648 | tf_op jit(solution)/shard_map/ppermute | solution.py:700
  19.8 6.0 %copy-start.21 = (bf16[80,768]{1,0:T(8,128)(2,1)}, bf16[80,768]{1,0:T(8,128)(2,1)S(1)}, u32[]{:S(2)}) copy-start(bf16[80,768]{1,0:T(8,128)(2,1)S(1)} %collective-permute-done.5.refs_14_) | copy-start | bytes 368644
  19.8 6.1 %collective-permute-start.6 = (bf16[80,768]{1,0:T(8,128)(2,1)S(1)}, bf16[80,768]{1,0:T(8,128)(2,1)S(1)}, u32[]{:S(2)}, u32[]{:S(2)}) collective-permute-start(bf16[80,768]{1,0:T(8,128)(2,1)S(1)} %collective-permute-done.5.refs_14_), channel_id=1, source_target_pairs={{0,1},{1,0},{2,3},{3,2},{4,5},{5,4},{6,7},{7,6},{8,9},{9,8},{10,11... | collective-permute-start | bytes 368648 | tf_op jit(solution)/shard_map/ppermute | solution.py:700
  55.0 9.1 %collective-permute-start.8 = (bf16[3840,384]{1,0:T(8,128)(2,1)}, bf16[3840,384]{1,0:T(8,128)(2,1)S(1)}, u32[]{:S(2)}, u32[]{:S(2)}) collective-permute-start(bf16[3840,384]{1,0:T(8,128)(2,1)} %get-tuple-element.133), channel_id=1, source_target_pairs={{0,8},{8,0},{16,24},{24,16},{1,9},{9,1},{17,25},{25,17},{2,10},{10... | collective-permute-start | bytes 8847368 | tf_op jit(solution)/shard_map/ppermute | solution.py:697
  55.1 16.6 %collective-permute-start.7 = (bf16[3072,384]{1,0:T(8,128)(2,1)}, bf16[3072,384]{1,0:T(8,128)(2,1)S(1)}, u32[]{:S(2)}, u32[]{:S(2)}) collective-permute-start(bf16[3072,384]{1,0:T(8,128)(2,1)} %get-tuple-element.130), channel_id=1, source_target_pairs={{0,8},{8,0},{16,24},{24,16},{1,9},{9,1},{17,25},{25,17},{2,10},{10... | collective-permute-start | bytes 7077896 | tf_op jit(solution)/shard_map/ppermute | solution.py:697
  55.6 8.6 %copy-start.6 = (s32[5]{0:T(128)S(1)}, s32[5]{0:T(128)}, u32[]{:S(2)}) copy-start(s32[5]{0:T(128)} %stack.23.refs_0_.pos_ref) | copy-start | bytes 64
  55.6 8.6 %copy-start.10 = (bf16[1280,384]{1,0:T(8,128)(2,1)S(1)}, bf16[1280,384]{1,0:T(8,128)(2,1)}, u32[]{:S(2)}) copy-start(bf16[1280,384]{1,0:T(8,128)(2,1)} %get-tuple-element.132.refs_1_) | copy-start | bytes 2949124
  66.7 5.0 %copy-start.7 = (bf16[3072,384]{1,0:T(8,128)(2,1)S(1)}, bf16[3072,384]{1,0:T(8,128)(2,1)}, u32[]{:S(2)}) copy-start(bf16[3072,384]{1,0:T(8,128)(2,1)} %get-tuple-element.129.refs_0_) | copy-start | bytes 7077892
  68.8 13.2 %collective-permute-start.10 = (bf16[640,384]{1,0:T(8,128)(2,1)S(1)}, bf16[640,384]{1,0:T(8,128)(2,1)S(1)}, u32[]{:S(2)}, u32[]{:S(2)}) collective-permute-start(bf16[640,384]{1,0:T(8,128)(2,1)S(1)} %get-tuple-element.140), channel_id=1, source_target_pairs={{0,2},{1,3},{2,0},{3,1},{4,6},{5,7},{6,4},{7,5},{8,10},{9,11},{10,... | collective-permute-start | bytes 1474568 | tf_op jit(solution)/shard_map/ppermute | solution.py:700
  70.2 25.0 %collective-permute-start.13 = (bf16[1280,384]{1,0:T(8,128)(2,1)}, bf16[1280,384]{1,0:T(8,128)(2,1)}, u32[]{:S(2)}, u32[]{:S(2)}) collective-permute-start(bf16[1280,384]{1,0:T(8,128)(2,1)} %get-tuple-element.134.refs_2_), channel_id=1, source_target_pairs={{0,16},{8,24},{16,0},{24,8},{1,17},{9,25},{17,1},{25,9},{2,18},{10... | collective-permute-start | bytes 2949128 | tf_op jit(solution)/shard_map/ppermute | solution.py:697
  71.7 2.7 %copy-start.9 = (bf16[768,768]{1,0:T(8,128)(2,1)S(1)}, bf16[768,768]{1,0:T(8,128)(2,1)}, u32[]{:S(2)}) copy-start(bf16[768,768]{1,0:T(8,128)(2,1)} %get-tuple-element.128.refs_1_) | copy-start | bytes 3538948
  71.7 2.7 %copy-start.15 = (bf16[768,768]{1,0:T(8,128)(2,1)S(1)}, bf16[768,768]{1,0:T(8,128)(2,1)}, u32[]{:S(2)}) copy-start(bf16[768,768]{1,0:T(8,128)(2,1)} %get-tuple-element.122.refs_3_.refs_1_) | copy-start | bytes 3538948
  71.7 2.7 %copy-start.16 = (bf16[768,768]{1,0:T(8,128)(2,1)S(1)}, bf16[768,768]{1,0:T(8,128)(2,1)}, u32[]{:S(2)}) copy-start(bf16[768,768]{1,0:T(8,128)(2,1)} %get-tuple-element.123.refs_4_.refs_2_) | copy-start | bytes 3538948
  71.7 2.7 %copy-start.18 = (bf16[256,768]{1,0:T(8,128)(2,1)S(1)}, bf16[256,768]{1,0:T(8,128)(2,1)}, u32[]{:S(2)}) copy-start(bf16[256,768]{1,0:T(8,128)(2,1)} %get-tuple-element.121.refs_3_.refs_2_.refs_0_) | copy-start | bytes 1179652
  73.9 29.2 %collective-permute-start.12 = (bf16[1536,384]{1,0:T(8,128)(2,1)}, bf16[1536,384]{1,0:T(8,128)(2,1)}, u32[]{:S(2)}, u32[]{:S(2)}) collective-permute-start(bf16[1536,384]{1,0:T(8,128)(2,1)} %get-tuple-element.135.refs_5_), channel_id=1, source_target_pairs={{0,1},{1,0},{2,3},{3,2},{4,5},{5,4},{6,7},{7,6},{8,9},{9,8},{10,11... | collective-permute-start | bytes 3538952 | tf_op jit(solution)/shard_map/ppermute | solution.py:700
  74.4 2.3 %copy-start = (bf16[768,768]{1,0:T(8,128)(2,1)S(1)}, bf16[768,768]{1,0:T(8,128)(2,1)}, u32[]{:S(2)}) copy-start(bf16[768,768]{1,0:T(8,128)(2,1)} %refs_4_.1) | copy-start | bytes 3538948
  76.6 9.1 %collective-permute-start.9 = (bf16[8,288,384]{2,1,0:T(8,128)(2,1)S(1)}, bf16[8,288,384]{2,1,0:T(8,128)(2,1)S(1)}, u32[]{:S(2)}, u32[]{:S(2)}) collective-permute-start(bf16[8,288,384]{2,1,0:T(8,128)(2,1)S(1)} %shard_map.347.refs_11_), channel_id=1, source_target_pairs={{0,8},{8,0},{16,24},{24,16},{1,9},{9,1},{17,25},{25,17},{2,10},{10... | collective-permute-start | bytes 5308424 | tf_op jit(solution)/shard_map/ppermute | solution.py:697
  83.4 36.4 %collective-permute-start.19 = (bf16[320,384]{1,0:T(8,128)(2,1)}, bf16[320,384]{1,0:T(8,128)(2,1)}, u32[]{:S(2)}, u32[]{:S(2)}) collective-permute-start(bf16[320,384]{1,0:T(8,128)(2,1)} %get-tuple-element.141.refs_8_), channel_id=1, source_target_pairs={{0,4},{1,5},{2,6},{3,7},{4,0},{5,1},{6,2},{7,3},{8,12},{9,13},{10,... | collective-permute-start | bytes 737288 | tf_op jit(solution)/shard_map/ppermute | solution.py:700
  88.8 19.4 %collective-permute-start.11 = (bf16[800,384]{1,0:T(8,128)(2,1)S(1)}, bf16[800,384]{1,0:T(8,128)(2,1)S(1)}, u32[]{:S(2)}, u32[]{:S(2)}) collective-permute-start(bf16[800,384]{1,0:T(8,128)(2,1)S(1)} %get-tuple-element.143), channel_id=1, source_target_pairs={{0,16},{8,24},{16,0},{24,8},{1,17},{9,25},{17,1},{25,9},{2,18},{10... | collective-permute-start | bytes 1843208 | tf_op jit(solution)/shard_map/ppermute | solution.py:697
  90.3 27.6 %collective-permute-start.14 = (bf16[896,384]{1,0:T(8,128)(2,1)}, bf16[896,384]{1,0:T(8,128)(2,1)}, u32[]{:S(2)}, u32[]{:S(2)}) collective-permute-start(bf16[896,384]{1,0:T(8,128)(2,1)} %get-tuple-element.146.refs_2_), channel_id=1, source_target_pairs={{0,1},{1,0},{2,3},{3,2},{4,5},{5,4},{6,7},{7,6},{8,9},{9,8},{10,11... | collective-permute-start | bytes 2064392 | tf_op jit(solution)/shard_map/ppermute | solution.py:700
  96.7 12.8 %collective-permute-start.15 = (bf16[640,384]{1,0:T(8,128)(2,1)S(1)}, bf16[640,384]{1,0:T(8,128)(2,1)S(1)}, u32[]{:S(2)}, u32[]{:S(2)}) collective-permute-start(bf16[640,384]{1,0:T(8,128)(2,1)S(1)} %get-tuple-element.147.refs_2_), channel_id=1, source_target_pairs={{0,2},{1,3},{2,0},{3,1},{4,6},{5,7},{6,4},{7,5},{8,10},{9,11},{10,... | collective-permute-start | bytes 1474568 | tf_op jit(solution)/shard_map/ppermute | solution.py:700
  104.8 15.7 %collective-permute-start.20 = (bf16[768,384]{1,0:T(8,128)(2,1)S(1)}, bf16[768,384]{1,0:T(8,128)(2,1)S(1)}, u32[]{:S(2)}, u32[]{:S(2)}) collective-permute-start(bf16[768,384]{1,0:T(8,128)(2,1)S(1)} %get-tuple-element.148.refs_3_), channel_id=1, source_target_pairs={{0,16},{8,24},{16,0},{24,8},{1,17},{9,25},{17,1},{25,9},{2,18},{10... | collective-permute-start | bytes 1769480 | tf_op jit(solution)/shard_map/ppermute | solution.py:697
  108.9 16.0 %collective-permute-start.16 = (bf16[416,384]{1,0:T(8,128)(2,1)S(1)}, bf16[416,384]{1,0:T(8,128)(2,1)S(1)}, u32[]{:S(2)}, u32[]{:S(2)}) collective-permute-start(bf16[416,384]{1,0:T(8,128)(2,1)S(1)} %get-tuple-element.153.refs_2_), channel_id=1, source_target_pairs={{0,1},{1,0},{2,3},{3,2},{4,5},{5,4},{6,7},{7,6},{8,9},{9,8},{10,11... | collective-permute-start | bytes 958472 | tf_op jit(solution)/shard_map/ppermute | solution.py:700
  110.2 11.7 %collective-permute-start.18 = (bf16[320,384]{1,0:T(8,128)(2,1)S(1)}, bf16[320,384]{1,0:T(8,128)(2,1)S(1)}, u32[]{:S(2)}, u32[]{:S(2)}) collective-permute-start(bf16[320,384]{1,0:T(8,128)(2,1)S(1)} %get-tuple-element.154.refs_3_), channel_id=1, source_target_pairs={{0,4},{1,5},{2,6},{3,7},{4,0},{5,1},{6,2},{7,3},{8,12},{9,13},{10,... | collective-permute-start | bytes 737288 | tf_op jit(solution)/shard_map/ppermute | solution.py:700
  119.1 5.8 %collective-permute-start.17 = (bf16[192,384]{1,0:T(8,128)(2,1)S(1)}, bf16[192,384]{1,0:T(8,128)(2,1)S(1)}, u32[]{:S(2)}, u32[]{:S(2)}) collective-permute-start(bf16[192,384]{1,0:T(8,128)(2,1)S(1)} %get-tuple-element.157.refs_6_), channel_id=1, source_target_pairs={{0,16},{8,24},{16,0},{24,8},{1,17},{9,25},{17,1},{25,9},{2,18},{10... | collective-permute-start | bytes 442376 | tf_op jit(solution)/shard_map/ppermute | solution.py:697
  119.7 16.7 %collective-permute-start.22 = (bf16[256,384]{1,0:T(8,128)(2,1)S(1)}, bf16[256,384]{1,0:T(8,128)(2,1)S(1)}, u32[]{:S(2)}, u32[]{:S(2)}) collective-permute-start(bf16[256,384]{1,0:T(8,128)(2,1)S(1)} %get-tuple-element.167), channel_id=1, source_target_pairs={{0,2},{1,3},{2,0},{3,1},{4,6},{5,7},{6,4},{7,5},{8,10},{9,11},{10,... | collective-permute-start | bytes 589832 | tf_op jit(solution)/shard_map/ppermute | solution.py:700
  123.3 10.5 %collective-permute-start.23 = (bf16[384,384]{1,0:T(8,128)(2,1)S(1)}, bf16[384,384]{1,0:T(8,128)(2,1)S(1)}, u32[]{:S(2)}, u32[]{:S(2)}) collective-permute-start(bf16[384,384]{1,0:T(8,128)(2,1)S(1)} %get-tuple-element.161.refs_5_), channel_id=1, source_target_pairs={{0,2},{1,3},{2,0},{3,1},{4,6},{5,7},{6,4},{7,5},{8,10},{9,11},{10,... | collective-permute-start | bytes 884744 | tf_op jit(solution)/shard_map/ppermute | solution.py:700
  123.3 6.9 %collective-permute-start.24 = (bf16[320,384]{1,0:T(8,128)(2,1)S(1)}, bf16[320,384]{1,0:T(8,128)(2,1)S(1)}, u32[]{:S(2)}, u32[]{:S(2)}) collective-permute-start(bf16[320,384]{1,0:T(8,128)(2,1)S(1)} %get-tuple-element.170), channel_id=1, source_target_pairs={{0,1},{1,0},{2,3},{3,2},{4,5},{5,4},{6,7},{7,6},{8,9},{9,8},{10,11... | collective-permute-start | bytes 737288 | tf_op jit(solution)/shard_map/ppermute | solution.py:700
  125.6 13.6 %collective-permute-start.21 = (bf16[320,384]{1,0:T(8,128)(2,1)S(1)}, bf16[320,384]{1,0:T(8,128)(2,1)S(1)}, u32[]{:S(2)}, u32[]{:S(2)}) collective-permute-start(bf16[320,384]{1,0:T(8,128)(2,1)S(1)} %get-tuple-element.166.refs_4_), channel_id=1, source_target_pairs={{0,2},{1,3},{2,0},{3,1},{4,6},{5,7},{6,4},{7,5},{8,10},{9,11},{10,... | collective-permute-start | bytes 737288 | tf_op jit(solution)/shard_map/ppermute | solution.py:700
  134.4 5.4 %collective-permute-start.27 = (bf16[80,384]{1,0:T(8,128)(2,1)S(1)}, bf16[80,384]{1,0:T(8,128)(2,1)S(1)}, u32[]{:S(2)}, u32[]{:S(2)}) collective-permute-start(bf16[80,384]{1,0:T(8,128)(2,1)S(1)} %get-tuple-element.180), channel_id=1, source_target_pairs={{0,16},{8,24},{16,0},{24,8},{1,17},{9,25},{17,1},{25,9},{2,18},{10... | collective-permute-start | bytes 184328 | tf_op jit(solution)/shard_map/ppermute | solution.py:697
  136.0 7.0 %collective-permute-start.26 = (bf16[192,384]{1,0:T(8,128)(2,1)S(1)}, bf16[192,384]{1,0:T(8,128)(2,1)S(1)}, u32[]{:S(2)}, u32[]{:S(2)}) collective-permute-start(bf16[192,384]{1,0:T(8,128)(2,1)S(1)} %get-tuple-element.171.refs_6_), channel_id=1, source_target_pairs={{0,4},{1,5},{2,6},{3,7},{4,0},{5,1},{6,2},{7,3},{8,12},{9,13},{10,... | collective-permute-start | bytes 442376 | tf_op jit(solution)/shard_map/ppermute | solution.py:700
  143.6 5.2 %collective-permute-start.28 = (bf16[192,384]{1,0:T(8,128)(2,1)S(1)}, bf16[192,384]{1,0:T(8,128)(2,1)S(1)}, u32[]{:S(2)}, u32[]{:S(2)}) collective-permute-start(bf16[192,384]{1,0:T(8,128)(2,1)S(1)} %shard_map.361), channel_id=1, source_target_pairs={{0,16},{8,24},{16,0},{24,8},{1,17},{9,25},{17,1},{25,9},{2,18},{10... | collective-permute-start | bytes 442376 | tf_op jit(solution)/shard_map/ppermute | solution.py:697
  144.9 10.4 %collective-permute-start.25 = (bf16[304,384]{1,0:T(8,128)(2,1)S(1)}, bf16[304,384]{1,0:T(8,128)(2,1)S(1)}, u32[]{:S(2)}, u32[]{:S(2)}) collective-permute-start(bf16[304,384]{1,0:T(8,128)(2,1)S(1)} %get-tuple-element.176.refs_4_), channel_id=1, source_target_pairs={{0,4},{1,5},{2,6},{3,7},{4,0},{5,1},{6,2},{7,3},{8,12},{9,13},{10,... | collective-permute-start | bytes 700424 | tf_op jit(solution)/shard_map/ppermute | solution.py:700
  144.9 5.9 %collective-permute-start.30 = (bf16[240,384]{1,0:T(8,128)(2,1)S(1)}, bf16[240,384]{1,0:T(8,128)(2,1)S(1)}, u32[]{:S(2)}, u32[]{:S(2)}) collective-permute-start(bf16[240,384]{1,0:T(8,128)(2,1)S(1)} %get-tuple-element.181.refs_2_), channel_id=1, source_target_pairs={{0,16},{8,24},{16,0},{24,8},{1,17},{9,25},{17,1},{25,9},{2,18},{10... | collective-permute-start | bytes 552968 | tf_op jit(solution)/shard_map/ppermute | solution.py:697
  148.9 2.1 %collective-permute-start.29 = (bf16[384,384]{1,0:T(8,128)(2,1)S(1)}, bf16[384,384]{1,0:T(8,128)(2,1)S(1)}, u32[]{:S(2)}, u32[]{:S(2)}) collective-permute-start(bf16[384,384]{1,0:T(8,128)(2,1)S(1)} %pad_maximum_fusion.1), channel_id=1, source_target_pairs={{0,8},{8,0},{16,24},{24,16},{1,9},{9,1},{17,25},{25,17},{2,10},{10... | collective-permute-start | bytes 884744 | tf_op jit(solution)/shard_map/ppermute | solution.py:697
  151.0 1.8 %collective-permute-start.31 = (bf16[480,384]{1,0:T(8,128)(2,1)S(1)}, bf16[480,384]{1,0:T(8,128)(2,1)S(1)}, u32[]{:S(2)}, u32[]{:S(2)}) collective-permute-start(bf16[480,384]{1,0:T(8,128)(2,1)S(1)} %pad_maximum_fusion), channel_id=1, source_target_pairs={{0,8},{8,0},{16,24},{24,16},{1,9},{9,1},{17,25},{25,17},{2,10},{10... | collective-permute-start | bytes 1105928 | tf_op jit(solution)/shard_map/ppermute | solution.py:697
  151.3 3.9 %copy-start.4 = (f32[96,3072]{1,0:T(8,128)}, f32[96,3072]{1,0:T(8,128)S(1)}, u32[]{:S(2)}) copy-start(f32[96,3072]{1,0:T(8,128)S(1)} %slice_dynamic-update-slice_fusion.refs_5_) | copy-start | bytes 3538948
  153.1 2.8 %copy-start.2 = (f32[384,768]{1,0:T(8,128)}, f32[384,768]{1,0:T(8,128)S(1)}, u32[]{:S(2)}) copy-start(f32[384,768]{1,0:T(8,128)S(1)} %maximum_maximum_fusion.refs_6_) | copy-start | bytes 3538948
  155.9 5.8 %collective-permute-start.33 = (bf16[144,384]{1,0:T(8,128)(2,1)S(1)}, bf16[144,384]{1,0:T(8,128)(2,1)S(1)}, u32[]{:S(2)}, u32[]{:S(2)}) collective-permute-start(bf16[144,384]{1,0:T(8,128)(2,1)S(1)} %constant_dynamic-update-slice_fusion), channel_id=1, source_target_pairs={{0,16},{8,24},{16,0},{24,8},{1,17},{9,25},{17,1},{25,9},{2,18},{10... | collective-permute-start | bytes 331784 | tf_op jit(solution)/shard_map/ppermute | solution.py:697
  156.3 5.5 %collective-permute-start.34 = (bf16[144,384]{1,0:T(8,128)(2,1)S(1)}, bf16[144,384]{1,0:T(8,128)(2,1)S(1)}, u32[]{:S(2)}, u32[]{:S(2)}) collective-permute-start(bf16[144,384]{1,0:T(8,128)(2,1)S(1)} %constant_dynamic-update-slice_fusion), channel_id=1, source_target_pairs={{0,24},{8,16},{16,8},{24,0},{1,25},{9,17},{17,9},{25,1},{2,26},{10... | collective-permute-start | bytes 331784 | tf_op jit(solution)/shard_map/ppermute | solution.py:697
  156.7 5.1 %collective-permute-start.32 = (bf16[176,384]{1,0:T(8,128)(2,1)S(1)}, bf16[176,384]{1,0:T(8,128)(2,1)S(1)}, u32[]{:S(2)}, u32[]{:S(2)}) collective-permute-start(bf16[176,384]{1,0:T(8,128)(2,1)S(1)} %pad_maximum_fusion.5), channel_id=1, source_target_pairs={{0,8},{8,0},{16,24},{24,16},{1,9},{9,1},{17,25},{25,17},{2,10},{10... | collective-permute-start | bytes 405512 | tf_op jit(solution)/shard_map/ppermute | solution.py:697
  (13 other events, 21.4 us)

commit v7 on v6

--- a/solution.py
+++ b/solution.py
@@ -140,7 +140,7 @@
             pltpu.VMEM(v.shape, v.dtype) for v in (query_w, key_w, value_w, query_b, value_b, seg, turn)
         ]
         + [pltpu.SemaphoreType.DMA((7,))],
-        compiler_params=pltpu.CompilerParams(vmem_limit_bytes=60 * MIB),
+        compiler_params=pltpu.CompilerParams(vmem_limit_bytes=54 * MIB),
         cost_estimate=pl.CostEstimate(flops=100000000, bytes_accessed=MIB, transcendentals=0),
     )(layer_input, query_w, key_w, value_w, query_b, value_b, seg, turn)
 

time: 167 us -> 167 us (level)
  no operation moved by 1% of the time
where the time goes in v7:
time: 167 us; the launch traced here: 165 us
  Pallas kernels  70.1 us (42%)
  waiting for transfers between devices  47.7 us (29%)
  starting transfers between devices  35.6 us (21%)
  local copies, waits for them, and re-layouts  7 us (4%)
  other arithmetic  3.1 us (2%)
    ppermute x20, waiting for transfers between devices, swap_blk(): return lax.ppermute(value, 'blk', [(i, i ^ mask) for i in range(blocks)])  33.1 us
    ppermute x20, starting transfers between devices, swap_blk(): return lax.ppermute(value, 'blk', [(i, i ^ mask) for i in range(blocks)])  24.7 us
    pallas_call x1, Pallas kernels, middle_part(): pl.pallas_call(lambda *refs: middle_kernel(packets, *refs), in_specs=[pl....  17.8 us
    pallas_call x15, Pallas kernels, combine(): pl.pallas_call(body, in_specs=[pl.BlockSpec(memory_space=pltpu.SMEM)] + [...  17.3 us
    ppermute x15, waiting for transfers between devices, swap_grp(): return lax.ppermute(value, 'grp', [(i, i ^ mask) for i in range(grps)])  14.6 us
    ppermute x15, starting transfers between devices, swap_grp(): return lax.ppermute(value, 'grp', [(i, i ^ mask) for i in range(grps)])  10.9 us
    pallas_call x1, Pallas kernels, attend(): pl.pallas_call(lambda *refs: attend_kernel(views, *refs), grid=(width //...  10.4 us
    pallas_call x1, Pallas kernels, attend_back(): pl.pallas_call(attend_back_kernel, grid=(width // group,), in_specs=[lane...  8.55 us
  transfers between devices with their start and end apart: 35, of which 17 were waited for; matrix products, arithmetic and copies ran while one was open for 2% of the time, Pallas kernels for 23%

profile of v7, /device:TPU:0, one launch (start us, length us, event | category | flops | bytes accessed | tf_op | source)
XLA Modules:
  0.0 164.9 jit_solution(1632904195695193077)
XLA Ops:
  0.7 2.0 %shard_map.340 = (bf16[80,768]{1,0:T(8,128)(2,1)}, bf16[256,768]{1,0:T(8,128)(2,1)}) custom-call(bf16[256,768]{1,0:T(8,128)(2,1)} %refs_1_.3, s32[256]{0:T(256)} %seg_any.3, s32[256]{0:T(256)} %refs_7_.3, bf16[2,768]{1,0:T(2,128)(2,1)} %refs_3_.2), custom_call_target="tpu_custom_call" | custom-call | tf_op jit(solution)/shard_map/pallas_call | solution.py:97
  2.7 3.1 %collective-permute-start.1 = (bf16[80,768]{1,0:T(8,128)(2,1)}, bf16[80,768]{1,0:T(8,128)(2,1)S(1)}, u32[]{:S(2)}, u32[]{:S(2)}) collective-permute-start(bf16[80,768]{1,0:T(8,128)(2,1)} %get-tuple-element.114.refs_8_), channel_id=1, source_target_pairs={{0,2},{1,3},{2,0},{3,1},{4,6},{5,7},{6,4},{7,5},{8,10},{9,11},{10,... | collective-permute-start | bytes 368648 | tf_op jit(solution)/shard_map/ppermute | solution.py:700
  5.8 2.6 %collective-permute-start.3 = (bf16[80,768]{1,0:T(8,128)(2,1)}, bf16[80,768]{1,0:T(8,128)(2,1)S(1)}, u32[]{:S(2)}, u32[]{:S(2)}) collective-permute-start(bf16[80,768]{1,0:T(8,128)(2,1)} %get-tuple-element.114.refs_8_), channel_id=1, source_target_pairs={{0,4},{1,5},{2,6},{3,7},{4,0},{5,1},{6,2},{7,3},{8,12},{9,13},{10,... | collective-permute-start | bytes 368648 | tf_op jit(solution)/shard_map/ppermute | solution.py:700
  8.4 1.7 %collective-permute-start = (bf16[80,768]{1,0:T(8,128)(2,1)}, bf16[80,768]{1,0:T(8,128)(2,1)S(1)}, u32[]{:S(2)}, u32[]{:S(2)}) collective-permute-start(bf16[80,768]{1,0:T(8,128)(2,1)} %get-tuple-element.114.refs_8_), channel_id=1, source_target_pairs={{0,1},{1,0},{2,3},{3,2},{4,5},{5,4},{6,7},{7,6},{8,9},{9,8},{10,11... | collective-permute-start | bytes 368648 | tf_op jit(solution)/shard_map/ppermute | solution.py:700
  10.7 1.7 %collective-permute-start.2 = (bf16[80,768]{1,0:T(8,128)(2,1)S(1)}, bf16[80,768]{1,0:T(8,128)(2,1)S(1)}, u32[]{:S(2)}, u32[]{:S(2)}) collective-permute-start(bf16[80,768]{1,0:T(8,128)(2,1)S(1)} %collective-permute-done.1.refs_10_), channel_id=1, source_target_pairs={{0,1},{1,0},{2,3},{3,2},{4,5},{5,4},{6,7},{7,6},{8,9},{9,8},{10,11... | collective-permute-start | bytes 368648 | tf_op jit(solution)/shard_map/ppermute | solution.py:700
  12.4 5.9 %collective-permute-done.3.refs_12_ = bf16[80,768]{1,0:T(8,128)(2,1)S(1)} collective-permute-done((bf16[80,768]{1,0:T(8,128)(2,1)}, bf16[80,768]{1,0:T(8,128)(2,1)S(1)}, u32[]{:S(2)}, u32[]{:S(2)}) %collective-permute-start.3) | collective-permute-done | bytes 122912 | tf_op jit(solution)/shard_map/ppermute | solution.py:700
  18.3 1.5 collective-permute-start.4
  21.0 4.9 %shard_map.341 = (bf16[256,768]{1,0:T(8,128)(2,1)}, bf16[256,768]{1,0:T(8,128)(2,1)}, bf16[256,768]{1,0:T(8,128)(2,1)}, f32[256,256]{1,0:T(8,128)}, f32[1,768]{1,0:T(1,128)}) custom-call(bf16[256,768]{1,0:T(8,128)(2,1)} %get-tuple-element.108.input_ref.refs_0_, bf16[768,768]{1,0:T(8,128)(2,1)} %refs_3_.3, bf16[768,768]{1,0:T(8,128)(2,1)} %refs_4_.1, ...), custom_call_target="tpu_custom_call" | custom-call | flops 100000000 | bytes 1048576 | tf_op jit(solution)/shard_map/pallas_call | solution.py:133
  26.7 10.4 %shard_map.342 = (bf16[768,768]{1,0:T(8,128)(2,1)}, bf16[768,768]{1,0:T(8,128)(2,1)}, bf16[12,256,768]{2,1,0:T(8,128)(2,1)}, f32[256,768]{1,0:T(8,128)}, bf16[768,768]{1,0:T(8,128)(2,1)}, /*index=5*/f32[8,512]{1,0:T(8,128)}) custom-call(bf16[256,768]{1,0:T(8,128)(2,1)} %get-tuple-element.108.input_ref.refs_0_, bf16[768,768]{1,0:T(8,128)(2,1)} %refs_4_.1, ...), custom_call_target="tpu_custom_call" | custom-call | flops 100000000 | bytes 1048576 | tf_op jit(solution)/shard_map/pallas_call | solution.py:206
  37.1 17.8 %shard_map.343 = (bf16[256,768]{1,0:T(8,128)(2,1)}, bf16[256,768]{1,0:T(8,128)(2,1)}, f32[256,768]{1,0:T(8,128)}, f32[8,768]{1,0:T(8,128)}, f32[1,3072]{1,0:T(1,...) custom-call(s32[5]{0:T(128)} %stack.23.refs_0_.pos_ref, ...), custom_call_target="tpu_custom_call" | custom-call | flops 100000000 | bytes 1048576 | tf_op jit(solution)/shard_map/pallas_call | solution.py:398
  55.6 8.6 %shard_map.344 = (bf16[256,768]{1,0:T(8,128)(2,1)}, bf16[768,768]{1,0:T(8,128)(2,1)}, bf16[768,768]{1,0:T(8,128)(2,1)}) custom-call(bf16[256,768]{1,0:T(8,128)(2,1)} %get-tuple-element.110.refs_4_.q_ref, bf16[768,768]{1,0:T(8,128)(2,1)} %get-tuple-element.117.keys_ref, bf16[768,768]{1,0:T(8,128)(2,1)} %get-tuple-element.118.values_ref, ...), custom_call_target="tpu_custom_call" | custom-call | flops 40000000000 | bytes 1048576 | tf_op jit(solution)/shard_map/pallas_call | solution.py:438
  64.2 1.5 copy-done.8
  66.7 2.1 %shard_map.345 = (bf16[1280,384]{1,0:T(8,128)(2,1)S(1)}, bf16[640,384]{1,0:T(8,128)(2,1)S(1)}, bf16[1280,384]{1,0:T(8,128)(2,1)}, bf16[640,384]{1,0:T(8,128)(2,1)S(1)}) custom-call(s32[5]{0:T(128)S(1)} %copy-done.6, bf16[2560,384]{1,0:T(8,128)(2,1)S(1)} %copy-done.8, bf16[1280,384]{1,0:T(8,128)(2,1)S(1)} %copy-done.10, ...), custom_call_target="tpu_custom_call" | custom-call | flops 40000000000 | bytes 1048576 | tf_op jit(solution)/shard_map/pallas_call | solution.py:642
  68.8 1.4 collective-permute-start.10
  70.2 1.5 collective-permute-start.13
  71.7 2.2 %shard_map.346 = (bf16[1536,384]{1,0:T(8,128)(2,1)S(1)}, bf16[1536,384]{1,0:T(8,128)(2,1)}) custom-call(s32[5]{0:T(128)S(1)} %copy-done.6, bf16[3072,384]{1,0:T(8,128)(2,1)S(1)} %copy-done.7, bf16[3072,384]{1,0:T(8,128)(2,1)S(1)} %collective-permute-done.7.refs_1_, bf16[1280,384]{1,0:T(8,128)(2,1)} %get-tuple-element.134.refs_2_), custom_call_target="tpu_custom_call" | custom-call | flops 40000000000 | bytes 1048576 | tf_op jit(solution)/shard_map/pallas_call | solution.py:642
  74.5 2.1 %shard_map.347.refs_11_ = bf16[8,288,384]{2,1,0:T(8,128)(2,1)S(1)} custom-call(s32[5]{0:T(128)S(1)} %copy-done.6, bf16[768,768]{1,0:T(8,128)(2,1)S(1)} %copy-done.9, bf16[256,768]{1,0:T(8,128)(2,1)S(1)} %copy-done.18, bf16[768,768]{1,0:T(8,128)(2,1)S(1)} %copy-done.15, bf16[768,768]{1,0:T(8,128)(2,1)S(1)} %copy-done.16, ...), custom_call_target="tpu_custom_call" | custom-call | flops 40000000000 | bytes 1048576 | tf_op jit(solution)/shard_map/pallas_call | solution.py:664
  76.8 3.8 %shard_map.348 = (bf16[512,384]{1,0:T(8,128)(2,1)S(1)}, bf16[512,384]{1,0:T(8,128)(2,1)S(1)}, f32[256,768]{1,0:T(8,128)}, f32[32,384]{1,0:T(8,128)S(1)}) custom-call(bf16[256,768]{1,0:T(8,128)(2,1)S(1)} %copy-done.18, bf16[768,768]{1,0:T(8,128)(2,1)S(1)} %copy-done.15, bf16[768,768]{1,0:T(8,128)(2,1)S(1)} %copy-done.16, bf16[768,768]{1,0:T(8,128)(2,1)S(1)} %copy-done.3, ...), custom_call_target="tpu_custom_call" | custom-call | flops 40000000000 | bytes 1048576 | tf_op jit(solution)/shard_map/pallas_call | solution.py:571
  80.6 1.4 collective-permute-done.10.refs_1_
  82.0 1.4 shard_map.349
  83.4 2.4 %collective-permute-start.19 = (bf16[320,384]{1,0:T(8,128)(2,1)}, bf16[320,384]{1,0:T(8,128)(2,1)}, u32[]{:S(2)}, u32[]{:S(2)}) collective-permute-start(bf16[320,384]{1,0:T(8,128)(2,1)} %get-tuple-element.141.refs_8_), channel_id=1, source_target_pairs={{0,4},{1,5},{2,6},{3,7},{4,0},{5,1},{6,2},{7,3},{8,12},{9,13},{10,... | collective-permute-start | bytes 737288 | tf_op jit(solution)/shard_map/ppermute | solution.py:700
  85.7 3.1 %shard_map.350 = (bf16[768,384]{1,0:T(8,128)(2,1)S(1)}, bf16[800,384]{1,0:T(8,128)(2,1)S(1)}, bf16[384,384]{1,0:T(8,128)(2,1)S(1)}, bf16[896,384]{1,0:T(8,128)(2,1)}) custom-call(s32[5]{0:T(128)S(1)} %copy-done.6, bf16[768,768]{1,0:T(8,128)(2,1)S(1)} %copy-done.9, bf16[256,768]{1,0:T(8,128)(2,1)S(1)} %copy-done.18, bf16[768,768]{1,0:T(8,128)(2,1)S(1)} %copy-done.15, ...), custom_call_target="tpu_custom_call" | custom-call | flops 40000000000 | bytes 1048576 | tf_op jit(solution)/shard_map/pallas_call | solution.py:664
  88.8 1.5 collective-permute-start.11
  90.8 4.3 %collective-permute-done.13.refs_1_ = bf16[1280,384]{1,0:T(8,128)(2,1)} collective-permute-done((bf16[1280,384]{1,0:T(8,128)(2,1)}, bf16[1280,384]{1,0:T(8,128)(2,1)}, u32[]{:S(2)}, u32[]{:S(2)}) %collective-permute-start.13) | collective-permute-done | bytes 983072 | tf_op jit(solution)/shard_map/ppermute | solution.py:697
  95.1 1.5 shard_map.351
  97.4 5.7 %collective-permute-done.12.refs_1_ = bf16[1536,384]{1,0:T(8,128)(2,1)} collective-permute-done((bf16[1536,384]{1,0:T(8,128)(2,1)}, bf16[1536,384]{1,0:T(8,128)(2,1)}, u32[]{:S(2)}, u32[]{:S(2)}) %collective-permute-start.12) | collective-permute-done | bytes 1179680 | tf_op jit(solution)/shard_map/ppermute | solution.py:700
  103.1 1.7 %shard_map.352 = (bf16[768,384]{1,0:T(8,128)(2,1)S(1)}, bf16[768,384]{1,0:T(8,128)(2,1)S(1)}) custom-call(s32[5]{0:T(128)S(1)} %copy-done.6, bf16[1536,384]{1,0:T(8,128)(2,1)S(1)} %get-tuple-element.144.refs_0_, bf16[1536,384]{1,0:T(8,128)(2,1)} %collective-permute-done.12.refs_1_, bf16[640,384]{1,0:T(8,128)(2,1)S(1)} %get-tuple-element.147.refs_2_), custom_call_target="tpu_custom_call" | custom-call | flops 40000000000 | bytes 1048576 | tf_op jit(solution)/shard_map/pallas_call | solution.py:642
  105.4 2.8 %collective-permute-done.11.refs_2_ = bf16[800,384]{1,0:T(8,128)(2,1)S(1)} collective-permute-done((bf16[800,384]{1,0:T(8,128)(2,1)S(1)}, bf16[800,384]{1,0:T(8,128)(2,1)S(1)}, u32[]{:S(2)}, u32[]{:S(2)}) %collective-permute-start.11) | collective-permute-done | bytes 614432 | tf_op jit(solution)/shard_map/ppermute | solution.py:697
  110.2 2.6 %collective-permute-start.18 = (bf16[320,384]{1,0:T(8,128)(2,1)S(1)}, bf16[320,384]{1,0:T(8,128)(2,1)S(1)}, u32[]{:S(2)}, u32[]{:S(2)}) collective-permute-start(bf16[320,384]{1,0:T(8,128)(2,1)S(1)} %get-tuple-element.154.refs_3_), channel_id=1, source_target_pairs={{0,4},{1,5},{2,6},{3,7},{4,0},{5,1},{6,2},{7,3},{8,12},{9,13},{10,... | collective-permute-start | bytes 737288 | tf_op jit(solution)/shard_map/ppermute | solution.py:700
  112.9 5.0 %collective-permute-done.14.refs_2_ = bf16[896,384]{1,0:T(8,128)(2,1)} collective-permute-done((bf16[896,384]{1,0:T(8,128)(2,1)}, bf16[896,384]{1,0:T(8,128)(2,1)}, u32[]{:S(2)}, u32[]{:S(2)}) %collective-permute-start.14) | collective-permute-done | bytes 688160 | tf_op jit(solution)/shard_map/ppermute | solution.py:700
  117.8 1.3 shard_map.355
  120.4 1.5 collective-permute-done.18.refs_3_
  122.0 1.3 shard_map.356
  123.3 1.6 collective-permute-start.24
  125.6 2.0 %collective-permute-start.21 = (bf16[320,384]{1,0:T(8,128)(2,1)S(1)}, bf16[320,384]{1,0:T(8,128)(2,1)S(1)}, u32[]{:S(2)}, u32[]{:S(2)}) collective-permute-start(bf16[320,384]{1,0:T(8,128)(2,1)S(1)} %get-tuple-element.166.refs_4_), channel_id=1, source_target_pairs={{0,2},{1,3},{2,0},{3,1},{4,6},{5,7},{6,4},{7,5},{8,10},{9,11},{10,... | collective-permute-start | bytes 737288 | tf_op jit(solution)/shard_map/ppermute | solution.py:700
  127.6 2.6 %collective-permute-done.24.refs_3_.refs_2_ = bf16[320,384]{1,0:T(8,128)(2,1)S(1)} collective-permute-done((bf16[320,384]{1,0:T(8,128)(2,1)S(1)}, bf16[320,384]{1,0:T(8,128)(2,1)S(1)}, u32[]{:S(2)}, u32[]{:S(2)}) %collective-permute-start.24) | collective-permute-done | bytes 245792 | tf_op jit(solution)/shard_map/ppermute | solution.py:700
  130.2 3.5 %collective-permute-done.23.refs_2_ = bf16[384,384]{1,0:T(8,128)(2,1)S(1)} collective-permute-done((bf16[384,384]{1,0:T(8,128)(2,1)S(1)}, bf16[384,384]{1,0:T(8,128)(2,1)S(1)}, u32[]{:S(2)}, u32[]{:S(2)}) %collective-permute-start.23) | collective-permute-done | bytes 294944 | tf_op jit(solution)/shard_map/ppermute | solution.py:700
  134.4 1.6 collective-permute-start.27
  136.5 2.7 %collective-permute-done.21.refs_4_ = bf16[320,384]{1,0:T(8,128)(2,1)S(1)} collective-permute-done((bf16[320,384]{1,0:T(8,128)(2,1)S(1)}, bf16[320,384]{1,0:T(8,128)(2,1)S(1)}, u32[]{:S(2)}, u32[]{:S(2)}) %collective-permute-start.21) | collective-permute-done | bytes 245792 | tf_op jit(solution)/shard_map/ppermute | solution.py:700
  139.9 1.2 shard_map.360
  141.1 1.9 %collective-permute-done.26.refs_1_ = bf16[192,384]{1,0:T(8,128)(2,1)S(1)} collective-permute-done((bf16[192,384]{1,0:T(8,128)(2,1)S(1)}, bf16[192,384]{1,0:T(8,128)(2,1)S(1)}, u32[]{:S(2)}, u32[]{:S(2)}) %collective-permute-start.26) | collective-permute-done | bytes 147488 | tf_op jit(solution)/shard_map/ppermute | solution.py:700
  143.6 1.3 collective-permute-start.28
  145.7 3.1 %collective-permute-done.28 = bf16[192,384]{1,0:T(8,128)(2,1)S(1)} collective-permute-done((bf16[192,384]{1,0:T(8,128)(2,1)S(1)}, bf16[192,384]{1,0:T(8,128)(2,1)S(1)}, u32[]{:S(2)}, u32[]{:S(2)}) %collective-permute-start.28) | collective-permute-done | bytes 147488 | tf_op jit(solution)/shard_map/ppermute | solution.py:697
  149.0 1.8 %collective-permute-done.30 = bf16[240,384]{1,0:T(8,128)(2,1)S(1)} collective-permute-done((bf16[240,384]{1,0:T(8,128)(2,1)S(1)}, bf16[240,384]{1,0:T(8,128)(2,1)S(1)}, u32[]{:S(2)}, u32[]{:S(2)}) %collective-permute-start.30) | collective-permute-done | bytes 184352 | tf_op jit(solution)/shard_map/ppermute | solution.py:697
  151.3 1.4 collective-permute-done.31
  153.1 2.2 %collective-permute-done.25.refs_4_ = bf16[304,384]{1,0:T(8,128)(2,1)S(1)} collective-permute-done((bf16[304,384]{1,0:T(8,128)(2,1)S(1)}, bf16[304,384]{1,0:T(8,128)(2,1)S(1)}, u32[]{:S(2)}, u32[]{:S(2)}) %collective-permute-start.25) | collective-permute-done | bytes 233504 | tf_op jit(solution)/shard_map/ppermute | solution.py:700
  156.7 1.5 collective-permute-start.32
  158.2 1.6 fusion
  (152 shorter events, 20.9 us)
Async XLA Ops:
  2.7 8.0 %collective-permute-start.1 = (bf16[80,768]{1,0:T(8,128)(2,1)}, bf16[80,768]{1,0:T(8,128)(2,1)S(1)}, u32[]{:S(2)}, u32[]{:S(2)}) collective-permute-start(bf16[80,768]{1,0:T(8,128)(2,1)} %get-tuple-element.114.refs_8_), channel_id=1, source_target_pairs={{0,2},{1,3},{2,0},{3,1},{4,6},{5,7},{6,4},{7,5},{8,10},{9,11},{10,... | collective-permute-start | bytes 368648 | tf_op jit(solution)/shard_map/ppermute | solution.py:700
  5.8 12.5 %collective-permute-start.3 = (bf16[80,768]{1,0:T(8,128)(2,1)}, bf16[80,768]{1,0:T(8,128)(2,1)S(1)}, u32[]{:S(2)}, u32[]{:S(2)}) collective-permute-start(bf16[80,768]{1,0:T(8,128)(2,1)} %get-tuple-element.114.refs_8_), channel_id=1, source_target_pairs={{0,4},{1,5},{2,6},{3,7},{4,0},{5,1},{6,2},{7,3},{8,12},{9,13},{10,... | collective-permute-start | bytes 368648 | tf_op jit(solution)/shard_map/ppermute | solution.py:700
  8.4 11.5 %collective-permute-start.5 = (bf16[80,768]{1,0:T(8,128)(2,1)}, bf16[80,768]{1,0:T(8,128)(2,1)S(1)}, u32[]{:S(2)}, u32[]{:S(2)}) collective-permute-start(bf16[80,768]{1,0:T(8,128)(2,1)} %get-tuple-element.114.refs_8_), channel_id=1, source_target_pairs={{0,6},{1,7},{2,4},{3,5},{4,2},{5,3},{6,0},{7,1},{8,14},{9,15},{10,... | collective-permute-start | bytes 368648 | tf_op jit(solution)/shard_map/ppermute | solution.py:700
  8.4 17.5 %collective-permute-start = (bf16[80,768]{1,0:T(8,128)(2,1)}, bf16[80,768]{1,0:T(8,128)(2,1)S(1)}, u32[]{:S(2)}, u32[]{:S(2)}) collective-permute-start(bf16[80,768]{1,0:T(8,128)(2,1)} %get-tuple-element.114.refs_8_), channel_id=1, source_target_pairs={{0,1},{1,0},{2,3},{3,2},{4,5},{5,4},{6,7},{7,6},{8,9},{9,8},{10,11... | collective-permute-start | bytes 368648 | tf_op jit(solution)/shard_map/ppermute | solution.py:700
  10.7 15.2 %copy-start.19 = (bf16[80,768]{1,0:T(8,128)(2,1)}, bf16[80,768]{1,0:T(8,128)(2,1)S(1)}, u32[]{:S(2)}) copy-start(bf16[80,768]{1,0:T(8,128)(2,1)S(1)} %collective-permute-done.1.refs_10_) | copy-start | bytes 368644
  10.7 15.3 %collective-permute-start.2 = (bf16[80,768]{1,0:T(8,128)(2,1)S(1)}, bf16[80,768]{1,0:T(8,128)(2,1)S(1)}, u32[]{:S(2)}, u32[]{:S(2)}) collective-permute-start(bf16[80,768]{1,0:T(8,128)(2,1)S(1)} %collective-permute-done.1.refs_10_), channel_id=1, source_target_pairs={{0,1},{1,0},{2,3},{3,2},{4,5},{5,4},{6,7},{7,6},{8,9},{9,8},{10,11... | collective-permute-start | bytes 368648 | tf_op jit(solution)/shard_map/ppermute | solution.py:700
  18.3 7.5 %copy-start.20 = (bf16[80,768]{1,0:T(8,128)(2,1)}, bf16[80,768]{1,0:T(8,128)(2,1)S(1)}, u32[]{:S(2)}) copy-start(bf16[80,768]{1,0:T(8,128)(2,1)S(1)} %collective-permute-done.3.refs_12_) | copy-start | bytes 368644
  18.3 7.6 %collective-permute-start.4 = (bf16[80,768]{1,0:T(8,128)(2,1)S(1)}, bf16[80,768]{1,0:T(8,128)(2,1)S(1)}, u32[]{:S(2)}, u32[]{:S(2)}) collective-permute-start(bf16[80,768]{1,0:T(8,128)(2,1)S(1)} %collective-permute-done.3.refs_12_), channel_id=1, source_target_pairs={{0,1},{1,0},{2,3},{3,2},{4,5},{5,4},{6,7},{7,6},{8,9},{9,8},{10,11... | collective-permute-start | bytes 368648 | tf_op jit(solution)/shard_map/ppermute | solution.py:700
  19.8 6.0 %copy-start.21 = (bf16[80,768]{1,0:T(8,128)(2,1)}, bf16[80,768]{1,0:T(8,128)(2,1)S(1)}, u32[]{:S(2)}) copy-start(bf16[80,768]{1,0:T(8,128)(2,1)S(1)} %collective-permute-done.5.refs_14_) | copy-start | bytes 368644
  19.8 6.1 %collective-permute-start.6 = (bf16[80,768]{1,0:T(8,128)(2,1)S(1)}, bf16[80,768]{1,0:T(8,128)(2,1)S(1)}, u32[]{:S(2)}, u32[]{:S(2)}) collective-permute-start(bf16[80,768]{1,0:T(8,128)(2,1)S(1)} %collective-permute-done.5.refs_14_), channel_id=1, source_target_pairs={{0,1},{1,0},{2,3},{3,2},{4,5},{5,4},{6,7},{7,6},{8,9},{9,8},{10,11... | collective-permute-start | bytes 368648 | tf_op jit(solution)/shard_map/ppermute | solution.py:700
  55.0 9.1 %collective-permute-start.8 = (bf16[3840,384]{1,0:T(8,128)(2,1)}, bf16[3840,384]{1,0:T(8,128)(2,1)S(1)}, u32[]{:S(2)}, u32[]{:S(2)}) collective-permute-start(bf16[3840,384]{1,0:T(8,128)(2,1)} %get-tuple-element.133), channel_id=1, source_target_pairs={{0,8},{8,0},{16,24},{24,16},{1,9},{9,1},{17,25},{25,17},{2,10},{10... | collective-permute-start | bytes 8847368 | tf_op jit(solution)/shard_map/ppermute | solution.py:697
  55.1 16.6 %collective-permute-start.7 = (bf16[3072,384]{1,0:T(8,128)(2,1)}, bf16[3072,384]{1,0:T(8,128)(2,1)S(1)}, u32[]{:S(2)}, u32[]{:S(2)}) collective-permute-start(bf16[3072,384]{1,0:T(8,128)(2,1)} %get-tuple-element.130), channel_id=1, source_target_pairs={{0,8},{8,0},{16,24},{24,16},{1,9},{9,1},{17,25},{25,17},{2,10},{10... | collective-permute-start | bytes 7077896 | tf_op jit(solution)/shard_map/ppermute | solution.py:697
  55.6 8.6 %copy-start.6 = (s32[5]{0:T(128)S(1)}, s32[5]{0:T(128)}, u32[]{:S(2)}) copy-start(s32[5]{0:T(128)} %stack.23.refs_0_.pos_ref) | copy-start | bytes 64
  55.6 8.6 %copy-start.10 = (bf16[1280,384]{1,0:T(8,128)(2,1)S(1)}, bf16[1280,384]{1,0:T(8,128)(2,1)}, u32[]{:S(2)}) copy-start(bf16[1280,384]{1,0:T(8,128)(2,1)} %get-tuple-element.132.refs_1_) | copy-start | bytes 2949124
  66.7 5.0 %copy-start.7 = (bf16[3072,384]{1,0:T(8,128)(2,1)S(1)}, bf16[3072,384]{1,0:T(8,128)(2,1)}, u32[]{:S(2)}) copy-start(bf16[3072,384]{1,0:T(8,128)(2,1)} %get-tuple-element.129.refs_0_) | copy-start | bytes 7077892
  68.8 13.2 %collective-permute-start.10 = (bf16[640,384]{1,0:T(8,128)(2,1)S(1)}, bf16[640,384]{1,0:T(8,128)(2,1)S(1)}, u32[]{:S(2)}, u32[]{:S(2)}) collective-permute-start(bf16[640,384]{1,0:T(8,128)(2,1)S(1)} %get-tuple-element.140), channel_id=1, source_target_pairs={{0,2},{1,3},{2,0},{3,1},{4,6},{5,7},{6,4},{7,5},{8,10},{9,11},{10,... | collective-permute-start | bytes 1474568 | tf_op jit(solution)/shard_map/ppermute | solution.py:700
  70.2 25.0 %collective-permute-start.13 = (bf16[1280,384]{1,0:T(8,128)(2,1)}, bf16[1280,384]{1,0:T(8,128)(2,1)}, u32[]{:S(2)}, u32[]{:S(2)}) collective-permute-start(bf16[1280,384]{1,0:T(8,128)(2,1)} %get-tuple-element.134.refs_2_), channel_id=1, source_target_pairs={{0,16},{8,24},{16,0},{24,8},{1,17},{9,25},{17,1},{25,9},{2,18},{10... | collective-permute-start | bytes 2949128 | tf_op jit(solution)/shard_map/ppermute | solution.py:697
  71.7 2.7 %copy-start.9 = (bf16[768,768]{1,0:T(8,128)(2,1)S(1)}, bf16[768,768]{1,0:T(8,128)(2,1)}, u32[]{:S(2)}) copy-start(bf16[768,768]{1,0:T(8,128)(2,1)} %get-tuple-element.128.refs_1_) | copy-start | bytes 3538948
  71.7 2.7 %copy-start.15 = (bf16[768,768]{1,0:T(8,128)(2,1)S(1)}, bf16[768,768]{1,0:T(8,128)(2,1)}, u32[]{:S(2)}) copy-start(bf16[768,768]{1,0:T(8,128)(2,1)} %get-tuple-element.122.refs_3_.refs_1_) | copy-start | bytes 3538948
  71.7 2.7 %copy-start.16 = (bf16[768,768]{1,0:T(8,128)(2,1)S(1)}, bf16[768,768]{1,0:T(8,128)(2,1)}, u32[]{:S(2)}) copy-start(bf16[768,768]{1,0:T(8,128)(2,1)} %get-tuple-element.123.refs_4_.refs_2_) | copy-start | bytes 3538948
  71.7 2.7 %copy-start.18 = (bf16[256,768]{1,0:T(8,128)(2,1)S(1)}, bf16[256,768]{1,0:T(8,128)(2,1)}, u32[]{:S(2)}) copy-start(bf16[256,768]{1,0:T(8,128)(2,1)} %get-tuple-element.121.refs_3_.refs_2_.refs_0_) | copy-start | bytes 1179652
  73.9 29.2 %collective-permute-start.12 = (bf16[1536,384]{1,0:T(8,128)(2,1)}, bf16[1536,384]{1,0:T(8,128)(2,1)}, u32[]{:S(2)}, u32[]{:S(2)}) collective-permute-start(bf16[1536,384]{1,0:T(8,128)(2,1)} %get-tuple-element.135.refs_5_), channel_id=1, source_target_pairs={{0,1},{1,0},{2,3},{3,2},{4,5},{5,4},{6,7},{7,6},{8,9},{9,8},{10,11... | collective-permute-start | bytes 3538952 | tf_op jit(solution)/shard_map/ppermute | solution.py:700
  74.4 2.3 %copy-start = (bf16[768,768]{1,0:T(8,128)(2,1)S(1)}, bf16[768,768]{1,0:T(8,128)(2,1)}, u32[]{:S(2)}) copy-start(bf16[768,768]{1,0:T(8,128)(2,1)} %refs_4_.1) | copy-start | bytes 3538948
  76.6 9.1 %collective-permute-start.9 = (bf16[8,288,384]{2,1,0:T(8,128)(2,1)S(1)}, bf16[8,288,384]{2,1,0:T(8,128)(2,1)S(1)}, u32[]{:S(2)}, u32[]{:S(2)}) collective-permute-start(bf16[8,288,384]{2,1,0:T(8,128)(2,1)S(1)} %shard_map.347.refs_11_), channel_id=1, source_target_pairs={{0,8},{8,0},{16,24},{24,16},{1,9},{9,1},{17,25},{25,17},{2,10},{10... | collective-permute-start | bytes 5308424 | tf_op jit(solution)/shard_map/ppermute | solution.py:697
  83.4 36.4 %collective-permute-start.19 = (bf16[320,384]{1,0:T(8,128)(2,1)}, bf16[320,384]{1,0:T(8,128)(2,1)}, u32[]{:S(2)}, u32[]{:S(2)}) collective-permute-start(bf16[320,384]{1,0:T(8,128)(2,1)} %get-tuple-element.141.refs_8_), channel_id=1, source_target_pairs={{0,4},{1,5},{2,6},{3,7},{4,0},{5,1},{6,2},{7,3},{8,12},{9,13},{10,... | collective-permute-start | bytes 737288 | tf_op jit(solution)/shard_map/ppermute | solution.py:700
  88.8 19.4 %collective-permute-start.11 = (bf16[800,384]{1,0:T(8,128)(2,1)S(1)}, bf16[800,384]{1,0:T(8,128)(2,1)S(1)}, u32[]{:S(2)}, u32[]{:S(2)}) collective-permute-start(bf16[800,384]{1,0:T(8,128)(2,1)S(1)} %get-tuple-element.143), channel_id=1, source_target_pairs={{0,16},{8,24},{16,0},{24,8},{1,17},{9,25},{17,1},{25,9},{2,18},{10... | collective-permute-start | bytes 1843208 | tf_op jit(solution)/shard_map/ppermute | solution.py:697
  90.3 27.6 %collective-permute-start.14 = (bf16[896,384]{1,0:T(8,128)(2,1)}, bf16[896,384]{1,0:T(8,128)(2,1)}, u32[]{:S(2)}, u32[]{:S(2)}) collective-permute-start(bf16[896,384]{1,0:T(8,128)(2,1)} %get-tuple-element.146.refs_2_), channel_id=1, source_target_pairs={{0,1},{1,0},{2,3},{3,2},{4,5},{5,4},{6,7},{7,6},{8,9},{9,8},{10,11... | collective-permute-start | bytes 2064392 | tf_op jit(solution)/shard_map/ppermute | solution.py:700
  96.7 12.8 %collective-permute-start.15 = (bf16[640,384]{1,0:T(8,128)(2,1)S(1)}, bf16[640,384]{1,0:T(8,128)(2,1)S(1)}, u32[]{:S(2)}, u32[]{:S(2)}) collective-permute-start(bf16[640,384]{1,0:T(8,128)(2,1)S(1)} %get-tuple-element.147.refs_2_), channel_id=1, source_target_pairs={{0,2},{1,3},{2,0},{3,1},{4,6},{5,7},{6,4},{7,5},{8,10},{9,11},{10,... | collective-permute-start | bytes 1474568 | tf_op jit(solution)/shard_map/ppermute | solution.py:700
  104.8 15.7 %collective-permute-start.20 = (bf16[768,384]{1,0:T(8,128)(2,1)S(1)}, bf16[768,384]{1,0:T(8,128)(2,1)S(1)}, u32[]{:S(2)}, u32[]{:S(2)}) collective-permute-start(bf16[768,384]{1,0:T(8,128)(2,1)S(1)} %get-tuple-element.148.refs_3_), channel_id=1, source_target_pairs={{0,16},{8,24},{16,0},{24,8},{1,17},{9,25},{17,1},{25,9},{2,18},{10... | collective-permute-start | bytes 1769480 | tf_op jit(solution)/shard_map/ppermute | solution.py:697
  108.9 16.0 %collective-permute-start.16 = (bf16[416,384]{1,0:T(8,128)(2,1)S(1)}, bf16[416,384]{1,0:T(8,128)(2,1)S(1)}, u32[]{:S(2)}, u32[]{:S(2)}) collective-permute-start(bf16[416,384]{1,0:T(8,128)(2,1)S(1)} %get-tuple-element.153.refs_2_), channel_id=1, source_target_pairs={{0,1},{1,0},{2,3},{3,2},{4,5},{5,4},{6,7},{7,6},{8,9},{9,8},{10,11... | collective-permute-start | bytes 958472 | tf_op jit(solution)/shard_map/ppermute | solution.py:700
  110.2 11.7 %collective-permute-start.18 = (bf16[320,384]{1,0:T(8,128)(2,1)S(1)}, bf16[320,384]{1,0:T(8,128)(2,1)S(1)}, u32[]{:S(2)}, u32[]{:S(2)}) collective-permute-start(bf16[320,384]{1,0:T(8,128)(2,1)S(1)} %get-tuple-element.154.refs_3_), channel_id=1, source_target_pairs={{0,4},{1,5},{2,6},{3,7},{4,0},{5,1},{6,2},{7,3},{8,12},{9,13},{10,... | collective-permute-start | bytes 737288 | tf_op jit(solution)/shard_map/ppermute | solution.py:700
  119.1 5.8 %collective-permute-start.17 = (bf16[192,384]{1,0:T(8,128)(2,1)S(1)}, bf16[192,384]{1,0:T(8,128)(2,1)S(1)}, u32[]{:S(2)}, u32[]{:S(2)}) collective-permute-start(bf16[192,384]{1,0:T(8,128)(2,1)S(1)} %get-tuple-element.157.refs_6_), channel_id=1, source_target_pairs={{0,16},{8,24},{16,0},{24,8},{1,17},{9,25},{17,1},{25,9},{2,18},{10... | collective-permute-start | bytes 442376 | tf_op jit(solution)/shard_map/ppermute | solution.py:697
  119.7 16.7 %collective-permute-start.22 = (bf16[256,384]{1,0:T(8,128)(2,1)S(1)}, bf16[256,384]{1,0:T(8,128)(2,1)S(1)}, u32[]{:S(2)}, u32[]{:S(2)}) collective-permute-start(bf16[256,384]{1,0:T(8,128)(2,1)S(1)} %get-tuple-element.167), channel_id=1, source_target_pairs={{0,2},{1,3},{2,0},{3,1},{4,6},{5,7},{6,4},{7,5},{8,10},{9,11},{10,... | collective-permute-start | bytes 589832 | tf_op jit(solution)/shard_map/ppermute | solution.py:700
  123.3 10.5 %collective-permute-start.23 = (bf16[384,384]{1,0:T(8,128)(2,1)S(1)}, bf16[384,384]{1,0:T(8,128)(2,1)S(1)}, u32[]{:S(2)}, u32[]{:S(2)}) collective-permute-start(bf16[384,384]{1,0:T(8,128)(2,1)S(1)} %get-tuple-element.161.refs_5_), channel_id=1, source_target_pairs={{0,2},{1,3},{2,0},{3,1},{4,6},{5,7},{6,4},{7,5},{8,10},{9,11},{10,... | collective-permute-start | bytes 884744 | tf_op jit(solution)/shard_map/ppermute | solution.py:700
  123.3 6.9 %collective-permute-start.24 = (bf16[320,384]{1,0:T(8,128)(2,1)S(1)}, bf16[320,384]{1,0:T(8,128)(2,1)S(1)}, u32[]{:S(2)}, u32[]{:S(2)}) collective-permute-start(bf16[320,384]{1,0:T(8,128)(2,1)S(1)} %get-tuple-element.170), channel_id=1, source_target_pairs={{0,1},{1,0},{2,3},{3,2},{4,5},{5,4},{6,7},{7,6},{8,9},{9,8},{10,11... | collective-permute-start | bytes 737288 | tf_op jit(solution)/shard_map/ppermute | solution.py:700
  125.6 13.6 %collective-permute-start.21 = (bf16[320,384]{1,0:T(8,128)(2,1)S(1)}, bf16[320,384]{1,0:T(8,128)(2,1)S(1)}, u32[]{:S(2)}, u32[]{:S(2)}) collective-permute-start(bf16[320,384]{1,0:T(8,128)(2,1)S(1)} %get-tuple-element.166.refs_4_), channel_id=1, source_target_pairs={{0,2},{1,3},{2,0},{3,1},{4,6},{5,7},{6,4},{7,5},{8,10},{9,11},{10,... | collective-permute-start | bytes 737288 | tf_op jit(solution)/shard_map/ppermute | solution.py:700
  134.4 5.4 %collective-permute-start.27 = (bf16[80,384]{1,0:T(8,128)(2,1)S(1)}, bf16[80,384]{1,0:T(8,128)(2,1)S(1)}, u32[]{:S(2)}, u32[]{:S(2)}) collective-permute-start(bf16[80,384]{1,0:T(8,128)(2,1)S(1)} %get-tuple-element.180), channel_id=1, source_target_pairs={{0,16},{8,24},{16,0},{24,8},{1,17},{9,25},{17,1},{25,9},{2,18},{10... | collective-permute-start | bytes 184328 | tf_op jit(solution)/shard_map/ppermute | solution.py:697
  136.0 7.0 %collective-permute-start.26 = (bf16[192,384]{1,0:T(8,128)(2,1)S(1)}, bf16[192,384]{1,0:T(8,128)(2,1)S(1)}, u32[]{:S(2)}, u32[]{:S(2)}) collective-permute-start(bf16[192,384]{1,0:T(8,128)(2,1)S(1)} %get-tuple-element.171.refs_6_), channel_id=1, source_target_pairs={{0,4},{1,5},{2,6},{3,7},{4,0},{5,1},{6,2},{7,3},{8,12},{9,13},{10,... | collective-permute-start | bytes 442376 | tf_op jit(solution)/shard_map/ppermute | solution.py:700
  143.6 5.2 %collective-permute-start.28 = (bf16[192,384]{1,0:T(8,128)(2,1)S(1)}, bf16[192,384]{1,0:T(8,128)(2,1)S(1)}, u32[]{:S(2)}, u32[]{:S(2)}) collective-permute-start(bf16[192,384]{1,0:T(8,128)(2,1)S(1)} %shard_map.361), channel_id=1, source_target_pairs={{0,16},{8,24},{16,0},{24,8},{1,17},{9,25},{17,1},{25,9},{2,18},{10... | collective-permute-start | bytes 442376 | tf_op jit(solution)/shard_map/ppermute | solution.py:697
  144.9 10.4 %collective-permute-start.25 = (bf16[304,384]{1,0:T(8,128)(2,1)S(1)}, bf16[304,384]{1,0:T(8,128)(2,1)S(1)}, u32[]{:S(2)}, u32[]{:S(2)}) collective-permute-start(bf16[304,384]{1,0:T(8,128)(2,1)S(1)} %get-tuple-element.176.refs_4_), channel_id=1, source_target_pairs={{0,4},{1,5},{2,6},{3,7},{4,0},{5,1},{6,2},{7,3},{8,12},{9,13},{10,... | collective-permute-start | bytes 700424 | tf_op jit(solution)/shard_map/ppermute | solution.py:700
  144.9 5.9 %collective-permute-start.30 = (bf16[240,384]{1,0:T(8,128)(2,1)S(1)}, bf16[240,384]{1,0:T(8,128)(2,1)S(1)}, u32[]{:S(2)}, u32[]{:S(2)}) collective-permute-start(bf16[240,384]{1,0:T(8,128)(2,1)S(1)} %get-tuple-element.181.refs_2_), channel_id=1, source_target_pairs={{0,16},{8,24},{16,0},{24,8},{1,17},{9,25},{17,1},{25,9},{2,18},{10... | collective-permute-start | bytes 552968 | tf_op jit(solution)/shard_map/ppermute | solution.py:697
  148.9 2.1 %collective-permute-start.29 = (bf16[384,384]{1,0:T(8,128)(2,1)S(1)}, bf16[384,384]{1,0:T(8,128)(2,1)S(1)}, u32[]{:S(2)}, u32[]{:S(2)}) collective-permute-start(bf16[384,384]{1,0:T(8,128)(2,1)S(1)} %pad_maximum_fusion.1), channel_id=1, source_target_pairs={{0,8},{8,0},{16,24},{24,16},{1,9},{9,1},{17,25},{25,17},{2,10},{10... | collective-permute-start | bytes 884744 | tf_op jit(solution)/shard_map/ppermute | solution.py:697
  151.0 1.8 %collective-permute-start.31 = (bf16[480,384]{1,0:T(8,128)(2,1)S(1)}, bf16[480,384]{1,0:T(8,128)(2,1)S(1)}, u32[]{:S(2)}, u32[]{:S(2)}) collective-permute-start(bf16[480,384]{1,0:T(8,128)(2,1)S(1)} %pad_maximum_fusion), channel_id=1, source_target_pairs={{0,8},{8,0},{16,24},{24,16},{1,9},{9,1},{17,25},{25,17},{2,10},{10... | collective-permute-start | bytes 1105928 | tf_op jit(solution)/shard_map/ppermute | solution.py:697
  151.3 3.9 %copy-start.4 = (f32[96,3072]{1,0:T(8,128)}, f32[96,3072]{1,0:T(8,128)S(1)}, u32[]{:S(2)}) copy-start(f32[96,3072]{1,0:T(8,128)S(1)} %slice_dynamic-update-slice_fusion.refs_5_) | copy-start | bytes 3538948
  153.1 2.8 %copy-start.2 = (f32[384,768]{1,0:T(8,128)}, f32[384,768]{1,0:T(8,128)S(1)}, u32[]{:S(2)}) copy-start(f32[384,768]{1,0:T(8,128)S(1)} %maximum_maximum_fusion.refs_6_) | copy-start | bytes 3538948
  155.9 5.8 %collective-permute-start.33 = (bf16[144,384]{1,0:T(8,128)(2,1)S(1)}, bf16[144,384]{1,0:T(8,128)(2,1)S(1)}, u32[]{:S(2)}, u32[]{:S(2)}) collective-permute-start(bf16[144,384]{1,0:T(8,128)(2,1)S(1)} %constant_dynamic-update-slice_fusion), channel_id=1, source_target_pairs={{0,16},{8,24},{16,0},{24,8},{1,17},{9,25},{17,1},{25,9},{2,18},{10... | collective-permute-start | bytes 331784 | tf_op jit(solution)/shard_map/ppermute | solution.py:697
  156.3 5.5 %collective-permute-start.34 = (bf16[144,384]{1,0:T(8,128)(2,1)S(1)}, bf16[144,384]{1,0:T(8,128)(2,1)S(1)}, u32[]{:S(2)}, u32[]{:S(2)}) collective-permute-start(bf16[144,384]{1,0:T(8,128)(2,1)S(1)} %constant_dynamic-update-slice_fusion), channel_id=1, source_target_pairs={{0,24},{8,16},{16,8},{24,0},{1,25},{9,17},{17,9},{25,1},{2,26},{10... | collective-permute-start | bytes 331784 | tf_op jit(solution)/shard_map/ppermute | solution.py:697
  156.7 5.1 %collective-permute-start.32 = (bf16[176,384]{1,0:T(8,128)(2,1)S(1)}, bf16[176,384]{1,0:T(8,128)(2,1)S(1)}, u32[]{:S(2)}, u32[]{:S(2)}) collective-permute-start(bf16[176,384]{1,0:T(8,128)(2,1)S(1)} %pad_maximum_fusion.5), channel_id=1, source_target_pairs={{0,8},{8,0},{16,24},{24,16},{1,9},{9,1},{17,25},{25,17},{2,10},{10... | collective-permute-start | bytes 405512 | tf_op jit(solution)/shard_map/ppermute | solution.py:697
  (13 other events, 21.4 us)
